TPU v7x, 32 devices: a whole 2x2x4 slice. The times are simulated.
32 devices in a mesh: dp: 2 (over x), ctx: 4 (over z), exp: 4 (over y, core).
Axes of the slice: x: 2, y: 2, z: 4, core: 2. Of those that a mesh axis runs over, the one named last changes fastest.
Arguments:
- tokens: bfloat16 [16, 1024, 2048], P(('dp', 'exp'), 'ctx'), may hold values from -6 to 6
- segments: int32 [16, 1024], P(('dp', 'exp')), may hold values from 0 to 5, as said below
- routes: int32 [16, 1024, 2], P(('dp', 'exp'), 'ctx'), may hold values from 0 to 3, all different within a row; in each aligned block of 256 rows (0 to 255, 256 to 511, ..., all dimensions but the last counted through in order) at most 160 rows name the same one
- attn_norm: float32 [2048], replicated, may hold values from 0.25 to 1.75
- query_weight: bfloat16 [2048, 2048], P(('dp', 'ctx', 'exp')), may hold values from -0.125 to 0.125
- key_weight: bfloat16 [2048, 2048], P(('dp', 'ctx', 'exp')), may hold values from -0.125 to 0.125
- value_weight: bfloat16 [2048, 2048], P(('dp', 'ctx', 'exp')), may hold values from -0.125 to 0.125
- output_weight: bfloat16 [2048, 2048], P(('dp', 'ctx', 'exp')), may hold values from -1 to 1
- expert_norm: float32 [2048], replicated, may hold values from 0.25 to 1.75
- router: bfloat16 [2048, 4], replicated, may hold values from -0.079589844 to 0.079589844
- gate_weight: bfloat16 [4, 2048, 5632], P('exp', None, 'dp'), may hold values from -0.125 to 0.125
- up_weight: bfloat16 [4, 2048, 5632], P('exp', None, 'dp'), may hold values from -0.125 to 0.125
- down_weight: bfloat16 [4, 5632, 2048], P('exp', 'dp'), may hold values from -0.15625 to 0.15625
- grad_out: bfloat16 [16, 1024, 2048], P(('dp', 'exp'), 'ctx'), may hold values from -6 to 6
Outputs:
- output: bfloat16 [16, 1024, 2048], P(('dp', 'exp'), 'ctx')
- grad_tokens: float32 [16, 1024, 2048], P(('dp', 'exp'), 'ctx')
- grad_attn_norm: float32 [2048], P(('dp', 'ctx', 'exp'))
- grad_query: float32 [2048, 2048], P(('dp', 'ctx', 'exp'))
- grad_key: float32 [2048, 2048], P(('dp', 'ctx', 'exp'))
- grad_value: float32 [2048, 2048], P(('dp', 'ctx', 'exp'))
- grad_output: float32 [2048, 2048], P(('dp', 'ctx', 'exp'))
- grad_expert_norm: float32 [2048], P(('dp', 'ctx', 'exp'))
- grad_router: float32 [2048, 4], P(('dp', 'ctx', 'exp'))
- grad_gate: float32 [4, 2048, 5632], P('exp', 'ctx', 'dp')
- grad_up: float32 [4, 2048, 5632], P('exp', 'ctx', 'dp')
- grad_down: float32 [4, 5632, 2048], P('exp', 'dp', 'ctx')
Inputs may be any that keep to these rules, and one draw needn't show every extreme that they name: `segments`: segment numbers start at 0 and never fall along a sequence; a document has 200 to 2000 positions, except the last of a sequence, which may be shorter; in each group of 2 consecutive sequences one, drawn from the seed, is a single document; in every draw one other sequence, drawn from the seed, is made of documents of exactly 200 positions. `routes`: A token names 2 different experts. In each aligned block of 256 rows (one sequence's positions on one device) no expert is named more than 160 times, a bound that some block reaches.
All inputs are finite; a program needn't handle non-finite values.
Results may differ from a plain program's by a relative error of at most 0.02.
Values may be sent and summed in bfloat16 or wider, within the bound.
A program may use at most 448 MiB of HBM per device.

v0:
```python
import jax
import jax.numpy as jnp
from jax import lax
from jax.sharding import PartitionSpec as P

HEADS = 16


epsilon = 1e-05
theta_base = 10000.0
masked_score = -1e30


def product(matrix_one, matrix_two):
    return jnp.dot(matrix_one, matrix_two, preferred_element_type=jnp.float32)


def rotary_tables(positions, head_size):
    half_size = head_size // 2
    frequency = theta_base ** (-jnp.arange(half_size, dtype=jnp.float32) / half_size)
    angles = positions[:, None] * frequency[None, :]
    return (jnp.cos(angles)[:, None, :], jnp.sin(angles)[:, None, :])


def rotate(values, cosine_table, sine_table):
    half_size = values.shape[-1] // 2
    front_half = values[..., :half_size]
    back_half = values[..., half_size:]
    return jnp.concatenate(
        [
            front_half * cosine_table - back_half * sine_table,
            back_half * cosine_table + front_half * sine_table,
        ],
        axis=-1,
    )


def norm_backward(grad_rows, normed, inverse, gain):
    weighted = grad_rows * gain
    mean_term = jnp.mean(weighted * normed, axis=-1, keepdims=True)
    return (inverse * (weighted - normed * mean_term), jnp.sum(grad_rows * normed, axis=0))


def on_device(
    tokens,
    segments,
    routes,
    attn_norm,
    query_weight,
    key_weight,
    value_weight,
    output_weight,
    expert_norm,
    router,
    gate_weight,
    up_weight,
    down_weight,
    grad_out,
):
    seq_count, seq_dev, model_width = tokens.shape
    token_count = seq_count * seq_dev
    head_size = model_width // HEADS
    score_scale = head_size ** (-0.5)
    experts = router.shape[1]
    topk_count = routes.shape[2]
    capacity = 5 * seq_dev * topk_count // (4 * experts)
    slot_count = experts * seq_count * capacity
    ctx_index = lax.axis_index("ctx")
    query_places = ctx_index * seq_dev + jnp.arange(seq_dev, dtype=jnp.int32)
    cosine_table, sine_table = rotary_tables(query_places.astype(jnp.float32), head_size)
    shape_heads = (seq_count, seq_dev, HEADS, head_size)
    full_query, full_key, full_value, full_output = (
        lax.all_gather(query_weight, ("dp", "ctx", "exp"), axis=0, tiled=True),
        lax.all_gather(key_weight, ("dp", "ctx", "exp"), axis=0, tiled=True),
        lax.all_gather(value_weight, ("dp", "ctx", "exp"), axis=0, tiled=True),
        lax.all_gather(output_weight, ("dp", "ctx", "exp"), axis=0, tiled=True),
    )
    token_float = tokens.reshape(token_count, model_width).astype(jnp.float32)
    inverse_one = lax.rsqrt(jnp.mean(token_float * token_float, axis=-1, keepdims=True) + epsilon)
    normed_one = token_float * inverse_one
    hidden_one = (normed_one * attn_norm).astype(jnp.bfloat16)
    query_rows = rotate(
        product(hidden_one, full_query).reshape(shape_heads), cosine_table, sine_table
    ).astype(jnp.bfloat16)
    key_rows = rotate(
        product(hidden_one, full_key).reshape(shape_heads), cosine_table, sine_table
    ).astype(jnp.bfloat16)
    value_rows = product(hidden_one, full_value).astype(jnp.bfloat16).reshape(shape_heads)
    all_keys, all_values = (
        lax.all_gather(key_rows, "ctx", axis=1, tiled=True),
        lax.all_gather(value_rows, "ctx", axis=1, tiled=True),
    )
    length = all_keys.shape[1]
    key_places = jnp.arange(length, dtype=jnp.int32)
    query_segments = lax.dynamic_slice_in_dim(segments, ctx_index * seq_dev, seq_dev, 1)
    visible = (query_segments[:, :, None] == segments[:, None, :]) & (
        key_places[None, None, :] <= query_places[None, :, None]
    )
    visible = visible[:, None, :, :]

    def masked_scores():
        raw_scores = (
            jnp.einsum("sqhd,skhd->shqk", query_rows, all_keys, preferred_element_type=jnp.float32)
            * score_scale
        )
        return jnp.where(visible, raw_scores, masked_score)

    scores = masked_scores()
    row_top = jnp.max(scores, axis=-1, keepdims=True)
    weights = jnp.exp(scores - row_top)
    row_total = jnp.sum(weights, axis=-1)
    summed = jnp.einsum(
        "shqk,skhd->sqhd",
        weights.astype(jnp.bfloat16),
        all_values,
        preferred_element_type=jnp.float32,
    )
    total_heads = jnp.transpose(row_total, (0, 2, 1))[..., None]
    attended = summed / total_heads
    mixed_heads = attended.astype(jnp.bfloat16).reshape(token_count, model_width)
    branch = product(mixed_heads, full_output)
    residual = token_float + branch
    inverse_two = lax.rsqrt(jnp.mean(residual * residual, axis=-1, keepdims=True) + epsilon)
    normed_two = residual * inverse_two
    hidden_two = (normed_two * expert_norm).astype(jnp.bfloat16)
    logits = product(hidden_two, router)
    flat_routes = routes.reshape(token_count, topk_count)
    expert_hot = flat_routes[:, :, None] == jnp.arange(experts, dtype=jnp.int32)[None, None, :]
    chosen = jnp.sum(jnp.where(expert_hot, logits[:, None, :], 0.0), axis=2)
    gate_values = jax.nn.softmax(chosen, axis=-1)
    pair_routes = routes.reshape(seq_count, seq_dev * topk_count)
    onehot = (
        pair_routes[:, :, None] == jnp.arange(experts, dtype=jnp.int32)[None, None, :]
    ).astype(jnp.int32)
    earlier = jnp.cumsum(onehot, axis=1) - onehot
    slot_rank = jnp.sum(earlier * onehot, axis=2)
    seq_ids = jnp.arange(seq_count, dtype=jnp.int32)[:, None]
    buffer_index = (pair_routes * (seq_count * capacity) + seq_ids * capacity + slot_rank).reshape(
        -1
    )
    pair_ids = jnp.arange(token_count * topk_count, dtype=jnp.int32)
    pair_of_slot = (
        jnp.full((slot_count,), token_count * topk_count, jnp.int32).at[buffer_index].set(pair_ids)
    )
    padded_hidden = jnp.concatenate([hidden_two, jnp.zeros((1, model_width), jnp.bfloat16)], axis=0)
    send_rows = padded_hidden[pair_of_slot // topk_count].reshape(
        experts, seq_count, capacity, model_width
    )
    arrived = lax.all_to_all(send_rows, "exp", split_axis=0, concat_axis=0, tiled=True)
    expert_input = lax.all_gather(
        arrived.reshape(slot_count, model_width), "dp", axis=0, tiled=True
    )
    gate_one = gate_weight[0]
    up_one = up_weight[0]
    down_one = down_weight[0]
    gate_pre = product(expert_input, gate_one)
    up_pre = product(expert_input, up_one)
    sigmoid_gate = jax.nn.sigmoid(gate_pre)
    silu_gate = gate_pre * sigmoid_gate
    hidden_units = (silu_gate * up_pre).astype(jnp.bfloat16)
    partial_rows = product(hidden_units, down_one)
    expert_rows = lax.psum_scatter(
        partial_rows.astype(jnp.bfloat16), "dp", scatter_dimension=0, tiled=True
    )
    returned = lax.all_to_all(
        expert_rows.reshape(experts, seq_count, capacity, model_width),
        "exp",
        split_axis=0,
        concat_axis=0,
        tiled=True,
    )
    pair_outputs = returned.reshape(slot_count, model_width)[buffer_index].reshape(
        token_count, topk_count, model_width
    )
    mixture = jnp.sum(gate_values[:, :, None] * pair_outputs.astype(jnp.float32), axis=1)
    output = (residual + mixture).astype(jnp.bfloat16).reshape(seq_count, seq_dev, model_width)
    grad_rows = grad_out.reshape(token_count, model_width).astype(jnp.float32)
    gate_grad = jnp.sum(grad_rows[:, None, :] * pair_outputs.astype(jnp.float32), axis=2)
    pair_grad = (
        (gate_values[:, :, None] * grad_rows[:, None, :])
        .astype(jnp.bfloat16)
        .reshape(token_count * topk_count, model_width)
    )
    padded_grad = jnp.concatenate([pair_grad, jnp.zeros((1, model_width), jnp.bfloat16)], axis=0)
    send_grad = padded_grad[pair_of_slot].reshape(experts, seq_count, capacity, model_width)
    arrived_grad = lax.all_to_all(send_grad, "exp", split_axis=0, concat_axis=0, tiled=True)
    expert_grad_in = lax.all_gather(
        arrived_grad.reshape(slot_count, model_width), "dp", axis=0, tiled=True
    )
    units_grad = jnp.einsum(
        "rd,fd->rf", expert_grad_in, down_one, preferred_element_type=jnp.float32
    )
    silu_slope = sigmoid_gate * (1.0 + gate_pre * (1.0 - sigmoid_gate))
    gate_pre_grad = (units_grad * up_pre * silu_slope).astype(jnp.bfloat16)
    up_pre_grad = (units_grad * silu_gate).astype(jnp.bfloat16)
    input_partial = jnp.einsum(
        "rf,df->rd", gate_pre_grad, gate_one, preferred_element_type=jnp.float32
    ) + jnp.einsum("rf,df->rd", up_pre_grad, up_one, preferred_element_type=jnp.float32)
    input_rows = lax.psum_scatter(
        input_partial.astype(jnp.bfloat16), "dp", scatter_dimension=0, tiled=True
    )
    returned_grad = lax.all_to_all(
        input_rows.reshape(experts, seq_count, capacity, model_width),
        "exp",
        split_axis=0,
        concat_axis=0,
        tiled=True,
    )
    pair_input_grad = returned_grad.reshape(slot_count, model_width)[buffer_index].reshape(
        token_count, topk_count, model_width
    )
    expert_part = jnp.sum(pair_input_grad.astype(jnp.float32), axis=1)
    gate_part = jnp.einsum(
        "rc,rf->cf", expert_input, gate_pre_grad, preferred_element_type=jnp.float32
    )
    up_part = jnp.einsum("rc,rf->cf", expert_input, up_pre_grad, preferred_element_type=jnp.float32)
    down_part = jnp.einsum(
        "rc,rf->cf", expert_grad_in, hidden_units, preferred_element_type=jnp.float32
    )
    expert_sums = lax.psum_scatter(
        jnp.concatenate([gate_part, up_part, down_part], axis=1).astype(jnp.bfloat16),
        "ctx",
        scatter_dimension=0,
        tiled=True,
    ).astype(jnp.float32)
    units_half = gate_one.shape[1]
    grad_gate = expert_sums[:, :units_half][None]
    grad_up = expert_sums[:, units_half : 2 * units_half][None]
    grad_down = jnp.transpose(expert_sums[:, 2 * units_half :])[None]
    gate_mean = jnp.sum(gate_values * gate_grad, axis=1, keepdims=True)
    chosen_grad = gate_values * (gate_grad - gate_mean)
    logit_grad = jnp.sum(jnp.where(expert_hot, chosen_grad[:, :, None], 0.0), axis=1).astype(
        jnp.bfloat16
    )
    router_grad = jnp.einsum(
        "td,te->de", hidden_two, logit_grad, preferred_element_type=jnp.float32
    )
    hidden_two_grad = expert_part + jnp.einsum(
        "te,de->td", logit_grad, router, preferred_element_type=jnp.float32
    )
    residual_grad, expert_norm_grad = norm_backward(
        hidden_two_grad, normed_two, inverse_two, expert_norm
    )
    residual_grad = residual_grad + grad_rows
    branch_grad = residual_grad.astype(jnp.bfloat16)
    output_weight_grad = jnp.einsum(
        "tc,td->cd", mixed_heads, branch_grad, preferred_element_type=jnp.float32
    )
    full_query, full_key, full_value, full_output = (
        lax.all_gather(query_weight, ("dp", "ctx", "exp"), axis=0, tiled=True),
        lax.all_gather(key_weight, ("dp", "ctx", "exp"), axis=0, tiled=True),
        lax.all_gather(value_weight, ("dp", "ctx", "exp"), axis=0, tiled=True),
        lax.all_gather(output_weight, ("dp", "ctx", "exp"), axis=0, tiled=True),
    )
    mixed_grad = (
        jnp.einsum("td,cd->tc", branch_grad, full_output, preferred_element_type=jnp.float32)
        .astype(jnp.bfloat16)
        .reshape(shape_heads)
    )
    delta_rows = jnp.sum(mixed_grad.astype(jnp.float32) * attended, axis=-1)
    unit_grad = (mixed_grad.astype(jnp.float32) / total_heads).astype(jnp.bfloat16)
    weights_again = jnp.exp(masked_scores() - row_top)
    prob_grad = jnp.einsum(
        "sqhd,skhd->shqk", unit_grad, all_values, preferred_element_type=jnp.float32
    )
    delta_scaled = jnp.transpose(delta_rows, (0, 2, 1)) / row_total
    score_grad = (weights_again * (prob_grad - delta_scaled[..., None])).astype(jnp.bfloat16)
    query_grad = (
        jnp.einsum("shqk,skhd->sqhd", score_grad, all_keys, preferred_element_type=jnp.float32)
        * score_scale
    )
    key_grad_all = (
        jnp.einsum("shqk,sqhd->skhd", score_grad, query_rows, preferred_element_type=jnp.float32)
        * score_scale
    )
    value_grad_all = jnp.einsum(
        "shqk,sqhd->skhd",
        weights_again.astype(jnp.bfloat16),
        unit_grad,
        preferred_element_type=jnp.float32,
    )
    key_grad, value_grad = (
        lax.psum_scatter(
            key_grad_all.astype(jnp.bfloat16), "ctx", scatter_dimension=1, tiled=True
        ).astype(jnp.float32),
        lax.psum_scatter(
            value_grad_all.astype(jnp.bfloat16), "ctx", scatter_dimension=1, tiled=True
        ).astype(jnp.float32),
    )
    query_pre = (
        rotate(query_grad, cosine_table, -sine_table)
        .astype(jnp.bfloat16)
        .reshape(token_count, model_width)
    )
    key_pre = (
        rotate(key_grad, cosine_table, -sine_table)
        .astype(jnp.bfloat16)
        .reshape(token_count, model_width)
    )
    value_pre = value_grad.astype(jnp.bfloat16).reshape(token_count, model_width)
    query_weight_grad = jnp.einsum(
        "tc,td->cd", hidden_one, query_pre, preferred_element_type=jnp.float32
    )
    key_weight_grad = jnp.einsum(
        "tc,td->cd", hidden_one, key_pre, preferred_element_type=jnp.float32
    )
    value_weight_grad = jnp.einsum(
        "tc,td->cd", hidden_one, value_pre, preferred_element_type=jnp.float32
    )
    hidden_one_grad = jnp.einsum(
        "td,cd->tc", query_pre, full_query, preferred_element_type=jnp.float32
    )
    hidden_one_grad = hidden_one_grad + jnp.einsum(
        "td,cd->tc", key_pre, full_key, preferred_element_type=jnp.float32
    )
    hidden_one_grad = hidden_one_grad + jnp.einsum(
        "td,cd->tc", value_pre, full_value, preferred_element_type=jnp.float32
    )
    token_grad, attn_norm_grad = norm_backward(hidden_one_grad, normed_one, inverse_one, attn_norm)
    token_grad = token_grad + residual_grad
    reduced = (
        lax.psum_scatter(query_weight_grad, ("dp", "ctx", "exp"), scatter_dimension=0, tiled=True),
        lax.psum_scatter(key_weight_grad, ("dp", "ctx", "exp"), scatter_dimension=0, tiled=True),
        lax.psum_scatter(value_weight_grad, ("dp", "ctx", "exp"), scatter_dimension=0, tiled=True),
        lax.psum_scatter(output_weight_grad, ("dp", "ctx", "exp"), scatter_dimension=0, tiled=True),
        lax.psum_scatter(attn_norm_grad, ("dp", "ctx", "exp"), scatter_dimension=0, tiled=True),
        lax.psum_scatter(expert_norm_grad, ("dp", "ctx", "exp"), scatter_dimension=0, tiled=True),
        lax.psum_scatter(router_grad, ("dp", "ctx", "exp"), scatter_dimension=0, tiled=True),
    )
    return (
        output,
        token_grad.reshape(seq_count, seq_dev, model_width),
        reduced[4],
        reduced[0],
        reduced[1],
        reduced[2],
        reduced[3],
        reduced[5],
        reduced[6],
        grad_gate,
        grad_up,
        grad_down,
    )


def solution(mesh):
    return jax.shard_map(
        on_device,
        mesh=mesh,
        in_specs=(
            P(("dp", "exp"), "ctx", None),
            P(("dp", "exp"), None),
            P(("dp", "exp"), "ctx", None),
            P(),
            P(("dp", "ctx", "exp"), None),
            P(("dp", "ctx", "exp"), None),
            P(("dp", "ctx", "exp"), None),
            P(("dp", "ctx", "exp"), None),
            P(),
            P(),
            P("exp", None, "dp"),
            P("exp", None, "dp"),
            P("exp", "dp", None),
            P(("dp", "exp"), "ctx", None),
        ),
        out_specs=(
            P(("dp", "exp"), "ctx", None),
            P(("dp", "exp"), "ctx", None),
            P(("dp", "ctx", "exp")),
            P(("dp", "ctx", "exp"), None),
            P(("dp", "ctx", "exp"), None),
            P(("dp", "ctx", "exp"), None),
            P(("dp", "ctx", "exp"), None),
            P(("dp", "ctx", "exp")),
            P(("dp", "ctx", "exp"), None),
            P("exp", "ctx", "dp"),
            P("exp", "ctx", "dp"),
            P("exp", "dp", "ctx"),
        ),
        check_vma=False,
    )
```

profile of v0, /device:TPU:1, one launch (start us, length us, event | category | flops | bytes accessed | tf_op | source)
XLA Modules:
  0.0 3226.7 jit_solution(8005535610840103553)
XLA Ops:
  15.1 75.9 %all-gather.15.cloned.1.call-done = bf16[2048,2048]{1,0:T(8,128)(2,1)} async-done(((bf16[64,2048]{1,0:T(8,128)(2,1)}), bf16[2048,2048]{1,0:T(8,128)(2,1)}) %all-gather.15.cloned.1.call-update) | async-done | bytes 8388624 | tf_op jit(solution)/shard_map/all_gather | solution.py:74
  103.3 66.8 %all-gather.13.cloned.1.call-done = bf16[2048,2048]{1,0:T(8,128)(2,1)} async-done(((bf16[64,2048]{1,0:T(8,128)(2,1)}), bf16[2048,2048]{1,0:T(8,128)(2,1)}) %all-gather.13.cloned.1.call-update) | async-done | bytes 8388624 | tf_op jit(solution)/shard_map/all_gather | solution.py:73
  201.7 47.5 %all-gather.9.cloned.1.call-done = bf16[2048,2048]{1,0:T(8,128)(2,1)} async-done(((bf16[64,2048]{1,0:T(8,128)(2,1)}), bf16[2048,2048]{1,0:T(8,128)(2,1)}) %all-gather.9.cloned.1.call-update) | async-done | bytes 8388624 | tf_op jit(solution)/shard_map/all_gather | solution.py:75
  275.3 123.3 %all-gather.17.cloned.1.call-done = bf16[2,1024,16,128]{1,3,2,0:T(8,128)(2,1)} async-done(((bf16[2,256,16,128]{1,3,2,0:T(8,128)(2,1)}), bf16[2,1024,16,128]{1,3,2,0:T(8,128)(2,1)}) %all-gather.17.cloned.1.call-update) | async-done | bytes 8388624 | tf_op jit(solution)/shard_map/all_gather | solution.py:90
  434.1 113.8 %all-gather.11.cloned.1.call-done = bf16[2,1024,16,128]{1,3,2,0:T(8,128)(2,1)} async-done(((bf16[2,256,16,128]{1,3,2,0:T(8,128)(2,1)}), bf16[2,1024,16,128]{1,3,2,0:T(8,128)(2,1)}) %all-gather.11.cloned.1.call-update) | async-done | bytes 8388624 | tf_op jit(solution)/shard_map/all_gather | solution.py:91
  572.0 54.7 %all-gather.19.cloned.1.call-done = bf16[2048,2048]{1,0:T(8,128)(2,1)} async-done(((bf16[64,2048]{1,0:T(8,128)(2,1)}), bf16[2048,2048]{1,0:T(8,128)(2,1)}) %all-gather.19.cloned.1.call-update) | async-done | bytes 8388624 | tf_op jit(solution)/shard_map/all_gather | solution.py:76
  643.1 64.9 %all_to_all.20 = bf16[4,2,160,2048]{3,2,1,0:T(8,128)(2,1)} all-to-all(bf16[4,2,160,2048]{3,2,1,0:T(8,128)(2,1)} %bitcast.189), channel_id=1, replica_groups=mesh['dp'=2,'ctx'=4,'exp'=4] {'exp'}, dimensions={0} | all-to-all | bytes 10485760 | tf_op jit(solution)/shard_map/all_to_all | solution.py:149
  749.8 65.8 %all_to_all.21 = bf16[4,2,160,2048]{3,2,1,0:T(8,128)(2,1)} all-to-all(bf16[4,2,160,2048]{3,2,1,0:T(8,128)(2,1)} %bitcast.190), channel_id=1, replica_groups=mesh['dp'=2,'ctx'=4,'exp'=4] {'exp'}, dimensions={0} | all-to-all | bytes 10485760 | tf_op jit(solution)/shard_map/all_to_all | solution.py:186
  912.6 55.0 %all-gather.23.cloned.1.call-done = bf16[2560,2048]{1,0:T(8,128)(2,1)} async-done(((bf16[1280,2048]{1,0:T(8,128)(2,1)}), bf16[2560,2048]{1,0:T(8,128)(2,1)}) %all-gather.23.cloned.1.call-update) | async-done | bytes 10485776 | tf_op jit(solution)/shard_map/all_gather | solution.py:187
  967.7 56.1 %multiply_convert_fusion.1 = (bf16[2560,2816]{1,0:T(8,128)(2,1)}, bf16[2560,2816]{1,0:T(8,128)(2,1)}, bf16[2560,2816]{1,0:T(8,128)(2,1)}) fusion(f32[2560,2816]{1,0:T(8,128)} %fusion.13, f32[2560,2816]{1,0:T(8,128)} %fusion.9, bf16[2560,2048]{1,0:T(8,128)(2,1)} %all-gather.23.cloned.1.call-done, bf16[1,2816,2048]{2,1,0:T(8,128)(2,1)} %param.26), kind=kOutput, calls=%fused_computation.10 | convolution fusion | flops 29636034560 | bytes 122945536 | tf_op jit(solution)/shard_map/rd,fd->rf/dot_general | solution.py:190
  1061.0 38.6 %fusion.11 = f32[2560,2048]{1,0:T(8,128)} fusion(bf16[2560,2816]{1,0:T(8,128)(2,1)} %get-tuple-element.81, bf16[1,2048,2816]{2,1,0:T(8,128)(2,1)} %param.24), kind=kOutput, calls=%fused_computation.26 | convolution fusion | flops 29527900160 | bytes 46923776 | tf_op jit(solution)/shard_map/rf,df->rd/dot_general | solution.py:196
  1138.3 44.7 %reduce-scatter.15.cloned.1.call-done = bf16[1280,2048]{1,0:T(8,128)(2,1)} async-done(((bf16[2560,2048]{1,0:T(8,128)(2,1)}), bf16[1280,2048]{1,0:T(8,128)(2,1)}) %reduce-scatter.15.cloned.1.call-update) | async-done | bytes 5242896 | tf_op jit(solution)/shard_map/reduce_scatter | solution.py:162
  1188.7 118.4 %reduce-scatter.17.cloned.1.call-done = bf16[1280,2048]{1,0:T(8,128)(2,1)} async-done(((bf16[2560,2048]{1,0:T(8,128)(2,1)}), bf16[1280,2048]{1,0:T(8,128)(2,1)}) %reduce-scatter.17.cloned.1.call-update) | async-done | bytes 5242896 | tf_op jit(solution)/shard_map/reduce_scatter | solution.py:199
  1471.5 39.7 %convolution_convert_fusion = bf16[2048,2816]{1,0:T(8,128)(2,1)} fusion(bf16[2560,2048]{1,0:T(8,128)(2,1)} %all-gather.23.cloned.1.call-done, bf16[2560,2816]{1,0:T(8,128)(2,1)} %get-tuple-element.82), kind=kOutput, calls=%fused_computation.30 | convolution fusion | flops 29533667328 | bytes 36438016 | tf_op jit(solution)/shard_map/rc,rf->cf/dot_general | solution.py:217
  1528.4 38.8 %convolution_convert_fusion.1 = bf16[2048,2816]{1,0:T(8,128)(2,1)} fusion(bf16[2560,2048]{1,0:T(8,128)(2,1)} %all-gather.21.cloned.1.call-done, bf16[2560,2816]{1,0:T(8,128)(2,1)} %get-tuple-element.80), kind=kOutput, calls=%fused_computation.31 | convolution fusion | flops 29533667328 | bytes 36438016 | tf_op jit(solution)/shard_map/rc,rf->cf/dot_general | solution.py:216
  1567.2 38.8 %convolution_convert_fusion.2 = bf16[2048,2816]{1,0:T(8,128)(2,1)} fusion(bf16[2560,2048]{1,0:T(8,128)(2,1)} %all-gather.21.cloned.1.call-done, bf16[2560,2816]{1,0:T(8,128)(2,1)} %get-tuple-element.81), kind=kOutput, calls=%fused_computation.32 | convolution fusion | flops 29533667328 | bytes 36438016 | tf_op jit(solution)/shard_map/rc,rf->cf/dot_general | solution.py:213
  1694.3 68.3 %reduce-scatter.21.cloned.1.call-done = bf16[2,256,16,128]{1,3,2,0:T(8,128)(2,1)} async-done(((bf16[2,1024,16,128]{1,3,2,0:T(8,128)(2,1)}), bf16[2,256,16,128]{1,3,2,0:T(8,128)(2,1)}) %reduce-scatter.21.cloned.1.call-update) | async-done | bytes 2097168 | tf_op jit(solution)/shard_map/reduce_scatter | solution.py:286
  1777.1 118.2 %reduce-scatter.31.cloned.1.call-done = f32[64,4]{1,0:T(8,128)} async-done(((f32[2048,4]{1,0:T(8,128)}), f32[64,4]{1,0:T(8,128)}) %reduce-scatter.31.cloned.1.call-update) | async-done | bytes 1040
  1925.8 46.1 %all-reduce.5 = (f32[2048]{0:T(1024)S(1)}, f32[2048]{0:T(1024)S(1)}) all-reduce(f32[2048]{0:T(1024)S(1)} %get-tuple-element.76, f32[2048]{0:T(1024)S(1)} %copy-done.50), channel_id=6, replica_groups=mesh['dp'=2,'ctx'=4,'exp'=4] {'dp','ctx','exp'}, use_global_device_ids=true, to_apply=%region_24.25.clone | all-reduce | flops 4096 | bytes 32768
  1979.7 489.2 %reduce-scatter.33.cloned.1.call-done = bf16[512,8448]{1,0:T(8,128)(2,1)} async-done(((bf16[2048,8448]{1,0:T(8,128)(2,1)}), bf16[512,8448]{1,0:T(8,128)(2,1)}) %reduce-scatter.33.cloned.1.call-update) | async-done | bytes 8650768
  2498.8 157.9 %reduce-scatter.29.cloned.1.call-done = f32[64,2048]{1,0:T(8,128)} async-done(((f32[2048,2048]{1,0:T(8,128)}), f32[64,2048]{1,0:T(8,128)}) %reduce-scatter.29.cloned.1.call-update) | async-done | bytes 524304 | tf_op jit(solution)/shard_map/reduce_scatter | solution.py:325
  2656.7 187.4 %reduce-scatter.25.cloned.1.call-done = f32[64,2048]{1,0:T(8,128)} async-done(((f32[2048,2048]{1,0:T(8,128)}), f32[64,2048]{1,0:T(8,128)}) %reduce-scatter.25.cloned.1.call-update) | async-done | bytes 524304 | tf_op jit(solution)/shard_map/reduce_scatter | solution.py:323
  2844.1 187.6 %reduce-scatter.23.cloned.1.call-done = f32[64,2048]{1,0:T(8,128)} async-done(((f32[2048,2048]{1,0:T(8,128)}), f32[64,2048]{1,0:T(8,128)}) %reduce-scatter.23.cloned.1.call-update) | async-done | bytes 524304 | tf_op jit(solution)/shard_map/reduce_scatter | solution.py:322
  3031.8 187.8 %reduce-scatter.27.cloned.1.call-done = f32[64,2048]{1,0:T(8,128)} async-done(((f32[2048,2048]{1,0:T(8,128)}), f32[64,2048]{1,0:T(8,128)}) %reduce-scatter.27.cloned.1.call-update) | async-done | bytes 524304 | tf_op jit(solution)/shard_map/reduce_scatter | solution.py:324
  (280 shorter events, 726.0 us)
Async XLA Ops:
  7.2 720.7 %copy-start = (bf16[2048,4]{0,1:T(4,128)(2,1)S(1)}, bf16[2048,4]{0,1:T(4,128)(2,1)}, u32[]{:S(2)}) copy-start(bf16[2048,4]{0,1:T(4,128)(2,1)} %param.23) | copy-start | bytes 49156
  7.2 83.8 %all-gather.15.cloned.1.call-start = ((), (), s32[]{:S(2)}) async-start(), calls=%async_computation.17 | async-start | bytes 8650752 | tf_op jit(solution)/shard_map/all_gather | solution.py:74
  7.9 162.2 %all-gather.13.cloned.1.call-start = ((), (), s32[]{:S(2)}) async-start(), calls=%async_computation.16 | async-start | bytes 8650752 | tf_op jit(solution)/shard_map/all_gather | solution.py:73
  8.7 240.5 %all-gather.9.cloned.1.call-start = ((), (), s32[]{:S(2)}) async-start(), calls=%async_computation.14 | async-start | bytes 8650752 | tf_op jit(solution)/shard_map/all_gather | solution.py:75
  9.4 389.2 %all-gather.17.cloned.1.call-start = ((), (), s32[]{:S(2)}) async-start(), calls=%async_computation.18 | async-start | bytes 10485760 | tf_op jit(solution)/shard_map/all_gather | solution.py:90
  12.5 182.3 %copy-start.29 = (f32[256,64]{0,1:T(8,128)}, f32[256,64]{0,1:T(8,128)S(1)}, u32[]{:S(2)}) copy-start(f32[256,64]{0,1:T(8,128)S(1)} %get-tuple-element.106) | copy-start | bytes 196612
  197.3 201.3 %copy-start.15 = (bf16[2,256,16,64]{1,3,2,0:T(8,128)(2,1)}, bf16[2,256,16,64]{1,3,2,0:T(8,128)(2,1)S(1)}, u32[]{:S(2)}) copy-start(bf16[2,256,16,64]{1,3,2,0:T(8,128)(2,1)S(1)} %get-tuple-element.90) | copy-start | bytes 3145732
  198.9 349.1 %all-gather.11.cloned.1.call-start = ((), (), s32[]{:S(2)}) async-start(), calls=%async_computation.15 | async-start | bytes 10485760 | tf_op jit(solution)/shard_map/all_gather | solution.py:91
  264.0 362.6 %all-gather.19.cloned.1.call-start = ((), (), s32[]{:S(2)}) async-start(), calls=%async_computation.19 | async-start | bytes 8650752 | tf_op jit(solution)/shard_map/all_gather | solution.py:76
  264.6 572.0 %all-gather.21.cloned.1.call-start = ((), (), s32[]{:S(2)}) async-start(), calls=%async_computation.20 | async-start | bytes 15728640 | tf_op jit(solution)/shard_map/all_gather | solution.py:150
  434.1 133.3 %copy-start.36 = (f32[2,16,256]{2,1,0:T(8,128)}, f32[2,16,256]{2,1,0:T(8,128)S(1)}, u32[]{:S(2)}) copy-start(f32[2,16,256]{2,1,0:T(8,128)S(1)} %fusion.2) | copy-start | bytes 98308
  708.0 259.7 %all-gather.23.cloned.1.call-start = ((), (), s32[]{:S(2)}) async-start(), calls=%async_computation.22 | async-start | bytes 15728640 | tf_op jit(solution)/shard_map/all_gather | solution.py:187
  815.7 367.3 %reduce-scatter.15.cloned.1.call-start = ((), (), s32[]{:S(2)}) async-start(), calls=%async_computation.21 | async-start | bytes 15728640 | tf_op jit(solution)/shard_map/reduce_scatter | solution.py:162
  1061.0 246.1 %reduce-scatter.17.cloned.1.call-start = ((), (), s32[]{:S(2)}) async-start(), calls=%async_computation.23 | async-start | bytes 15728640 | tf_op jit(solution)/shard_map/reduce_scatter | solution.py:199
  1183.0 124.0 %all-to-all-start.1 = ((bf16[4,2,160,2048]{3,2,1,0:T(8,128)(2,1)}), bf16[4,2,160,2048]{3,2,1,0:T(8,128)(2,1)}, u32[]{:S(2)}, u32[]{:S(2)}) async-start(bf16[4,2,160,2048]{3,2,1,0:T(8,128)(2,1)} %bitcast.202), calls=%async_computation.2 | async-start | bytes 10485760 | tf_op jit(solution)/shard_map/all_to_all | solution.py:165
  1307.0 64.4 %all-to-all-start.3 = ((bf16[4,2,160,2048]{3,2,1,0:T(8,128)(2,1)}), bf16[4,2,160,2048]{3,2,1,0:T(8,128)(2,1)}, u32[]{:S(2)}, u32[]{:S(2)}) async-start(bf16[4,2,160,2048]{3,2,1,0:T(8,128)(2,1)} %bitcast.201), calls=%async_computation.5 | async-start | bytes 10485760 | tf_op jit(solution)/shard_map/all_to_all | solution.py:202
  1312.8 342.9 %reduce-scatter.19.cloned.1.call-start = ((), (), s32[]{:S(2)}) async-start(), calls=%async_computation.24 | async-start | bytes 10485760 | tf_op jit(solution)/shard_map/reduce_scatter | solution.py:283
  1471.4 291.2 %reduce-scatter.21.cloned.1.call-start = ((), (), s32[]{:S(2)}) async-start(), calls=%async_computation.25 | async-start | bytes 10485760 | tf_op jit(solution)/shard_map/reduce_scatter | solution.py:286
  1528.3 367.0 %reduce-scatter.31.cloned.1.call-start = ((), (), s32[]{:S(2)}) async-start(), calls=%async_computation.30 | async-start | bytes 1081344
  1607.8 861.2 %reduce-scatter.33.cloned.1.call-start = ((), (), s32[]{:S(2)}) async-start(), calls=%async_computation.31 | async-start | bytes 43253760
  1631.2 1025.6 %reduce-scatter.29.cloned.1.call-start = ((), (), s32[]{:S(2)}) async-start(), calls=%async_computation.29 | async-start | bytes 17301504 | tf_op jit(solution)/shard_map/reduce_scatter | solution.py:325
  1643.3 1200.8 %reduce-scatter.25.cloned.1.call-start = ((), (), s32[]{:S(2)}) async-start(), calls=%async_computation.27 | async-start | bytes 17301504 | tf_op jit(solution)/shard_map/reduce_scatter | solution.py:323
  1677.0 1354.7 %reduce-scatter.23.cloned.1.call-start = ((), (), s32[]{:S(2)}) async-start(), calls=%async_computation.26 | async-start | bytes 17301504 | tf_op jit(solution)/shard_map/reduce_scatter | solution.py:322
  1694.2 1525.4 %reduce-scatter.27.cloned.1.call-start = ((), (), s32[]{:S(2)}) async-start(), calls=%async_computation.28 | async-start | bytes 17301504 | tf_op jit(solution)/shard_map/reduce_scatter | solution.py:324
  (57 other events, 966.4 us)
Sparse Core Ops, SparseCore 0:
  10.9 80.0 all-gather.14
  93.9 76.1 all-gather.12
  173.0 76.1 all-gather.8
  251.2 147.4 all-gather.16
  400.6 147.3 all-gather.10
  550.7 75.8 all-gather.18
  708.1 128.4 all-gather.20
  838.1 129.5 all-gather.22
  1061.1 121.8 reduce-scatter.14
  1185.1 121.8 reduce-scatter.16
  1471.5 143.5 reduce-scatter.18
  1617.4 145.1 reduce-scatter.20
  1764.8 130.3 reduce-scatter.30
  1897.6 571.2 reduce-scatter.32
  2471.8 184.9 reduce-scatter.28
  2659.5 184.5 reduce-scatter.24
  2847.0 184.7 reduce-scatter.22
  3034.6 184.9 reduce-scatter.26
where the time goes:
time: 3240 us; the launch traced here: 3230 us
  waiting for transfers between devices  2130 us (66%)
  matrix products  588 us (18%)
  blocking collectives  177 us (5%)
  local copies, waits for them, and re-layouts  173 us (5%)
  other arithmetic  126 us (4%)
    unnamed x20, waiting for transfers between devices  610 us
    reduce_scatter x1, waiting for transfers between devices, on_device(): lax.psum_scatter(value_weight_grad, ('dp', 'ctx', 'exp'), scatter_dimensi...  188 us
    reduce_scatter x1, waiting for transfers between devices, on_device(): lax.psum_scatter(query_weight_grad, ('dp', 'ctx', 'exp'), scatter_dimensi...  188 us
    reduce_scatter x1, waiting for transfers between devices, on_device(): lax.psum_scatter(key_weight_grad, ('dp', 'ctx', 'exp'), scatter_dimension...  187 us
    reduce_scatter x1, waiting for transfers between devices, on_device(): lax.psum_scatter(output_weight_grad, ('dp', 'ctx', 'exp'), scatter_dimens...  158 us
    dot_general x8, matrix products, product(): return jnp.dot(matrix_one, matrix_two, preferred_element_type=jnp.float32)  142 us
    all_gather x1, waiting for transfers between devices, on_device(): lax.all_gather(key_rows, 'ctx', axis=1, tiled=True)  123 us
    reduce_scatter x1, waiting for transfers between devices, on_device(): lax.psum_scatter(input_partial.astype(jnp.bfloat16), 'dp', scatter_dimens...  118 us
  transfers between devices with their start and end apart: 20, of which 18 were waited for; matrix products, arithmetic and copies ran while one was open for 21% of the time, Pallas kernels for 0%

commit v1 on v0

v1 whole, which is shorter than its diff:
```python
import functools

import jax
import jax.numpy as jnp
from jax import lax
from jax.experimental import pallas as pl
from jax.experimental.pallas import tpu as pltpu
from jax.sharding import Mesh, PartitionSpec as P

HEADS = 16
CORES = 2

epsilon = 1e-05
theta_base = 10000.0
masked_score = -1e30
bf16 = jnp.bfloat16
f32 = jnp.float32

PLANE = ("dp", "y", "core")
CHIP = ("r", "core")
SPREAD = ("dp", "seq", "y")
CTX = ("seq", "r")
EVERY = ("dp", "seq", "r", "y", "core")


def product(a, b):
    return jnp.dot(a, b, preferred_element_type=f32)


def product_t(a, b):
    return lax.dot_general(a, b, (((1,), (1,)), ((), ())), preferred_element_type=f32)


def t_product(a, b):
    return lax.dot_general(a, b, (((0,), (0,)), ((), ())), preferred_element_type=f32)


def swap(a, axis):
    return lax.ppermute(a, axis, [(0, 1), (1, 0)])


def halves(a, axis):
    size = a.shape[axis] // 2
    me = lax.axis_index("core")
    mine = lax.dynamic_slice_in_dim(a, me * size, size, axis)
    other = lax.dynamic_slice_in_dim(a, (1 - me) * size, size, axis)
    return mine, other


def by_core(mine, other, axis):
    first = lax.axis_index("core") == 0
    return jnp.concatenate([jnp.where(first, mine, other), jnp.where(first, other, mine)], axis=axis)


def chip_gather(a, axis, parts):
    if parts == 2:
        return by_core(a, swap(a, "core"), axis)
    return lax.all_gather(a, CHIP, axis=axis, tiled=True)


def chip_scatter(a, axis, parts):
    if parts == 2:
        mine, other = halves(a, axis)
        return mine.astype(f32) + swap(other, "core").astype(f32)
    return lax.psum_scatter(a, CHIP, scatter_dimension=axis, tiled=True).astype(f32)


def chip_exchange(a, split, concat, parts):
    if parts == 2:
        mine, other = halves(a, split)
        return by_core(mine, swap(other, "core"), concat)
    return lax.all_to_all(a, CHIP, split_axis=split, concat_axis=concat, tiled=True)


def core_exchange(a, split, concat):
    mine, other = halves(a, split)
    return by_core(mine, swap(other, "core"), concat)


def to_sequences(a):
    a = core_exchange(a, 1, 0)
    return lax.all_to_all(a, "seq", split_axis=0, concat_axis=0, tiled=True)


def from_sequences(a):
    a = lax.all_to_all(a, "seq", split_axis=0, concat_axis=0, tiled=True)
    return core_exchange(a, 0, 1)


def plane_scatter(rows, width):
    count = rows.shape[0] // 8
    blocks = rows.reshape(2, 2, 2, count, width)
    got = swap(blocks[:, :, 1], "core")
    held = (blocks[:, :, 0].astype(f32) + got.astype(f32)).astype(bf16)
    half = count // 2
    by_x = swap(held[1, 1, :half], "dp")
    by_y = swap(held[1, 1, half:], "y")
    to_x = jnp.concatenate(
        [held[1, 0, :half], (held[1, 0, half:].astype(f32) + by_y.astype(f32)).astype(bf16)], axis=0
    )
    to_y = jnp.concatenate(
        [(held[0, 1, :half].astype(f32) + by_x.astype(f32)).astype(bf16), held[0, 1, half:]], axis=0
    )
    from_x = swap(to_x, "dp")
    from_y = swap(to_y, "y")
    return held[0, 0].astype(f32) + from_x.astype(f32) + from_y.astype(f32)


def visible_block(seg_row, seg_col, start, rows, cols):
    row_place = start + lax.broadcasted_iota(jnp.int32, (rows, cols), 0)
    col_place = lax.broadcasted_iota(jnp.int32, (rows, cols), 1)
    return (seg_col == seg_row) & (col_place <= row_place)


def turned(u, cosine, sine):
    return u * cosine + pltpu.roll(u, u.shape[1] // 2, 1) * sine


def attend_kernel(scale, block, qp, kp, vp, cosine, sine, seg_row, seg_col, q_out, k_out, v_out, mixed):
    length = qp.shape[0]
    q_out[...] = turned(qp[...], cosine[...], sine[...]).astype(bf16)
    k_out[...] = turned(kp[...], cosine[...], sine[...]).astype(bf16)
    v_out[...] = vp[...].astype(bf16)
    for start in range(0, length, block):
        stop = start + block
        scores = product_t(q_out[start:stop, :], k_out[:stop, :]) * scale
        seen = visible_block(seg_row[:, :stop], seg_col[start:stop, :], start, block, stop)
        scores = jnp.where(seen, scores, masked_score)
        top = jnp.max(scores, axis=1, keepdims=True)
        weights = jnp.exp(scores - top)
        total = jnp.sum(weights, axis=1, keepdims=True)
        summed = product(weights.astype(bf16), v_out[:stop, :])
        mixed[start:stop, :] = (summed / total).astype(bf16)


def attend(qkv, cosine, sine, seg_row, seg_col, heads):
    length, head = qkv.shape[0], cosine.shape[1]
    block = min(256, length)

    def column(offset):
        return pl.BlockSpec((length, head), lambda h: (0, offset + h))

    def whole(shape):
        return pl.BlockSpec(shape, lambda h: (0, 0))

    out = jax.ShapeDtypeStruct((length, heads * head), bf16)
    pairs = length * (length + block) // 2 * heads
    return pl.pallas_call(
        functools.partial(attend_kernel, head**-0.5, block),
        grid=(heads,),
        in_specs=[
            column(0),
            column(heads),
            column(2 * heads),
            whole((length, head)),
            whole((length, head)),
            whole((1, length)),
            whole((length, 1)),
        ],
        out_specs=[column(0)] * 4,
        out_shape=[out] * 4,
        compiler_params=pltpu.CompilerParams(vmem_limit_bytes=48 * 2**20),
        cost_estimate=pl.CostEstimate(
            flops=4 * pairs * head, bytes_accessed=20 * length * heads * head, transcendentals=pairs
        ),
        name="attend",
    )(qkv, qkv, qkv, cosine, sine, seg_row, seg_col)


def attend_back_kernel(
    scale, block, q, k, v, mixed, dmixed, cosine, sine, seg_row, seg_col, dq_out, dk_out, dv_out, dk_sum, dv_sum
):
    length = q.shape[0]
    dk_sum[...] = jnp.zeros_like(dk_sum)
    dv_sum[...] = jnp.zeros_like(dv_sum)
    for start in range(0, length, block):
        stop = start + block
        scores = product_t(q[start:stop, :], k[:stop, :]) * scale
        seen = visible_block(seg_row[:, :stop], seg_col[start:stop, :], start, block, stop)
        scores = jnp.where(seen, scores, masked_score)
        top = jnp.max(scores, axis=1, keepdims=True)
        weights = jnp.exp(scores - top)
        inverse = 1.0 / jnp.sum(weights, axis=1, keepdims=True)
        grad = dmixed[start:stop, :].astype(f32)
        delta = jnp.sum(grad * mixed[start:stop, :].astype(f32), axis=1, keepdims=True) * inverse
        unit = (grad * inverse).astype(bf16)
        dweights = product_t(unit, v[:stop, :])
        dscores = (weights * (dweights - delta)).astype(bf16)
        dq = product(dscores, k[:stop, :]) * scale
        dq_out[start:stop, :] = turned(dq, cosine[start:stop, :], -sine[start:stop, :]).astype(bf16)
        dk_sum[:stop, :] += t_product(dscores, q[start:stop, :])
        dv_sum[:stop, :] += t_product(weights.astype(bf16), unit)
    dk_out[...] = turned(dk_sum[...] * scale, cosine[...], -sine[...]).astype(bf16)
    dv_out[...] = dv_sum[...].astype(bf16)


def attend_back(q, k, v, mixed, dmixed, cosine, sine, seg_row, seg_col, heads):
    length, head = q.shape[0], cosine.shape[1]
    block = min(256, length)
    column = pl.BlockSpec((length, head), lambda h: (0, h))

    def whole(shape):
        return pl.BlockSpec(shape, lambda h: (0, 0))

    out = jax.ShapeDtypeStruct((length, heads * head), bf16)
    pairs = length * (length + block) // 2 * heads
    return pl.pallas_call(
        functools.partial(attend_back_kernel, head**-0.5, block),
        grid=(heads,),
        in_specs=[column] * 5
        + [whole((length, head)), whole((length, head)), whole((1, length)), whole((length, 1))],
        out_specs=[column] * 3,
        out_shape=[out] * 3,
        scratch_shapes=[pltpu.VMEM((length, head), f32)] * 2,
        compiler_params=pltpu.CompilerParams(vmem_limit_bytes=48 * 2**20),
        cost_estimate=pl.CostEstimate(
            flops=10 * pairs * head, bytes_accessed=16 * length * heads * head, transcendentals=pairs
        ),
        name="attend_back",
    )(q, k, v, mixed, dmixed, cosine, sine, seg_row, seg_col)


def units_kernel(chunk, x, dy, gate, up, down, units, dgate, dup):
    gate_w, up_w, down_w = gate[...], up[...], down[...]

    def step(i, carry):
        rows = pl.ds(pl.multiple_of(i * chunk, chunk), chunk)
        gpre = product(x[rows, :], gate_w)
        upre = product(x[rows, :], up_w)
        dunits = product_t(dy[rows, :], down_w)
        s = jax.nn.sigmoid(gpre)
        silu = gpre * s
        units[rows, :] = (silu * upre).astype(bf16)
        dgate[rows, :] = (dunits * upre * (s * (1.0 + gpre * (1.0 - s)))).astype(bf16)
        dup[rows, :] = (dunits * silu).astype(bf16)
        return carry

    lax.fori_loop(0, x.shape[0] // chunk, step, 0)


def expert_units(x, dy, gate, up, down):
    rows, width = x.shape
    units = gate.shape[1]
    chunk = max(c for c in range(16, 513, 16) if rows % c == 0)
    tile = 256 if units % 256 == 0 else units
    once = pl.BlockSpec((rows, width), lambda j: (0, 0), pipeline_mode=pl.Buffered(1))
    out = jax.ShapeDtypeStruct((rows, units), bf16)
    return pl.pallas_call(
        functools.partial(units_kernel, chunk),
        grid=(units // tile,),
        in_specs=[
            once,
            once,
            pl.BlockSpec((width, tile), lambda j: (0, j)),
            pl.BlockSpec((width, tile), lambda j: (0, j)),
            pl.BlockSpec((tile, width), lambda j: (j, 0)),
        ],
        out_specs=[pl.BlockSpec((rows, tile), lambda j: (0, j))] * 3,
        out_shape=[out] * 3,
        compiler_params=pltpu.CompilerParams(vmem_limit_bytes=56 * 2**20),
        cost_estimate=pl.CostEstimate(
            flops=6 * rows * width * units,
            bytes_accessed=4 * rows * width + 6 * width * units + 6 * rows * units,
            transcendentals=rows * units,
        ),
        name="expert_units",
    )(x, dy, gate, up, down)


def counts_before(flags):
    rows = flags.reshape(-1, 128).astype(bf16)
    lanes = jnp.arange(128)
    inside = product(rows, (lanes[:, None] < lanes[None, :]).astype(bf16))
    lines = jnp.arange(rows.shape[0])
    earlier = (lines[None, :] < lines[:, None]).astype(f32)
    ahead = jnp.sum(earlier * jnp.sum(rows.astype(f32), axis=1)[None, :], axis=1)
    return (inside + ahead[:, None]).astype(jnp.int32).reshape(-1)


def norm_backward(grad_rows, normed, inverse, gain):
    weighted = grad_rows * gain
    mean_term = jnp.mean(weighted * normed, axis=-1, keepdims=True)
    return inverse * (weighted - normed * mean_term), jnp.sum(grad_rows * normed, axis=0)


def pick(a, index, axis):
    return lax.dynamic_index_in_dim(a, index, axis, keepdims=False)


def on_device(
    sizes,
    tokens,
    segments,
    routes,
    attn_norm,
    query_weight,
    key_weight,
    value_weight,
    output_weight,
    expert_norm,
    router,
    gate_weight,
    up_weight,
    down_weight,
    grad_out,
):
    dp_n, seq_n, r_n, y_n, core_n = sizes
    parts = r_n * core_n
    seq_count, seq_dev, width = tokens.shape
    piece = seq_dev // core_n
    length = segments.shape[1]
    home = seq_n * piece
    head = width // HEADS
    heads = HEADS // parts
    columns = width // parts
    experts = router.shape[1]
    topk = routes.shape[2]
    plane = 8 * home
    capacity = (5 * seq_dev * topk // (4 * experts)) * (plane // seq_dev)
    dp_i, seq_i, r_i, y_i, core_i = (lax.axis_index(a) for a in EVERY)
    group, member = seq_i // seq_count, seq_i % seq_count

    own_segments = lax.dynamic_slice_in_dim(segments, (seq_i * r_n + r_i) * seq_dev, seq_dev, 1)
    small = jnp.concatenate(
        [jnp.transpose(routes, (2, 0, 1)), own_segments[None]], axis=0
    ).reshape((topk + 1) * seq_count, seq_dev)
    small = lax.all_gather(small, EVERY, axis=0, tiled=True).reshape(
        dp_n, seq_n, r_n, y_n, core_n, topk + 1, seq_count, seq_dev
    )
    small = pick(pick(small, group, 4), member, 5)
    segment = pick(pick(small, dp_i, 0), y_i, 2)[:, :, topk].reshape(length)
    plane_routes = (
        pick(small, r_i, 2)[:, :, :, :topk]
        .reshape(dp_n, seq_n, y_n, topk, core_n, piece)
        .transpose(3, 0, 2, 4, 1, 5)
        .reshape(topk, dp_n, y_n, core_n, home)
    )

    local = jnp.concatenate([query_weight, key_weight, value_weight, output_weight], axis=1)
    rows_here = local.shape[0]
    local = local.reshape(rows_here, 4, parts, columns)
    local = chip_exchange(local, 2, 0, parts).reshape(parts, rows_here, 4 * columns)

    def gathered(block):
        whole = lax.all_gather(block.reshape(parts * rows_here, -1), SPREAD, axis=0, tiled=True)
        if r_n > 1:
            whole = (
                whole.reshape(dp_n * seq_n, y_n, r_n, core_n * rows_here, -1)
                .transpose(0, 2, 1, 3, 4)
                .reshape(width, -1)
            )
        return whole

    weight_in = gathered(local[:, :, : 3 * columns])
    weight_out = gathered(local[:, :, 3 * columns :])

    token_float = to_sequences(tokens).astype(f32)
    grad_home = to_sequences(grad_out)
    inverse_one = lax.rsqrt(jnp.mean(token_float * token_float, axis=-1, keepdims=True) + epsilon)
    hidden_one = (token_float * inverse_one * attn_norm).astype(bf16)
    hidden_full = chip_gather(hidden_one, 1, parts).reshape(length, width)

    grad_plane = lax.all_gather(grad_home.reshape(home, width), PLANE, axis=0, tiled=True)

    half = head // 2
    frequency = theta_base ** (-jnp.arange(half, dtype=f32) / half)
    angles = jnp.arange(length, dtype=f32)[:, None] * frequency[None, :]
    cosine = jnp.concatenate([jnp.cos(angles)] * 2, axis=1)
    sine = jnp.concatenate([-jnp.sin(angles), jnp.sin(angles)], axis=1)
    seg_row, seg_col = segment[None, :], segment[:, None]

    qkv = product(hidden_full, weight_in)
    query, keys, values, mixed = attend(qkv, cosine, sine, seg_row, seg_col, heads)
    mixed_full = chip_gather(mixed, 1, parts)
    branch = product(mixed_full, weight_out).reshape(seq_n, parts, piece, columns)
    branch = chip_exchange(branch, 1, 3, parts).reshape(seq_n, piece, width)
    residual = token_float + branch
    inverse_two = lax.rsqrt(jnp.mean(residual * residual, axis=-1, keepdims=True) + epsilon)
    normed_two = residual * inverse_two
    hidden_two = (normed_two * expert_norm).astype(bf16).reshape(home, width)

    hidden_plane = lax.all_gather(hidden_two, PLANE, axis=0, tiled=True)
    all_routes = plane_routes.reshape(topk, plane)
    mine = y_i * core_n + core_i
    to_me = all_routes == mine
    chosen_here = jnp.any(to_me, axis=0)
    rank = counts_before(chosen_here)
    ends = rank + chosen_here.astype(jnp.int32)
    slots = jnp.arange(capacity, dtype=jnp.int32)
    source = jnp.sum((ends[None, :] <= slots[:, None]).astype(jnp.int32), axis=1)
    filled = source < plane
    source = jnp.minimum(source, plane - 1)

    def gates_of(rows, where):
        logits = product(rows, router)
        hot = where[:, :, None] == jnp.arange(experts, dtype=jnp.int32)[None, None, :]
        picked = jnp.sum(jnp.where(hot, logits[None], 0.0), axis=2)
        return jax.nn.softmax(picked, axis=0), hot

    plane_gates, _ = gates_of(hidden_plane, all_routes)
    my_gate = jnp.sum(jnp.where(to_me, plane_gates, 0.0), axis=0)
    row_gate = jnp.where(filled, my_gate[source], 0.0)[:, None]
    expert_in = hidden_plane[source]
    dout_rows = grad_plane[source]
    dy_rows = (row_gate * dout_rows.astype(f32)).astype(bf16)

    gate_one, up_one, down_one = gate_weight[0], up_weight[0], down_weight[0]
    units, dgpre, dupre = expert_units(expert_in, dy_rows, gate_one, up_one, down_one)

    def over_ctx(part):
        return lax.psum_scatter(part.astype(bf16), CTX, scatter_dimension=0, tiled=True).astype(f32)

    grad_down = jnp.transpose(over_ctx(t_product(dy_rows, units)))[None]
    grad_gate = over_ctx(t_product(expert_in, dgpre))[None]
    grad_up = over_ctx(t_product(expert_in, dupre))[None]

    ypair = product(units, down_one).astype(bf16)
    dgate_rows = jnp.sum(dout_rows.astype(f32) * ypair.astype(f32), axis=1)
    weighted = (row_gate * ypair.astype(f32)).astype(bf16)
    dinput = (product_t(dgpre, gate_one) + product_t(dupre, up_one)).astype(bf16)

    def relative(a):
        a = a.reshape(dp_n, y_n, core_n, home)
        for axis, index in ((0, dp_i), (1, y_i), (2, core_i)):
            a = jnp.where(index == 0, a, jnp.flip(a, axis))
        return a.reshape(plane)

    place = relative(jnp.where(chosen_here, rank, -1))
    has = (place >= 0)[:, None]
    place = jnp.maximum(place, 0)

    def returned(rows):
        return plane_scatter(jnp.where(has, rows[place], jnp.zeros((), bf16)), width)

    dgate_plane = jnp.where(chosen_here, dgate_rows[jnp.minimum(rank, capacity - 1)], 0.0)
    dgate_home = lax.all_to_all(
        dgate_plane.reshape(8, home), PLANE, split_axis=0, concat_axis=0, tiled=True
    ).reshape(dp_n, experts, home).sum(axis=0)

    mixture = returned(weighted).reshape(seq_n, piece, width)
    output = from_sequences((residual + mixture).astype(bf16))

    my_routes = pick(pick(pick(plane_routes, dp_i, 1), y_i, 1), core_i, 1)
    gates, hot = gates_of(hidden_two, my_routes)
    dgate = jnp.sum(jnp.where(hot, jnp.transpose(dgate_home)[None], 0.0), axis=2)
    dsel = gates * (dgate - jnp.sum(gates * dgate, axis=0, keepdims=True))
    dlogits = jnp.sum(jnp.where(hot, dsel[:, :, None], 0.0), axis=0).astype(bf16)
    router_grad = t_product(hidden_two, dlogits)
    dhidden_two = returned(dinput) + product_t(dlogits, router)

    flat_two = normed_two.reshape(home, width)
    dresid, expert_norm_grad = norm_backward(
        dhidden_two, flat_two, inverse_two.reshape(home, 1), expert_norm
    )
    dresid = dresid + grad_home.reshape(home, width).astype(f32)
    dbranch = chip_gather(dresid.astype(bf16).reshape(seq_n, piece, width), 1, parts).reshape(length, width)
    column_start = (r_i * core_n + core_i) * columns
    dbranch_here = lax.dynamic_slice_in_dim(dbranch, column_start, columns, 1)
    out_grad = t_product(mixed_full, dbranch_here)
    dmixed = chip_scatter(product_t(dbranch_here, weight_out).astype(bf16), 1, parts).astype(bf16)
    dqpre, dkpre, dvpre = attend_back(
        query, keys, values, mixed, dmixed, cosine, sine, seg_row, seg_col, heads
    )
    dqkv = jnp.concatenate([dqpre, dkpre, dvpre], axis=1)
    in_grad = t_product(hidden_full, dqkv)
    dhidden_one = chip_scatter(
        product_t(dqkv, weight_in).astype(bf16).reshape(seq_n, parts * piece, width), 1, parts
    )
    normed_one = token_float * inverse_one
    dtokens, attn_norm_grad = norm_backward(
        dhidden_one.reshape(home, width),
        normed_one.reshape(home, width),
        inverse_one.reshape(home, 1),
        attn_norm,
    )
    grad_tokens = from_sequences((dtokens + dresid).astype(bf16).reshape(seq_n, piece, width)).astype(f32)

    def spread_sum(part):
        if r_n > 1:
            part = (
                part.reshape(dp_n * seq_n, r_n, y_n, core_n * rows_here, -1)
                .transpose(0, 2, 1, 3, 4)
                .reshape(width, -1)
            )
        part = lax.psum_scatter(part.astype(bf16), SPREAD, scatter_dimension=0, tiled=True)
        part = part.reshape(parts, rows_here, -1, 1, columns)
        return chip_exchange(part, 0, 3, parts).reshape(rows_here, -1, width).astype(f32)

    [grad_output] = jnp.moveaxis(spread_sum(out_grad), 1, 0)
    grad_query, grad_key, grad_value = jnp.moveaxis(spread_sum(in_grad), 1, 0)

    gains = jnp.concatenate(
        [attn_norm_grad[:, None], expert_norm_grad[:, None], router_grad], axis=1
    )
    gains = lax.psum_scatter(gains, EVERY, scatter_dimension=0, tiled=True)
    return (
        output,
        grad_tokens,
        gains[:, 0],
        grad_query,
        grad_key,
        grad_value,
        grad_output,
        gains[:, 1],
        gains[:, 2:],
        grad_gate,
        grad_up,
        grad_down,
    )


def solution(mesh):
    dp_n, ctx_n, exp_n = mesh.shape["dp"], mesh.shape["ctx"], mesh.shape["exp"]

    def block(*arrays):
        tokens = arrays[0]
        seq_count = tokens.shape[0] // (dp_n * exp_n)
        seq_n = seq_count * CORES
        sizes = (dp_n, seq_n, ctx_n // seq_n, exp_n // CORES, CORES)
        fine = Mesh(mesh.devices.reshape(sizes), EVERY)
        group = ("dp", "y", "core")
        exp = ("y", "core")
        return jax.shard_map(
            functools.partial(on_device, sizes),
            mesh=fine,
            in_specs=(
                P(group, CTX, None),
                P(group, None),
                P(group, CTX, None),
                P(),
                P(EVERY, None),
                P(EVERY, None),
                P(EVERY, None),
                P(EVERY, None),
                P(),
                P(),
                P(exp, None, "dp"),
                P(exp, None, "dp"),
                P(exp, "dp", None),
                P(group, CTX, None),
            ),
            out_specs=(
                P(group, CTX, None),
                P(group, CTX, None),
                P(EVERY),
                P(EVERY, None),
                P(EVERY, None),
                P(EVERY, None),
                P(EVERY, None),
                P(EVERY),
                P(EVERY, None),
                P(exp, CTX, "dp"),
                P(exp, CTX, "dp"),
                P(exp, "dp", CTX),
            ),
            check_vma=False,
        )(*arrays)

    return block
```

time: 3240 us -> 2240 us (0.69)
  waiting for transfers between devices: 2130 us -> 999 us
  matrix products: 588 us -> 328 us
  Pallas kernels: 0 us -> 175 us
  blocking collectives: 177 us -> 315 us
  local copies, waits for them, and re-layouts: 173 us -> 235 us
    unnamed x20 -> x11, waiting for transfers between devices: 610 us -> 0.17 us
    all_gather x8 -> x4, waiting for transfers between devices: 558 us -> 111 us  [the longest x1 63.3 us: on_device(): hidden_plane = lax.all_gather(hidden_two, PLANE, axis=0, tiled=True)]
    dot_general x29 -> x17, matrix products: 586 us -> 328 us  [the longest x6 144 us: t_product(): lax.dot_general(a, b, (((0,), (0,)), ((), ())), preferred_element_type=f32)]
    reduce_scatter x8 -> x5, waiting for transfers between devices: 952 us -> 758 us  [the longest x3 551 us: over_ctx(): lax.psum_scatter(part.astype(bf16), CTX, scatter_dimension=0, tiled=True)]
    pallas_call x0 -> x3, Pallas kernels: none -> 175 us  [the longest x1 114 us: expert_units(): pl.pallas_call(functools.partial(units_kernel, chunk), grid=(units // til...]
    all_to_all x2 -> x3, blocking collectives: 131 us -> 275 us  [the longest x2 200 us: to_sequences(): return lax.all_to_all(a, 'seq', split_axis=0, concat_axis=0, tiled=True)]
    gather x4 -> x7, local copies, waits for them, and re-layouts: 43.7 us -> 166 us  [the longest x2 73.3 us: returned(): rows[place]]
    ppermute x0 -> x23, waiting for transfers between devices: none -> 58.9 us  [swap(): return lax.ppermute(a, axis, [(0, 1), (1, 0)])]
  transfers between devices with their start and end apart: 20 -> 35, of which waited for: 18 -> 18; matrix products, arithmetic and copies ran while one was open for 21% -> 17% of each run, Pallas kernels for 0% -> 3%
where the time goes in v1:
time: 2240 us
  waiting for transfers between devices  999 us (45%)
  matrix products  328 us (15%)
  blocking collectives  315 us (14%)
  local copies, waits for them, and re-layouts  235 us (10%)
  Pallas kernels  175 us (8%)
  other arithmetic  135 us (6%)
  starting transfers between devices  33.9 us (2%)
    reduce_scatter x3, waiting for transfers between devices, over_ctx(): lax.psum_scatter(part.astype(bf16), CTX, scatter_dimension=0, tiled=True)  551 us
    reduce_scatter x2, waiting for transfers between devices, spread_sum(): lax.psum_scatter(part.astype(bf16), SPREAD, scatter_dimension=0, tiled=True)  207 us
    all_to_all x2, blocking collectives, to_sequences(): return lax.all_to_all(a, 'seq', split_axis=0, concat_axis=0, tiled=True)  200 us
    dot_general x6, matrix products, t_product(): lax.dot_general(a, b, (((0,), (0,)), ((), ())), preferred_element_type=f32)  144 us
    pallas_call x1, Pallas kernels, expert_units(): pl.pallas_call(functools.partial(units_kernel, chunk), grid=(units // til...  114 us
    dot_general x5, matrix products, product_t(): lax.dot_general(a, b, (((1,), (1,)), ((), ())), preferred_element_type=f32)  106 us
    dot_general x6, matrix products, product(): return jnp.dot(a, b, preferred_element_type=f32)  78.4 us
    all_to_all x1, blocking collectives, from_sequences(): a = lax.all_to_all(a, 'seq', split_axis=0, concat_axis=0, tiled=True)  74.8 us
  transfers between devices with their start and end apart: 35, of which 18 were waited for; matrix products, arithmetic and copies ran while one was open for 17% of the time, Pallas kernels for 3%

profile of v1, /device:TPU:1, one launch (start us, length us, event | category | flops | bytes accessed | tf_op | source)
XLA Modules:
  0.0 2236.6 jit_solution(2566644702999795456)
XLA Ops:
  24.0 98.6 %all_to_all.26 = bf16[4,128,2048]{2,1,0:T(8,128)(2,1)} all-to-all(bf16[4,128,2048]{2,1,0:T(8,128)(2,1)S(1)} %pad_maximum_fusion.6), channel_id=1, replica_groups=mesh['dp'=2,'seq'=4,'r'=1,'y'=2,'core'=2] {'seq'}, dimensions={0} | all-to-all | bytes 4194304 | tf_op jit(solution)/shard_map/all_to_all | solution.py:82
  126.8 101.4 %all_to_all.27 = bf16[4,128,2048]{2,1,0:T(8,128)(2,1)S(1)} all-to-all(bf16[4,128,2048]{2,1,0:T(8,128)(2,1)S(1)} %pad_maximum_fusion.5), channel_id=1, replica_groups=mesh['dp'=2,'seq'=4,'r'=1,'y'=2,'core'=2] {'seq'}, dimensions={0} | all-to-all | bytes 4194304 | tf_op jit(solution)/shard_map/all_to_all | solution.py:82
  234.9 40.5 %all-gather = s32[32,6,256]{2,1,0:T(8,128)S(1)} all-gather(s32[1,6,256]{2,1,0:T(8,128)S(1)} %reshape.487), channel_id=1, replica_groups=mesh['dp'=2,'seq'=4,'r'=1,'y'=2,'core'=2] {'dp','seq','r','y','core'}, dimensions={0}, use_global_device_ids=true | all-gather | bytes 202752 | tf_op jit(solution)/shard_map/all_gather | solution.py:327
  302.9 28.1 %attend.1 = (bf16[1024,1024]{1,0:T(8,128)(2,1)S(1)}, bf16[1024,1024]{1,0:T(8,128)(2,1)S(1)}, bf16[1024,1024]{1,0:T(8,128)(2,1)}, bf16[1024,1024]{1,0:T(8,128)(2,1)}) custom-call(f32[1024,3072]{1,0:T(8,128)} %fusion.54.qp.kp.vp, f32[1024,3072]{1,0:T(8,128)} %fusion.54.qp.kp.vp, f32[1024,3072]{1,0:T(8,128)} %fusion.54.qp.kp.vp, ...), custom_call_target="tpu_custom_call" | custom-call | flops 2684354560 | bytes 20971520 | tf_op jit(solution)/shard_map/attend/pallas_call | solution.py:148
  368.0 48.0 %all-gather.12.cloned.1.call-done = bf16[4096,2048]{1,0:T(8,128)(2,1)} async-done(((bf16[512,2048]{1,0:T(8,128)(2,1)}), bf16[4096,2048]{1,0:T(8,128)(2,1)}) %all-gather.12.cloned.1.call-update) | async-done | bytes 16777232 | tf_op jit(solution)/shard_map/all_gather | solution.py:363
  416.0 28.3 %gather_fusion.2 = bf16[2560,2048]{1,0:T(8,128)(2,1)} fusion(bf16[4096,2048]{1,0:T(8,128)(2,1)} %all-gather.12.cloned.1.call-done, s32[3072]{0:T(1024)S(1)} %pad_clamp_fusion), kind=kCustom, calls=%fused_computation.2 | custom fusion | bytes 20981760 | tf_op jit(solution)/shard_map/gather | solution.py:404
  444.3 63.3 %all-gather.10.cloned.1.call-done = bf16[4096,2048]{1,0:T(8,128)(2,1)} async-done(((bf16[512,2048]{1,0:T(8,128)(2,1)}), bf16[4096,2048]{1,0:T(8,128)(2,1)}) %all-gather.10.cloned.1.call-update) | async-done | bytes 16777232 | tf_op jit(solution)/shard_map/all_gather | solution.py:382
  542.5 28.1 %gather_fusion.1 = bf16[2560,2048]{1,0:T(8,128)(2,1)} fusion(bf16[4096,2048]{1,0:T(8,128)(2,1)} %all-gather.10.cloned.1.call-done, s32[3072]{0:T(1024)S(1)} %pad_clamp_fusion), kind=kCustom, calls=%fused_computation.1 | custom fusion | bytes 20981760 | tf_op jit(solution)/shard_map/gather | solution.py:403
  570.7 114.3 %expert_units.1 = (bf16[2560,2816]{1,0:T(8,128)(2,1)}, bf16[2560,2816]{1,0:T(8,128)(2,1)}, bf16[2560,2816]{1,0:T(8,128)(2,1)}) custom-call(bf16[2560,2048]{1,0:T(8,128)(2,1)} %gather_fusion.1, bf16[2560,2048]{1,0:T(8,128)(2,1)} %fusion.dy, bf16[2048,2816]{1,0:T(8,128)(2,1)} %bitcast.294, bf16[2048,2816]{1,0:T(8,128)(2,1)} %bitcast.295, ...), custom_call_target="tpu_custom_call" | custom-call | flops 88583700480 | bytes 98828288 | tf_op jit(solution)/shard_map/expert_units/pallas_call | solution.py:248
  685.0 39.4 %fusion.2 = (f32[2560]{0:T(1024)}, bf16[2560,2048]{1,0:T(8,128)(2,1)}) fusion(bf16[2560,2048]{1,0:T(8,128)(2,1)} %gather_fusion.2, f32[2560]{0:T(1024)S(1)} %compare_select_fusion.2, bf16[2560,2816]{1,0:T(8,128)(2,1)} %get-tuple-element.23, bf16[1,2816,2048]{2,1,0:T(8,128)(2,1)} %param.26), kind=kOutput, calls=%fused_computation.13 | convolution fusion | flops 29564598272 | bytes 46944256 | tf_op jit(solution)/shard_map/dot_general | solution.py:27
  724.3 38.1 %fusion.44 = f32[2560,2048]{1,0:T(8,128)} fusion(bf16[2560,2816]{1,0:T(8,128)(2,1)} %get-tuple-element.27, bf16[1,2048,2816]{2,1,0:T(8,128)(2,1)} %param.24), kind=kOutput, calls=%fused_computation.220 | convolution fusion | flops 29527900160 | bytes 46923776 | tf_op jit(solution)/shard_map/dot_general | solution.py:31
  762.5 38.8 %add_convert_fusion = bf16[2560,2048]{1,0:T(8,128)(2,1)} fusion(f32[2560,2048]{1,0:T(8,128)} %fusion.44, bf16[2560,2816]{1,0:T(8,128)(2,1)} %get-tuple-element.28, bf16[1,2048,2816]{2,1,0:T(8,128)(2,1)} %param.25), kind=kOutput, calls=%fused_computation.14 | convolution fusion | flops 29538385920 | bytes 57409536 | tf_op jit(solution)/shard_map/dot_general | solution.py:31
  801.3 36.7 %gather_fusion.4 = bf16[4096,2048]{1,0:T(8,128)(2,1)} fusion(bf16[2560,2048]{1,0:T(8,128)(2,1)} %add_convert_fusion, s32[4096]{0:T(1024)S(1)} %copy-done.26), kind=kCustom, calls=%fused_computation.4 | custom fusion | bytes 33570816 | tf_op jit(solution)/shard_map/gather | solution.py:433
  838.0 36.7 %gather_fusion.3 = bf16[4096,2048]{1,0:T(8,128)(2,1)} fusion(bf16[2560,2048]{1,0:T(8,128)(2,1)} %get-tuple-element.155, s32[4096]{0:T(1024)S(1)} %copy-done.26), kind=kCustom, calls=%fused_computation.3 | custom fusion | bytes 33570816 | tf_op jit(solution)/shard_map/gather | solution.py:433
  1058.0 33.0 %attend_back.1 = (bf16[1024,1024]{1,0:T(8,128)(2,1)S(1)}, bf16[1024,1024]{1,0:T(8,128)(2,1)S(1)}, bf16[1024,1024]{1,0:T(8,128)(2,1)}) custom-call(bf16[1024,1024]{1,0:T(8,128)(2,1)} %copy-done.1, bf16[1024,1024]{1,0:T(8,128)(2,1)} %copy-done.2, bf16[1024,1024]{1,0:T(8,128)(2,1)} %get-tuple-element.26.v, bf16[1024,1024]{1,0:T(8,128)(2,1)} %get-tuple-element.22.mixed, ...), custom_call_target="tpu_custom_call" | custom-call | flops 6710886400 | bytes 16777216 | tf_op jit(solution)/shard_map/attend_back/pallas_call | solution.py:207
  1140.7 38.4 %convolution_convert_fusion = bf16[2048,2816]{1,0:T(8,128)(2,1)} fusion(bf16[2560,2048]{1,0:T(8,128)(2,1)} %fusion.dy, bf16[2560,2816]{1,0:T(8,128)(2,1)} %get-tuple-element.23), kind=kOutput, calls=%fused_computation.21 | convolution fusion | flops 29533667328 | bytes 36438016 | tf_op jit(solution)/shard_map/dot_general | solution.py:35
  1179.4 38.5 %convolution_convert_fusion.1 = bf16[2048,2816]{1,0:T(8,128)(2,1)} fusion(bf16[2560,2048]{1,0:T(8,128)(2,1)} %gather_fusion.1, bf16[2560,2816]{1,0:T(8,128)(2,1)} %get-tuple-element.28), kind=kOutput, calls=%fused_computation.22 | convolution fusion | flops 29533667328 | bytes 36438016 | tf_op jit(solution)/shard_map/dot_general | solution.py:35
  1237.9 38.4 %convolution_convert_fusion.2 = bf16[2048,2816]{1,0:T(8,128)(2,1)} fusion(bf16[2560,2048]{1,0:T(8,128)(2,1)} %gather_fusion.1, bf16[2560,2816]{1,0:T(8,128)(2,1)} %get-tuple-element.27), kind=kOutput, calls=%fused_computation.23 | convolution fusion | flops 29533667328 | bytes 36438016 | tf_op jit(solution)/shard_map/dot_general | solution.py:35
  1284.9 74.8 %all_to_all.28 = bf16[4,128,2048]{2,1,0:T(8,128)(2,1)S(1)} all-to-all(bf16[4,128,2048]{2,1,0:T(8,128)(2,1)S(1)} %bitcast.258), channel_id=1, replica_groups=mesh['dp'=2,'seq'=4,'r'=1,'y'=2,'core'=2] {'seq'}, dimensions={0} | all-to-all | bytes 4194304 | tf_op jit(solution)/shard_map/all_to_all | solution.py:86
  1372.8 53.7 %all-to-all-done.2 = bf16[4,128,2048]{2,1,0:T(8,128)(2,1)} async-done(((bf16[4,128,2048]{2,1,0:T(8,128)(2,1)}), bf16[4,128,2048]{2,1,0:T(8,128)(2,1)}, u32[]{:S(2)}, u32[]{:S(2)}) %all-to-all-start.2) | async-done | bytes 2097184 | tf_op jit(solution)/shard_map/all_to_all | solution.py:86
  1442.6 166.3 %reduce-scatter.17.cloned.1.call-done = bf16[512,2816]{1,0:T(8,128)(2,1)} async-done(((bf16[2048,2816]{1,0:T(8,128)(2,1)}), bf16[512,2816]{1,0:T(8,128)(2,1)}) %reduce-scatter.17.cloned.1.call-update) | async-done | bytes 2883600 | tf_op jit(solution)/shard_map/reduce_scatter | solution.py:411
  1613.6 192.1 %reduce-scatter.15.cloned.1.call-done = bf16[512,2816]{1,0:T(8,128)(2,1)} async-done(((bf16[2048,2816]{1,0:T(8,128)(2,1)}), bf16[512,2816]{1,0:T(8,128)(2,1)}) %reduce-scatter.15.cloned.1.call-update) | async-done | bytes 2883600 | tf_op jit(solution)/shard_map/reduce_scatter | solution.py:411
  1810.4 206.8 %reduce-scatter.9.cloned.1.call-done = bf16[128,3072]{1,0:T(8,128)(2,1)} async-done(((bf16[2048,3072]{1,0:T(8,128)(2,1)}), bf16[128,3072]{1,0:T(8,128)(2,1)}) %reduce-scatter.9.cloned.1.call-update) | async-done | bytes 786448 | tf_op jit(solution)/shard_map/reduce_scatter | solution.py:485
  2021.3 192.8 %reduce-scatter.13.cloned.1.call-done = bf16[512,2816]{1,0:T(8,128)(2,1)} async-done(((bf16[2048,2816]{1,0:T(8,128)(2,1)}), bf16[512,2816]{1,0:T(8,128)(2,1)}) %reduce-scatter.13.cloned.1.call-update) | async-done | bytes 2883600 | tf_op jit(solution)/shard_map/reduce_scatter | solution.py:411
  (329 shorter events, 445.9 us)
Async XLA Ops:
  7.2 276.7 %all-gather.6.cloned.1.call-start = ((), (), s32[]{:S(2)}) async-start(), calls=%async_computation.11 | async-start | bytes 13369344 | tf_op jit(solution)/shard_map/all_gather | solution.py:345
  17.3 324.7 %all-gather.8.cloned.1.call-start = ((), (), s32[]{:S(2)}) async-start(), calls=%async_computation.12 | async-start | bytes 4456448 | tf_op jit(solution)/shard_map/all_gather | solution.py:345
  18.1 397.9 %all-gather.12.cloned.1.call-start = ((), (), s32[]{:S(2)}) async-start(), calls=%async_computation.14 | async-start | bytes 18874368 | tf_op jit(solution)/shard_map/all_gather | solution.py:363
  122.6 385.0 %all-gather.10.cloned.1.call-start = ((), (), s32[]{:S(2)}) async-start(), calls=%async_computation.13 | async-start | bytes 18874368 | tf_op jit(solution)/shard_map/all_gather | solution.py:382
  231.4 46.7 %collective-permute-start.1 = (bf16[4,128,2048]{2,1,0:T(8,128)(2,1)}, bf16[4,128,2048]{2,1,0:T(8,128)(2,1)}, u32[]{:S(2)}, u32[]{:S(2)}) collective-permute-start(bf16[4,128,2048]{2,1,0:T(8,128)(2,1)} %multiply_convert_fusion.1), channel_id=1, source_target_pairs={{0,1},{1,0},{2,3},{3,2},{4,5},{5,4},{6,7},{7,6},{8,9},{9,8},{10,11... | collective-permute-start | bytes 6291464 | tf_op jit(solution)/shard_map/ppermute | solution.py:39
  914.3 101.9 %collective-permute-start.6 = (bf16[2,2,512,2048]{3,2,1,0:T(8,128)(2,1)}, bf16[2,2,512,2048]{3,2,1,0:T(8,128)(2,1)}, u32[]{:S(2)}, u32[]{:S(2)}) collective-permute-start(bf16[2,2,512,2048]{3,2,1,0:T(8,128)(2,1)} %slice_bitcast_fusion.2), channel_id=1, source_target_pairs={{0,1},{1,0},{2,3},{3,2},{4,5},{5,4},{6,7},{7,6},{8,9},{9,8},{10,11... | collective-permute-start | bytes 25165832 | tf_op jit(solution)/shard_map/ppermute | solution.py:39
  927.7 24.6 %collective-permute-start.15 = (bf16[256,2048]{1,0:T(8,128)(2,1)S(1)}, bf16[256,2048]{1,0:T(8,128)(2,1)S(1)}, u32[]{:S(2)}, u32[]{:S(2)}) collective-permute-start(bf16[256,2048]{1,0:T(8,128)(2,1)S(1)} %get-tuple-element.158), channel_id=1, source_target_pairs={{0,16},{16,0},{1,17},{17,1},{2,18},{18,2},{3,19},{19,3},{4,20},{20... | collective-permute-start | bytes 3145736 | tf_op jit(solution)/shard_map/ppermute | solution.py:39
  928.9 24.2 %collective-permute-start.13 = (bf16[256,2048]{1,0:T(8,128)(2,1)S(1)}, bf16[256,2048]{1,0:T(8,128)(2,1)S(1)}, u32[]{:S(2)}, u32[]{:S(2)}) collective-permute-start(bf16[256,2048]{1,0:T(8,128)(2,1)S(1)} %get-tuple-element.159), channel_id=1, source_target_pairs={{0,2},{2,0},{1,3},{3,1},{4,6},{6,4},{5,7},{7,5},{8,10},{10,8},{9,1... | collective-permute-start | bytes 3145736 | tf_op jit(solution)/shard_map/ppermute | solution.py:39
  955.6 51.4 %collective-permute-start.16 = (bf16[512,2048]{1,0:T(8,128)(2,1)}, bf16[512,2048]{1,0:T(8,128)(2,1)}, u32[]{:S(2)}, u32[]{:S(2)}) collective-permute-start(bf16[512,2048]{1,0:T(8,128)(2,1)} %pad_maximum_fusion.11), channel_id=1, source_target_pairs={{0,2},{2,0},{1,3},{3,1},{4,6},{6,4},{5,7},{7,5},{8,10},{10,8},{9,1... | collective-permute-start | bytes 6291464 | tf_op jit(solution)/shard_map/ppermute | solution.py:39
  957.4 49.6 %collective-permute-start.14 = (bf16[512,2048]{1,0:T(8,128)(2,1)}, bf16[512,2048]{1,0:T(8,128)(2,1)}, u32[]{:S(2)}, u32[]{:S(2)}) collective-permute-start(bf16[512,2048]{1,0:T(8,128)(2,1)} %pad_maximum_fusion.10), channel_id=1, source_target_pairs={{0,16},{16,0},{1,17},{17,1},{2,18},{18,2},{3,19},{19,3},{4,20},{20... | collective-permute-start | bytes 6291464 | tf_op jit(solution)/shard_map/ppermute | solution.py:39
  981.8 24.3 %all-to-all-start.3 = ((f32[8,1,512]{2,1,0:T(1,128)}), f32[8,1,512]{2,1,0:T(1,128)S(1)}, u32[]{:S(2)}, u32[]{:S(2)}) async-start(f32[8,1,512]{2,1,0:T(1,128)} %copy.238), calls=%async_computation.3 | async-start | bytes 32768 | tf_op jit(solution)/shard_map/all_to_all | solution.py:436
  987.2 443.4 %reduce-scatter.19.cloned.1.call-start = ((), (), s32[]{:S(2)}) async-start(), calls=%async_computation.20 | async-start | bytes 1081344
  1025.5 25.0 %collective-permute-start.9 = (bf16[256,2048]{1,0:T(8,128)(2,1)}, bf16[256,2048]{1,0:T(8,128)(2,1)S(1)}, u32[]{:S(2)}, u32[]{:S(2)}) collective-permute-start(bf16[256,2048]{1,0:T(8,128)(2,1)} %get-tuple-element.164), channel_id=1, source_target_pairs={{0,16},{16,0},{1,17},{17,1},{2,18},{18,2},{3,19},{19,3},{4,20},{20... | collective-permute-start | bytes 3145736 | tf_op jit(solution)/shard_map/ppermute | solution.py:39
  1025.8 24.7 %collective-permute-start.7 = (bf16[256,2048]{1,0:T(8,128)(2,1)S(1)}, bf16[256,2048]{1,0:T(8,128)(2,1)S(1)}, u32[]{:S(2)}, u32[]{:S(2)}) collective-permute-start(bf16[256,2048]{1,0:T(8,128)(2,1)S(1)} %get-tuple-element.165), channel_id=1, source_target_pairs={{0,2},{2,0},{1,3},{3,1},{4,6},{6,4},{5,7},{7,5},{8,10},{10,8},{9,1... | collective-permute-start | bytes 3145736 | tf_op jit(solution)/shard_map/ppermute | solution.py:39
  1052.9 66.4 %collective-permute-start.10 = (bf16[512,2048]{1,0:T(8,128)(2,1)}, bf16[512,2048]{1,0:T(8,128)(2,1)}, u32[]{:S(2)}, u32[]{:S(2)}) collective-permute-start(bf16[512,2048]{1,0:T(8,128)(2,1)} %pad_maximum_fusion.8), channel_id=1, source_target_pairs={{0,2},{2,0},{1,3},{3,1},{4,6},{6,4},{5,7},{7,5},{8,10},{10,8},{9,1... | collective-permute-start | bytes 6291464 | tf_op jit(solution)/shard_map/ppermute | solution.py:39
  1054.9 64.5 %collective-permute-start.8 = (bf16[512,2048]{1,0:T(8,128)(2,1)}, bf16[512,2048]{1,0:T(8,128)(2,1)}, u32[]{:S(2)}, u32[]{:S(2)}) collective-permute-start(bf16[512,2048]{1,0:T(8,128)(2,1)} %pad_maximum_fusion.7), channel_id=1, source_target_pairs={{0,16},{16,0},{1,17},{17,1},{2,18},{18,2},{3,19},{19,3},{4,20},{20... | collective-permute-start | bytes 6291464 | tf_op jit(solution)/shard_map/ppermute | solution.py:39
  1131.3 302.8 %reduce-scatter.11.cloned.1.call-start = ((), (), s32[]{:S(2)}) async-start(), calls=%async_computation.16 | async-start | bytes 4456448 | tf_op jit(solution)/shard_map/reduce_scatter | solution.py:485
  1140.6 468.2 %reduce-scatter.17.cloned.1.call-start = ((), (), s32[]{:S(2)}) async-start(), calls=%async_computation.19 | async-start | bytes 14417920 | tf_op jit(solution)/shard_map/reduce_scatter | solution.py:411
  1179.1 626.5 %reduce-scatter.15.cloned.1.call-start = ((), (), s32[]{:S(2)}) async-start(), calls=%async_computation.18 | async-start | bytes 14417920 | tf_op jit(solution)/shard_map/reduce_scatter | solution.py:411
  1217.8 799.3 %reduce-scatter.9.cloned.1.call-start = ((), (), s32[]{:S(2)}) async-start(), calls=%async_computation.15 | async-start | bytes 13369344 | tf_op jit(solution)/shard_map/reduce_scatter | solution.py:485
  1237.5 976.6 %reduce-scatter.13.cloned.1.call-start = ((), (), s32[]{:S(2)}) async-start(), calls=%async_computation.17 | async-start | bytes 14417920 | tf_op jit(solution)/shard_map/reduce_scatter | solution.py:411
  1359.7 66.9 %all-to-all-start.2 = ((bf16[4,128,2048]{2,1,0:T(8,128)(2,1)}), bf16[4,128,2048]{2,1,0:T(8,128)(2,1)}, u32[]{:S(2)}, u32[]{:S(2)}) async-start(bf16[4,128,2048]{2,1,0:T(8,128)(2,1)} %get-tuple-element.185), calls=%async_computation.2 | async-start | bytes 4194304 | tf_op jit(solution)/shard_map/all_to_all | solution.py:86
  1371.6 63.6 %collective-permute-start.20 = (bf16[2,128,2048]{2,1,0:T(8,128)(2,1)}, bf16[2,128,2048]{2,1,0:T(8,128)(2,1)S(1)}, u32[]{:S(2)}, u32[]{:S(2)}) collective-permute-start(bf16[2,128,2048]{2,1,0:T(8,128)(2,1)} %constant_dynamic-slice_fusion.3), channel_id=1, source_target_pairs={{0,1},{1,0},{2,3},{3,2},{4,5},{5,4},{6,7},{7,6},{8,9},{9,8},{10,11... | collective-permute-start | bytes 3145736 | tf_op jit(solution)/shard_map/ppermute | solution.py:39
  2020.5 204.7 %collective-permute-start.21 = (bf16[1,64,3,1,1024]{4,1,3,2,0:T(8,128)(2,1)S(1)}, bf16[1,64,3,1,1024]{4,1,3,2,0:T(8,128)(2,1)S(1)}, u32[]{:S(2)}, u32[]{:S(2)}) collective-permute-start(bf16[1,64,3,1,1024]{4,1,3,2,0:T(8,128)(2,1)S(1)} %copy.263), channel_id=1, source_target_pairs={{0,1},{1,0},{2,3},{3,2},{4,5},{5,4},{6,7},{7,6},{8,9},{9,8},{10,11... | collective-permute-start | bytes 1179656 | tf_op jit(solution)/shard_map/ppermute | solution.py:39
  (56 other events, 1203.1 us)
Sparse Core Ops, SparseCore 0:
  17.4 229.0 all-gather.5
  249.8 74.1 all-gather.7
  325.9 90.0 all-gather.11
  417.7 89.8 all-gather.9
  1131.4 129.1 reduce-scatter.18
  1263.5 109.7 reduce-scatter.10
  1375.7 233.0 reduce-scatter.16
  1611.3 194.3 reduce-scatter.14
  1812.3 204.8 reduce-scatter.8
  2019.4 194.7 reduce-scatter.12

commit v2 on v1

--- a/solution.py
+++ b/solution.py
@@ -87,12 +87,10 @@
     return core_exchange(a, 0, 1)
 
 
-def plane_scatter(rows, width):
-    count = rows.shape[0] // 8
-    blocks = rows.reshape(2, 2, 2, count, width)
+def plane_scatter(blocks):
     got = swap(blocks[:, :, 1], "core")
     held = (blocks[:, :, 0].astype(f32) + got.astype(f32)).astype(bf16)
-    half = count // 2
+    half = blocks.shape[3] // 2
     by_x = swap(held[1, 1, :half], "dp")
     by_y = swap(held[1, 1, half:], "y")
     to_x = jnp.concatenate(
@@ -168,8 +166,9 @@
 
 
 def attend_back_kernel(
-    scale, block, q, k, v, mixed, dmixed, cosine, sine, seg_row, seg_col, dq_out, dk_out, dv_out, dk_sum, dv_sum
+    scale, block, q, k, v, mixed, dmixed, cosine, sine, seg_row, seg_col, *rest
 ):
+    dq_out, dk_out, dv_out, dk_sum, dv_sum = rest[-5:]
     length = q.shape[0]
     dk_sum[...] = jnp.zeros_like(dk_sum)
     dv_sum[...] = jnp.zeros_like(dv_sum)
@@ -194,7 +193,7 @@
     dv_out[...] = dv_sum[...].astype(bf16)
 
 
-def attend_back(q, k, v, mixed, dmixed, cosine, sine, seg_row, seg_col, heads):
+def attend_back(q, k, v, mixed, dmixed, cosine, sine, seg_row, seg_col, heads, *before):
     length, head = q.shape[0], cosine.shape[1]
     block = min(256, length)
     column = pl.BlockSpec((length, head), lambda h: (0, h))
@@ -208,7 +207,8 @@
         functools.partial(attend_back_kernel, head**-0.5, block),
         grid=(heads,),
         in_specs=[column] * 5
-        + [whole((length, head)), whole((length, head)), whole((1, length)), whole((length, 1))],
+        + [whole((length, head)), whole((length, head)), whole((1, length)), whole((length, 1))]
+        + [pl.BlockSpec(memory_space=pl.ANY)] * len(before),
         out_specs=[column] * 3,
         out_shape=[out] * 3,
         scratch_shapes=[pltpu.VMEM((length, head), f32)] * 2,
@@ -217,7 +217,7 @@
             flops=10 * pairs * head, bytes_accessed=16 * length * heads * head, transcendentals=pairs
         ),
         name="attend_back",
-    )(q, k, v, mixed, dmixed, cosine, sine, seg_row, seg_col)
+    )(q, k, v, mixed, dmixed, cosine, sine, seg_row, seg_col, *before)
 
 
 def units_kernel(chunk, x, dy, gate, up, down, units, dgate, dup):
@@ -267,14 +267,211 @@
     )(x, dy, gate, up, down)
 
 
-def counts_before(flags):
-    rows = flags.reshape(-1, 128).astype(bf16)
-    lanes = jnp.arange(128)
-    inside = product(rows, (lanes[:, None] < lanes[None, :]).astype(bf16))
-    lines = jnp.arange(rows.shape[0])
-    earlier = (lines[None, :] < lines[:, None]).astype(f32)
-    ahead = jnp.sum(earlier * jnp.sum(rows.astype(f32), axis=1)[None, :], axis=1)
-    return (inside + ahead[:, None]).astype(jnp.int32).reshape(-1)
+def dispatch_kernel(me, hidden, dout, slot, routes, router, rows, dy_rows, gate):
+    size = hidden.shape[1] * hidden.shape[3]
+    width = hidden.shape[4]
+    mine = me[3]
+    tokens = hidden[...].reshape(size, width)
+    logits = product(tokens, router[...])
+    lanes = lax.broadcasted_iota(jnp.int32, logits.shape, 1)
+    first, second = routes[0, :, 0:1], routes[0, :, 1:2]
+    one = jnp.sum(jnp.where(lanes == first, logits, 0.0), axis=1, keepdims=True)
+    two = jnp.sum(jnp.where(lanes == second, logits, 0.0), axis=1, keepdims=True)
+    top = jnp.maximum(one, two)
+    one, two = jnp.exp(one - top), jnp.exp(two - top)
+    share = jnp.where(first == mine, one, jnp.where(second == mine, two, 0.0)) / (one + two)
+    gate[0] = share
+    chosen = (
+        lax.broadcasted_iota(jnp.int32, (rows.shape[1], size), 0) == slot[0]
+    ).astype(bf16)
+    rows[0] = product(chosen, tokens).astype(bf16)
+    dy = (share * dout[...].reshape(size, width).astype(f32)).astype(bf16)
+    dy_rows[0] = product(chosen, dy).astype(bf16)
+
+
+def plane_block(seq_n, piece, width):
+    return pl.BlockSpec((1, 2, 1, piece, width), lambda b, me: (b // seq_n, 0, b % seq_n, 0, 0))
+
+
+def relative_block(seq_n, piece, width):
+    return pl.BlockSpec(
+        (1, 1, 2, 1, piece, width),
+        lambda b, me: (
+            lax.rem(b // (2 * seq_n) + me[0], 2),
+            lax.rem(b // seq_n + me[1], 2),
+            0,
+            b % seq_n,
+            0,
+            0,
+        ),
+    )
+
+
+def dispatch(me, hidden, dout, slot, routes, router, seq_n, piece, cap):
+    blocks, size = slot.shape[0], slot.shape[2]
+    width = hidden.shape[1]
+    seen = (4, 2, seq_n, piece, width)
+    each = pl.BlockSpec((1, cap, width), lambda b, me: (b, 0, 0))
+    out = jax.ShapeDtypeStruct((blocks, cap, width), bf16)
+    spare = jnp.zeros((width, 128 - router.shape[1]), router.dtype)
+    return pl.pallas_call(
+        dispatch_kernel,
+        grid_spec=pltpu.PrefetchScalarGridSpec(
+            num_scalar_prefetch=1,
+            grid=(blocks,),
+            in_specs=[
+                plane_block(seq_n, piece, width),
+                plane_block(seq_n, piece, width),
+                pl.BlockSpec((1, 1, size), lambda b, me: (b, 0, 0)),
+                pl.BlockSpec((1, size, routes.shape[2]), lambda b, me: (b, 0, 0)),
+                pl.BlockSpec((width, 128), lambda b, me: (0, 0)),
+            ],
+            out_specs=[each, each, pl.BlockSpec((1, size, 1), lambda b, me: (b, 0, 0))],
+        ),
+        out_shape=[out, out, jax.ShapeDtypeStruct((blocks, size, 1), f32)],
+        compiler_params=pltpu.CompilerParams(vmem_limit_bytes=40 * 2**20),
+        cost_estimate=pl.CostEstimate(
+            flops=4 * blocks * size * width * (cap + 64),
+            bytes_accessed=4 * blocks * (size + cap) * width,
+            transcendentals=2 * blocks * size,
+        ),
+        name="dispatch",
+    )(
+        me,
+        hidden.reshape(seen),
+        dout.reshape(seen),
+        slot,
+        routes,
+        jnp.concatenate([router, spare], axis=1),
+    )
+
+
+def spread_rows(slot, rows):
+    size, cap = slot.shape[0], rows.shape[0]
+    chosen = (lax.broadcasted_iota(jnp.int32, (size, cap), 1) == slot).astype(bf16)
+    return product(chosen, rows)
+
+
+def place_cores(me, out, dense):
+    piece = out.shape[4]
+    for core in range(2):
+        out[0, 0, lax.rem(me[2] + core, 2), 0] = dense[core * piece : (core + 1) * piece, :].astype(bf16)
+
+
+def combine_kernel(me, rows, slot, gate, dout, out, dgate):
+    dense = spread_rows(slot[0], rows[0])
+    grads = dout[...].reshape(dense.shape).astype(f32)
+    dgate[0] = jnp.sum(grads * dense, axis=1, keepdims=True)
+    place_cores(me, out, gate[0] * dense)
+
+
+def collect_kernel(me, rows, slot, out):
+    place_cores(me, out, spread_rows(slot[0], rows[0]))
+
+
+def combine(me, rows, slot, seq_n, piece, gate=None, dout=None):
+    blocks, cap, width = rows.shape
+    size = slot.shape[1]
+    column = pl.BlockSpec((1, size, 1), lambda b, me: (b, 0, 0))
+    weigh = gate is not None
+    operands = [rows, slot]
+    in_specs = [pl.BlockSpec((1, cap, width), lambda b, me: (b, 0, 0)), column]
+    out_specs = [relative_block(seq_n, piece, width)]
+    out_shape = [jax.ShapeDtypeStruct((2, 2, 2, seq_n, piece, width), bf16)]
+    if weigh:
+        operands += [gate, dout.reshape(4, 2, seq_n, piece, width)]
+        in_specs += [column, plane_block(seq_n, piece, width)]
+        out_specs += [column]
+        out_shape += [jax.ShapeDtypeStruct((blocks, size, 1), f32)]
+    return pl.pallas_call(
+        combine_kernel if weigh else collect_kernel,
+        grid_spec=pltpu.PrefetchScalarGridSpec(
+            num_scalar_prefetch=1, grid=(blocks,), in_specs=in_specs, out_specs=out_specs
+        ),
+        out_shape=out_shape,
+        compiler_params=pltpu.CompilerParams(vmem_limit_bytes=40 * 2**20),
+        cost_estimate=pl.CostEstimate(
+            flops=2 * blocks * size * width * cap,
+            bytes_accessed=2 * blocks * (2 * size + cap) * width,
+            transcendentals=0,
+        ),
+        name="combine" if weigh else "collect",
+    )(me, *operands)
+
+
+def down_kernel(units, down, *rest):
+    rest[-1][...] = product(units[...], down[...]).astype(bf16)
+
+
+def expert_down(units, down, *before):
+    rows, inner = units.shape
+    width = down.shape[1]
+    m, n = tile_of(rows), tile_of(width)
+    return pl.pallas_call(
+        down_kernel,
+        grid=(width // n, rows // m),
+        in_specs=[
+            pl.BlockSpec((m, inner), lambda j, i: (i, 0)),
+            pl.BlockSpec((inner, n), lambda j, i: (0, j)),
+        ]
+        + [pl.BlockSpec(memory_space=pl.ANY)] * len(before),
+        out_specs=pl.BlockSpec((m, n), lambda j, i: (i, j)),
+        out_shape=jax.ShapeDtypeStruct((rows, width), bf16),
+        compiler_params=pltpu.CompilerParams(vmem_limit_bytes=48 * 2**20),
+        cost_estimate=pl.CostEstimate(
+            flops=2 * rows * inner * width,
+            bytes_accessed=2 * (rows * inner + inner * width + rows * width),
+            transcendentals=0,
+        ),
+        name="expert_down",
+    )(units, down, *before)
+
+
+def input_kernel(dgate, dup, gate, up, *rest):
+    total = product_t(dgate[...], gate[...]) + product_t(dup[...], up[...])
+    rest[-1][...] = total.astype(bf16)
+
+
+def expert_input_grad(dgate, dup, gate, up, *before):
+    rows, inner = dgate.shape
+    width = gate.shape[0]
+    m, n = tile_of(rows), tile_of(width)
+    left = pl.BlockSpec((m, inner), lambda j, i: (i, 0))
+    right = pl.BlockSpec((n, inner), lambda j, i: (j, 0))
+    return pl.pallas_call(
+        input_kernel,
+        grid=(width // n, rows // m),
+        in_specs=[left, left, right, right] + [pl.BlockSpec(memory_space=pl.ANY)] * len(before),
+        out_specs=pl.BlockSpec((m, n), lambda j, i: (i, j)),
+        out_shape=jax.ShapeDtypeStruct((rows, width), bf16),
+        compiler_params=pltpu.CompilerParams(vmem_limit_bytes=52 * 2**20),
+        cost_estimate=pl.CostEstimate(
+            flops=4 * rows * inner * width,
+            bytes_accessed=2 * (2 * rows * inner + 2 * inner * width + rows * width),
+            transcendentals=0,
+        ),
+        name="expert_input_grad",
+    )(dgate, dup, gate, up, *before)
+
+
+def tile_of(size):
+    return max(c for c in range(16, 513, 16) if size % c == 0)
+
+
+def anchor_kernel(*refs):
+    pass
+
+
+def after(a, *before):
+    return pl.pallas_call(
+        anchor_kernel,
+        in_specs=[pl.BlockSpec(memory_space=pl.ANY)] * (1 + len(before)),
+        out_specs=pl.BlockSpec(memory_space=pl.ANY),
+        out_shape=jax.ShapeDtypeStruct(a.shape, a.dtype),
+        input_output_aliases={0: 0},
+        cost_estimate=pl.CostEstimate(flops=0, bytes_accessed=0, transcendentals=0),
+        name="after",
+    )(a, *before)
 
 
 def norm_backward(grad_rows, normed, inverse, gain):
@@ -316,7 +513,8 @@
     experts = router.shape[1]
     topk = routes.shape[2]
     plane = 8 * home
-    capacity = (5 * seq_dev * topk // (4 * experts)) * (plane // seq_dev)
+    blocks = plane // seq_dev
+    cap = 5 * seq_dev * topk // (4 * experts)
     dp_i, seq_i, r_i, y_i, core_i = (lax.axis_index(a) for a in EVERY)
     group, member = seq_i // seq_count, seq_i % seq_count
 
@@ -329,12 +527,14 @@
     )
     small = pick(pick(small, group, 4), member, 5)
     segment = pick(pick(small, dp_i, 0), y_i, 2)[:, :, topk].reshape(length)
-    plane_routes = (
-        pick(small, r_i, 2)[:, :, :, :topk]
-        .reshape(dp_n, seq_n, y_n, topk, core_n, piece)
-        .transpose(3, 0, 2, 4, 1, 5)
-        .reshape(topk, dp_n, y_n, core_n, home)
-    )
+    plane_routes = pick(small, r_i, 2)[:, :, :, :topk].transpose(0, 2, 1, 3, 4)
+    block_routes = plane_routes.reshape(blocks, topk, seq_dev)
+    home_routes = (
+        pick(pick(plane_routes, dp_i, 0), y_i, 0)
+        .reshape(seq_n, topk, core_n, piece)
+        .transpose(1, 2, 0, 3)
+    )
+    home_routes = pick(home_routes, core_i, 1).reshape(topk, home)
 
     local = jnp.concatenate([query_weight, key_weight, value_weight, output_weight], axis=1)
     rows_here = local.shape[0]
@@ -351,8 +551,8 @@
             )
         return whole
 
-    weight_in = gathered(local[:, :, : 3 * columns])
-    weight_out = gathered(local[:, :, 3 * columns :])
+    weights = gathered(local)
+    weight_in, weight_out = weights[:, : 3 * columns], weights[:, 3 * columns :]
 
     token_float = to_sequences(tokens).astype(f32)
     grad_home = to_sequences(grad_out)
@@ -380,73 +580,64 @@
     hidden_two = (normed_two * expert_norm).astype(bf16).reshape(home, width)
 
     hidden_plane = lax.all_gather(hidden_two, PLANE, axis=0, tiled=True)
-    all_routes = plane_routes.reshape(topk, plane)
     mine = y_i * core_n + core_i
-    to_me = all_routes == mine
-    chosen_here = jnp.any(to_me, axis=0)
-    rank = counts_before(chosen_here)
-    ends = rank + chosen_here.astype(jnp.int32)
-    slots = jnp.arange(capacity, dtype=jnp.int32)
-    source = jnp.sum((ends[None, :] <= slots[:, None]).astype(jnp.int32), axis=1)
-    filled = source < plane
-    source = jnp.minimum(source, plane - 1)
-
-    def gates_of(rows, where):
-        logits = product(rows, router)
-        hot = where[:, :, None] == jnp.arange(experts, dtype=jnp.int32)[None, None, :]
-        picked = jnp.sum(jnp.where(hot, logits[None], 0.0), axis=2)
-        return jax.nn.softmax(picked, axis=0), hot
-
-    plane_gates, _ = gates_of(hidden_plane, all_routes)
-    my_gate = jnp.sum(jnp.where(to_me, plane_gates, 0.0), axis=0)
-    row_gate = jnp.where(filled, my_gate[source], 0.0)[:, None]
-    expert_in = hidden_plane[source]
-    dout_rows = grad_plane[source]
-    dy_rows = (row_gate * dout_rows.astype(f32)).astype(bf16)
+    chosen = jnp.any(block_routes == mine, axis=1)
+    places = jnp.arange(seq_dev)
+    rank = product(chosen.astype(bf16), (places[:, None] < places[None, :]).astype(bf16))
+    slot = jnp.where(chosen, rank.astype(jnp.int32), -1)
+    slot_row, slot_col = slot[:, None, :], slot[:, :, None]
+    me = jnp.stack([dp_i, y_i, core_i, mine]).astype(jnp.int32)
+    expert_rows, dy_rows, row_gate = dispatch(
+        me,
+        hidden_plane,
+        grad_plane,
+        slot_row,
+        jnp.transpose(block_routes, (0, 2, 1)),
+        router,
+        seq_n,
+        piece,
+        cap,
+    )
+    expert_in = expert_rows.reshape(blocks * cap, width)
+    dy_rows = dy_rows.reshape(blocks * cap, width)
 
     gate_one, up_one, down_one = gate_weight[0], up_weight[0], down_weight[0]
     units, dgpre, dupre = expert_units(expert_in, dy_rows, gate_one, up_one, down_one)
 
     def over_ctx(part):
-        return lax.psum_scatter(part.astype(bf16), CTX, scatter_dimension=0, tiled=True).astype(f32)
-
-    grad_down = jnp.transpose(over_ctx(t_product(dy_rows, units)))[None]
-    grad_gate = over_ctx(t_product(expert_in, dgpre))[None]
-    grad_up = over_ctx(t_product(expert_in, dupre))[None]
-
-    ypair = product(units, down_one).astype(bf16)
-    dgate_rows = jnp.sum(dout_rows.astype(f32) * ypair.astype(f32), axis=1)
-    weighted = (row_gate * ypair.astype(f32)).astype(bf16)
-    dinput = (product_t(dgpre, gate_one) + product_t(dupre, up_one)).astype(bf16)
-
-    def relative(a):
-        a = a.reshape(dp_n, y_n, core_n, home)
-        for axis, index in ((0, dp_i), (1, y_i), (2, core_i)):
-            a = jnp.where(index == 0, a, jnp.flip(a, axis))
-        return a.reshape(plane)
-
-    place = relative(jnp.where(chosen_here, rank, -1))
-    has = (place >= 0)[:, None]
-    place = jnp.maximum(place, 0)
-
-    def returned(rows):
-        return plane_scatter(jnp.where(has, rows[place], jnp.zeros((), bf16)), width)
-
-    dgate_plane = jnp.where(chosen_here, dgate_rows[jnp.minimum(rank, capacity - 1)], 0.0)
+        return lax.psum_scatter(part, CTX, scatter_dimension=0, tiled=True)
+
+    down_part = t_product(dy_rows, units).astype(bf16)
+    gate_part = t_product(expert_in, dgpre).astype(bf16)
+    up_part = t_product(expert_in, dupre).astype(bf16)
+    down_sum, gate_sum, up_sum = over_ctx(down_part), over_ctx(gate_part), over_ctx(up_part)
+    grad_down = jnp.transpose(down_sum.astype(f32))[None]
+    grad_gate = gate_sum.astype(f32)[None]
+    grad_up = up_sum.astype(f32)[None]
+
+    dinput = expert_input_grad(dgpre, dupre, gate_one, up_one, down_part, gate_part, up_part)
+    [back] = combine(me, dinput.reshape(blocks, cap, width), slot_col, seq_n, piece)
+    ypair = expert_down(units, down_one, dinput)
+    mixed_rows, dgate_plane = combine(
+        me, ypair.reshape(blocks, cap, width), slot_col, seq_n, piece, row_gate, grad_plane
+    )
+
+    dgate_plane = dgate_plane.reshape(dp_n * y_n, seq_n, core_n, piece).transpose(0, 2, 1, 3)
     dgate_home = lax.all_to_all(
         dgate_plane.reshape(8, home), PLANE, split_axis=0, concat_axis=0, tiled=True
     ).reshape(dp_n, experts, home).sum(axis=0)
 
-    mixture = returned(weighted).reshape(seq_n, piece, width)
+    mixture = plane_scatter(mixed_rows)
     output = from_sequences((residual + mixture).astype(bf16))
 
-    my_routes = pick(pick(pick(plane_routes, dp_i, 1), y_i, 1), core_i, 1)
-    gates, hot = gates_of(hidden_two, my_routes)
+    logits = product(hidden_two, router)
+    hot = home_routes[:, :, None] == jnp.arange(experts, dtype=jnp.int32)[None, None, :]
+    gates = jax.nn.softmax(jnp.sum(jnp.where(hot, logits[None], 0.0), axis=2), axis=0)
     dgate = jnp.sum(jnp.where(hot, jnp.transpose(dgate_home)[None], 0.0), axis=2)
     dsel = gates * (dgate - jnp.sum(gates * dgate, axis=0, keepdims=True))
     dlogits = jnp.sum(jnp.where(hot, dsel[:, :, None], 0.0), axis=0).astype(bf16)
     router_grad = t_product(hidden_two, dlogits)
-    dhidden_two = returned(dinput) + product_t(dlogits, router)
+    dhidden_two = plane_scatter(back).reshape(home, width) + product_t(dlogits, router)
 
     flat_two = normed_two.reshape(home, width)
     dresid, expert_norm_grad = norm_backward(
@@ -459,7 +650,7 @@
     out_grad = t_product(mixed_full, dbranch_here)
     dmixed = chip_scatter(product_t(dbranch_here, weight_out).astype(bf16), 1, parts).astype(bf16)
     dqpre, dkpre, dvpre = attend_back(
-        query, keys, values, mixed, dmixed, cosine, sine, seg_row, seg_col, heads
+        query, keys, values, mixed, dmixed, cosine, sine, seg_row, seg_col, heads, down_sum
     )
     dqkv = jnp.concatenate([dqpre, dkpre, dvpre], axis=1)
     in_grad = t_product(hidden_full, dqkv)
@@ -476,13 +667,20 @@
     grad_tokens = from_sequences((dtokens + dresid).astype(bf16).reshape(seq_n, piece, width)).astype(f32)
 
     def spread_sum(part):
-        if r_n > 1:
-            part = (
-                part.reshape(dp_n * seq_n, r_n, y_n, core_n * rows_here, -1)
-                .transpose(0, 2, 1, 3, 4)
-                .reshape(width, -1)
-            )
-        part = lax.psum_scatter(part.astype(bf16), SPREAD, scatter_dimension=0, tiled=True)
+        part = part.astype(bf16).reshape(dp_n, seq_n, r_n, y_n, core_n * rows_here, -1)
+        count = part.shape[-1] // 2
+
+        def half(a, axis, index, name):
+            keep, give = pick(a, index, axis), pick(a, 1 - index, axis)
+            return (keep.astype(f32) + swap(give, name).astype(f32)).astype(bf16)
+
+        one = half(part[..., :count], 0, dp_i, "dp")
+        two = half(part[..., count:], 3, y_i, "y")
+        one = half(one, 2, y_i, "y")
+        two = half(two, 0, dp_i, "dp")
+        part = jnp.concatenate([one, two], axis=-1)
+        part = lax.all_to_all(part, "seq", split_axis=0, concat_axis=0, tiled=True)
+        part = jnp.sum(part.astype(f32), axis=0).astype(bf16)
         part = part.reshape(parts, rows_here, -1, 1, columns)
         return chip_exchange(part, 0, 3, parts).reshape(rows_here, -1, width).astype(f32)
 

time: 2240 us -> 1620 us (0.72)
  waiting for transfers between devices: 999 us -> 543 us
  Pallas kernels: 175 us -> 357 us
  local copies, waits for them, and re-layouts: 235 us -> 92.4 us
  matrix products: 328 us -> 192 us
  blocking collectives: 315 us -> 229 us
    reduce_scatter x5 -> x3, waiting for transfers between devices: 758 us -> 0.02 us  [over_ctx(): return lax.psum_scatter(part, CTX, scatter_dimension=0, tiled=True)]
    pallas_call x0 -> x5, Pallas kernels: none -> 181 us  [the longest x1 73.9 us: expert_input_grad(): pl.pallas_call(input_kernel, grid=(width // n, rows // m), in_specs=[left...]
    gather x7 -> x0, local copies, waits for them, and re-layouts: 166 us -> none  [the longest x2 73.3 us: returned(): rows[place]]
    unnamed x11 -> x8, waiting for transfers between devices: 0.17 us -> 125 us
    ppermute x23 -> x31, waiting for transfers between devices: 58.9 us -> 181 us  [swap(): return lax.ppermute(a, axis, [(0, 1), (1, 0)])]
    dot_general x5 -> x3, matrix products: 106 us -> 24.6 us  [product_t(): lax.dot_general(a, b, (((1,), (1,)), ((), ())), preferred_element_type=f32)]
    all_to_all x1 -> x0, blocking collectives: 74.8 us -> none  [from_sequences(): a = lax.all_to_all(a, 'seq', split_axis=0, concat_axis=0, tiled=True)]
    all_gather x2 -> x1, waiting for transfers between devices: 0.01 us -> 58.1 us  [gathered(): lax.all_gather(block.reshape(parts * rows_here, -1), SPREAD, axis=0, tile...]
  transfers between devices with their start and end apart: 35 -> 43, of which waited for: 18 -> 22; matrix products, arithmetic and copies ran while one was open for 17% -> 20% of each run, Pallas kernels for 3% -> 13%
where the time goes in v2:
time: 1620 us; the launch traced here: 1600 us
  waiting for transfers between devices  543 us (34%)
  Pallas kernels  357 us (22%)
  blocking collectives  229 us (14%)
  matrix products  192 us (12%)
  other arithmetic  124 us (8%)
  local copies, waits for them, and re-layouts  92.4 us (6%)
  starting transfers between devices  51.4 us (3%)
    all_to_all x2, blocking collectives, to_sequences(): return lax.all_to_all(a, 'seq', split_axis=0, concat_axis=0, tiled=True)  185 us
    ppermute x31, waiting for transfers between devices, swap(): return lax.ppermute(a, axis, [(0, 1), (1, 0)])  181 us
    dot_general x6, matrix products, t_product(): lax.dot_general(a, b, (((0,), (0,)), ((), ())), preferred_element_type=f32)  138 us
    unnamed x8, waiting for transfers between devices  125 us
    pallas_call x1, Pallas kernels, expert_units(): pl.pallas_call(functools.partial(units_kernel, chunk), grid=(units // til...  115 us
    all_gather x1, waiting for transfers between devices, on_device(): hidden_plane = lax.all_gather(hidden_two, PLANE, axis=0, tiled=True)  91.7 us
    pallas_call x1, Pallas kernels, expert_input_grad(): pl.pallas_call(input_kernel, grid=(width // n, rows // m), in_specs=[left...  73.9 us
    all_gather x1, waiting for transfers between devices, gathered(): lax.all_gather(block.reshape(parts * rows_here, -1), SPREAD, axis=0, tile...  58.1 us
  transfers between devices with their start and end apart: 43, of which 22 were waited for; matrix products, arithmetic and copies ran while one was open for 20% of the time, Pallas kernels for 13%

profile of v2, /device:TPU:1, one launch (start us, length us, event | category | flops | bytes accessed | tf_op | source)
XLA Modules:
  0.0 1604.6 jit_solution(8069905710742958929)
XLA Ops:
  30.4 89.4 %all_to_all.39 = bf16[4,128,2048]{2,1,0:T(8,128)(2,1)} all-to-all(bf16[4,128,2048]{2,1,0:T(8,128)(2,1)S(1)} %pad_maximum_fusion.8), channel_id=1, replica_groups=mesh['dp'=2,'seq'=4,'r'=1,'y'=2,'core'=2] {'seq'}, dimensions={0} | all-to-all | bytes 4194304 | tf_op jit(solution)/shard_map/all_to_all | solution.py:82
  126.6 96.0 %all_to_all.40 = bf16[4,128,2048]{2,1,0:T(8,128)(2,1)S(1)} all-to-all(bf16[4,128,2048]{2,1,0:T(8,128)(2,1)S(1)} %pad_maximum_fusion.6), channel_id=1, replica_groups=mesh['dp'=2,'seq'=4,'r'=1,'y'=2,'core'=2] {'seq'}, dimensions={0} | all-to-all | bytes 4194304 | tf_op jit(solution)/shard_map/all_to_all | solution.py:82
  226.2 43.8 %all-gather = s32[32,6,256]{2,1,0:T(8,128)S(1)} all-gather(s32[1,6,256]{2,1,0:T(8,128)S(1)} %reshape.443), channel_id=1, replica_groups=mesh['dp'=2,'seq'=4,'r'=1,'y'=2,'core'=2] {'dp','seq','r','y','core'}, dimensions={0}, use_global_device_ids=true | all-gather | bytes 202752 | tf_op jit(solution)/shard_map/all_gather | solution.py:525
  278.8 58.1 %all-gather.5.cloned.1.call-done = bf16[2048,4096]{0,1:T(8,128)(2,1)} async-done(((bf16[128,4096]{0,1:T(8,128)(2,1)}), bf16[2048,4096]{0,1:T(8,128)(2,1)}) %all-gather.5.cloned.1.call-update) | async-done | bytes 16777232 | tf_op jit(solution)/shard_map/all_gather | solution.py:545
  336.9 19.1 %fusion.4.qp.kp.vp = f32[1024,3072]{1,0:T(8,128)} fusion(bf16[1024,2048]{1,0:T(8,128)(2,1)} %bitcast.304, bf16[2048,4096]{0,1:T(8,128)(2,1)} %all-gather.5.cloned.1.call-done), kind=kOutput, calls=%fused_computation.10 | convolution fusion | flops 12884901888 | bytes 29360128 | tf_op jit(solution)/shard_map/dot_general | solution.py:27
  356.0 28.0 %attend.1 = (bf16[1024,1024]{1,0:T(8,128)(2,1)S(1)}, bf16[1024,1024]{1,0:T(8,128)(2,1)S(1)}, bf16[1024,1024]{1,0:T(8,128)(2,1)}, bf16[1024,1024]{1,0:T(8,128)(2,1)}) custom-call(f32[1024,3072]{1,0:T(8,128)} %fusion.4.qp.kp.vp, f32[1024,3072]{1,0:T(8,128)} %fusion.4.qp.kp.vp, f32[1024,3072]{1,0:T(8,128)} %fusion.4.qp.kp.vp, ...), custom_call_target="tpu_custom_call" | custom-call | flops 2684354560 | bytes 20971520 | tf_op jit(solution)/shard_map/attend/pallas_call | solution.py:146
  428.7 91.7 %all-gather.7.cloned.1.call-done = bf16[4096,2048]{1,0:T(8,128)(2,1)} async-done(((bf16[512,2048]{1,0:T(8,128)(2,1)}), bf16[4096,2048]{1,0:T(8,128)(2,1)}) %all-gather.7.cloned.1.call-update) | async-done | bytes 16777232 | tf_op jit(solution)/shard_map/all_gather | solution.py:582
  520.4 25.9 %dispatch.1 = (bf16[16,160,2048]{2,1,0:T(8,128)(2,1)}, bf16[16,160,2048]{2,1,0:T(8,128)(2,1)}, f32[16,256,1]{2,1,0:T(8,128)S(1)}) custom-call(s32[4]{0:T(128)S(1)} %pad_add_fusion.1.me, bf16[4,2,4,128,2048]{4,3,2,1,0:T(8,128)(2,1)} %bitcast.292, bf16[4,2,4,128,2048]{4,3,2,1,0:T(8,128)(2,1)} %bitcast.286, s32[16,1,256]{2,1,0:T(1,128)S(1)} %broadcast_in_dim.87.slot, ...), custom_call_target="tpu_custom_call" | custom-call | flops 7516192768 | bytes 54525952 | tf_op jit(solution)/shard_map/dispatch/pallas_call | solution.py:317
  547.7 114.9 %expert_units.1 = (bf16[2560,2816]{1,0:T(8,128)(2,1)}, bf16[2560,2816]{1,0:T(8,128)(2,1)}, bf16[2560,2816]{1,0:T(8,128)(2,1)}) custom-call(bf16[2560,2048]{1,0:T(8,128)(2,1)} %bitcast.333, bf16[2560,2048]{1,0:T(8,128)(2,1)} %bitcast.336, bf16[2048,2816]{1,0:T(8,128)(2,1)} %bitcast.327, bf16[2048,2816]{1,0:T(8,128)(2,1)} %bitcast.329, ...), custom_call_target="tpu_custom_call" | custom-call | flops 88583700480 | bytes 98828288 | tf_op jit(solution)/shard_map/expert_units/pallas_call | solution.py:248
  662.6 38.4 %convolution_convert_fusion.2.rest_0_ = bf16[2048,2816]{1,0:T(8,128)(2,1)} fusion(bf16[2560,2048]{1,0:T(8,128)(2,1)} %bitcast.337, bf16[2560,2816]{1,0:T(8,128)(2,1)} %get-tuple-element.30.units), kind=kOutput, calls=%fused_computation.6 | convolution fusion | flops 29533667328 | bytes 36438016 | tf_op jit(solution)/shard_map/dot_general | solution.py:35
  701.7 39.3 %convolution_convert_fusion.1.rest_1_ = bf16[2048,2816]{1,0:T(8,128)(2,1)} fusion(bf16[2560,2048]{1,0:T(8,128)(2,1)} %bitcast.334, bf16[2560,2816]{1,0:T(8,128)(2,1)} %get-tuple-element.31.dgate), kind=kOutput, calls=%fused_computation.5 | convolution fusion | flops 29533667328 | bytes 36438016 | tf_op jit(solution)/shard_map/dot_general | solution.py:35
  741.0 38.9 %convolution_convert_fusion.rest_2_ = bf16[2048,2816]{1,0:T(8,128)(2,1)} fusion(bf16[2560,2048]{1,0:T(8,128)(2,1)} %bitcast.335, bf16[2560,2816]{1,0:T(8,128)(2,1)} %get-tuple-element.32.dup), kind=kOutput, calls=%fused_computation.4 | convolution fusion | flops 29533667328 | bytes 36438016 | tf_op jit(solution)/shard_map/dot_general | solution.py:35
  779.8 73.9 %expert_input_grad.1.rest_0_ = bf16[2560,2048]{1,0:T(8,128)(2,1)} custom-call(bf16[2560,2816]{1,0:T(8,128)(2,1)} %get-tuple-element.31.dgate, bf16[2560,2816]{1,0:T(8,128)(2,1)} %get-tuple-element.32.dup, bf16[2048,2816]{1,0:T(8,128)(2,1)} %bitcast.328, bf16[2048,2816]{1,0:T(8,128)(2,1)} %bitcast.330, bf16[2048,2816]{1,0:T(8,128)(2,1)} %convolution_convert_fusion.2.rest_0_, ...), custom_call_target="tpu_custom_call" | custom-call | flops 59055800320 | bytes 62390272 | tf_op jit(solution)/shard_map/expert_input_grad/pallas_call | solution.py:441
  879.9 43.8 %expert_down.1 = bf16[2560,2048]{1,0:T(8,128)(2,1)} custom-call(bf16[2560,2816]{1,0:T(8,128)(2,1)} %get-tuple-element.30.units, bf16[2816,2048]{1,0:T(8,128)(2,1)} %bitcast.332, bf16[2560,2048]{1,0:T(8,128)(2,1)} %expert_input_grad.1.rest_0_), custom_call_target="tpu_custom_call" | custom-call | flops 29527900160 | bytes 36438016 | tf_op jit(solution)/shard_map/expert_down/pallas_call | solution.py:410
  923.8 24.4 %combine.1 = (bf16[2,2,2,4,128,2048]{5,4,3,2,1,0:T(8,128)(2,1)}, f32[16,256,1]{2,1,0:T(8,128)S(1)}) custom-call(s32[4]{0:T(128)S(1)} %pad_add_fusion.1.me, bf16[16,160,2048]{2,1,0:T(8,128)(2,1)} %bitcast.294, s32[16,256,1]{2,1,0:T(8,128)S(1)} %copy.144.slot, f32[16,256,1]{2,1,0:T(8,128)S(1)} %copy-done.10, bf16[4,2,4,128,2048]{4,3,2,1,0:T(8,128)(2,1)} %bitcast.287), custom_call_target="tpu_custom_call" | custom-call | flops 2684354560 | bytes 44040192 | tf_op jit(solution)/shard_map/combine/pallas_call | solution.py:386
  967.4 23.4 %collective-permute-done.13 = bf16[2,128,2048]{2,1,0:T(8,128)(2,1)S(1)} collective-permute-done((bf16[2,128,2048]{2,1,0:T(8,128)(2,1)S(1)}, bf16[2,128,2048]{2,1,0:T(8,128)(2,1)S(1)}, u32[]{:S(2)}, u32[]{:S(2)}) %collective-permute-start.13) | collective-permute-done | bytes 1048608 | tf_op jit(solution)/shard_map/ppermute | solution.py:39
  1005.9 38.2 %all-to-all-done.3 = f32[8,1,512]{2,1,0:T(1,128)S(1)} async-done(((f32[8,1,512]{2,1,0:T(1,128)}), f32[8,1,512]{2,1,0:T(1,128)S(1)}, u32[]{:S(2)}, u32[]{:S(2)}) %all-to-all-start.3) | async-done | bytes 16416 | tf_op jit(solution)/shard_map/all_to_all | solution.py:626
  1092.9 17.8 %collective-permute-done.28 = bf16[2,4,1,128,512]{4,3,1,2,0:T(8,128)(2,1)S(1)} collective-permute-done((bf16[2,4,1,128,512]{4,3,1,2,0:T(8,128)(2,1)S(1)}, bf16[2,4,1,128,512]{4,3,1,2,0:T(8,128)(2,1)S(1)}, u32[]{:S(2)}, u32[]{:S(2)}) %collective-permute-start.28) | collective-permute-done | bytes 1048608 | tf_op jit(solution)/shard_map/ppermute | solution.py:39
  1123.3 43.7 %collective-permute-done.27 = bf16[4,1,128,512]{3,2,1,0:T(8,128)(2,1)S(1)} collective-permute-done((bf16[4,1,128,512]{3,2,1,0:T(8,128)(2,1)S(1)}, bf16[4,1,128,512]{3,2,1,0:T(8,128)(2,1)S(1)}, u32[]{:S(2)}, u32[]{:S(2)}) %collective-permute-start.27) | collective-permute-done | bytes 524320 | tf_op jit(solution)/shard_map/ppermute | solution.py:39
  1177.6 32.8 %attend_back.1 = (bf16[1024,1024]{1,0:T(8,128)(2,1)S(1)}, bf16[1024,1024]{1,0:T(8,128)(2,1)S(1)}, bf16[1024,1024]{1,0:T(8,128)(2,1)}) custom-call(bf16[1024,1024]{1,0:T(8,128)(2,1)} %copy-done.15, bf16[1024,1024]{1,0:T(8,128)(2,1)} %copy-done.16, bf16[1024,1024]{1,0:T(8,128)(2,1)} %get-tuple-element.37.v, bf16[1024,1024]{1,0:T(8,128)(2,1)} %get-tuple-element.27.mixed, ...), custom_call_target="tpu_custom_call" | custom-call | flops 6710886400 | bytes 16777216 | tf_op jit(solution)/shard_map/attend_back/pallas_call | solution.py:206
  1281.2 41.6 %collective-permute-done.23 = bf16[2,4,1,128,1536]{4,3,1,2,0:T(8,128)(2,1)} collective-permute-done((bf16[2,4,1,128,1536]{4,3,1,2,0:T(8,128)(2,1)}, bf16[2,4,1,128,1536]{4,3,1,2,0:T(8,128)(2,1)}, u32[]{:S(2)}, u32[]{:S(2)}) %collective-permute-start.23) | collective-permute-done | bytes 3145760 | tf_op jit(solution)/shard_map/ppermute | solution.py:39
  1328.8 30.3 %all-to-all-done.4 = bf16[4,128,2048]{2,1,0:T(8,128)(2,1)} async-done(((bf16[4,128,2048]{2,1,0:T(8,128)(2,1)}), bf16[4,128,2048]{2,1,0:T(8,128)(2,1)}, u32[]{:S(2)}, u32[]{:S(2)}) %all-to-all-start.4) | async-done | bytes 2097184 | tf_op jit(solution)/shard_map/all_to_all | solution.py:86
  1384.4 21.6 %collective-permute-done.22 = bf16[4,1,128,1536]{3,2,1,0:T(8,128)(2,1)} collective-permute-done((bf16[4,1,128,1536]{3,2,1,0:T(8,128)(2,1)}, bf16[4,1,128,1536]{3,2,1,0:T(8,128)(2,1)}, u32[]{:S(2)}, u32[]{:S(2)}) %collective-permute-start.22) | collective-permute-done | bytes 1572896 | tf_op jit(solution)/shard_map/ppermute | solution.py:39
  1443.5 124.5 %reduce-scatter.13.cloned.1.call-done = f32[64,6]{1,0:T(8,128)} async-done(((f32[2048,6]{1,0:T(8,128)}), f32[64,6]{1,0:T(8,128)}) %reduce-scatter.13.cloned.1.call-update) | async-done | bytes 1552
  (366 shorter events, 389.3 us)
Async XLA Ops:
  7.2 329.7 %all-gather.5.cloned.1.call-start = ((), (), s32[]{:S(2)}) async-start(), calls=%async_computation.11 | async-start | bytes 17825792 | tf_op jit(solution)/shard_map/all_gather | solution.py:545
  24.3 404.4 %all-gather.9.cloned.1.call-start = ((), (), s32[]{:S(2)}) async-start(), calls=%async_computation.13 | async-start | bytes 18874368 | tf_op jit(solution)/shard_map/all_gather | solution.py:563
  119.9 400.6 %all-gather.7.cloned.1.call-start = ((), (), s32[]{:S(2)}) async-start(), calls=%async_computation.12 | async-start | bytes 18874368 | tf_op jit(solution)/shard_map/all_gather | solution.py:582
  409.3 768.2 %reduce-scatter.7.cloned.1.call-start = ((), (), s32[]{:S(2)}) async-start(), calls=%async_computation.14 | async-start | bytes 14417920 | tf_op jit(solution)/shard_map/reduce_scatter | solution.py:608
  701.0 721.2 %reduce-scatter.9.cloned.1.call-start = ((), (), s32[]{:S(2)}) async-start(), calls=%async_computation.15 | async-start | bytes 14417920 | tf_op jit(solution)/shard_map/reduce_scatter | solution.py:608
  879.5 78.5 %collective-permute-start.12 = (bf16[2,2,4,128,2048]{4,3,2,1,0:T(8,128)(2,1)}, bf16[2,2,4,128,2048]{4,3,2,1,0:T(8,128)(2,1)}, u32[]{:S(2)}, u32[]{:S(2)}) collective-permute-start(bf16[2,2,4,128,2048]{4,3,2,1,0:T(8,128)(2,1)} %slice_bitcast_fusion), channel_id=1, source_target_pairs={{0,1},{1,0},{2,3},{3,2},{4,5},{5,4},{6,7},{7,6},{8,9},{9,8},{10,11... | collective-permute-start | bytes 25165832 | tf_op jit(solution)/shard_map/ppermute | solution.py:39
  958.0 95.2 %collective-permute-start.6 = (bf16[2,2,4,128,2048]{4,3,2,1,0:T(8,128)(2,1)}, bf16[2,2,4,128,2048]{4,3,2,1,0:T(8,128)(2,1)}, u32[]{:S(2)}, u32[]{:S(2)}) collective-permute-start(bf16[2,2,4,128,2048]{4,3,2,1,0:T(8,128)(2,1)} %slice_bitcast_fusion.3), channel_id=1, source_target_pairs={{0,1},{1,0},{2,3},{3,2},{4,5},{5,4},{6,7},{7,6},{8,9},{9,8},{10,11... | collective-permute-start | bytes 25165832 | tf_op jit(solution)/shard_map/ppermute | solution.py:39
  993.3 51.1 %collective-permute-start.16 = (bf16[4,128,2048]{2,1,0:T(8,128)(2,1)}, bf16[4,128,2048]{2,1,0:T(8,128)(2,1)}, u32[]{:S(2)}, u32[]{:S(2)}) collective-permute-start(bf16[4,128,2048]{2,1,0:T(8,128)(2,1)} %pad_maximum_fusion.13), channel_id=1, source_target_pairs={{0,2},{2,0},{1,3},{3,1},{4,6},{6,4},{5,7},{7,5},{8,10},{10,8},{9,1... | collective-permute-start | bytes 6291464 | tf_op jit(solution)/shard_map/ppermute | solution.py:39
  995.9 48.5 %collective-permute-start.14 = (bf16[4,128,2048]{2,1,0:T(8,128)(2,1)}, bf16[4,128,2048]{2,1,0:T(8,128)(2,1)}, u32[]{:S(2)}, u32[]{:S(2)}) collective-permute-start(bf16[4,128,2048]{2,1,0:T(8,128)(2,1)} %pad_maximum_fusion.12), channel_id=1, source_target_pairs={{0,16},{16,0},{1,17},{17,1},{2,18},{18,2},{3,19},{19,3},{4,20},{20... | collective-permute-start | bytes 6291464 | tf_op jit(solution)/shard_map/ppermute | solution.py:39
  1003.6 428.9 %reduce-scatter.11.cloned.1.call-start = ((), (), s32[]{:S(2)}) async-start(), calls=%async_computation.16 | async-start | bytes 14417920 | tf_op jit(solution)/shard_map/reduce_scatter | solution.py:608
  1084.8 88.3 %collective-permute-start.18 = (bf16[1024,1024]{1,0:T(8,128)(2,1)}, bf16[1024,1024]{1,0:T(8,128)(2,1)}, u32[]{:S(2)}, u32[]{:S(2)}) collective-permute-start(bf16[1024,1024]{1,0:T(8,128)(2,1)} %constant_dynamic-slice_fusion.9), channel_id=1, source_target_pairs={{0,1},{1,0},{2,3},{3,2},{4,5},{5,4},{6,7},{7,6},{8,9},{9,8},{10,11... | collective-permute-start | bytes 6291464 | tf_op jit(solution)/shard_map/ppermute | solution.py:39
  1092.5 167.0 %collective-permute-start.10 = (bf16[4,128,2048]{2,1,0:T(8,128)(2,1)}, bf16[4,128,2048]{2,1,0:T(8,128)(2,1)}, u32[]{:S(2)}, u32[]{:S(2)}) collective-permute-start(bf16[4,128,2048]{2,1,0:T(8,128)(2,1)} %pad_maximum_fusion.10), channel_id=1, source_target_pairs={{0,2},{2,0},{1,3},{3,1},{4,6},{6,4},{5,7},{7,5},{8,10},{10,8},{9,1... | collective-permute-start | bytes 6291464 | tf_op jit(solution)/shard_map/ppermute | solution.py:39
  1112.3 54.7 %collective-permute-start.27 = (bf16[4,1,128,512]{3,2,1,0:T(8,128)(2,1)S(1)}, bf16[4,1,128,512]{3,2,1,0:T(8,128)(2,1)S(1)}, u32[]{:S(2)}, u32[]{:S(2)}) collective-permute-start(bf16[4,1,128,512]{3,2,1,0:T(8,128)(2,1)S(1)} %dynamic-slice_bitcast_fusion.6), channel_id=1, source_target_pairs={{0,2},{2,0},{1,3},{3,1},{4,6},{6,4},{5,7},{7,5},{8,10},{10,8},{9,1... | collective-permute-start | bytes 1572872 | tf_op jit(solution)/shard_map/ppermute | solution.py:39
  1114.6 144.9 %collective-permute-start.8 = (bf16[4,128,2048]{2,1,0:T(8,128)(2,1)}, bf16[4,128,2048]{2,1,0:T(8,128)(2,1)}, u32[]{:S(2)}, u32[]{:S(2)}) collective-permute-start(bf16[4,128,2048]{2,1,0:T(8,128)(2,1)} %pad_maximum_fusion.9), channel_id=1, source_target_pairs={{0,16},{16,0},{1,17},{17,1},{2,18},{18,2},{3,19},{19,3},{4,20},{20... | collective-permute-start | bytes 6291464 | tf_op jit(solution)/shard_map/ppermute | solution.py:39
  1168.2 105.0 %all-to-all-start.6 = ((bf16[4,1,128,1024]{3,2,1,0:T(8,128)(2,1)}), bf16[4,1,128,1024]{3,2,1,0:T(8,128)(2,1)}, u32[]{:S(2)}, u32[]{:S(2)}) async-start(bf16[4,1,128,1024]{3,2,1,0:T(8,128)(2,1)} %pad_maximum_fusion.15), calls=%async_computation.7 | async-start | bytes 2097152 | tf_op jit(solution)/shard_map/all_to_all | solution.py:682
  1254.0 68.7 %collective-permute-start.23 = (bf16[2,4,1,128,1536]{4,3,1,2,0:T(8,128)(2,1)}, bf16[2,4,1,128,1536]{4,3,1,2,0:T(8,128)(2,1)}, u32[]{:S(2)}, u32[]{:S(2)}) collective-permute-start(bf16[2,4,1,128,1536]{4,3,1,2,0:T(8,128)(2,1)} %dynamic-slice_bitcast_fusion), channel_id=1, source_target_pairs={{0,2},{2,0},{1,3},{3,1},{4,6},{6,4},{5,7},{7,5},{8,10},{10,8},{9,1... | collective-permute-start | bytes 9437192 | tf_op jit(solution)/shard_map/ppermute | solution.py:39
  1273.2 85.9 %all-to-all-start.4 = ((bf16[4,128,2048]{2,1,0:T(8,128)(2,1)}), bf16[4,128,2048]{2,1,0:T(8,128)(2,1)}, u32[]{:S(2)}, u32[]{:S(2)}) async-start(bf16[4,128,2048]{2,1,0:T(8,128)(2,1)} %bitcast.297), calls=%async_computation.5 | async-start | bytes 4194304 | tf_op jit(solution)/shard_map/all_to_all | solution.py:86
  1280.5 83.1 %collective-permute-start.21 = (bf16[4,1,2,128,1536]{4,3,0,2,1:T(8,128)(2,1)}, bf16[4,1,2,128,1536]{4,3,0,2,1:T(8,128)(2,1)}, u32[]{:S(2)}, u32[]{:S(2)}) collective-permute-start(bf16[4,1,2,128,1536]{4,3,0,2,1:T(8,128)(2,1)} %bitcast.275), channel_id=1, source_target_pairs={{0,16},{16,0},{1,17},{17,1},{2,18},{18,2},{3,19},{19,3},{4,20},{20... | collective-permute-start | bytes 9437192 | tf_op jit(solution)/shard_map/ppermute | solution.py:39
  1327.7 54.8 %collective-permute-start.24 = (bf16[4,1,128,1536]{3,2,1,0:T(8,128)(2,1)}, bf16[4,1,128,1536]{3,2,1,0:T(8,128)(2,1)}, u32[]{:S(2)}, u32[]{:S(2)}) collective-permute-start(bf16[4,1,128,1536]{3,2,1,0:T(8,128)(2,1)} %dynamic-slice_bitcast_fusion.2), channel_id=1, source_target_pairs={{0,16},{16,0},{1,17},{17,1},{2,18},{18,2},{3,19},{19,3},{4,20},{20... | collective-permute-start | bytes 4718600 | tf_op jit(solution)/shard_map/ppermute | solution.py:39
  1359.1 52.3 %all-to-all-start.2 = ((bf16[4,128,2048]{2,1,0:T(8,128)(2,1)}), bf16[4,128,2048]{2,1,0:T(8,128)(2,1)}, u32[]{:S(2)}, u32[]{:S(2)}) async-start(bf16[4,128,2048]{2,1,0:T(8,128)(2,1)} %get-tuple-element.162), calls=%async_computation.2 | async-start | bytes 4194304 | tf_op jit(solution)/shard_map/all_to_all | solution.py:86
  1411.4 164.6 %all-to-all-start.5 = ((bf16[4,1,128,3072]{3,2,1,0:T(8,128)(2,1)}), bf16[4,1,128,3072]{3,2,1,0:T(8,128)(2,1)}, u32[]{:S(2)}, u32[]{:S(2)}) async-start(bf16[4,1,128,3072]{3,2,1,0:T(8,128)(2,1)} %pad_maximum_fusion.3), calls=%async_computation.6 | async-start | bytes 6291456 | tf_op jit(solution)/shard_map/all_to_all | solution.py:682
  1416.1 152.0 %reduce-scatter.13.cloned.1.call-start = ((), (), s32[]{:S(2)}) async-start(), calls=%async_computation.17 | async-start | bytes 1081344
  1429.6 142.0 %collective-permute-start.20 = (bf16[2,128,2048]{2,1,0:T(8,128)(2,1)S(1)}, bf16[2,128,2048]{2,1,0:T(8,128)(2,1)S(1)}, u32[]{:S(2)}, u32[]{:S(2)}) collective-permute-start(bf16[2,128,2048]{2,1,0:T(8,128)(2,1)S(1)} %constant_dynamic-slice_fusion.7), channel_id=1, source_target_pairs={{0,1},{1,0},{2,3},{3,2},{4,5},{5,4},{6,7},{7,6},{8,9},{9,8},{10,11... | collective-permute-start | bytes 3145736 | tf_op jit(solution)/shard_map/ppermute | solution.py:39
  1432.4 140.2 %collective-permute-start.11 = (bf16[2,128,2048]{2,1,0:T(8,128)(2,1)S(1)}, bf16[2,128,2048]{2,1,0:T(8,128)(2,1)}, u32[]{:S(2)}, u32[]{:S(2)}) collective-permute-start(bf16[2,128,2048]{2,1,0:T(8,128)(2,1)S(1)} %constant_dynamic-slice_fusion.12), channel_id=1, source_target_pairs={{0,1},{1,0},{2,3},{3,2},{4,5},{5,4},{6,7},{7,6},{8,9},{9,8},{10,11... | collective-permute-start | bytes 3145736 | tf_op jit(solution)/shard_map/ppermute | solution.py:39
  (83 other events, 1583.0 us)
Sparse Core Ops, SparseCore 0:
  24.5 312.3 all-gather.4
  338.8 89.8 all-gather.8
  430.6 89.8 all-gather.6
  701.1 194.5 reduce-scatter.6
  897.9 195.9 reduce-scatter.8
  1096.2 237.9 reduce-scatter.10
  1428.4 139.5 reduce-scatter.12

commit v3 on v2

--- a/solution.py
+++ b/solution.py
@@ -220,7 +220,8 @@
     )(q, k, v, mixed, dmixed, cosine, sine, seg_row, seg_col, *before)
 
 
-def units_kernel(chunk, x, dy, gate, up, down, units, dgate, dup):
+def units_kernel(chunk, x, dy, gate, up, down, *rest):
+    units, dgate, dup = rest[-3:]
     gate_w, up_w, down_w = gate[...], up[...], down[...]
 
     def step(i, carry):
@@ -238,11 +239,12 @@
     lax.fori_loop(0, x.shape[0] // chunk, step, 0)
 
 
-def expert_units(x, dy, gate, up, down):
+def expert_units(x, dy, gate, up, down, start, stop, *before):
     rows, width = x.shape
-    units = gate.shape[1]
-    chunk = max(c for c in range(16, 513, 16) if rows % c == 0)
-    tile = 256 if units % 256 == 0 else units
+    units = stop - start
+    chunk = tile_of(rows)
+    tile = unit_tile(gate.shape[1])
+    first = start // tile
     once = pl.BlockSpec((rows, width), lambda j: (0, 0), pipeline_mode=pl.Buffered(1))
     out = jax.ShapeDtypeStruct((rows, units), bf16)
     return pl.pallas_call(
@@ -251,10 +253,11 @@
         in_specs=[
             once,
             once,
-            pl.BlockSpec((width, tile), lambda j: (0, j)),
-            pl.BlockSpec((width, tile), lambda j: (0, j)),
-            pl.BlockSpec((tile, width), lambda j: (j, 0)),
-        ],
+            pl.BlockSpec((width, tile), lambda j: (0, first + j)),
+            pl.BlockSpec((width, tile), lambda j: (0, first + j)),
+            pl.BlockSpec((tile, width), lambda j: (first + j, 0)),
+        ]
+        + [pl.BlockSpec(memory_space=pl.ANY)] * len(before),
         out_specs=[pl.BlockSpec((rows, tile), lambda j: (0, j))] * 3,
         out_shape=[out] * 3,
         compiler_params=pltpu.CompilerParams(vmem_limit_bytes=56 * 2**20),
@@ -264,7 +267,16 @@
             transcendentals=rows * units,
         ),
         name="expert_units",
-    )(x, dy, gate, up, down)
+    )(x, dy, gate, up, down, *before)
+
+
+def unit_tile(units):
+    return 256 if units % 256 == 0 else units
+
+
+def unit_cut(units):
+    tile = unit_tile(units)
+    return units // tile // 2 * tile
 
 
 def dispatch_kernel(me, hidden, dout, slot, routes, router, rows, dy_rows, gate):
@@ -399,19 +411,21 @@
     )(me, *operands)
 
 
-def down_kernel(units, down, *rest):
-    rest[-1][...] = product(units[...], down[...]).astype(bf16)
-
-
-def expert_down(units, down, *before):
-    rows, inner = units.shape
-    width = down.shape[1]
+def down_kernel(cut, units_a, units_b, down, *rest):
+    total = product(units_a[...], down[:cut, :]) + product(units_b[...], down[cut:, :])
+    rest[-1][...] = total.astype(bf16)
+
+
+def expert_down(units_a, units_b, down, *before):
+    rows, cut = units_a.shape
+    inner, width = down.shape
     m, n = tile_of(rows), tile_of(width)
     return pl.pallas_call(
-        down_kernel,
+        functools.partial(down_kernel, cut),
         grid=(width // n, rows // m),
         in_specs=[
-            pl.BlockSpec((m, inner), lambda j, i: (i, 0)),
+            pl.BlockSpec((m, cut), lambda j, i: (i, 0)),
+            pl.BlockSpec((m, inner - cut), lambda j, i: (i, 0)),
             pl.BlockSpec((inner, n), lambda j, i: (0, j)),
         ]
         + [pl.BlockSpec(memory_space=pl.ANY)] * len(before),
@@ -424,24 +438,27 @@
             transcendentals=0,
         ),
         name="expert_down",
-    )(units, down, *before)
-
-
-def input_kernel(dgate, dup, gate, up, *rest):
-    total = product_t(dgate[...], gate[...]) + product_t(dup[...], up[...])
+    )(units_a, units_b, down, *before)
+
+
+def input_kernel(cut, dgate_a, dgate_b, dup_a, dup_b, gate, up, *rest):
+    total = product_t(dgate_a[...], gate[:, :cut]) + product_t(dgate_b[...], gate[:, cut:])
+    total += product_t(dup_a[...], up[:, :cut]) + product_t(dup_b[...], up[:, cut:])
     rest[-1][...] = total.astype(bf16)
 
 
-def expert_input_grad(dgate, dup, gate, up, *before):
-    rows, inner = dgate.shape
-    width = gate.shape[0]
+def expert_input_grad(dgate_a, dgate_b, dup_a, dup_b, gate, up, *before):
+    rows, cut = dgate_a.shape
+    width, inner = gate.shape
     m, n = tile_of(rows), tile_of(width)
-    left = pl.BlockSpec((m, inner), lambda j, i: (i, 0))
+    left_a = pl.BlockSpec((m, cut), lambda j, i: (i, 0))
+    left_b = pl.BlockSpec((m, inner - cut), lambda j, i: (i, 0))
     right = pl.BlockSpec((n, inner), lambda j, i: (j, 0))
     return pl.pallas_call(
-        input_kernel,
+        functools.partial(input_kernel, cut),
         grid=(width // n, rows // m),
-        in_specs=[left, left, right, right] + [pl.BlockSpec(memory_space=pl.ANY)] * len(before),
+        in_specs=[left_a, left_b, left_a, left_b, right, right]
+        + [pl.BlockSpec(memory_space=pl.ANY)] * len(before),
         out_specs=pl.BlockSpec((m, n), lambda j, i: (i, j)),
         out_shape=jax.ShapeDtypeStruct((rows, width), bf16),
         compiler_params=pltpu.CompilerParams(vmem_limit_bytes=52 * 2**20),
@@ -451,7 +468,7 @@
             transcendentals=0,
         ),
         name="expert_input_grad",
-    )(dgate, dup, gate, up, *before)
+    )(dgate_a, dgate_b, dup_a, dup_b, gate, up, *before)
 
 
 def tile_of(size):
@@ -602,22 +619,25 @@
     dy_rows = dy_rows.reshape(blocks * cap, width)
 
     gate_one, up_one, down_one = gate_weight[0], up_weight[0], down_weight[0]
-    units, dgpre, dupre = expert_units(expert_in, dy_rows, gate_one, up_one, down_one)
+    inner = gate_one.shape[1]
+    cut = unit_cut(inner)
+    full = (gate_one, up_one, down_one)
 
     def over_ctx(part):
         return lax.psum_scatter(part, CTX, scatter_dimension=0, tiled=True)
 
-    down_part = t_product(dy_rows, units).astype(bf16)
-    gate_part = t_product(expert_in, dgpre).astype(bf16)
-    up_part = t_product(expert_in, dupre).astype(bf16)
-    down_sum, gate_sum, up_sum = over_ctx(down_part), over_ctx(gate_part), over_ctx(up_part)
-    grad_down = jnp.transpose(down_sum.astype(f32))[None]
-    grad_gate = gate_sum.astype(f32)[None]
-    grad_up = up_sum.astype(f32)[None]
-
-    dinput = expert_input_grad(dgpre, dupre, gate_one, up_one, down_part, gate_part, up_part)
+    def rows_product(rows, part):
+        return t_product(rows, part).astype(bf16)
+
+    units_a, dgpre_a, dupre_a = expert_units(expert_in, dy_rows, *full, 0, cut)
+    down_a = rows_product(dy_rows, units_a)
+    units_b, dgpre_b, dupre_b = expert_units(expert_in, dy_rows, *full, cut, inner, down_a)
+    down_b = rows_product(dy_rows, units_b)
+    dinput = expert_input_grad(dgpre_a, dgpre_b, dupre_a, dupre_b, gate_one, up_one, down_b)
     [back] = combine(me, dinput.reshape(blocks, cap, width), slot_col, seq_n, piece)
-    ypair = expert_down(units, down_one, dinput)
+    gate_a = rows_product(expert_in, after(dgpre_a, back))
+    gate_b = rows_product(expert_in, after(dgpre_b, back))
+    ypair = expert_down(units_a, units_b, down_one, gate_a)
     mixed_rows, dgate_plane = combine(
         me, ypair.reshape(blocks, cap, width), slot_col, seq_n, piece, row_gate, grad_plane
     )
@@ -626,9 +646,6 @@
     dgate_home = lax.all_to_all(
         dgate_plane.reshape(8, home), PLANE, split_axis=0, concat_axis=0, tiled=True
     ).reshape(dp_n, experts, home).sum(axis=0)
-
-    mixture = plane_scatter(mixed_rows)
-    output = from_sequences((residual + mixture).astype(bf16))
 
     logits = product(hidden_two, router)
     hot = home_routes[:, :, None] == jnp.arange(experts, dtype=jnp.int32)[None, None, :]
@@ -650,10 +667,17 @@
     out_grad = t_product(mixed_full, dbranch_here)
     dmixed = chip_scatter(product_t(dbranch_here, weight_out).astype(bf16), 1, parts).astype(bf16)
     dqpre, dkpre, dvpre = attend_back(
-        query, keys, values, mixed, dmixed, cosine, sine, seg_row, seg_col, heads, down_sum
+        query, keys, values, mixed, dmixed, cosine, sine, seg_row, seg_col, heads, gate_b
     )
     dqkv = jnp.concatenate([dqpre, dkpre, dvpre], axis=1)
-    in_grad = t_product(hidden_full, dqkv)
+    in_grad = t_product(hidden_full, dqkv).astype(bf16)
+    up_a = rows_product(expert_in, after(dupre_a, dqpre))
+    up_b = rows_product(expert_in, after(dupre_b, dqpre))
+
+    grad_down = jnp.concatenate([over_ctx(down_a), over_ctx(down_b)], axis=1).astype(f32).T[None]
+    grad_gate = jnp.concatenate([over_ctx(gate_a), over_ctx(gate_b)], axis=1).astype(f32)[None]
+    grad_up = jnp.concatenate([over_ctx(up_a), over_ctx(up_b)], axis=1).astype(f32)[None]
+
     dhidden_one = chip_scatter(
         product_t(dqkv, weight_in).astype(bf16).reshape(seq_n, parts * piece, width), 1, parts
     )
@@ -666,31 +690,33 @@
     )
     grad_tokens = from_sequences((dtokens + dresid).astype(bf16).reshape(seq_n, piece, width)).astype(f32)
 
-    def spread_sum(part):
-        part = part.astype(bf16).reshape(dp_n, seq_n, r_n, y_n, core_n * rows_here, -1)
-        count = part.shape[-1] // 2
-
-        def half(a, axis, index, name):
-            keep, give = pick(a, index, axis), pick(a, 1 - index, axis)
-            return (keep.astype(f32) + swap(give, name).astype(f32)).astype(bf16)
-
-        one = half(part[..., :count], 0, dp_i, "dp")
-        two = half(part[..., count:], 3, y_i, "y")
-        one = half(one, 2, y_i, "y")
-        two = half(two, 0, dp_i, "dp")
-        part = jnp.concatenate([one, two], axis=-1)
-        part = lax.all_to_all(part, "seq", split_axis=0, concat_axis=0, tiled=True)
-        part = jnp.sum(part.astype(f32), axis=0).astype(bf16)
-        part = part.reshape(parts, rows_here, -1, 1, columns)
-        return chip_exchange(part, 0, 3, parts).reshape(rows_here, -1, width).astype(f32)
-
-    [grad_output] = jnp.moveaxis(spread_sum(out_grad), 1, 0)
-    grad_query, grad_key, grad_value = jnp.moveaxis(spread_sum(in_grad), 1, 0)
-
-    gains = jnp.concatenate(
-        [attn_norm_grad[:, None], expert_norm_grad[:, None], router_grad], axis=1
-    )
-    gains = lax.psum_scatter(gains, EVERY, scatter_dimension=0, tiled=True)
+    mixture = plane_scatter(after(mixed_rows, dqpre))
+    output = from_sequences((residual + mixture).astype(bf16))
+
+    gains = jnp.concatenate([attn_norm_grad[:, None], expert_norm_grad[:, None], router_grad], axis=1)
+    gain_n = gains.shape[1]
+    gains = jnp.pad(gains, ((0, 0), (0, 128 - gain_n))).astype(bf16)
+
+    def seen(part):
+        return part.reshape(dp_n, seq_n, r_n, y_n, core_n * rows_here, -1)
+
+    def half(a, axis, index, name):
+        keep, give = pick(a, index, axis), pick(a, 1 - index, axis)
+        return (keep.astype(f32) + swap(give, name).astype(f32)).astype(bf16)
+
+    one = seen(jnp.concatenate([out_grad.astype(bf16), in_grad[:, :columns]], axis=1))
+    two = seen(jnp.concatenate([in_grad[:, columns:], gains], axis=1))
+    one = half(half(one, 0, dp_i, "dp"), 2, y_i, "y")
+    two = half(half(two, 3, y_i, "y"), 0, dp_i, "dp")
+    part = jnp.concatenate([one, two], axis=-1)
+    part = lax.all_to_all(part, "seq", split_axis=0, concat_axis=0, tiled=True)
+    part = jnp.sum(part.astype(f32), axis=0).astype(bf16)
+    part = part.reshape(parts, rows_here, -1)
+    gains = chip_scatter(part[:, :, 4 * columns :], 0, parts)[0, :, :gain_n]
+    part = part[:, :, : 4 * columns].reshape(parts, rows_here, 4, 1, columns)
+    part = chip_exchange(part, 0, 3, parts).reshape(rows_here, 4, width).astype(f32)
+    grad_output, grad_query, grad_key, grad_value = (part[:, i] for i in range(4))
+
     return (
         output,
         grad_tokens,

time: 1620 us -> 1650 us (1.019)
  waiting for transfers between devices: 543 us -> 401 us
  local copies, waits for them, and re-layouts: 92.4 us -> 227 us
  other arithmetic: 124 us -> 147 us
  matrix products: 192 us -> 213 us
    unnamed x8 -> x9, waiting for transfers between devices: 125 us -> 0.15 us
    ppermute x31 -> x27, waiting for transfers between devices: 181 us -> 68.9 us  [swap(): return lax.ppermute(a, axis, [(0, 1), (1, 0)])]
    all_to_all x2, waiting for transfers between devices: 31.9 us -> 101 us  [from_sequences(): a = lax.all_to_all(a, 'seq', split_axis=0, concat_axis=0, tiled=True)]
    all_to_all x2 -> x1, waiting for transfers between devices: 0.01 us -> 64.1 us  [on_device(): part = lax.all_to_all(part, 'seq', split_axis=0, concat_axis=0, tiled=True)]
    unnamed x147 -> x158, local copies, waits for them, and re-layouts: 33.2 us -> 91.9 us
    dynamic_slice x5 -> x6, local copies, waits for them, and re-layouts: 4.06 us -> 41.4 us  [pick(): return lax.dynamic_index_in_dim(a, index, axis, keepdims=False)]
    all_to_all x1, waiting for transfers between devices: 38.2 us -> 1.76 us  [on_device(): lax.all_to_all(dgate_plane.reshape(8, home), PLANE, split_axis=0, concat_...]
    reshape x1 -> x3, local copies, waits for them, and re-layouts: 3.57 us -> 31.4 us  [the longest x2 29.5 us: seen(): return part.reshape(dp_n, seq_n, r_n, y_n, core_n * rows_here, -1)]
  transfers between devices with their start and end apart: 43 -> 40, of which waited for: 22 -> 18; matrix products, arithmetic and copies ran while one was open for 20% -> 31% of each run, Pallas kernels for 13% -> 17%
where the time goes in v3:
time: 1650 us; the launch traced here: 1640 us
  waiting for transfers between devices  401 us (24%)
  Pallas kernels  368 us (22%)
  blocking collectives  229 us (14%)
  local copies, waits for them, and re-layouts  227 us (14%)
  matrix products  213 us (13%)
  other arithmetic  147 us (9%)
  starting transfers between devices  37.5 us (2%)
    all_to_all x2, blocking collectives, to_sequences(): return lax.all_to_all(a, 'seq', split_axis=0, concat_axis=0, tiled=True)  185 us
    dot_general x9, matrix products, t_product(): lax.dot_general(a, b, (((0,), (0,)), ((), ())), preferred_element_type=f32)  153 us
    pallas_call x2, Pallas kernels, expert_units(): pl.pallas_call(functools.partial(units_kernel, chunk), grid=(units // til...  127 us
    all_to_all x2, waiting for transfers between devices, from_sequences(): a = lax.all_to_all(a, 'seq', split_axis=0, concat_axis=0, tiled=True)  101 us
    unnamed x158, local copies, waits for them, and re-layouts  91.9 us
    all_gather x1, waiting for transfers between devices, on_device(): hidden_plane = lax.all_gather(hidden_two, PLANE, axis=0, tiled=True)  91.8 us
    pallas_call x1, Pallas kernels, expert_input_grad(): pl.pallas_call(functools.partial(input_kernel, cut), grid=(width // n, ro...  74.1 us
    ppermute x27, waiting for transfers between devices, swap(): return lax.ppermute(a, axis, [(0, 1), (1, 0)])  68.9 us
  transfers between devices with their start and end apart: 40, of which 18 were waited for; matrix products, arithmetic and copies ran while one was open for 31% of the time, Pallas kernels for 17%

profile of v3, /device:TPU:1, one launch (start us, length us, event | category | flops | bytes accessed | tf_op | source)
XLA Modules:
  0.0 1637.3 jit_solution(5605214017085501214)
XLA Ops:
  30.4 89.4 %all_to_all.34 = bf16[4,128,2048]{2,1,0:T(8,128)(2,1)} all-to-all(bf16[4,128,2048]{2,1,0:T(8,128)(2,1)S(1)} %pad_maximum_fusion.9), channel_id=1, replica_groups=mesh['dp'=2,'seq'=4,'r'=1,'y'=2,'core'=2] {'seq'}, dimensions={0} | all-to-all | bytes 4194304 | tf_op jit(solution)/shard_map/all_to_all | solution.py:82
  126.6 96.0 %all_to_all.35 = bf16[4,128,2048]{2,1,0:T(8,128)(2,1)S(1)} all-to-all(bf16[4,128,2048]{2,1,0:T(8,128)(2,1)S(1)} %pad_maximum_fusion.7), channel_id=1, replica_groups=mesh['dp'=2,'seq'=4,'r'=1,'y'=2,'core'=2] {'seq'}, dimensions={0} | all-to-all | bytes 4194304 | tf_op jit(solution)/shard_map/all_to_all | solution.py:82
  226.2 43.8 %all-gather = s32[32,6,256]{2,1,0:T(8,128)S(1)} all-gather(s32[1,6,256]{2,1,0:T(8,128)S(1)} %reshape.429), channel_id=1, replica_groups=mesh['dp'=2,'seq'=4,'r'=1,'y'=2,'core'=2] {'dp','seq','r','y','core'}, dimensions={0}, use_global_device_ids=true | all-gather | bytes 202752 | tf_op jit(solution)/shard_map/all_gather | solution.py:542
  278.8 58.1 %all-gather.5.cloned.1.call-done = bf16[2048,4096]{0,1:T(8,128)(2,1)} async-done(((bf16[128,4096]{0,1:T(8,128)(2,1)}), bf16[2048,4096]{0,1:T(8,128)(2,1)}) %all-gather.5.cloned.1.call-update) | async-done | bytes 16777232 | tf_op jit(solution)/shard_map/all_gather | solution.py:562
  356.1 28.0 %attend.1 = (bf16[1024,1024]{1,0:T(8,128)(2,1)S(1)}, bf16[1024,1024]{1,0:T(8,128)(2,1)S(1)}, bf16[1024,1024]{1,0:T(8,128)(2,1)}, bf16[1024,1024]{1,0:T(8,128)(2,1)}) custom-call(f32[1024,3072]{1,0:T(8,128)} %fusion.4.qp.kp.vp, f32[1024,3072]{1,0:T(8,128)} %fusion.4.qp.kp.vp, f32[1024,3072]{1,0:T(8,128)} %fusion.4.qp.kp.vp, ...), custom_call_target="tpu_custom_call" | custom-call | flops 2684354560 | bytes 20971520 | tf_op jit(solution)/shard_map/attend/pallas_call | solution.py:146
  428.7 91.8 %all-gather.7.cloned.1.call-done = bf16[4096,2048]{1,0:T(8,128)(2,1)} async-done(((bf16[512,2048]{1,0:T(8,128)(2,1)}), bf16[4096,2048]{1,0:T(8,128)(2,1)}) %all-gather.7.cloned.1.call-update) | async-done | bytes 16777232 | tf_op jit(solution)/shard_map/all_gather | solution.py:599
  522.0 25.9 %dispatch.1 = (bf16[16,160,2048]{2,1,0:T(8,128)(2,1)}, bf16[16,160,2048]{2,1,0:T(8,128)(2,1)}, f32[16,256,1]{2,1,0:T(8,128)S(1)}) custom-call(s32[4]{0:T(128)S(1)} %pad_add_fusion.1.me, bf16[4,2,4,128,2048]{4,3,2,1,0:T(8,128)(2,1)} %bitcast.264, bf16[4,2,4,128,2048]{4,3,2,1,0:T(8,128)(2,1)} %bitcast.258, s32[16,1,256]{2,1,0:T(1,128)S(1)} %broadcast_in_dim.79.slot, ...), custom_call_target="tpu_custom_call" | custom-call | flops 7516192768 | bytes 54525952 | tf_op jit(solution)/shard_map/dispatch/pallas_call | solution.py:329
  549.3 57.9 %expert_units.2 = (bf16[2560,1280]{1,0:T(8,128)(2,1)}, bf16[2560,1280]{1,0:T(8,128)(2,1)}, bf16[2560,1280]{1,0:T(8,128)(2,1)}) custom-call(bf16[2560,2048]{1,0:T(8,128)(2,1)} %bitcast.306, bf16[2560,2048]{1,0:T(8,128)(2,1)} %bitcast.314, bf16[2048,2816]{1,0:T(8,128)(2,1)} %bitcast.297, bf16[2048,2816]{1,0:T(8,128)(2,1)} %bitcast.300, ...), custom_call_target="tpu_custom_call" | custom-call | flops 40265318400 | bytes 56360960 | tf_op jit(solution)/shard_map/expert_units/pallas_call | solution.py:250
  607.2 20.1 %convolution_convert_fusion.6.rest_0_ = bf16[2048,1280]{1,0:T(8,128)(2,1)} fusion(bf16[2560,2048]{1,0:T(8,128)(2,1)} %bitcast.315, bf16[2560,1280]{1,0:T(8,128)(2,1)} %get-tuple-element.33.units_a), kind=kOutput, calls=%fused_computation.24 | convolution fusion | flops 13424394240 | bytes 22282240 | tf_op jit(solution)/shard_map/dot_general | solution.py:35
  627.4 68.6 %expert_units.3 = (bf16[2560,1536]{1,0:T(8,128)(2,1)}, bf16[2560,1536]{1,0:T(8,128)(2,1)}, bf16[2560,1536]{1,0:T(8,128)(2,1)}) custom-call(bf16[2560,2048]{1,0:T(8,128)(2,1)} %bitcast.307, bf16[2560,2048]{1,0:T(8,128)(2,1)} %bitcast.316, bf16[2048,2816]{1,0:T(8,128)(2,1)} %bitcast.298, bf16[2048,2816]{1,0:T(8,128)(2,1)} %bitcast.301, ...), custom_call_target="tpu_custom_call" | custom-call | flops 48318382080 | bytes 63438848 | tf_op jit(solution)/shard_map/expert_units/pallas_call | solution.py:250
  696.0 22.4 %convolution_convert_fusion.3.rest_0_ = bf16[2048,1536]{1,0:T(8,128)(2,1)} fusion(bf16[2560,2048]{1,0:T(8,128)(2,1)} %bitcast.317, bf16[2560,1536]{1,0:T(8,128)(2,1)} %get-tuple-element.34.units_b), kind=kOutput, calls=%fused_computation.21 | convolution fusion | flops 16109273088 | bytes 24641536 | tf_op jit(solution)/shard_map/dot_general | solution.py:35
  718.4 74.1 %expert_input_grad.1 = bf16[2560,2048]{1,0:T(8,128)(2,1)} custom-call(bf16[2560,1280]{1,0:T(8,128)(2,1)} %get-tuple-element.35.dgate_a.refs_0_, bf16[2560,1536]{1,0:T(8,128)(2,1)} %get-tuple-element.36.dgate_b.refs_0_, bf16[2560,1280]{1,0:T(8,128)(2,1)} %get-tuple-element.37.dup_a.refs_0_, bf16[2560,1536]{1,0:T(8,128)(2,1)} %get-tuple-element.38.dup_b.refs_0_, ...), custom_call_target="tpu_custom_call" | custom-call | flops 59055800320 | bytes 62390272 | tf_op jit(solution)/shard_map/expert_input_grad/pallas_call | solution.py:457
  877.7 42.9 %expert_down.1 = bf16[2560,2048]{1,0:T(8,128)(2,1)} custom-call(bf16[2560,1280]{1,0:T(8,128)(2,1)} %get-tuple-element.33.units_a, bf16[2560,1536]{1,0:T(8,128)(2,1)} %get-tuple-element.34.units_b, bf16[2816,2048]{1,0:T(8,128)(2,1)} %bitcast.305, bf16[2048,1280]{1,0:T(8,128)(2,1)S(1)} %bitcast.250), custom_call_target="tpu_custom_call" | custom-call | flops 29527900160 | bytes 36438016 | tf_op jit(solution)/shard_map/expert_down/pallas_call | solution.py:423
  920.7 24.2 %combine.1 = (bf16[2,2,2,4,128,2048]{5,4,3,2,1,0:T(8,128)(2,1)}, f32[16,256,1]{2,1,0:T(8,128)S(1)}) custom-call(s32[4]{0:T(128)S(1)} %pad_add_fusion.1.me, bf16[16,160,2048]{2,1,0:T(8,128)(2,1)} %bitcast.265, s32[16,256,1]{2,1,0:T(8,128)S(1)} %copy.190.slot, f32[16,256,1]{2,1,0:T(8,128)S(1)} %copy-done.13, bf16[4,2,4,128,2048]{4,3,2,1,0:T(8,128)(2,1)} %bitcast.259), custom_call_target="tpu_custom_call" | custom-call | flops 2684354560 | bytes 44040192 | tf_op jit(solution)/shard_map/combine/pallas_call | solution.py:398
  1009.4 33.0 %attend_back.1 = (bf16[1024,1024]{1,0:T(8,128)(2,1)S(1)}, bf16[1024,1024]{1,0:T(8,128)(2,1)S(1)}, bf16[1024,1024]{1,0:T(8,128)(2,1)}) custom-call(bf16[1024,1024]{1,0:T(8,128)(2,1)} %copy-done.17, bf16[1024,1024]{1,0:T(8,128)(2,1)} %copy-done.18, bf16[1024,1024]{1,0:T(8,128)(2,1)} %get-tuple-element.43.v, bf16[1024,1024]{1,0:T(8,128)(2,1)} %get-tuple-element.30.mixed, ...), custom_call_target="tpu_custom_call" | custom-call | flops 6710886400 | bytes 16777216 | tf_op jit(solution)/shard_map/attend_back/pallas_call | solution.py:206
  1101.9 20.5 %convolution_convert_fusion.4 = bf16[2048,1280]{1,0:T(8,128)(2,1)} fusion(bf16[2560,2048]{1,0:T(8,128)(2,1)} %bitcast.309, bf16[2560,1280]{1,0:T(8,128)(2,1)} %after.8), kind=kOutput, calls=%fused_computation.22 | convolution fusion | flops 13424394240 | bytes 22282240 | tf_op jit(solution)/shard_map/dot_general | solution.py:35
  1243.6 21.4 %constant_dynamic-slice_fusion.4 = (bf16[2,4,1,1,128,2176]{4,3,1,0,5,2:T(2,128)(2,1)}, bf16[2,4,1,1,128,2176]{4,3,1,0,5,2:T(2,128)(2,1)}) fusion(bf16[2,4,1,2,128,2176]{4,3,1,0,5,2:T(2,128)(2,1)} %reshape.412, s32[]{:T(128)S(6)} %select_n.236, s32[]{:T(128)S(6)} %select_n.265), kind=kLoop, calls=%fused_computation.169 | loop fusion | bytes 17825800 | tf_op jit(solution)/shard_map/jit(dynamic_index_in_dim)/dynamic_slice | solution.py:501
  1265.0 20.8 %copy.224 = bf16[2,4,1,1,128,2176]{5,4,1,0,3,2:T(8,128)(2,1)} copy(bf16[2,4,1,1,128,2176]{4,3,1,0,5,2:T(2,128)(2,1)} %get-tuple-element.146) | data formatting | bytes 8912896
  1286.3 22.6 %convolution_convert_fusion.1 = bf16[2048,1536]{1,0:T(8,128)(2,1)} fusion(bf16[2560,2048]{1,0:T(8,128)(2,1)} %bitcast.310, bf16[2560,1536]{1,0:T(8,128)(2,1)} %after.9), kind=kOutput, calls=%fused_computation.19 | convolution fusion | flops 16109273088 | bytes 24641536 | tf_op jit(solution)/shard_map/dot_general | solution.py:35
  1333.0 20.8 %copy.223 = bf16[2,4,1,1,128,2176]{5,4,1,0,3,2:T(8,128)(2,1)} copy(bf16[2,4,1,1,128,2176]{4,3,1,0,5,2:T(2,128)(2,1)} %get-tuple-element.145) | data formatting | bytes 8912896
  1353.8 29.3 %collective-permute-done.23 = bf16[2,4,1,128,2176]{4,3,1,0,2:T(8,128)(2,1)} collective-permute-done((bf16[2,4,1,128,2176]{4,3,1,0,2:T(8,128)(2,1)}, bf16[2,4,1,128,2176]{4,3,1,0,2:T(8,128)(2,1)}, u32[]{:S(2)}, u32[]{:S(2)}) %collective-permute-start.23) | collective-permute-done | bytes 4456480 | tf_op jit(solution)/shard_map/ppermute | solution.py:39
  1392.2 35.5 %all-to-all-done.4 = bf16[4,128,2048]{2,1,0:T(8,128)(2,1)S(1)} async-done(((bf16[4,128,2048]{2,1,0:T(8,128)(2,1)}), bf16[4,128,2048]{2,1,0:T(8,128)(2,1)S(1)}, u32[]{:S(2)}, u32[]{:S(2)}) %all-to-all-start.4) | async-done | bytes 2097184 | tf_op jit(solution)/shard_map/all_to_all | solution.py:86
  1443.6 65.8 %all-to-all-done.3 = bf16[4,128,2048]{2,1,0:T(8,128)(2,1)} async-done(((bf16[4,128,2048]{2,1,0:T(8,128)(2,1)}), bf16[4,128,2048]{2,1,0:T(8,128)(2,1)}, u32[]{:S(2)}, u32[]{:S(2)}) %all-to-all-start.3) | async-done | bytes 2097184 | tf_op jit(solution)/shard_map/all_to_all | solution.py:86
  1546.0 64.1 %all-to-all-done.5 = bf16[4,1,128,4224]{3,2,1,0:T(8,128)(2,1)} async-done(((bf16[4,1,128,4224]{3,2,1,0:T(8,128)(2,1)}), bf16[4,1,128,4224]{3,2,1,0:T(8,128)(2,1)}, u32[]{:S(2)}, u32[]{:S(2)}) %all-to-all-start.5) | async-done | bytes 4325408 | tf_op jit(solution)/shard_map/all_to_all | solution.py:712
  (384 shorter events, 544.8 us)
Async XLA Ops:
  7.2 329.7 %all-gather.5.cloned.1.call-start = ((), (), s32[]{:S(2)}) async-start(), calls=%async_computation.12 | async-start | bytes 17825792 | tf_op jit(solution)/shard_map/all_gather | solution.py:562
  24.3 404.3 %all-gather.9.cloned.1.call-start = ((), (), s32[]{:S(2)}) async-start(), calls=%async_computation.14 | async-start | bytes 18874368 | tf_op jit(solution)/shard_map/all_gather | solution.py:580
  119.9 400.6 %all-gather.7.cloned.1.call-start = ((), (), s32[]{:S(2)}) async-start(), calls=%async_computation.13 | async-start | bytes 18874368 | tf_op jit(solution)/shard_map/all_gather | solution.py:599
  225.8 47.1 %collective-permute-start.1 = (bf16[4,128,2048]{2,1,0:T(8,128)(2,1)}, bf16[4,128,2048]{2,1,0:T(8,128)(2,1)}, u32[]{:S(2)}, u32[]{:S(2)}) collective-permute-start(bf16[4,128,2048]{2,1,0:T(8,128)(2,1)} %multiply_convert_fusion.1), channel_id=1, source_target_pairs={{0,1},{1,0},{2,3},{3,2},{4,5},{5,4},{6,7},{7,6},{8,9},{9,8},{10,11... | collective-permute-start | bytes 6291464 | tf_op jit(solution)/shard_map/ppermute | solution.py:39
  409.3 1109.7 %reduce-scatter.15.cloned.1.call-start = ((), (), s32[]{:S(2)}) async-start(), calls=%async_computation.19 | async-start | bytes 6553600 | tf_op jit(solution)/shard_map/reduce_scatter | solution.py:627
  627.4 891.6 %reduce-scatter.17.cloned.1.call-start = ((), (), s32[]{:S(2)}) async-start(), calls=%async_computation.20 | async-start | bytes 7864320 | tf_op jit(solution)/shard_map/reduce_scatter | solution.py:627
  875.5 82.8 %collective-permute-start.10 = (bf16[4,128,2048]{2,1,0:T(8,128)(2,1)}, bf16[4,128,2048]{2,1,0:T(8,128)(2,1)}, u32[]{:S(2)}, u32[]{:S(2)}) collective-permute-start(bf16[4,128,2048]{2,1,0:T(8,128)(2,1)} %pad_maximum_fusion.11), channel_id=1, source_target_pairs={{0,2},{2,0},{1,3},{3,1},{4,6},{6,4},{5,7},{7,5},{8,10},{10,8},{9,1... | collective-permute-start | bytes 6291464 | tf_op jit(solution)/shard_map/ppermute | solution.py:39
  877.2 81.2 %collective-permute-start.8 = (bf16[4,128,2048]{2,1,0:T(8,128)(2,1)}, bf16[4,128,2048]{2,1,0:T(8,128)(2,1)}, u32[]{:S(2)}, u32[]{:S(2)}) collective-permute-start(bf16[4,128,2048]{2,1,0:T(8,128)(2,1)} %pad_maximum_fusion.10), channel_id=1, source_target_pairs={{0,16},{16,0},{1,17},{17,1},{2,18},{18,2},{3,19},{19,3},{4,20},{20... | collective-permute-start | bytes 6291464 | tf_op jit(solution)/shard_map/ppermute | solution.py:39
  954.1 575.8 %reduce-scatter.7.cloned.1.call-start = ((), (), s32[]{:S(2)}) async-start(), calls=%async_computation.15 | async-start | bytes 6553600 | tf_op jit(solution)/shard_map/reduce_scatter | solution.py:627
  966.8 563.1 %reduce-scatter.9.cloned.1.call-start = ((), (), s32[]{:S(2)}) async-start(), calls=%async_computation.16 | async-start | bytes 7864320 | tf_op jit(solution)/shard_map/reduce_scatter | solution.py:627
  1053.5 38.3 %collective-permute-start.13 = (bf16[2,2,4,128,2048]{4,3,2,1,0:T(8,128)(2,1)}, bf16[2,2,4,128,2048]{4,3,2,1,0:T(8,128)(2,1)}, u32[]{:S(2)}, u32[]{:S(2)}) collective-permute-start(bf16[2,2,4,128,2048]{4,3,2,1,0:T(8,128)(2,1)} %slice_bitcast_fusion), channel_id=1, source_target_pairs={{0,1},{1,0},{2,3},{3,2},{4,5},{5,4},{6,7},{7,6},{8,9},{9,8},{10,11... | collective-permute-start | bytes 25165832 | tf_op jit(solution)/shard_map/ppermute | solution.py:39
  1054.0 480.6 %reduce-scatter.11.cloned.1.call-start = ((), (), s32[]{:S(2)}) async-start(), calls=%async_computation.17 | async-start | bytes 6553600 | tf_op jit(solution)/shard_map/reduce_scatter | solution.py:627
  1101.1 25.5 %collective-permute-start.16 = (bf16[2,128,2048]{2,1,0:T(8,128)(2,1)}, bf16[2,128,2048]{2,1,0:T(8,128)(2,1)S(1)}, u32[]{:S(2)}, u32[]{:S(2)}) collective-permute-start(bf16[2,128,2048]{2,1,0:T(8,128)(2,1)} %get-tuple-element.151), channel_id=1, source_target_pairs={{0,16},{16,0},{1,17},{17,1},{2,18},{18,2},{3,19},{19,3},{4,20},{20... | collective-permute-start | bytes 3145736 | tf_op jit(solution)/shard_map/ppermute | solution.py:39
  1125.6 87.0 %collective-permute-start.19 = (bf16[4,128,2048]{2,1,0:T(8,128)(2,1)}, bf16[4,128,2048]{2,1,0:T(8,128)(2,1)}, u32[]{:S(2)}, u32[]{:S(2)}) collective-permute-start(bf16[4,128,2048]{2,1,0:T(8,128)(2,1)} %constant_dynamic-slice_fusion.8), channel_id=1, source_target_pairs={{0,1},{1,0},{2,3},{3,2},{4,5},{5,4},{6,7},{7,6},{8,9},{9,8},{10,11... | collective-permute-start | bytes 6291464 | tf_op jit(solution)/shard_map/ppermute | solution.py:39
  1126.5 408.1 %reduce-scatter.13.cloned.1.call-start = ((), (), s32[]{:S(2)}) async-start(), calls=%async_computation.18 | async-start | bytes 7864320 | tf_op jit(solution)/shard_map/reduce_scatter | solution.py:627
  1130.8 81.8 %collective-permute-start.17 = (bf16[4,128,2048]{2,1,0:T(8,128)(2,1)}, bf16[4,128,2048]{2,1,0:T(8,128)(2,1)}, u32[]{:S(2)}, u32[]{:S(2)}) collective-permute-start(bf16[4,128,2048]{2,1,0:T(8,128)(2,1)} %pad_maximum_fusion.13), channel_id=1, source_target_pairs={{0,2},{2,0},{1,3},{3,1},{4,6},{6,4},{5,7},{7,5},{8,10},{10,8},{9,1... | collective-permute-start | bytes 6291464 | tf_op jit(solution)/shard_map/ppermute | solution.py:39
  1133.4 79.2 %collective-permute-start.15 = (bf16[4,128,2048]{2,1,0:T(8,128)(2,1)}, bf16[4,128,2048]{2,1,0:T(8,128)(2,1)}, u32[]{:S(2)}, u32[]{:S(2)}) collective-permute-start(bf16[4,128,2048]{2,1,0:T(8,128)(2,1)} %pad_maximum_fusion.12), channel_id=1, source_target_pairs={{0,16},{16,0},{1,17},{17,1},{2,18},{18,2},{3,19},{19,3},{4,20},{20... | collective-permute-start | bytes 6291464 | tf_op jit(solution)/shard_map/ppermute | solution.py:39
  1212.2 111.0 %collective-permute-start.21 = (bf16[4,1,2,128,2048]{4,3,0,2,1:T(8,128)(2,1)}, bf16[4,1,2,128,2048]{4,3,0,2,1:T(8,128)(2,1)}, u32[]{:S(2)}, u32[]{:S(2)}) collective-permute-start(bf16[4,1,2,128,2048]{4,3,0,2,1:T(8,128)(2,1)} %bitcast.279), channel_id=1, source_target_pairs={{0,16},{16,0},{1,17},{17,1},{2,18},{18,2},{3,19},{19,3},{4,20},{20... | collective-permute-start | bytes 12582920 | tf_op jit(solution)/shard_map/ppermute | solution.py:39
  1285.8 97.3 %collective-permute-start.23 = (bf16[2,4,1,128,2176]{4,3,1,0,2:T(8,128)(2,1)}, bf16[2,4,1,128,2176]{4,3,1,0,2:T(8,128)(2,1)}, u32[]{:S(2)}, u32[]{:S(2)}) collective-permute-start(bf16[2,4,1,128,2176]{4,3,1,0,2:T(8,128)(2,1)} %bitcast.271), channel_id=1, source_target_pairs={{0,2},{2,0},{1,3},{3,1},{4,6},{6,4},{5,7},{7,5},{8,10},{10,8},{9,1... | collective-permute-start | bytes 13369352 | tf_op jit(solution)/shard_map/ppermute | solution.py:39
  1318.9 108.7 %all-to-all-start.4 = ((bf16[4,128,2048]{2,1,0:T(8,128)(2,1)}), bf16[4,128,2048]{2,1,0:T(8,128)(2,1)S(1)}, u32[]{:S(2)}, u32[]{:S(2)}) async-start(bf16[4,128,2048]{2,1,0:T(8,128)(2,1)} %bitcast.268), calls=%async_computation.4 | async-start | bytes 4194304 | tf_op jit(solution)/shard_map/all_to_all | solution.py:86
  1332.2 100.0 %collective-permute-start.22 = (bf16[4,1,128,2048]{3,2,0,1:T(8,128)(2,1)}, bf16[4,1,128,2048]{3,2,0,1:T(8,128)(2,1)}, u32[]{:S(2)}, u32[]{:S(2)}) collective-permute-start(bf16[4,1,128,2048]{3,2,0,1:T(8,128)(2,1)} %dynamic-slice_bitcast_fusion.1), channel_id=1, source_target_pairs={{0,2},{2,0},{1,3},{3,1},{4,6},{6,4},{5,7},{7,5},{8,10},{10,8},{9,1... | collective-permute-start | bytes 6291464 | tf_op jit(solution)/shard_map/ppermute | solution.py:39
  1391.5 47.5 %collective-permute-start.24 = (bf16[4,1,128,2176]{3,2,0,1:T(8,128)(2,1)}, bf16[4,1,128,2176]{3,2,0,1:T(8,128)(2,1)}, u32[]{:S(2)}, u32[]{:S(2)}) collective-permute-start(bf16[4,1,128,2176]{3,2,0,1:T(8,128)(2,1)} %dynamic-slice_bitcast_fusion), channel_id=1, source_target_pairs={{0,16},{16,0},{1,17},{17,1},{2,18},{18,2},{3,19},{19,3},{4,20},{20... | collective-permute-start | bytes 6684680 | tf_op jit(solution)/shard_map/ppermute | solution.py:39
  1427.7 81.7 %all-to-all-start.3 = ((bf16[4,128,2048]{2,1,0:T(8,128)(2,1)}), bf16[4,128,2048]{2,1,0:T(8,128)(2,1)}, u32[]{:S(2)}, u32[]{:S(2)}) async-start(bf16[4,128,2048]{2,1,0:T(8,128)(2,1)} %get-tuple-element.182), calls=%async_computation.3 | async-start | bytes 4194304 | tf_op jit(solution)/shard_map/all_to_all | solution.py:86
  1509.4 100.7 %all-to-all-start.5 = ((bf16[4,1,128,4224]{3,2,1,0:T(8,128)(2,1)}), bf16[4,1,128,4224]{3,2,1,0:T(8,128)(2,1)}, u32[]{:S(2)}, u32[]{:S(2)}) async-start(bf16[4,1,128,4224]{3,2,1,0:T(8,128)(2,1)} %maximum_bitcast_fusion), calls=%async_computation.5 | async-start | bytes 8650752 | tf_op jit(solution)/shard_map/all_to_all | solution.py:712
  (88 other events, 1356.2 us)
Sparse Core Ops, SparseCore 0:
  24.5 312.3 all-gather.4
  338.8 89.8 all-gather.8
  430.6 89.8 all-gather.6
  627.5 93.3 reduce-scatter.14
  818.9 110.4 reduce-scatter.16
  966.9 92.4 reduce-scatter.6
  1061.7 111.2 reduce-scatter.8
  1175.3 94.2 reduce-scatter.10
  1309.0 166.0 reduce-scatter.12

commit v4 on v3

--- a/solution.py
+++ b/solution.py
@@ -77,14 +77,29 @@
     return by_core(mine, swap(other, "core"), concat)
 
 
+def seq_pieces(a):
+    count = a.shape[0]
+    me = lax.axis_index("seq")
+    pieces = [pick(a, me, 0)]
+    for step in range(1, count):
+        give = pick(a, lax.rem(me + step, count), 0)
+        pieces.append(lax.ppermute(give, "seq", [(i, (i + step) % count) for i in range(count)]))
+    return pieces
+
+
+def seq_exchange(a):
+    count = a.shape[0]
+    me = lax.axis_index("seq")
+    pieces = jnp.stack(seq_pieces(a))
+    return jnp.stack([pick(pieces, lax.rem(me + count - s, count), 0) for s in range(count)])
+
+
 def to_sequences(a):
-    a = core_exchange(a, 1, 0)
-    return lax.all_to_all(a, "seq", split_axis=0, concat_axis=0, tiled=True)
+    return seq_exchange(core_exchange(a, 1, 0))
 
 
 def from_sequences(a):
-    a = lax.all_to_all(a, "seq", split_axis=0, concat_axis=0, tiled=True)
-    return core_exchange(a, 0, 1)
+    return core_exchange(seq_exchange(a), 0, 1)
 
 
 def plane_scatter(blocks):
@@ -276,7 +291,7 @@
 
 def unit_cut(units):
     tile = unit_tile(units)
-    return units // tile // 2 * tile
+    return units // tile * 3 // 4 * tile
 
 
 def dispatch_kernel(me, hidden, dout, slot, routes, router, rows, dy_rows, gate):
@@ -377,17 +392,19 @@
     place_cores(me, out, gate[0] * dense)
 
 
-def collect_kernel(me, rows, slot, out):
-    place_cores(me, out, spread_rows(slot[0], rows[0]))
-
-
-def combine(me, rows, slot, seq_n, piece, gate=None, dout=None):
-    blocks, cap, width = rows.shape
+def collect_kernel(me, left, slot, right, *rest):
+    dense = [spread_rows(slot[0], left[0]), spread_rows(slot[0], right[0])]
+    place_cores(me, rest[-1], jnp.concatenate(dense, axis=1))
+
+
+def combine(me, rows, slot, seq_n, piece, gate=None, dout=None, right=None):
+    blocks, cap, part = rows.shape
     size = slot.shape[1]
+    width = part if right is None else 2 * part
     column = pl.BlockSpec((1, size, 1), lambda b, me: (b, 0, 0))
     weigh = gate is not None
     operands = [rows, slot]
-    in_specs = [pl.BlockSpec((1, cap, width), lambda b, me: (b, 0, 0)), column]
+    in_specs = [pl.BlockSpec((1, cap, part), lambda b, me: (b, 0, 0)), column]
     out_specs = [relative_block(seq_n, piece, width)]
     out_shape = [jax.ShapeDtypeStruct((2, 2, 2, seq_n, piece, width), bf16)]
     if weigh:
@@ -395,6 +412,9 @@
         in_specs += [column, plane_block(seq_n, piece, width)]
         out_specs += [column]
         out_shape += [jax.ShapeDtypeStruct((blocks, size, 1), f32)]
+    else:
+        operands += [right]
+        in_specs += in_specs[:1]
     return pl.pallas_call(
         combine_kernel if weigh else collect_kernel,
         grid_spec=pltpu.PrefetchScalarGridSpec(
@@ -447,13 +467,15 @@
     rest[-1][...] = total.astype(bf16)
 
 
-def expert_input_grad(dgate_a, dgate_b, dup_a, dup_b, gate, up, *before):
+def expert_input_grad(dgate_a, dgate_b, dup_a, dup_b, gate, up, start, stop, *before):
     rows, cut = dgate_a.shape
-    width, inner = gate.shape
+    inner = gate.shape[1]
+    width = stop - start
     m, n = tile_of(rows), tile_of(width)
+    first = start // n
     left_a = pl.BlockSpec((m, cut), lambda j, i: (i, 0))
     left_b = pl.BlockSpec((m, inner - cut), lambda j, i: (i, 0))
-    right = pl.BlockSpec((n, inner), lambda j, i: (j, 0))
+    right = pl.BlockSpec((n, inner), lambda j, i: (first + j, 0))
     return pl.pallas_call(
         functools.partial(input_kernel, cut),
         grid=(width // n, rows // m),
@@ -633,9 +655,13 @@
     down_a = rows_product(dy_rows, units_a)
     units_b, dgpre_b, dupre_b = expert_units(expert_in, dy_rows, *full, cut, inner, down_a)
     down_b = rows_product(dy_rows, units_b)
-    dinput = expert_input_grad(dgpre_a, dgpre_b, dupre_a, dupre_b, gate_one, up_one, down_b)
-    [back] = combine(me, dinput.reshape(blocks, cap, width), slot_col, seq_n, piece)
-    gate_a = rows_product(expert_in, after(dgpre_a, back))
+    down_sum_a, down_sum_b = over_ctx(down_a), over_ctx(down_b)
+    grads = (dgpre_a, dgpre_b, dupre_a, dupre_b, gate_one, up_one)
+    left = expert_input_grad(*grads, 0, width // 2, down_b)
+    right = expert_input_grad(*grads, width // 2, width, left)
+    left, right = (part.reshape(blocks, cap, width // 2) for part in (left, right))
+    [back] = combine(me, left, slot_col, seq_n, piece, right=right)
+    gate_a = rows_product(expert_in, after(dgpre_a, back, down_sum_a))
     gate_b = rows_product(expert_in, after(dgpre_b, back))
     ypair = expert_down(units_a, units_b, down_one, gate_a)
     mixed_rows, dgate_plane = combine(
@@ -664,17 +690,17 @@
     dbranch = chip_gather(dresid.astype(bf16).reshape(seq_n, piece, width), 1, parts).reshape(length, width)
     column_start = (r_i * core_n + core_i) * columns
     dbranch_here = lax.dynamic_slice_in_dim(dbranch, column_start, columns, 1)
-    out_grad = t_product(mixed_full, dbranch_here)
     dmixed = chip_scatter(product_t(dbranch_here, weight_out).astype(bf16), 1, parts).astype(bf16)
     dqpre, dkpre, dvpre = attend_back(
-        query, keys, values, mixed, dmixed, cosine, sine, seg_row, seg_col, heads, gate_b
+        query, keys, values, mixed, dmixed, cosine, sine, seg_row, seg_col, heads, gate_b, down_sum_b
     )
     dqkv = jnp.concatenate([dqpre, dkpre, dvpre], axis=1)
+    out_grad = t_product(mixed_full, after(dbranch_here, dqpre))
     in_grad = t_product(hidden_full, dqkv).astype(bf16)
     up_a = rows_product(expert_in, after(dupre_a, dqpre))
     up_b = rows_product(expert_in, after(dupre_b, dqpre))
 
-    grad_down = jnp.concatenate([over_ctx(down_a), over_ctx(down_b)], axis=1).astype(f32).T[None]
+    grad_down = jnp.concatenate([down_sum_a, down_sum_b], axis=1).astype(f32).T[None]
     grad_gate = jnp.concatenate([over_ctx(gate_a), over_ctx(gate_b)], axis=1).astype(f32)[None]
     grad_up = jnp.concatenate([over_ctx(up_a), over_ctx(up_b)], axis=1).astype(f32)[None]
 
@@ -693,10 +719,6 @@
     mixture = plane_scatter(after(mixed_rows, dqpre))
     output = from_sequences((residual + mixture).astype(bf16))
 
-    gains = jnp.concatenate([attn_norm_grad[:, None], expert_norm_grad[:, None], router_grad], axis=1)
-    gain_n = gains.shape[1]
-    gains = jnp.pad(gains, ((0, 0), (0, 128 - gain_n))).astype(bf16)
-
     def seen(part):
         return part.reshape(dp_n, seq_n, r_n, y_n, core_n * rows_here, -1)
 
@@ -704,18 +726,29 @@
         keep, give = pick(a, index, axis), pick(a, 1 - index, axis)
         return (keep.astype(f32) + swap(give, name).astype(f32)).astype(bf16)
 
-    one = seen(jnp.concatenate([out_grad.astype(bf16), in_grad[:, :columns]], axis=1))
-    two = seen(jnp.concatenate([in_grad[:, columns:], gains], axis=1))
-    one = half(half(one, 0, dp_i, "dp"), 2, y_i, "y")
-    two = half(half(two, 3, y_i, "y"), 0, dp_i, "dp")
-    part = jnp.concatenate([one, two], axis=-1)
-    part = lax.all_to_all(part, "seq", split_axis=0, concat_axis=0, tiled=True)
-    part = jnp.sum(part.astype(f32), axis=0).astype(bf16)
-    part = part.reshape(parts, rows_here, -1)
-    gains = chip_scatter(part[:, :, 4 * columns :], 0, parts)[0, :, :gain_n]
-    part = part[:, :, : 4 * columns].reshape(parts, rows_here, 4, 1, columns)
-    part = chip_exchange(part, 0, 3, parts).reshape(rows_here, 4, width).astype(f32)
-    grad_output, grad_query, grad_key, grad_value = (part[:, i] for i in range(4))
+    def over_plane(a, b):
+        a, b = half(seen(a), 0, dp_i, "dp"), half(seen(b), 3, y_i, "y")
+        return half(a, 2, y_i, "y"), half(b, 0, dp_i, "dp")
+
+    def over_seq(a):
+        return sum(piece.astype(f32) for piece in seq_pieces(a)).astype(bf16)
+
+    def to_rows(a):
+        a = a.reshape(parts, rows_here, -1, 1, columns)
+        return chip_exchange(a, 0, 3, parts).reshape(rows_here, -1, width).astype(f32)
+
+    one, two = over_plane(in_grad[:, : 3 * columns // 2], in_grad[:, 3 * columns // 2 :])
+    inward = to_rows(over_seq(jnp.concatenate([one, two], axis=-1)))
+    one, two = over_plane(*jnp.split(out_grad.astype(bf16), 2, axis=1))
+    outward = to_rows(over_seq(jnp.concatenate([one, two], axis=-1)))
+    grad_output = outward[:, 0]
+    grad_query, grad_key, grad_value = (inward[:, i] for i in range(3))
+
+    gains = jnp.concatenate([attn_norm_grad[None], expert_norm_grad[None], router_grad.T], axis=0)
+    gain_n = gains.shape[0]
+    gains = gains.reshape(gain_n, -1, rows_here).transpose(1, 0, 2)
+    gains = lax.all_to_all(gains, EVERY, split_axis=0, concat_axis=0, tiled=True)
+    gains = jnp.sum(gains, axis=0).T
 
     return (
         output,

time: 1650 us -> 1590 us (0.964)
  blocking collectives: 229 us -> 77.8 us
  local copies, waits for them, and re-layouts: 227 us -> 119 us
  waiting for transfers between devices: 401 us -> 505 us
  starting transfers between devices: 37.5 us -> 140 us
    ppermute x0 -> x18, waiting for transfers between devices: none -> 227 us  [seq_pieces(): lax.ppermute(give, 'seq', [(i, (i + step) % count) for i in range(count)])]
    all_to_all x2 -> x0, blocking collectives: 185 us -> none  [to_sequences(): return lax.all_to_all(a, 'seq', split_axis=0, concat_axis=0, tiled=True)]
    all_to_all x3 -> x1, waiting for transfers between devices: 165 us -> 0.01 us  [on_device(): lax.all_to_all(gains, EVERY, split_axis=0, concat_axis=0, tiled=True)]
    ppermute x0 -> x18, starting transfers between devices: none -> 78.8 us  [seq_pieces(): lax.ppermute(give, 'seq', [(i, (i + step) % count) for i in range(count)])]
    unnamed x158 -> x224, local copies, waits for them, and re-layouts: 91.9 us -> 36.7 us
    ppermute x27 -> x31, waiting for transfers between devices: 68.9 us -> 111 us  [swap(): return lax.ppermute(a, axis, [(0, 1), (1, 0)])]
    all_gather x1, blocking collectives: 43.8 us -> 77.8 us  [on_device(): lax.all_gather(small, EVERY, axis=0, tiled=True)]
    dynamic_slice x6 -> x13, local copies, waits for them, and re-layouts: 41.4 us -> 11.8 us  [pick(): return lax.dynamic_index_in_dim(a, index, axis, keepdims=False)]
  transfers between devices with their start and end apart: 40 -> 60, of which waited for: 18 -> 30; matrix products, arithmetic and copies ran while one was open for 31% -> 25% of each run, Pallas kernels for 17% -> 16%
where the time goes in v4:
time: 1590 us; the launch traced here: 1580 us
  waiting for transfers between devices  505 us (32%)
  Pallas kernels  367 us (23%)
  matrix products  217 us (14%)
  starting transfers between devices  140 us (9%)
  other arithmetic  133 us (8%)
  local copies, waits for them, and re-layouts  119 us (7%)
  blocking collectives  77.8 us (5%)
    ppermute x18, waiting for transfers between devices, seq_pieces(): lax.ppermute(give, 'seq', [(i, (i + step) % count) for i in range(count)])  227 us
    dot_general x9, matrix products, t_product(): lax.dot_general(a, b, (((0,), (0,)), ((), ())), preferred_element_type=f32)  156 us
    pallas_call x2, Pallas kernels, expert_units(): pl.pallas_call(functools.partial(units_kernel, chunk), grid=(units // til...  126 us
    ppermute x31, waiting for transfers between devices, swap(): return lax.ppermute(a, axis, [(0, 1), (1, 0)])  111 us
    all_gather x1, waiting for transfers between devices, on_device(): hidden_plane = lax.all_gather(hidden_two, PLANE, axis=0, tiled=True)  91.8 us
    ppermute x18, starting transfers between devices, seq_pieces(): lax.ppermute(give, 'seq', [(i, (i + step) % count) for i in range(count)])  78.8 us
    all_gather x1, blocking collectives, on_device(): lax.all_gather(small, EVERY, axis=0, tiled=True)  77.8 us
    pallas_call x2, Pallas kernels, expert_input_grad(): pl.pallas_call(functools.partial(input_kernel, cut), grid=(width // n, ro...  77.7 us
  transfers between devices with their start and end apart: 60, of which 30 were waited for; matrix products, arithmetic and copies ran while one was open for 25% of the time, Pallas kernels for 16%

profile of v4, /device:TPU:1, one launch (start us, length us, event | category | flops | bytes accessed | tf_op | source)
XLA Modules:
  0.0 1575.7 jit_solution(16260090674457762838)
XLA Ops:
  47.8 43.0 %collective-permute-done.10 = bf16[128,2048]{1,0:T(8,128)(2,1)S(1)} collective-permute-done((bf16[128,2048]{1,0:T(8,128)(2,1)S(1)}, bf16[128,2048]{1,0:T(8,128)(2,1)S(1)}, u32[]{:S(2)}, u32[]{:S(2)}) %collective-permute-start.10) | collective-permute-done | bytes 524320 | tf_op jit(solution)/shard_map/ppermute | solution.py:86
  99.2 34.1 %collective-permute-start.1 = (bf16[128,2048]{1,0:T(8,128)(2,1)S(1)}, bf16[128,2048]{1,0:T(8,128)(2,1)S(1)}, u32[]{:S(2)}, u32[]{:S(2)}) collective-permute-start(bf16[128,2048]{1,0:T(8,128)(2,1)S(1)} %get-tuple-element.198), channel_id=1, source_target_pairs={{0,4},{4,8},{8,12},{12,0},{1,5},{5,9},{9,13},{13,1},{2,6},{6,10},{... | collective-permute-start | bytes 1572872 | tf_op jit(solution)/shard_map/ppermute | solution.py:86
  152.5 33.3 %collective-permute-done.2 = bf16[128,2048]{1,0:T(8,128)(2,1)S(1)} collective-permute-done((bf16[128,2048]{1,0:T(8,128)(2,1)S(1)}, bf16[128,2048]{1,0:T(8,128)(2,1)S(1)}, u32[]{:S(2)}, u32[]{:S(2)}) %collective-permute-start.2) | collective-permute-done | bytes 524320 | tf_op jit(solution)/shard_map/ppermute | solution.py:86
  189.5 77.8 %all-gather = s32[32,6,256]{2,1,0:T(8,128)S(1)} all-gather(s32[1,6,256]{2,1,0:T(8,128)S(1)} %reshape.564), channel_id=1, replica_groups=mesh['dp'=2,'seq'=4,'r'=1,'y'=2,'core'=2] {'dp','seq','r','y','core'}, dimensions={0}, use_global_device_ids=true | all-gather | bytes 202752 | tf_op jit(solution)/shard_map/all_gather | solution.py:564
  275.2 58.6 %all-gather.5.cloned.1.call-done = bf16[2048,4096]{0,1:T(8,128)(2,1)} async-done(((bf16[128,4096]{0,1:T(8,128)(2,1)}), bf16[2048,4096]{0,1:T(8,128)(2,1)}) %all-gather.5.cloned.1.call-update) | async-done | bytes 16777232 | tf_op jit(solution)/shard_map/all_gather | solution.py:584
  352.9 28.0 %attend.1 = (bf16[1024,1024]{1,0:T(8,128)(2,1)S(1)}, bf16[1024,1024]{1,0:T(8,128)(2,1)S(1)}, bf16[1024,1024]{1,0:T(8,128)(2,1)}, bf16[1024,1024]{1,0:T(8,128)(2,1)}) custom-call(f32[1024,3072]{1,0:T(8,128)} %fusion.4.qp.kp.vp, f32[1024,3072]{1,0:T(8,128)} %fusion.4.qp.kp.vp, f32[1024,3072]{1,0:T(8,128)} %fusion.4.qp.kp.vp, ...), custom_call_target="tpu_custom_call" | custom-call | flops 2684354560 | bytes 20971520 | tf_op jit(solution)/shard_map/attend/pallas_call | solution.py:161
  428.5 91.8 %all-gather.7.cloned.1.call-done = bf16[4096,2048]{1,0:T(8,128)(2,1)} async-done(((bf16[512,2048]{1,0:T(8,128)(2,1)}), bf16[4096,2048]{1,0:T(8,128)(2,1)}) %all-gather.7.cloned.1.call-update) | async-done | bytes 16777232 | tf_op jit(solution)/shard_map/all_gather | solution.py:621
  520.3 25.8 %dispatch.1 = (bf16[16,160,2048]{2,1,0:T(8,128)(2,1)}, bf16[16,160,2048]{2,1,0:T(8,128)(2,1)}, f32[16,256,1]{2,1,0:T(8,128)S(1)}) custom-call(s32[4]{0:T(128)S(1)} %pad_add_fusion.1.me, bf16[4,2,4,128,2048]{4,3,2,1,0:T(8,128)(2,1)} %bitcast.371, bf16[4,2,4,128,2048]{4,3,2,1,0:T(8,128)(2,1)} %bitcast.360, s32[16,1,256]{2,1,0:T(1,128)S(1)} %broadcast_in_dim.45.slot, ...), custom_call_target="tpu_custom_call" | custom-call | flops 7516192768 | bytes 54525952 | tf_op jit(solution)/shard_map/dispatch/pallas_call | solution.py:344
  547.4 86.3 %expert_units.2 = (bf16[2560,2048]{1,0:T(8,128)(2,1)}, bf16[2560,2048]{1,0:T(8,128)(2,1)}, bf16[2560,2048]{1,0:T(8,128)(2,1)}) custom-call(bf16[2560,2048]{1,0:T(8,128)(2,1)} %bitcast.423, bf16[2560,2048]{1,0:T(8,128)(2,1)} %bitcast.429, bf16[2048,2816]{1,0:T(8,128)(2,1)} %bitcast.412, bf16[2048,2816]{1,0:T(8,128)(2,1)} %bitcast.416, ...), custom_call_target="tpu_custom_call" | custom-call | flops 64424509440 | bytes 77594624 | tf_op jit(solution)/shard_map/expert_units/pallas_call | solution.py:265
  633.7 28.8 %convolution_convert_fusion.3.rest_0_ = bf16[2048,2048]{1,0:T(8,128)(2,1)} fusion(bf16[2560,2048]{1,0:T(8,128)(2,1)} %bitcast.430, bf16[2560,2048]{1,0:T(8,128)(2,1)} %get-tuple-element.33.units_a), kind=kOutput, calls=%fused_computation.15 | convolution fusion | flops 21479030784 | bytes 29360128 | tf_op jit(solution)/shard_map/dot_general | solution.py:35
  663.7 39.6 %expert_units.3 = (bf16[2560,768]{1,0:T(8,128)(2,1)}, bf16[2560,768]{1,0:T(8,128)(2,1)}, bf16[2560,768]{1,0:T(8,128)(2,1)}) custom-call(bf16[2560,2048]{1,0:T(8,128)(2,1)} %bitcast.424, bf16[2560,2048]{1,0:T(8,128)(2,1)} %bitcast.431, bf16[2048,2816]{1,0:T(8,128)(2,1)} %bitcast.413, bf16[2048,2816]{1,0:T(8,128)(2,1)} %bitcast.417, ...), custom_call_target="tpu_custom_call" | custom-call | flops 24159191040 | bytes 42205184 | tf_op jit(solution)/shard_map/expert_units/pallas_call | solution.py:265
  716.9 38.8 %expert_input_grad.2.rest_0_ = bf16[2560,1024]{1,0:T(8,128)(2,1)} custom-call(bf16[2560,2048]{1,0:T(8,128)(2,1)} %get-tuple-element.35.dgate_a.refs_0_, bf16[2560,768]{1,0:T(8,128)(2,1)} %get-tuple-element.36.dgate_b.refs_0_, bf16[2560,2048]{1,0:T(8,128)(2,1)} %get-tuple-element.37.dup_a.refs_0_, bf16[2560,768]{1,0:T(8,128)(2,1)} %get-tuple-element.38.dup_b.refs_0_, ...), custom_call_target="tpu_custom_call" | custom-call | flops 29527900160 | bytes 45613056 | tf_op jit(solution)/shard_map/expert_input_grad/pallas_call | solution.py:479
  755.6 39.0 %expert_input_grad.3 = bf16[2560,1024]{1,0:T(8,128)(2,1)} custom-call(bf16[2560,2048]{1,0:T(8,128)(2,1)} %get-tuple-element.35.dgate_a.refs_0_, bf16[2560,768]{1,0:T(8,128)(2,1)} %get-tuple-element.36.dgate_b.refs_0_, bf16[2560,2048]{1,0:T(8,128)(2,1)} %get-tuple-element.37.dup_a.refs_0_, bf16[2560,768]{1,0:T(8,128)(2,1)} %get-tuple-element.38.dup_b.refs_0_, ...), custom_call_target="tpu_custom_call" | custom-call | flops 29527900160 | bytes 45613056 | tf_op jit(solution)/shard_map/expert_input_grad/pallas_call | solution.py:479
  877.7 29.2 %convolution_convert_fusion.2.rest_0_ = bf16[2048,2048]{1,0:T(8,128)(2,1)} fusion(bf16[2560,2048]{1,0:T(8,128)(2,1)} %bitcast.426, bf16[2560,2048]{1,0:T(8,128)(2,1)} %after.6), kind=kOutput, calls=%fused_computation.14 | convolution fusion | flops 21479030784 | bytes 29360128 | tf_op jit(solution)/shard_map/dot_general | solution.py:35
  909.0 40.5 %expert_down.1 = bf16[2560,2048]{1,0:T(8,128)(2,1)} custom-call(bf16[2560,2048]{1,0:T(8,128)(2,1)} %get-tuple-element.33.units_a, bf16[2560,768]{1,0:T(8,128)(2,1)S(1)} %copy-done.19, bf16[2816,2048]{1,0:T(8,128)(2,1)} %bitcast.422, bf16[2048,2048]{1,0:T(8,128)(2,1)} %convolution_convert_fusion.2.rest_0_), custom_call_target="tpu_custom_call" | custom-call | flops 29527900160 | bytes 36438016 | tf_op jit(solution)/shard_map/expert_down/pallas_call | solution.py:443
  949.5 24.2 %combine.1 = (bf16[2,2,2,4,128,2048]{5,4,3,2,1,0:T(8,128)(2,1)}, f32[16,256,1]{2,1,0:T(8,128)S(1)}) custom-call(s32[4]{0:T(128)S(1)} %pad_add_fusion.1.me, bf16[16,160,2048]{2,1,0:T(8,128)(2,1)} %bitcast.372, s32[16,256,1]{2,1,0:T(8,128)S(1)} %copy.174.slot, f32[16,256,1]{2,1,0:T(8,128)S(1)} %copy-done.13, bf16[4,2,4,128,2048]{4,3,2,1,0:T(8,128)(2,1)} %bitcast.361), custom_call_target="tpu_custom_call" | custom-call | flops 2684354560 | bytes 44040192 | tf_op jit(solution)/shard_map/combine/pallas_call | solution.py:418
  1030.2 32.3 %attend_back.1 = (bf16[1024,1024]{1,0:T(8,128)(2,1)S(1)}, bf16[1024,1024]{1,0:T(8,128)(2,1)}, bf16[1024,1024]{1,0:T(8,128)(2,1)}) custom-call(bf16[1024,1024]{1,0:T(8,128)(2,1)} %copy-done.17, bf16[1024,1024]{1,0:T(8,128)(2,1)} %copy-done.18, bf16[1024,1024]{1,0:T(8,128)(2,1)} %get-tuple-element.43.v, bf16[1024,1024]{1,0:T(8,128)(2,1)} %get-tuple-element.30.mixed, ...), custom_call_target="tpu_custom_call" | custom-call | flops 6710886400 | bytes 16777216 | tf_op jit(solution)/shard_map/attend_back/pallas_call | solution.py:221
  1098.1 19.5 %convolution_convert_fusion = bf16[2048,3072]{1,0:T(8,128)(2,1)} fusion(bf16[1024,2048]{1,0:T(8,128)(2,1)} %bitcast.385, bf16[1024,3072]{1,0:T(8,128)(2,1)} %constant_dynamic-update-slice_fusion), kind=kOutput, calls=%fused_computation.4 | convolution fusion | flops 12891193344 | bytes 23068672 | tf_op jit(solution)/shard_map/dot_general | solution.py:35
  1128.1 28.9 %convolution_convert_fusion.1 = bf16[2048,2048]{1,0:T(8,128)(2,1)} fusion(bf16[2560,2048]{1,0:T(8,128)(2,1)} %bitcast.428, bf16[2560,2048]{1,0:T(8,128)(2,1)} %after.10), kind=kOutput, calls=%fused_computation.13 | convolution fusion | flops 21479030784 | bytes 29360128 | tf_op jit(solution)/shard_map/dot_general | solution.py:35
  1219.0 22.8 %collective-permute-done.46 = bf16[1,128,1024]{2,1,0:T(8,128)(2,1)S(1)} collective-permute-done((bf16[1,128,1024]{2,1,0:T(8,128)(2,1)S(1)}, bf16[1,128,1024]{2,1,0:T(8,128)(2,1)S(1)}, u32[]{:S(2)}, u32[]{:S(2)}) %collective-permute-start.46) | collective-permute-done | bytes 262176 | tf_op jit(solution)/shard_map/ppermute | solution.py:86
  1276.5 23.6 %collective-permute-done.36 = bf16[4,1,128,1536]{3,2,1,0:T(8,128)(2,1)} collective-permute-done((bf16[4,1,128,1536]{3,2,1,0:T(8,128)(2,1)}, bf16[4,1,128,1536]{3,2,1,0:T(8,128)(2,1)}, u32[]{:S(2)}, u32[]{:S(2)}) %collective-permute-start.36) | collective-permute-done | bytes 1572896 | tf_op jit(solution)/shard_map/ppermute | solution.py:39
  1367.8 40.5 %collective-permute-done.38 = bf16[1,128,3072]{2,1,0:T(8,128)(2,1)} collective-permute-done((bf16[1,128,3072]{2,1,0:T(8,128)(2,1)}, bf16[1,128,3072]{2,1,0:T(8,128)(2,1)}, u32[]{:S(2)}, u32[]{:S(2)}) %collective-permute-start.38) | collective-permute-done | bytes 786464 | tf_op jit(solution)/shard_map/ppermute | solution.py:86
  1471.7 28.5 %collective-permute-done.30 = bf16[128,2048]{1,0:T(8,128)(2,1)} collective-permute-done((bf16[128,2048]{1,0:T(8,128)(2,1)}, bf16[128,2048]{1,0:T(8,128)(2,1)}, u32[]{:S(2)}, u32[]{:S(2)}) %collective-permute-start.30) | collective-permute-done | bytes 524320 | tf_op jit(solution)/shard_map/ppermute | solution.py:86
  1503.4 24.4 %collective-permute-start.32 = (bf16[2,128,2048]{2,1,0:T(8,128)(2,1)}, bf16[2,128,2048]{2,1,0:T(8,128)(2,1)S(1)}, u32[]{:S(2)}, u32[]{:S(2)}) collective-permute-start(bf16[2,128,2048]{2,1,0:T(8,128)(2,1)} %constant_dynamic-slice_fusion.8), channel_id=1, source_target_pairs={{0,1},{1,0},{2,3},{3,2},{4,5},{5,4},{6,7},{7,6},{8,9},{9,8},{10,11... | collective-permute-start | bytes 3145736 | tf_op jit(solution)/shard_map/ppermute | solution.py:39
  (513 shorter events, 621.0 us)
Async XLA Ops:
  7.2 326.6 %all-gather.5.cloned.1.call-start = ((), (), s32[]{:S(2)}) async-start(), calls=%async_computation.8 | async-start | bytes 17825792 | tf_op jit(solution)/shard_map/all_gather | solution.py:584
  24.3 404.1 %all-gather.9.cloned.1.call-start = ((), (), s32[]{:S(2)}) async-start(), calls=%async_computation.10 | async-start | bytes 18874368 | tf_op jit(solution)/shard_map/all_gather | solution.py:602
  94.0 426.3 %all-gather.7.cloned.1.call-start = ((), (), s32[]{:S(2)}) async-start(), calls=%async_computation.9 | async-start | bytes 18874368 | tf_op jit(solution)/shard_map/all_gather | solution.py:621
  189.2 81.0 %collective-permute-start.4 = (bf16[4,128,2048]{2,1,0:T(8,128)(2,1)}, bf16[4,128,2048]{2,1,0:T(8,128)(2,1)}, u32[]{:S(2)}, u32[]{:S(2)}) collective-permute-start(bf16[4,128,2048]{2,1,0:T(8,128)(2,1)} %fusion.20), channel_id=1, source_target_pairs={{0,1},{1,0},{2,3},{3,2},{4,5},{5,4},{6,7},{7,6},{8,9},{9,8},{10,11... | collective-permute-start | bytes 6291464 | tf_op jit(solution)/shard_map/ppermute | solution.py:39
  410.1 467.6 %reduce-scatter.7.cloned.1.call-start = ((), (), s32[]{:S(2)}) async-start(), calls=%async_computation.11 | async-start | bytes 10485760 | tf_op jit(solution)/shard_map/reduce_scatter | solution.py:649
  662.6 366.5 %reduce-scatter.9.cloned.1.call-start = ((), (), s32[]{:S(2)}) async-start(), calls=%async_computation.12 | async-start | bytes 3932160 | tf_op jit(solution)/shard_map/reduce_scatter | solution.py:649
  818.9 734.6 %reduce-scatter.13.cloned.1.call-start = ((), (), s32[]{:S(2)}) async-start(), calls=%async_computation.14 | async-start | bytes 3932160 | tf_op jit(solution)/shard_map/reduce_scatter | solution.py:649
  875.1 108.1 %collective-permute-start.16 = (bf16[4,128,2048]{2,1,0:T(8,128)(2,1)}, bf16[4,128,2048]{2,1,0:T(8,128)(2,1)}, u32[]{:S(2)}, u32[]{:S(2)}) collective-permute-start(bf16[4,128,2048]{2,1,0:T(8,128)(2,1)} %pad_maximum_fusion.12), channel_id=1, source_target_pairs={{0,2},{2,0},{1,3},{3,1},{4,6},{6,4},{5,7},{7,5},{8,10},{10,8},{9,1... | collective-permute-start | bytes 6291464 | tf_op jit(solution)/shard_map/ppermute | solution.py:39
  877.2 106.0 %collective-permute-start.14 = (bf16[4,128,2048]{2,1,0:T(8,128)(2,1)}, bf16[4,128,2048]{2,1,0:T(8,128)(2,1)}, u32[]{:S(2)}, u32[]{:S(2)}) collective-permute-start(bf16[4,128,2048]{2,1,0:T(8,128)(2,1)} %pad_maximum_fusion.11), channel_id=1, source_target_pairs={{0,16},{16,0},{1,17},{17,1},{2,18},{18,2},{3,19},{19,3},{4,20},{20... | collective-permute-start | bytes 6291464 | tf_op jit(solution)/shard_map/ppermute | solution.py:39
  983.2 570.3 %reduce-scatter.11.cloned.1.call-start = ((), (), s32[]{:S(2)}) async-start(), calls=%async_computation.13 | async-start | bytes 10485760 | tf_op jit(solution)/shard_map/reduce_scatter | solution.py:649
  989.3 574.8 %reduce-scatter.17.cloned.1.call-start = ((), (), s32[]{:S(2)}) async-start(), calls=%async_computation.16 | async-start | bytes 3932160 | tf_op jit(solution)/shard_map/reduce_scatter | solution.py:649
  1076.8 96.9 %collective-permute-start.43 = (bf16[2,4,1,128,512]{4,3,1,0,2:T(8,128)(2,1)}, bf16[2,4,1,128,512]{4,3,1,0,2:T(8,128)(2,1)}, u32[]{:S(2)}, u32[]{:S(2)}) collective-permute-start(bf16[2,4,1,128,512]{4,3,1,0,2:T(8,128)(2,1)} %dynamic-slice_bitcast_fusion.4), channel_id=1, source_target_pairs={{0,2},{2,0},{1,3},{3,1},{4,6},{6,4},{5,7},{7,5},{8,10},{10,8},{9,1... | collective-permute-start | bytes 3145736 | tf_op jit(solution)/shard_map/ppermute | solution.py:39
  1078.2 98.5 %collective-permute-start.41 = (bf16[4,1,2,128,512]{4,3,0,2,1:T(8,128)(2,1)}, bf16[4,1,2,128,512]{4,3,0,2,1:T(8,128)(2,1)}, u32[]{:S(2)}, u32[]{:S(2)}) collective-permute-start(bf16[4,1,2,128,512]{4,3,0,2,1:T(8,128)(2,1)} %bitcast.347), channel_id=1, source_target_pairs={{0,16},{16,0},{1,17},{17,1},{2,18},{18,2},{3,19},{19,3},{4,20},{20... | collective-permute-start | bytes 3145736 | tf_op jit(solution)/shard_map/ppermute | solution.py:39
  1117.6 446.5 %reduce-scatter.15.cloned.1.call-start = ((), (), s32[]{:S(2)}) async-start(), calls=%async_computation.15 | async-start | bytes 10485760 | tf_op jit(solution)/shard_map/reduce_scatter | solution.py:649
  1173.0 96.8 %collective-permute-start.19 = (bf16[2,2,4,128,2048]{4,3,2,1,0:T(8,128)(2,1)}, bf16[2,2,4,128,2048]{4,3,2,1,0:T(8,128)(2,1)}, u32[]{:S(2)}, u32[]{:S(2)}) collective-permute-start(bf16[2,2,4,128,2048]{4,3,2,1,0:T(8,128)(2,1)} %slice_bitcast_fusion), channel_id=1, source_target_pairs={{0,1},{1,0},{2,3},{3,2},{4,5},{5,4},{6,7},{7,6},{8,9},{9,8},{10,11... | collective-permute-start | bytes 25165832 | tf_op jit(solution)/shard_map/ppermute | solution.py:39
  1182.3 78.6 %collective-permute-start.35 = (bf16[2,4,1,128,1536]{4,3,1,2,0:T(8,128)(2,1)}, bf16[2,4,1,128,1536]{4,3,1,2,0:T(8,128)(2,1)}, u32[]{:S(2)}, u32[]{:S(2)}) collective-permute-start(bf16[2,4,1,128,1536]{4,3,1,2,0:T(8,128)(2,1)} %dynamic-slice_bitcast_fusion), channel_id=1, source_target_pairs={{0,2},{2,0},{1,3},{3,1},{4,6},{6,4},{5,7},{7,5},{8,10},{10,8},{9,1... | collective-permute-start | bytes 9437192 | tf_op jit(solution)/shard_map/ppermute | solution.py:39
  1183.6 82.6 %collective-permute-start.33 = (bf16[4,1,2,128,1536]{4,3,0,2,1:T(8,128)(2,1)}, bf16[4,1,2,128,1536]{4,3,0,2,1:T(8,128)(2,1)}, u32[]{:S(2)}, u32[]{:S(2)}) collective-permute-start(bf16[4,1,2,128,1536]{4,3,0,2,1:T(8,128)(2,1)} %bitcast.346), channel_id=1, source_target_pairs={{0,16},{16,0},{1,17},{17,1},{2,18},{18,2},{3,19},{19,3},{4,20},{20... | collective-permute-start | bytes 9437192 | tf_op jit(solution)/shard_map/ppermute | solution.py:39
  1241.8 181.8 %collective-permute-start.28 = (bf16[4,128,2048]{2,1,0:T(8,128)(2,1)}, bf16[4,128,2048]{2,1,0:T(8,128)(2,1)}, u32[]{:S(2)}, u32[]{:S(2)}) collective-permute-start(bf16[4,128,2048]{2,1,0:T(8,128)(2,1)} %constant_dynamic-slice_fusion.14), channel_id=1, source_target_pairs={{0,1},{1,0},{2,3},{3,2},{4,5},{5,4},{6,7},{7,6},{8,9},{9,8},{10,11... | collective-permute-start | bytes 6291464 | tf_op jit(solution)/shard_map/ppermute | solution.py:39
  1243.6 90.7 %collective-permute-start.48 = (bf16[1,64,1,1,1024]{4,3,1,2,0:T(2,128)(2,1)}, bf16[1,64,1,1,1024]{4,3,1,2,0:T(2,128)(2,1)S(1)}, u32[]{:S(2)}, u32[]{:S(2)}) collective-permute-start(bf16[1,64,1,1,1024]{4,3,1,2,0:T(2,128)(2,1)} %copy.212), channel_id=1, source_target_pairs={{0,1},{1,0},{2,3},{3,2},{4,5},{5,4},{6,7},{7,6},{8,9},{9,8},{10,11... | collective-permute-start | bytes 393224 | tf_op jit(solution)/shard_map/ppermute | solution.py:39
  1328.7 95.0 %collective-permute-start.23 = (bf16[4,128,2048]{2,1,0:T(8,128)(2,1)}, bf16[4,128,2048]{2,1,0:T(8,128)(2,1)}, u32[]{:S(2)}, u32[]{:S(2)}) collective-permute-start(bf16[4,128,2048]{2,1,0:T(8,128)(2,1)} %pad_maximum_fusion.14), channel_id=1, source_target_pairs={{0,2},{2,0},{1,3},{3,1},{4,6},{6,4},{5,7},{7,5},{8,10},{10,8},{9,1... | collective-permute-start | bytes 6291464 | tf_op jit(solution)/shard_map/ppermute | solution.py:39
  1330.8 92.8 %collective-permute-start.21 = (bf16[4,128,2048]{2,1,0:T(8,128)(2,1)}, bf16[4,128,2048]{2,1,0:T(8,128)(2,1)}, u32[]{:S(2)}, u32[]{:S(2)}) collective-permute-start(bf16[4,128,2048]{2,1,0:T(8,128)(2,1)} %pad_maximum_fusion.13), channel_id=1, source_target_pairs={{0,16},{16,0},{1,17},{17,1},{2,18},{18,2},{3,19},{19,3},{4,20},{20... | collective-permute-start | bytes 6291464 | tf_op jit(solution)/shard_map/ppermute | solution.py:39
  1461.0 89.9 %all-to-all-start.1 = ((f32[32,1,384]{2,1,0:T(1,128)}), f32[32,1,384]{2,1,0:T(1,128)S(1)}, u32[]{:S(2)}, u32[]{:S(2)}) async-start(f32[32,1,384]{2,1,0:T(1,128)} %reshape.573), calls=%async_computation.3 | async-start | bytes 98304 | tf_op jit(solution)/shard_map/all_to_all | solution.py:750
  1471.2 74.1 %collective-permute-start.25 = (bf16[128,2048]{1,0:T(8,128)(2,1)S(1)}, bf16[128,2048]{1,0:T(8,128)(2,1)S(1)}, u32[]{:S(2)}, u32[]{:S(2)}) collective-permute-start(bf16[128,2048]{1,0:T(8,128)(2,1)S(1)} %get-tuple-element.183), channel_id=1, source_target_pairs={{0,8},{4,12},{8,0},{12,4},{1,9},{5,13},{9,1},{13,5},{2,10},{6,14},... | collective-permute-start | bytes 1572872 | tf_op jit(solution)/shard_map/ppermute | solution.py:86
  1471.2 74.1 %collective-permute-start.24 = (bf16[128,2048]{1,0:T(8,128)(2,1)S(1)}, bf16[128,2048]{1,0:T(8,128)(2,1)S(1)}, u32[]{:S(2)}, u32[]{:S(2)}) collective-permute-start(bf16[128,2048]{1,0:T(8,128)(2,1)S(1)} %get-tuple-element.184), channel_id=1, source_target_pairs={{0,4},{4,8},{8,12},{12,0},{1,5},{5,9},{9,13},{13,1},{2,6},{6,10},{... | collective-permute-start | bytes 1572872 | tf_op jit(solution)/shard_map/ppermute | solution.py:86
  (140 other events, 3253.0 us)
Sparse Core Ops, SparseCore 0:
  24.5 309.2 all-gather.4
  335.7 92.7 all-gather.8
  430.3 89.8 all-gather.6
  662.7 143.8 reduce-scatter.6
  819.0 59.6 reduce-scatter.8
  880.8 60.2 reduce-scatter.12
  989.5 145.0 reduce-scatter.10
  1136.9 60.9 reduce-scatter.16
  1200.2 210.9 reduce-scatter.14

commit v5 on v4

--- a/solution.py
+++ b/solution.py
@@ -117,6 +117,272 @@
     from_x = swap(to_x, "dp")
     from_y = swap(to_y, "y")
     return held[0, 0].astype(f32) + from_x.astype(f32) + from_y.astype(f32)
+
+
+MESH = pl.DeviceIdType.MESH
+Z_UP, Z_DOWN, X_A, Y_A, Y_B, X_B, Y_A2, X_B2 = range(8)
+
+
+def first_kernel(
+    query,
+    key,
+    value,
+    output,
+    tokens,
+    grads,
+    segments,
+    weights,
+    tokens_out,
+    grads_out,
+    segments_out,
+    send,
+    recv,
+    core_send,
+    core_recv,
+    core_local,
+    row_send,
+    row_recv,
+    row_local,
+):
+    dp, z, y, core = (lax.axis_index(a) for a in ("dp", "seq", "y", "core"))
+    seq_n = weights.shape[1]
+    rows, columns = query.shape[0], weights.shape[4] // 4
+    half = weights.shape[4] // 2
+    piece = tokens_out.shape[1]
+    x_next, y_next, z_next, z_last, other = (
+        {"dp": 1 - dp},
+        {"y": 1 - y},
+        {"seq": lax.rem(z + 1, seq_n)},
+        {"seq": lax.rem(z + seq_n - 1, seq_n)},
+        {"core": 1 - core},
+    )
+
+    barrier = pltpu.get_barrier_semaphore()
+    partners = [x_next, y_next] + [
+        {"seq": lax.rem(z + dz, seq_n), "core": lax.rem(core + dc, 2)}
+        for dz in range(seq_n)
+        for dc in range(2)
+        if dz or dc
+    ]
+    for partner in partners:
+        pl.semaphore_signal(barrier, inc=1, device_id=partner, device_id_type=MESH)
+    pl.semaphore_wait(barrier, len(partners))
+
+    here = pl.ds(pl.multiple_of(core * rows, rows), rows)
+    locals_, remotes = [], []
+    for m, matrix in enumerate((query, key, value, output)):
+        place = weights.at[dp, z, y, here, pl.ds(m * columns, columns)]
+        mine = matrix.at[:, pl.ds(pl.multiple_of(core * columns, columns), columns)]
+        theirs = matrix.at[:, pl.ds(pl.multiple_of((1 - core) * columns, columns), columns)]
+        locals_.append(pltpu.make_async_copy(mine, place, core_local.at[m]))
+        remotes.append(
+            pltpu.make_async_remote_copy(
+                theirs, place, core_send.at[m], core_recv.at[m], device_id=other, device_id_type=MESH
+            )
+        )
+    segment_local = pltpu.make_async_copy(segments, segments_out.at[core], core_local.at[4])
+    segment_remote = pltpu.make_async_remote_copy(
+        segments, segments_out.at[core], core_send.at[4], core_recv.at[4], device_id=other, device_id_type=MESH
+    )
+    for copy in remotes + [segment_remote] + locals_ + [segment_local]:
+        copy.start()
+    for copy in remotes + locals_:
+        copy.wait()
+
+    def part(kind, dp_b, z_b, y_b, device):
+        if kind in (Z_UP, Z_DOWN):
+            ref = weights.at[dp_b, z_b, y_b]
+        else:
+            start = 0 if kind in (X_A, Y_A, Y_A2) else half
+            ref = weights.at[dp_b, z_b, y_b, :, pl.ds(start, half)]
+        return pltpu.make_async_remote_copy(
+            ref, ref, send.at[kind, z_b], recv.at[kind, z_b], device_id=device, device_id_type=MESH
+        )
+
+    def own(kind, z_b):
+        device = {Z_UP: z_next, Z_DOWN: z_last, X_A: x_next, X_B: x_next, Y_A: y_next, Y_B: y_next}[kind]
+        return part(kind, dp, z_b, y, device)
+
+    def from_x(kind, z_b):
+        return part(kind, 1 - dp, z_b, y, x_next)
+
+    def from_y(kind, z_b):
+        return part(kind, dp, z_b, 1 - y, y_next)
+
+    def on_y(z_b):
+        return part(Y_A2, 1 - dp, z_b, y, y_next)
+
+    def on_x(z_b):
+        return part(X_B2, dp, z_b, 1 - y, x_next)
+
+    def spread(z_b):
+        for kind in (X_A, Y_B, X_B, Y_A):
+            own(kind, z_b).start()
+
+    def relay(z_b):
+        from_x(X_A, z_b).wait_recv()
+        on_y(z_b).start()
+        from_y(Y_B, z_b).wait_recv()
+        on_x(z_b).start()
+
+    def at_step(step, act_up, act_down):
+        @pl.when(z - step >= 0)
+        def _():
+            act_up(z - step)
+
+        @pl.when(z + step < seq_n)
+        def _():
+            act_down(z + step)
+
+    def come_up(z_b):
+        own(Z_UP, z_b).wait_recv()
+
+        @pl.when(z < seq_n - 1)
+        def _():
+            own(Z_UP, z_b).start()
+
+        spread(z_b)
+
+    def come_down(z_b):
+        own(Z_DOWN, z_b).wait_recv()
+
+        @pl.when(z > 0)
+        def _():
+            own(Z_DOWN, z_b).start()
+
+        spread(z_b)
+
+    def rows_of(n, source, target, act):
+        for s in range(tokens.shape[0]):
+            z_to = tokens.shape[0] * core + s
+            for d in range(2):
+                core_to = lax.rem(core + d, 2)
+                ref = source.at[s, pl.ds(pl.multiple_of(core_to * piece, piece), piece), :]
+                copy = pltpu.make_async_remote_copy(
+                    ref,
+                    target.at[z],
+                    row_send.at[n, s, d],
+                    row_recv.at[n, z],
+                    device_id={"seq": z_to, "core": core_to},
+                    device_id_type=MESH,
+                )
+                if d:
+                    act(copy)
+                else:
+                    keep = pltpu.make_async_copy(ref, target.at[z], row_local.at[n])
+
+                    @pl.when(z_to != z)
+                    def _(copy=copy):
+                        act(copy)
+
+                    @pl.when(z_to == z)
+                    def _(keep=keep):
+                        if act is begin:
+                            keep.start()
+                        else:
+                            keep.wait()
+
+    def begin(copy):
+        copy.start()
+
+    def sent(copy):
+        copy.wait_send()
+
+    def rows_in(n, target):
+        group = z // tokens.shape[0]
+        for z_from in range(seq_n):
+            copy = pltpu.make_async_remote_copy(
+                target.at[z_from],
+                target.at[z_from],
+                row_send.at[n, 0, 0],
+                row_recv.at[n, z_from],
+                device_id=other,
+                device_id_type=MESH,
+            )
+
+            @pl.when((z_from != z) | (group != core))
+            def _(copy=copy):
+                copy.wait_recv()
+
+    @pl.when(z < seq_n - 1)
+    def _():
+        own(Z_UP, z).start()
+
+    @pl.when(z > 0)
+    def _():
+        own(Z_DOWN, z).start()
+
+    spread(z)
+    for step in range(1, seq_n):
+        at_step(step, come_up, come_down)
+        if step == 1:
+            relay(z)
+        else:
+            at_step(step - 1, relay, relay)
+        if step == seq_n - 2:
+            rows_of(0, tokens, tokens_out, begin)
+    rows_of(1, grads, grads_out, begin)
+    at_step(seq_n - 1, relay, relay)
+
+    segment_remote.wait()
+    segment_local.wait()
+    for z_b in range(seq_n):
+        from_y(Y_A, z_b).wait_recv()
+        from_x(X_B, z_b).wait_recv()
+        part(Y_A2, 1 - dp, z_b, 1 - y, y_next).wait_recv()
+        part(X_B2, 1 - dp, z_b, 1 - y, x_next).wait_recv()
+        for kind in (X_A, Y_B, X_B, Y_A):
+            own(kind, z_b).wait_send()
+        on_y(z_b).wait_send()
+        on_x(z_b).wait_send()
+
+        @pl.when((z < seq_n - 1) & (z_b <= z))
+        def _(z_b=z_b):
+            own(Z_UP, z_b).wait_send()
+
+        @pl.when((z > 0) & (z_b >= z))
+        def _(z_b=z_b):
+            own(Z_DOWN, z_b).wait_send()
+
+    rows_of(0, tokens, tokens_out, sent)
+    rows_of(1, grads, grads_out, sent)
+    rows_in(0, tokens_out)
+    rows_in(1, grads_out)
+
+
+def first_transfers(query, key, value, output, tokens, grads, segments, sizes):
+    dp_n, seq_n, r_n, y_n, core_n = sizes
+    rows, width = query.shape
+    piece = tokens.shape[1] // core_n
+    columns = width // core_n
+    held = pl.BlockSpec(memory_space=pl.ANY)
+    out = jax.ShapeDtypeStruct((seq_n, piece, width), bf16)
+    dma = pltpu.SemaphoreType.DMA
+    weights, tokens, grads, segments = pl.pallas_call(
+        first_kernel,
+        in_specs=[held] * 7,
+        out_specs=[held] * 4,
+        out_shape=[
+            jax.ShapeDtypeStruct((dp_n, seq_n, y_n, core_n * rows, 4 * columns), bf16),
+            out,
+            out,
+            jax.ShapeDtypeStruct((core_n,) + segments.shape, segments.dtype),
+        ],
+        scratch_shapes=[
+            dma((8, seq_n)),
+            dma((8, seq_n)),
+            dma((5,)),
+            dma((5,)),
+            dma((5,)),
+            dma((2, tokens.shape[0], 2)),
+            dma((2, seq_n)),
+            dma((2,)),
+        ],
+        compiler_params=pltpu.CompilerParams(collective_id=0, has_side_effects=True),
+        cost_estimate=pl.CostEstimate(flops=0, bytes_accessed=2 * 4 * columns * width, transcendentals=0),
+        name="first_transfers",
+    )(query, key, value, output, tokens, grads, segments)
+    return weights.reshape(width, 4 * columns), tokens, grads, segments
 
 
 def visible_block(seg_row, seg_col, start, rows, cols):
@@ -557,44 +823,29 @@
     dp_i, seq_i, r_i, y_i, core_i = (lax.axis_index(a) for a in EVERY)
     group, member = seq_i // seq_count, seq_i % seq_count
 
-    own_segments = lax.dynamic_slice_in_dim(segments, (seq_i * r_n + r_i) * seq_dev, seq_dev, 1)
-    small = jnp.concatenate(
-        [jnp.transpose(routes, (2, 0, 1)), own_segments[None]], axis=0
-    ).reshape((topk + 1) * seq_count, seq_dev)
-    small = lax.all_gather(small, EVERY, axis=0, tiled=True).reshape(
-        dp_n, seq_n, r_n, y_n, core_n, topk + 1, seq_count, seq_dev
-    )
-    small = pick(pick(small, group, 4), member, 5)
-    segment = pick(pick(small, dp_i, 0), y_i, 2)[:, :, topk].reshape(length)
-    plane_routes = pick(small, r_i, 2)[:, :, :, :topk].transpose(0, 2, 1, 3, 4)
-    block_routes = plane_routes.reshape(blocks, topk, seq_dev)
-    home_routes = (
-        pick(pick(plane_routes, dp_i, 0), y_i, 0)
-        .reshape(seq_n, topk, core_n, piece)
-        .transpose(1, 2, 0, 3)
-    )
-    home_routes = pick(home_routes, core_i, 1).reshape(topk, home)
-
-    local = jnp.concatenate([query_weight, key_weight, value_weight, output_weight], axis=1)
-    rows_here = local.shape[0]
-    local = local.reshape(rows_here, 4, parts, columns)
-    local = chip_exchange(local, 2, 0, parts).reshape(parts, rows_here, 4 * columns)
-
-    def gathered(block):
-        whole = lax.all_gather(block.reshape(parts * rows_here, -1), SPREAD, axis=0, tiled=True)
-        if r_n > 1:
-            whole = (
-                whole.reshape(dp_n * seq_n, y_n, r_n, core_n * rows_here, -1)
-                .transpose(0, 2, 1, 3, 4)
-                .reshape(width, -1)
-            )
-        return whole
-
-    weights = gathered(local)
+    rows_here = query_weight.shape[0]
+    if r_n == 1 and parts == 2 and dp_n == 2 and y_n == 2 and seq_n == 2 * seq_count:
+        weights, token_home, grad_home, chip_segments = first_transfers(
+            query_weight, key_weight, value_weight, output_weight, tokens, grad_out, segments, sizes
+        )
+        segment = pick(pick(chip_segments, group, 0), member, 0)
+    else:
+        local = jnp.concatenate([query_weight, key_weight, value_weight, output_weight], axis=1)
+        local = chip_exchange(local.reshape(rows_here, 4, parts, columns), 2, 0, parts)
+        weights = lax.all_gather(
+            local.reshape(parts * rows_here, 4 * columns), SPREAD, axis=0, tiled=True
+        )
+        weights = (
+            weights.reshape(dp_n * seq_n, y_n, r_n, core_n * rows_here, -1)
+            .transpose(0, 2, 1, 3, 4)
+            .reshape(width, -1)
+        )
+        token_home, grad_home = to_sequences(tokens), to_sequences(grad_out)
+        chip_segments = lax.all_gather(segments, "core")
+        segment = pick(pick(chip_segments, group, 0), member, 0)
     weight_in, weight_out = weights[:, : 3 * columns], weights[:, 3 * columns :]
 
-    token_float = to_sequences(tokens).astype(f32)
-    grad_home = to_sequences(grad_out)
+    token_float = token_home.astype(f32)
     inverse_one = lax.rsqrt(jnp.mean(token_float * token_float, axis=-1, keepdims=True) + epsilon)
     hidden_one = (token_float * inverse_one * attn_norm).astype(bf16)
     hidden_full = chip_gather(hidden_one, 1, parts).reshape(length, width)
@@ -619,6 +870,19 @@
     hidden_two = (normed_two * expert_norm).astype(bf16).reshape(home, width)
 
     hidden_plane = lax.all_gather(hidden_two, PLANE, axis=0, tiled=True)
+    small = after(jnp.transpose(routes, (2, 0, 1)).reshape(topk * seq_count, seq_dev), hidden_two)
+    small = lax.all_gather(small, EVERY, axis=0, tiled=True).reshape(
+        dp_n, seq_n, r_n, y_n, core_n, topk, seq_count, seq_dev
+    )
+    small = pick(pick(small, group, 4), member, 5)
+    plane_routes = pick(small, r_i, 2).transpose(0, 2, 1, 3, 4)
+    block_routes = plane_routes.reshape(blocks, topk, seq_dev)
+    home_routes = (
+        pick(pick(plane_routes, dp_i, 0), y_i, 0)
+        .reshape(seq_n, topk, core_n, piece)
+        .transpose(1, 2, 0, 3)
+    )
+    home_routes = pick(home_routes, core_i, 1).reshape(topk, home)
     mine = y_i * core_n + core_i
     chosen = jnp.any(block_routes == mine, axis=1)
     places = jnp.arange(seq_dev)
@@ -696,16 +960,17 @@
     )
     dqkv = jnp.concatenate([dqpre, dkpre, dvpre], axis=1)
     out_grad = t_product(mixed_full, after(dbranch_here, dqpre))
-    in_grad = t_product(hidden_full, dqkv).astype(bf16)
-    up_a = rows_product(expert_in, after(dupre_a, dqpre))
-    up_b = rows_product(expert_in, after(dupre_b, dqpre))
+    dhidden_part = product_t(dqkv, weight_in).astype(bf16)
+    in_grad = t_product(hidden_full, after(dqkv, dhidden_part)).astype(bf16)
+    up_b = rows_product(expert_in, after(dupre_b, in_grad))
+    up_a = rows_product(expert_in, after(dupre_a, in_grad))
 
     grad_down = jnp.concatenate([down_sum_a, down_sum_b], axis=1).astype(f32).T[None]
     grad_gate = jnp.concatenate([over_ctx(gate_a), over_ctx(gate_b)], axis=1).astype(f32)[None]
     grad_up = jnp.concatenate([over_ctx(up_a), over_ctx(up_b)], axis=1).astype(f32)[None]
 
     dhidden_one = chip_scatter(
-        product_t(dqkv, weight_in).astype(bf16).reshape(seq_n, parts * piece, width), 1, parts
+        dhidden_part.reshape(seq_n, parts * piece, width), 1, parts
     )
     normed_one = token_float * inverse_one
     dtokens, attn_norm_grad = norm_backward(
@@ -716,7 +981,7 @@
     )
     grad_tokens = from_sequences((dtokens + dresid).astype(bf16).reshape(seq_n, piece, width)).astype(f32)
 
-    mixture = plane_scatter(after(mixed_rows, dqpre))
+    mixture = plane_scatter(after(mixed_rows, dbranch))
     output = from_sequences((residual + mixture).astype(bf16))
 
     def seen(part):

time: 1590 us -> 1440 us (0.906)
  waiting for transfers between devices: 505 us -> 301 us
  Pallas kernels: 367 us -> 529 us
  starting transfers between devices: 140 us -> 102 us
  blocking collectives: 77.8 us -> 45 us
  other arithmetic: 133 us -> 114 us
    pallas_call x0 -> x1, Pallas kernels: none -> 162 us  [first_transfers(): pl.pallas_call(first_kernel, in_specs=[held] * 7, out_specs=[held] * 4, o...]
    ppermute x18 -> x12, waiting for transfers between devices: 227 us -> 67.2 us  [seq_pieces(): lax.ppermute(give, 'seq', [(i, (i + step) % count) for i in range(count)])]
    ppermute x31 -> x28, waiting for transfers between devices: 111 us -> 182 us  [swap(): return lax.ppermute(a, axis, [(0, 1), (1, 0)])]
    all_gather x1 -> x0, waiting for transfers between devices: 58.6 us -> none  [gathered(): lax.all_gather(block.reshape(parts * rows_here, -1), SPREAD, axis=0, tile...]
    all_gather x1, waiting for transfers between devices: 91.8 us -> 47.1 us  [on_device(): hidden_plane = lax.all_gather(hidden_two, PLANE, axis=0, tiled=True)]
    all_gather x1, blocking collectives: 77.8 us -> 45 us  [on_device(): lax.all_gather(small, EVERY, axis=0, tiled=True)]
    ppermute x18 -> x12, starting transfers between devices: 78.8 us -> 53.3 us  [seq_pieces(): lax.ppermute(give, 'seq', [(i, (i + step) % count) for i in range(count)])]
    all_gather x1, waiting for transfers between devices: 16 us -> 0.02 us  [on_device(): lax.all_gather(grad_home.reshape(home, width), PLANE, axis=0, tiled=True)]
  transfers between devices with their start and end apart: 60 -> 50, of which waited for: 30 -> 21; matrix products, arithmetic and copies ran while one was open for 25% -> 26% of each run, Pallas kernels for 16% -> 18%
where the time goes in v5:
time: 1440 us
  Pallas kernels  529 us (37%)
  waiting for transfers between devices  301 us (21%)
  matrix products  215 us (15%)
  local copies, waits for them, and re-layouts  115 us (8%)
  other arithmetic  114 us (8%)
  starting transfers between devices  102 us (7%)
  blocking collectives  45 us (3%)
  between operations  16 us (1%)
    ppermute x28, waiting for transfers between devices, swap(): return lax.ppermute(a, axis, [(0, 1), (1, 0)])  182 us
    pallas_call x1, Pallas kernels, first_transfers(): pl.pallas_call(first_kernel, in_specs=[held] * 7, out_specs=[held] * 4, o...  162 us
    dot_general x9, matrix products, t_product(): lax.dot_general(a, b, (((0,), (0,)), ((), ())), preferred_element_type=f32)  153 us
    pallas_call x2, Pallas kernels, expert_units(): pl.pallas_call(functools.partial(units_kernel, chunk), grid=(units // til...  126 us
    pallas_call x2, Pallas kernels, expert_input_grad(): pl.pallas_call(functools.partial(input_kernel, cut), grid=(width // n, ro...  77.7 us
    ppermute x12, waiting for transfers between devices, seq_pieces(): lax.ppermute(give, 'seq', [(i, (i + step) % count) for i in range(count)])  67.2 us
    ppermute x12, starting transfers between devices, seq_pieces(): lax.ppermute(give, 'seq', [(i, (i + step) % count) for i in range(count)])  53.3 us
    all_gather x1, waiting for transfers between devices, on_device(): hidden_plane = lax.all_gather(hidden_two, PLANE, axis=0, tiled=True)  47.1 us
  transfers between devices with their start and end apart: 50, of which 21 were waited for; matrix products, arithmetic and copies ran while one was open for 26% of the time, Pallas kernels for 18%

profile of v5, /device:TPU:1, one launch (start us, length us, event | category | flops | bytes accessed | tf_op | source)
XLA Modules:
  0.0 1436.7 jit_solution(10088475647483556195)
XLA Ops:
  7.2 162.4 %first_transfers.1 = (bf16[2,4,2,128,4096]{4,3,2,1,0:T(8,128)(2,1)}, bf16[4,128,2048]{2,1,0:T(8,128)(2,1)}, bf16[4,128,2048]{2,1,0:T(8,128)(2,1)}, s32[2,2,1024]{2,1,0:T(2,128)}) custom-call(bf16[64,2048]{1,0:T(8,128)(2,1)} %query.1, bf16[64,2048]{1,0:T(8,128)(2,1)} %key.1, bf16[64,2048]{1,0:T(8,128)(2,1)} %value.1, bf16[64,2048]{1,0:T(8,128)(2,1)} %output.1, ...), custom_call_target="tpu_custom_call" | custom-call | bytes 16777216 | tf_op jit(solution)/shard_map/first_transfers/pallas_call | solution.py:361
  183.8 20.0 %fusion.4.qp.kp.vp = f32[1024,3072]{1,0:T(8,128)} fusion(bf16[1024,2048]{1,0:T(8,128)(2,1)S(1)} %bitcast.354, bf16[2048,4096]{1,0:T(8,128)(2,1)} %bitcast.376), kind=kOutput, calls=%fused_computation.7 | convolution fusion | flops 12884901888 | bytes 29360128 | tf_op jit(solution)/shard_map/dot_general | solution.py:27
  203.8 27.9 %attend.1 = (bf16[1024,1024]{1,0:T(8,128)(2,1)S(1)}, bf16[1024,1024]{1,0:T(8,128)(2,1)S(1)}, bf16[1024,1024]{1,0:T(8,128)(2,1)}, bf16[1024,1024]{1,0:T(8,128)(2,1)}) custom-call(f32[1024,3072]{1,0:T(8,128)} %fusion.4.qp.kp.vp, f32[1024,3072]{1,0:T(8,128)} %fusion.4.qp.kp.vp, f32[1024,3072]{1,0:T(8,128)} %fusion.4.qp.kp.vp, ...), custom_call_target="tpu_custom_call" | custom-call | flops 2684354560 | bytes 20971520 | tf_op jit(solution)/shard_map/attend/pallas_call | solution.py:427
  268.1 45.0 %all-gather = s32[32,4,256]{2,1,0:T(4,128)S(1)} all-gather(s32[1,4,256]{2,1,0:T(4,128)} %bitcast.368), channel_id=1, replica_groups=mesh['dp'=2,'seq'=4,'r'=1,'y'=2,'core'=2] {'dp','seq','r','y','core'}, dimensions={0}, use_global_device_ids=true | all-gather | bytes 135168 | tf_op jit(solution)/shard_map/all_gather | solution.py:874
  315.4 47.1 %all-gather.4.cloned.1.call-done = bf16[4096,2048]{1,0:T(8,128)(2,1)} async-done(((bf16[512,2048]{1,0:T(8,128)(2,1)}), bf16[4096,2048]{1,0:T(8,128)(2,1)}) %all-gather.4.cloned.1.call-update) | async-done | bytes 16777232 | tf_op jit(solution)/shard_map/all_gather | solution.py:872
  362.5 26.1 %dispatch.1 = (bf16[16,160,2048]{2,1,0:T(8,128)(2,1)}, bf16[16,160,2048]{2,1,0:T(8,128)(2,1)}, f32[16,256,1]{2,1,0:T(8,128)S(1)}) custom-call(s32[4]{0:T(128)S(1)} %pad_add_fusion.me, bf16[4,2,4,128,2048]{4,3,2,1,0:T(8,128)(2,1)} %bitcast.341, bf16[4,2,4,128,2048]{4,3,2,1,0:T(8,128)(2,1)} %bitcast.327, s32[16,1,256]{2,1,0:T(1,128)S(1)} %broadcast_in_dim.45.slot, ...), custom_call_target="tpu_custom_call" | custom-call | flops 7516192768 | bytes 54525952 | tf_op jit(solution)/shard_map/dispatch/pallas_call | solution.py:610
  389.9 85.9 %expert_units.2 = (bf16[2560,2048]{1,0:T(8,128)(2,1)}, bf16[2560,2048]{1,0:T(8,128)(2,1)}, bf16[2560,2048]{1,0:T(8,128)(2,1)}) custom-call(bf16[2560,2048]{1,0:T(8,128)(2,1)} %bitcast.391, bf16[2560,2048]{1,0:T(8,128)(2,1)} %bitcast.397, bf16[2048,2816]{1,0:T(8,128)(2,1)} %bitcast.380, bf16[2048,2816]{1,0:T(8,128)(2,1)} %bitcast.384, ...), custom_call_target="tpu_custom_call" | custom-call | flops 64424509440 | bytes 77594624 | tf_op jit(solution)/shard_map/expert_units/pallas_call | solution.py:531
  475.8 28.9 %convolution_convert_fusion.3.rest_0_ = bf16[2048,2048]{1,0:T(8,128)(2,1)} fusion(bf16[2560,2048]{1,0:T(8,128)(2,1)} %bitcast.398, bf16[2560,2048]{1,0:T(8,128)(2,1)} %get-tuple-element.41.units_a), kind=kOutput, calls=%fused_computation.15 | convolution fusion | flops 21479030784 | bytes 29360128 | tf_op jit(solution)/shard_map/dot_general | solution.py:35
  505.4 39.7 %expert_units.3 = (bf16[2560,768]{1,0:T(8,128)(2,1)}, bf16[2560,768]{1,0:T(8,128)(2,1)}, bf16[2560,768]{1,0:T(8,128)(2,1)}) custom-call(bf16[2560,2048]{1,0:T(8,128)(2,1)} %bitcast.392, bf16[2560,2048]{1,0:T(8,128)(2,1)} %bitcast.399, bf16[2048,2816]{1,0:T(8,128)(2,1)} %bitcast.381, bf16[2048,2816]{1,0:T(8,128)(2,1)} %bitcast.385, ...), custom_call_target="tpu_custom_call" | custom-call | flops 24159191040 | bytes 42205184 | tf_op jit(solution)/shard_map/expert_units/pallas_call | solution.py:531
  558.7 38.8 %expert_input_grad.2.rest_0_ = bf16[2560,1024]{1,0:T(8,128)(2,1)} custom-call(bf16[2560,2048]{1,0:T(8,128)(2,1)} %get-tuple-element.43.dgate_a.refs_0_, bf16[2560,768]{1,0:T(8,128)(2,1)} %get-tuple-element.44.dgate_b.refs_0_, bf16[2560,2048]{1,0:T(8,128)(2,1)} %get-tuple-element.45.dup_a.refs_0_, bf16[2560,768]{1,0:T(8,128)(2,1)} %get-tuple-element.46.dup_b.refs_0_, ...), custom_call_target="tpu_custom_call" | custom-call | flops 29527900160 | bytes 45613056 | tf_op jit(solution)/shard_map/expert_input_grad/pallas_call | solution.py:745
  597.5 39.0 %expert_input_grad.3 = bf16[2560,1024]{1,0:T(8,128)(2,1)} custom-call(bf16[2560,2048]{1,0:T(8,128)(2,1)} %get-tuple-element.43.dgate_a.refs_0_, bf16[2560,768]{1,0:T(8,128)(2,1)} %get-tuple-element.44.dgate_b.refs_0_, bf16[2560,2048]{1,0:T(8,128)(2,1)} %get-tuple-element.45.dup_a.refs_0_, bf16[2560,768]{1,0:T(8,128)(2,1)} %get-tuple-element.46.dup_b.refs_0_, ...), custom_call_target="tpu_custom_call" | custom-call | flops 29527900160 | bytes 45613056 | tf_op jit(solution)/shard_map/expert_input_grad/pallas_call | solution.py:745
  719.7 29.2 %convolution_convert_fusion.2.rest_0_ = bf16[2048,2048]{1,0:T(8,128)(2,1)} fusion(bf16[2560,2048]{1,0:T(8,128)(2,1)} %bitcast.394, bf16[2560,2048]{1,0:T(8,128)(2,1)} %after.9), kind=kOutput, calls=%fused_computation.14 | convolution fusion | flops 21479030784 | bytes 29360128 | tf_op jit(solution)/shard_map/dot_general | solution.py:35
  751.1 40.4 %expert_down.1 = bf16[2560,2048]{1,0:T(8,128)(2,1)} custom-call(bf16[2560,2048]{1,0:T(8,128)(2,1)} %get-tuple-element.41.units_a, bf16[2560,768]{1,0:T(8,128)(2,1)S(1)} %copy-done.18, bf16[2816,2048]{1,0:T(8,128)(2,1)} %bitcast.390, bf16[2048,2048]{1,0:T(8,128)(2,1)} %convolution_convert_fusion.2.rest_0_), custom_call_target="tpu_custom_call" | custom-call | flops 29527900160 | bytes 36438016 | tf_op jit(solution)/shard_map/expert_down/pallas_call | solution.py:709
  791.5 24.1 %combine.1 = (bf16[2,2,2,4,128,2048]{5,4,3,2,1,0:T(8,128)(2,1)}, f32[16,256,1]{2,1,0:T(8,128)S(1)}) custom-call(s32[4]{0:T(128)S(1)} %pad_add_fusion.me, bf16[16,160,2048]{2,1,0:T(8,128)(2,1)} %bitcast.344, s32[16,256,1]{2,1,0:T(8,128)S(1)} %copy.174.slot, f32[16,256,1]{2,1,0:T(8,128)S(1)} %copy-done.11, bf16[4,2,4,128,2048]{4,3,2,1,0:T(8,128)(2,1)} %bitcast.328), custom_call_target="tpu_custom_call" | custom-call | flops 2684354560 | bytes 44040192 | tf_op jit(solution)/shard_map/combine/pallas_call | solution.py:684
  885.1 31.8 %attend_back.1 = (bf16[1024,1024]{1,0:T(8,128)(2,1)S(1)}, bf16[1024,1024]{1,0:T(8,128)(2,1)}, bf16[1024,1024]{1,0:T(8,128)(2,1)}) custom-call(bf16[1024,1024]{1,0:T(8,128)(2,1)} %copy-done.16, bf16[1024,1024]{1,0:T(8,128)(2,1)} %copy-done.17, bf16[1024,1024]{1,0:T(8,128)(2,1)} %get-tuple-element.52.v, bf16[1024,1024]{1,0:T(8,128)(2,1)} %get-tuple-element.37.mixed, ...), custom_call_target="tpu_custom_call" | custom-call | flops 6710886400 | bytes 16777216 | tf_op jit(solution)/shard_map/attend_back/pallas_call | solution.py:487
  924.8 17.7 %fusion.22.refs_1_ = bf16[1024,2048]{1,0:T(8,128)(2,1)} fusion(bf16[1024,3072]{1,0:T(8,128)(2,1)S(1)} %constant_dynamic-update-slice_fusion.refs_0_, bf16[2048,4096]{1,0:T(8,128)(2,1)} %bitcast.379), kind=kOutput, calls=%fused_computation.65 | convolution fusion | flops 12886999040 | bytes 23068672 | tf_op jit(solution)/shard_map/dot_general | solution.py:31
  942.5 19.4 %convolution_convert_fusion.refs_1_ = bf16[2048,3072]{1,0:T(8,128)(2,1)} fusion(bf16[1024,2048]{1,0:T(8,128)(2,1)} %bitcast.355, bf16[1024,3072]{1,0:T(8,128)(2,1)} %after.12), kind=kOutput, calls=%fused_computation.4 | convolution fusion | flops 12891193344 | bytes 23068672 | tf_op jit(solution)/shard_map/dot_general | solution.py:35
  1021.8 26.9 %convolution_convert_fusion.1 = bf16[2048,2048]{1,0:T(8,128)(2,1)} fusion(bf16[2560,2048]{1,0:T(8,128)(2,1)} %bitcast.396, bf16[2560,2048]{1,0:T(8,128)(2,1)S(1)} %copy-done.42), kind=kOutput, calls=%fused_computation.13 | convolution fusion | flops 21479030784 | bytes 29360128 | tf_op jit(solution)/shard_map/dot_general | solution.py:35
  1051.1 42.5 %collective-permute-done.33 = bf16[4,1,128,512]{3,2,0,1:T(8,128)(2,1)S(1)} collective-permute-done((bf16[4,1,128,512]{3,2,0,1:T(8,128)(2,1)S(1)}, bf16[4,1,128,512]{3,2,0,1:T(8,128)(2,1)S(1)}, u32[]{:S(2)}, u32[]{:S(2)}) %collective-permute-start.33) | collective-permute-done | bytes 524320 | tf_op jit(solution)/shard_map/ppermute | solution.py:39
  1174.9 18.1 %collective-permute-done.12 = bf16[2,128,2048]{2,1,0:T(8,128)(2,1)S(1)} collective-permute-done((bf16[2,128,2048]{2,1,0:T(8,128)(2,1)S(1)}, bf16[2,128,2048]{2,1,0:T(8,128)(2,1)S(1)}, u32[]{:S(2)}, u32[]{:S(2)}) %collective-permute-start.12) | collective-permute-done | bytes 1048608 | tf_op jit(solution)/shard_map/ppermute | solution.py:39
  1200.3 26.3 %collective-permute-done.27 = bf16[4,1,128,1536]{3,2,1,0:T(8,128)(2,1)S(1)} collective-permute-done((bf16[4,1,128,1536]{3,2,1,0:T(8,128)(2,1)S(1)}, bf16[4,1,128,1536]{3,2,1,0:T(8,128)(2,1)S(1)}, u32[]{:S(2)}, u32[]{:S(2)}) %collective-permute-start.27) | collective-permute-done | bytes 1572896 | tf_op jit(solution)/shard_map/ppermute | solution.py:39
  1232.6 38.4 %collective-permute-done.13 = bf16[4,128,2048]{2,1,0:T(8,128)(2,1)} collective-permute-done((bf16[4,128,2048]{2,1,0:T(8,128)(2,1)S(1)}, bf16[4,128,2048]{2,1,0:T(8,128)(2,1)}, u32[]{:S(2)}, u32[]{:S(2)}) %collective-permute-start.13) | collective-permute-done | bytes 2097184 | tf_op jit(solution)/shard_map/ppermute | solution.py:39
  1298.7 39.7 %collective-permute-start.16 = (bf16[128,2048]{1,0:T(8,128)(2,1)S(1)}, bf16[128,2048]{1,0:T(8,128)(2,1)S(1)}, u32[]{:S(2)}, u32[]{:S(2)}) collective-permute-start(bf16[128,2048]{1,0:T(8,128)(2,1)S(1)} %get-tuple-element.201), channel_id=1, source_target_pairs={{0,12},{4,0},{8,4},{12,8},{1,13},{5,1},{9,5},{13,9},{2,14},{6,2},{... | collective-permute-start | bytes 1572872 | tf_op jit(solution)/shard_map/ppermute | solution.py:86
  1356.8 33.1 %collective-permute-done.15 = bf16[128,2048]{1,0:T(8,128)(2,1)S(1)} collective-permute-done((bf16[128,2048]{1,0:T(8,128)(2,1)S(1)}, bf16[128,2048]{1,0:T(8,128)(2,1)S(1)}, u32[]{:S(2)}, u32[]{:S(2)}) %collective-permute-start.15) | collective-permute-done | bytes 524320 | tf_op jit(solution)/shard_map/ppermute | solution.py:86
  (431 shorter events, 472.2 us)
Async XLA Ops:
  7.2 308.2 %all-gather.6.cloned.1.call-start = ((), (), s32[]{:S(2)}) async-start(), calls=%async_computation.9 | async-start | bytes 18874368 | tf_op jit(solution)/shard_map/all_gather | solution.py:853
  169.7 192.8 %all-gather.4.cloned.1.call-start = ((), (), s32[]{:S(2)}) async-start(), calls=%async_computation.8 | async-start | bytes 18874368 | tf_op jit(solution)/shard_map/all_gather | solution.py:872
  266.9 452.8 %reduce-scatter.7.cloned.1.call-start = ((), (), s32[]{:S(2)}) async-start(), calls=%async_computation.10 | async-start | bytes 10485760 | tf_op jit(solution)/shard_map/reduce_scatter | solution.py:913
  504.7 355.7 %reduce-scatter.9.cloned.1.call-start = ((), (), s32[]{:S(2)}) async-start(), calls=%async_computation.11 | async-start | bytes 3932160 | tf_op jit(solution)/shard_map/reduce_scatter | solution.py:913
  660.8 758.9 %reduce-scatter.13.cloned.1.call-start = ((), (), s32[]{:S(2)}) async-start(), calls=%async_computation.13 | async-start | bytes 3932160 | tf_op jit(solution)/shard_map/reduce_scatter | solution.py:913
  717.3 108.1 %collective-permute-start.7 = (bf16[4,128,2048]{2,1,0:T(8,128)(2,1)}, bf16[4,128,2048]{2,1,0:T(8,128)(2,1)}, u32[]{:S(2)}, u32[]{:S(2)}) collective-permute-start(bf16[4,128,2048]{2,1,0:T(8,128)(2,1)} %pad_maximum_fusion.6), channel_id=1, source_target_pairs={{0,2},{2,0},{1,3},{3,1},{4,6},{6,4},{5,7},{7,5},{8,10},{10,8},{9,1... | collective-permute-start | bytes 6291464 | tf_op jit(solution)/shard_map/ppermute | solution.py:39
  719.2 106.2 %collective-permute-start.5 = (bf16[4,128,2048]{2,1,0:T(8,128)(2,1)}, bf16[4,128,2048]{2,1,0:T(8,128)(2,1)}, u32[]{:S(2)}, u32[]{:S(2)}) collective-permute-start(bf16[4,128,2048]{2,1,0:T(8,128)(2,1)} %pad_maximum_fusion.5), channel_id=1, source_target_pairs={{0,16},{16,0},{1,17},{17,1},{2,18},{18,2},{3,19},{19,3},{4,20},{20... | collective-permute-start | bytes 6291464 | tf_op jit(solution)/shard_map/ppermute | solution.py:39
  825.3 594.4 %reduce-scatter.11.cloned.1.call-start = ((), (), s32[]{:S(2)}) async-start(), calls=%async_computation.12 | async-start | bytes 10485760 | tf_op jit(solution)/shard_map/reduce_scatter | solution.py:913
  838.9 585.7 %reduce-scatter.17.cloned.1.call-start = ((), (), s32[]{:S(2)}) async-start(), calls=%async_computation.15 | async-start | bytes 3932160 | tf_op jit(solution)/shard_map/reduce_scatter | solution.py:913
  880.8 266.1 %collective-permute-start.9 = (bf16[2,2,4,128,2048]{4,3,2,1,0:T(8,128)(2,1)}, bf16[2,2,4,128,2048]{4,3,2,1,0:T(8,128)(2,1)}, u32[]{:S(2)}, u32[]{:S(2)}) collective-permute-start(bf16[2,2,4,128,2048]{4,3,2,1,0:T(8,128)(2,1)} %slice_bitcast_fusion), channel_id=1, source_target_pairs={{0,1},{1,0},{2,3},{3,2},{4,5},{5,4},{6,7},{7,6},{8,9},{9,8},{10,11... | collective-permute-start | bytes 25165832 | tf_op jit(solution)/shard_map/ppermute | solution.py:39
  985.0 439.5 %reduce-scatter.15.cloned.1.call-start = ((), (), s32[]{:S(2)}) async-start(), calls=%async_computation.14 | async-start | bytes 10485760 | tf_op jit(solution)/shard_map/reduce_scatter | solution.py:913
  1007.7 136.4 %collective-permute-start.26 = (bf16[2,4,1,128,1536]{4,3,1,2,0:T(8,128)(2,1)}, bf16[2,4,1,128,1536]{4,3,1,2,0:T(8,128)(2,1)}, u32[]{:S(2)}, u32[]{:S(2)}) collective-permute-start(bf16[2,4,1,128,1536]{4,3,1,2,0:T(8,128)(2,1)} %dynamic-slice_bitcast_fusion), channel_id=1, source_target_pairs={{0,2},{2,0},{1,3},{3,1},{4,6},{6,4},{5,7},{7,5},{8,10},{10,8},{9,1... | collective-permute-start | bytes 9437192 | tf_op jit(solution)/shard_map/ppermute | solution.py:39
  1020.6 73.0 %collective-permute-start.33 = (bf16[4,1,128,512]{3,2,0,1:T(8,128)(2,1)S(1)}, bf16[4,1,128,512]{3,2,0,1:T(8,128)(2,1)S(1)}, u32[]{:S(2)}, u32[]{:S(2)}) collective-permute-start(bf16[4,1,128,512]{3,2,0,1:T(8,128)(2,1)S(1)} %dynamic-slice_bitcast_fusion.6), channel_id=1, source_target_pairs={{0,2},{2,0},{1,3},{3,1},{4,6},{6,4},{5,7},{7,5},{8,10},{10,8},{9,1... | collective-permute-start | bytes 1572872 | tf_op jit(solution)/shard_map/ppermute | solution.py:39
  1101.3 69.2 %collective-permute-start.24 = (bf16[4,1,2,128,1536]{4,3,0,2,1:T(8,128)(2,1)}, bf16[4,1,2,128,1536]{4,3,0,2,1:T(8,128)(2,1)}, u32[]{:S(2)}, u32[]{:S(2)}) collective-permute-start(bf16[4,1,2,128,1536]{4,3,0,2,1:T(8,128)(2,1)} %bitcast.320), channel_id=1, source_target_pairs={{0,16},{16,0},{1,17},{17,1},{2,18},{18,2},{3,19},{19,3},{4,20},{20... | collective-permute-start | bytes 9437192 | tf_op jit(solution)/shard_map/ppermute | solution.py:39
  1130.8 99.8 %collective-permute-start.19 = (bf16[4,128,2048]{2,1,0:T(8,128)(2,1)}, bf16[4,128,2048]{2,1,0:T(8,128)(2,1)}, u32[]{:S(2)}, u32[]{:S(2)}) collective-permute-start(bf16[4,128,2048]{2,1,0:T(8,128)(2,1)} %constant_dynamic-slice_fusion.14), channel_id=1, source_target_pairs={{0,1},{1,0},{2,3},{3,2},{4,5},{5,4},{6,7},{7,6},{8,9},{9,8},{10,11... | collective-permute-start | bytes 6291464 | tf_op jit(solution)/shard_map/ppermute | solution.py:39
  1132.6 63.1 %collective-permute-start.39 = (bf16[1,64,1,1,1024]{4,3,1,2,0:T(2,128)(2,1)S(1)}, bf16[1,64,1,1,1024]{4,3,1,2,0:T(2,128)(2,1)S(1)}, u32[]{:S(2)}, u32[]{:S(2)}) collective-permute-start(bf16[1,64,1,1,1024]{4,3,1,2,0:T(2,128)(2,1)S(1)} %copy.206), channel_id=1, source_target_pairs={{0,1},{1,0},{2,3},{3,2},{4,5},{5,4},{6,7},{7,6},{8,9},{9,8},{10,11... | collective-permute-start | bytes 393224 | tf_op jit(solution)/shard_map/ppermute | solution.py:39
  1195.4 75.6 %collective-permute-start.13 = (bf16[4,128,2048]{2,1,0:T(8,128)(2,1)S(1)}, bf16[4,128,2048]{2,1,0:T(8,128)(2,1)}, u32[]{:S(2)}, u32[]{:S(2)}) collective-permute-start(bf16[4,128,2048]{2,1,0:T(8,128)(2,1)S(1)} %pad_maximum_fusion.8), channel_id=1, source_target_pairs={{0,2},{2,0},{1,3},{3,1},{4,6},{6,4},{5,7},{7,5},{8,10},{10,8},{9,1... | collective-permute-start | bytes 6291464 | tf_op jit(solution)/shard_map/ppermute | solution.py:39
  1195.7 75.9 %collective-permute-start.11 = (bf16[4,128,2048]{2,1,0:T(8,128)(2,1)S(1)}, bf16[4,128,2048]{2,1,0:T(8,128)(2,1)}, u32[]{:S(2)}, u32[]{:S(2)}) collective-permute-start(bf16[4,128,2048]{2,1,0:T(8,128)(2,1)S(1)} %pad_maximum_fusion.7), channel_id=1, source_target_pairs={{0,16},{16,0},{1,17},{17,1},{2,18},{18,2},{3,19},{19,3},{4,20},{20... | collective-permute-start | bytes 6291464 | tf_op jit(solution)/shard_map/ppermute | solution.py:39
  1229.4 58.6 %collective-permute-start.29 = (bf16[1,128,3072]{2,1,0:T(8,128)(2,1)}, bf16[1,128,3072]{2,1,0:T(8,128)(2,1)}, u32[]{:S(2)}, u32[]{:S(2)}) collective-permute-start(bf16[1,128,3072]{2,1,0:T(8,128)(2,1)} %get-tuple-element.178), channel_id=1, source_target_pairs={{0,8},{4,12},{8,0},{12,4},{1,9},{5,13},{9,1},{13,5},{2,10},{6,14},... | collective-permute-start | bytes 2359304 | tf_op jit(solution)/shard_map/ppermute | solution.py:86
  1286.7 58.4 %collective-permute-start.21 = (bf16[128,2048]{1,0:T(8,128)(2,1)}, bf16[128,2048]{1,0:T(8,128)(2,1)}, u32[]{:S(2)}, u32[]{:S(2)}) collective-permute-start(bf16[128,2048]{1,0:T(8,128)(2,1)} %get-tuple-element.193), channel_id=1, source_target_pairs={{0,8},{4,12},{8,0},{12,4},{1,9},{5,13},{9,1},{13,5},{2,10},{6,14},... | collective-permute-start | bytes 1572872 | tf_op jit(solution)/shard_map/ppermute | solution.py:86
  1287.0 58.1 %collective-permute-start.20 = (bf16[128,2048]{1,0:T(8,128)(2,1)}, bf16[128,2048]{1,0:T(8,128)(2,1)}, u32[]{:S(2)}, u32[]{:S(2)}) collective-permute-start(bf16[128,2048]{1,0:T(8,128)(2,1)} %get-tuple-element.194), channel_id=1, source_target_pairs={{0,4},{4,8},{8,12},{12,0},{1,5},{5,9},{9,13},{13,1},{2,6},{6,10},{... | collective-permute-start | bytes 1572872 | tf_op jit(solution)/shard_map/ppermute | solution.py:86
  1294.4 99.8 %collective-permute-start.31 = (bf16[1,64,3,1,1024]{4,1,3,2,0:T(8,128)(2,1)S(1)}, bf16[1,64,3,1,1024]{4,1,3,2,0:T(8,128)(2,1)S(1)}, u32[]{:S(2)}, u32[]{:S(2)}) collective-permute-start(bf16[1,64,3,1,1024]{4,1,3,2,0:T(8,128)(2,1)S(1)} %copy.203), channel_id=1, source_target_pairs={{0,1},{1,0},{2,3},{3,2},{4,5},{5,4},{6,7},{7,6},{8,9},{9,8},{10,11... | collective-permute-start | bytes 1179656 | tf_op jit(solution)/shard_map/ppermute | solution.py:39
  1298.7 58.1 %collective-permute-start.16 = (bf16[128,2048]{1,0:T(8,128)(2,1)S(1)}, bf16[128,2048]{1,0:T(8,128)(2,1)S(1)}, u32[]{:S(2)}, u32[]{:S(2)}) collective-permute-start(bf16[128,2048]{1,0:T(8,128)(2,1)S(1)} %get-tuple-element.201), channel_id=1, source_target_pairs={{0,12},{4,0},{8,4},{12,8},{1,13},{5,1},{9,5},{13,9},{2,14},{6,2},{... | collective-permute-start | bytes 1572872 | tf_op jit(solution)/shard_map/ppermute | solution.py:86
  1348.3 65.5 %collective-permute-start.23 = (bf16[2,128,2048]{2,1,0:T(8,128)(2,1)}, bf16[2,128,2048]{2,1,0:T(8,128)(2,1)S(1)}, u32[]{:S(2)}, u32[]{:S(2)}) collective-permute-start(bf16[2,128,2048]{2,1,0:T(8,128)(2,1)} %constant_dynamic-slice_fusion.8), channel_id=1, source_target_pairs={{0,1},{1,0},{2,3},{3,2},{4,5},{5,4},{6,7},{7,6},{8,9},{9,8},{10,11... | collective-permute-start | bytes 3145736 | tf_op jit(solution)/shard_map/ppermute | solution.py:39
  (113 other events, 2284.2 us)
Sparse Core Ops, SparseCore 0:
  169.8 96.0 all-gather.5
  267.8 94.6 all-gather.3
  504.9 143.8 reduce-scatter.6
  660.9 59.5 reduce-scatter.8
  722.7 60.2 reduce-scatter.12
  839.0 144.9 reduce-scatter.10
  986.2 60.9 reduce-scatter.16
  1049.6 161.1 reduce-scatter.14

commit v6 on v5

--- a/solution.py
+++ b/solution.py
@@ -102,21 +102,20 @@
     return core_exchange(seq_exchange(a), 0, 1)
 
 
-def plane_scatter(blocks):
-    got = swap(blocks[:, :, 1], "core")
-    held = (blocks[:, :, 0].astype(f32) + got.astype(f32)).astype(bf16)
+def total(*parts):
+    return sum(part.astype(f32) for part in parts)
+
+
+def plane_scatter(blocks, check=lambda stage, *arrays: arrays):
+    held = total(blocks[:, :, 0], swap(blocks[:, :, 1], "core")).astype(bf16)
+    [held] = check(0, held)
     half = blocks.shape[3] // 2
     by_x = swap(held[1, 1, :half], "dp")
     by_y = swap(held[1, 1, half:], "y")
-    to_x = jnp.concatenate(
-        [held[1, 0, :half], (held[1, 0, half:].astype(f32) + by_y.astype(f32)).astype(bf16)], axis=0
-    )
-    to_y = jnp.concatenate(
-        [(held[0, 1, :half].astype(f32) + by_x.astype(f32)).astype(bf16), held[0, 1, half:]], axis=0
-    )
-    from_x = swap(to_x, "dp")
-    from_y = swap(to_y, "y")
-    return held[0, 0].astype(f32) + from_x.astype(f32) + from_y.astype(f32)
+    to_x = jnp.concatenate([held[1, 0, :half], total(held[1, 0, half:], by_y).astype(bf16)], axis=0)
+    to_y = jnp.concatenate([total(held[0, 1, :half], by_x).astype(bf16), held[0, 1, half:]], axis=0)
+    to_x, to_y = check(1, to_x, to_y)
+    return total(held[0, 0], swap(to_x, "dp"), swap(to_y, "y"))
 
 
 MESH = pl.DeviceIdType.MESH
@@ -927,6 +926,7 @@
     [back] = combine(me, left, slot_col, seq_n, piece, right=right)
     gate_a = rows_product(expert_in, after(dgpre_a, back, down_sum_a))
     gate_b = rows_product(expert_in, after(dgpre_b, back))
+    gate_sum_a, gate_sum_b = over_ctx(gate_a), over_ctx(gate_b)
     ypair = expert_down(units_a, units_b, down_one, gate_a)
     mixed_rows, dgate_plane = combine(
         me, ypair.reshape(blocks, cap, width), slot_col, seq_n, piece, row_gate, grad_plane
@@ -955,20 +955,20 @@
     column_start = (r_i * core_n + core_i) * columns
     dbranch_here = lax.dynamic_slice_in_dim(dbranch, column_start, columns, 1)
     dmixed = chip_scatter(product_t(dbranch_here, weight_out).astype(bf16), 1, parts).astype(bf16)
+    stages = {}
+
+    def check(stage, *arrays):
+        stages[stage] = arrays
+        return arrays
+
+    mixture = plane_scatter(after(mixed_rows, dbranch), check)
     dqpre, dkpre, dvpre = attend_back(
-        query, keys, values, mixed, dmixed, cosine, sine, seg_row, seg_col, heads, gate_b, down_sum_b
+        query, keys, values, mixed, dmixed, cosine, sine, seg_row, seg_col, heads, down_sum_b, *stages[0]
     )
     dqkv = jnp.concatenate([dqpre, dkpre, dvpre], axis=1)
-    out_grad = t_product(mixed_full, after(dbranch_here, dqpre))
+    dqkv = after(dqkv, gate_sum_a)
     dhidden_part = product_t(dqkv, weight_in).astype(bf16)
-    in_grad = t_product(hidden_full, after(dqkv, dhidden_part)).astype(bf16)
-    up_b = rows_product(expert_in, after(dupre_b, in_grad))
-    up_a = rows_product(expert_in, after(dupre_a, in_grad))
-
-    grad_down = jnp.concatenate([down_sum_a, down_sum_b], axis=1).astype(f32).T[None]
-    grad_gate = jnp.concatenate([over_ctx(gate_a), over_ctx(gate_b)], axis=1).astype(f32)[None]
-    grad_up = jnp.concatenate([over_ctx(up_a), over_ctx(up_b)], axis=1).astype(f32)[None]
-
+    in_grad = t_product(hidden_full, after(dqkv, dhidden_part, *stages[1])).astype(bf16)
     dhidden_one = chip_scatter(
         dhidden_part.reshape(seq_n, parts * piece, width), 1, parts
     )
@@ -979,35 +979,33 @@
         inverse_one.reshape(home, 1),
         attn_norm,
     )
-    grad_tokens = from_sequences((dtokens + dresid).astype(bf16).reshape(seq_n, piece, width)).astype(f32)
-
-    mixture = plane_scatter(after(mixed_rows, dbranch))
-    output = from_sequences((residual + mixture).astype(bf16))
+    dtokens = (dtokens + dresid).astype(bf16).reshape(seq_n, piece, width)
+    out_grad = t_product(mixed_full, after(dbranch_here, in_grad)).astype(bf16)
+    up_b = rows_product(expert_in, after(dupre_b, out_grad, dtokens))
+    output = (residual + mixture).astype(bf16)
+    up_a = rows_product(expert_in, after(dupre_a, out_grad, output))
+
+    grad_down = jnp.concatenate([down_sum_a, down_sum_b], axis=1).astype(f32).T[None]
+    grad_gate = jnp.concatenate([gate_sum_a, gate_sum_b], axis=1).astype(f32)[None]
+    grad_up = jnp.concatenate([over_ctx(up_a), over_ctx(up_b)], axis=1).astype(f32)[None]
 
     def seen(part):
         return part.reshape(dp_n, seq_n, r_n, y_n, core_n * rows_here, -1)
 
     def half(a, axis, index, name):
         keep, give = pick(a, index, axis), pick(a, 1 - index, axis)
-        return (keep.astype(f32) + swap(give, name).astype(f32)).astype(bf16)
-
-    def over_plane(a, b):
-        a, b = half(seen(a), 0, dp_i, "dp"), half(seen(b), 3, y_i, "y")
-        return half(a, 2, y_i, "y"), half(b, 0, dp_i, "dp")
-
-    def over_seq(a):
-        return sum(piece.astype(f32) for piece in seq_pieces(a)).astype(bf16)
-
-    def to_rows(a):
-        a = a.reshape(parts, rows_here, -1, 1, columns)
-        return chip_exchange(a, 0, 3, parts).reshape(rows_here, -1, width).astype(f32)
-
-    one, two = over_plane(in_grad[:, : 3 * columns // 2], in_grad[:, 3 * columns // 2 :])
-    inward = to_rows(over_seq(jnp.concatenate([one, two], axis=-1)))
-    one, two = over_plane(*jnp.split(out_grad.astype(bf16), 2, axis=1))
-    outward = to_rows(over_seq(jnp.concatenate([one, two], axis=-1)))
-    grad_output = outward[:, 0]
-    grad_query, grad_key, grad_value = (inward[:, i] for i in range(3))
+        return total(keep, swap(give, name)).astype(bf16)
+
+    first = [half(seen(a), 0, dp_i, "dp") for a in (out_grad, in_grad[:, :columns])]
+    first.append(half(seen(in_grad[:, columns:]), 3, y_i, "y"))
+    second = [half(a, 2, y_i, "y") for a in first[:2]] + [half(first[2], 0, dp_i, "dp")]
+    grad_tokens = from_sequences(dtokens)
+    output = from_sequences(output)
+    part = total(*seq_pieces(jnp.concatenate(second, axis=-1))).astype(bf16)
+    part = part.reshape(parts, rows_here, 4, 1, columns)
+    part = chip_exchange(part, 0, 3, parts).reshape(rows_here, 4, width).astype(f32)
+    grad_output, grad_query, grad_key, grad_value = (part[:, i] for i in range(4))
+    grad_tokens = grad_tokens.astype(f32)
 
     gains = jnp.concatenate([attn_norm_grad[None], expert_norm_grad[None], router_grad.T], axis=0)
     gain_n = gains.shape[0]

time: 1440 us -> 1450 us (level)
  starting transfers between devices: 102 us -> 40.2 us
  waiting for transfers between devices: 301 us -> 350 us
    ppermute x12 -> x9, waiting for transfers between devices: 67.2 us -> 203 us  [seq_pieces(): lax.ppermute(give, 'seq', [(i, (i + step) % count) for i in range(count)])]
    ppermute x28 -> x25, waiting for transfers between devices: 182 us -> 102 us  [swap(): return lax.ppermute(a, axis, [(0, 1), (1, 0)])]
    ppermute x12 -> x9, starting transfers between devices: 53.3 us -> 11.2 us  [seq_pieces(): lax.ppermute(give, 'seq', [(i, (i + step) % count) for i in range(count)])]
    ppermute x28 -> x25, starting transfers between devices: 40 us -> 19 us  [swap(): return lax.ppermute(a, axis, [(0, 1), (1, 0)])]
    unnamed x184 -> x157, local copies, waits for them, and re-layouts: 40.6 us -> 34.1 us
    convert_element_type x19 -> x15, other arithmetic: 45.1 us -> 51.1 us  [the longest x2 16 us: plane_scatter(): held = total(blocks[:, :, 0], swap(blocks[:, :, 1], 'core')).astype(bf16)]
  transfers between devices with their start and end apart: 50 -> 44, of which waited for: 21 -> 16; matrix products, arithmetic and copies ran while one was open for 26% -> 28% of each run, Pallas kernels for 18% -> 18%
where the time goes in v6:
time: 1450 us; the launch traced here: 1440 us
  Pallas kernels  530 us (37%)
  waiting for transfers between devices  350 us (24%)
  matrix products  222 us (15%)
  other arithmetic  127 us (9%)
  local copies, waits for them, and re-layouts  114 us (8%)
  blocking collectives  45 us (3%)
  starting transfers between devices  40.2 us (3%)
  between operations  15.6 us (1%)
    ppermute x9, waiting for transfers between devices, seq_pieces(): lax.ppermute(give, 'seq', [(i, (i + step) % count) for i in range(count)])  203 us
    pallas_call x1, Pallas kernels, first_transfers(): pl.pallas_call(first_kernel, in_specs=[held] * 7, out_specs=[held] * 4, o...  162 us
    dot_general x9, matrix products, t_product(): lax.dot_general(a, b, (((0,), (0,)), ((), ())), preferred_element_type=f32)  159 us
    pallas_call x2, Pallas kernels, expert_units(): pl.pallas_call(functools.partial(units_kernel, chunk), grid=(units // til...  125 us
    ppermute x25, waiting for transfers between devices, swap(): return lax.ppermute(a, axis, [(0, 1), (1, 0)])  102 us
    pallas_call x2, Pallas kernels, expert_input_grad(): pl.pallas_call(functools.partial(input_kernel, cut), grid=(width // n, ro...  77.8 us
    all_gather x1, waiting for transfers between devices, on_device(): hidden_plane = lax.all_gather(hidden_two, PLANE, axis=0, tiled=True)  45.2 us
    all_gather x1, blocking collectives, on_device(): lax.all_gather(small, EVERY, axis=0, tiled=True)  45 us
  transfers between devices with their start and end apart: 44, of which 16 were waited for; matrix products, arithmetic and copies ran while one was open for 28% of the time, Pallas kernels for 18%

profile of v6, /device:TPU:1, one launch (start us, length us, event | category | flops | bytes accessed | tf_op | source)
XLA Modules:
  0.0 1443.6 jit_solution(13705959659101333146)
XLA Ops:
  7.2 162.4 %first_transfers.1 = (bf16[2,4,2,128,4096]{4,3,2,1,0:T(8,128)(2,1)}, bf16[4,128,2048]{2,1,0:T(8,128)(2,1)}, bf16[4,128,2048]{2,1,0:T(8,128)(2,1)}, s32[2,2,1024]{2,1,0:T(2,128)}) custom-call(bf16[64,2048]{1,0:T(8,128)(2,1)} %query.1, bf16[64,2048]{1,0:T(8,128)(2,1)} %key.1, bf16[64,2048]{1,0:T(8,128)(2,1)} %value.1, bf16[64,2048]{1,0:T(8,128)(2,1)} %output.1, ...), custom_call_target="tpu_custom_call" | custom-call | bytes 16777216 | tf_op jit(solution)/shard_map/first_transfers/pallas_call | solution.py:360
  183.7 20.0 %fusion.4.qp.kp.vp = f32[1024,3072]{1,0:T(8,128)} fusion(bf16[1024,2048]{1,0:T(8,128)(2,1)S(1)} %bitcast.327, bf16[2048,4096]{1,0:T(8,128)(2,1)} %bitcast.345), kind=kOutput, calls=%fused_computation.7 | convolution fusion | flops 12884901888 | bytes 29360128 | tf_op jit(solution)/shard_map/dot_general | solution.py:27
  203.8 27.9 %attend.1 = (bf16[1024,1024]{1,0:T(8,128)(2,1)S(1)}, bf16[1024,1024]{1,0:T(8,128)(2,1)S(1)}, bf16[1024,1024]{1,0:T(8,128)(2,1)}, bf16[1024,1024]{1,0:T(8,128)(2,1)}) custom-call(f32[1024,3072]{1,0:T(8,128)} %fusion.4.qp.kp.vp, f32[1024,3072]{1,0:T(8,128)} %fusion.4.qp.kp.vp, f32[1024,3072]{1,0:T(8,128)} %fusion.4.qp.kp.vp, ...), custom_call_target="tpu_custom_call" | custom-call | flops 2684354560 | bytes 20971520 | tf_op jit(solution)/shard_map/attend/pallas_call | solution.py:426
  268.0 45.0 %all-gather = s32[32,4,256]{2,1,0:T(4,128)S(1)} all-gather(s32[1,4,256]{2,1,0:T(4,128)} %bitcast.337), channel_id=1, replica_groups=mesh['dp'=2,'seq'=4,'r'=1,'y'=2,'core'=2] {'dp','seq','r','y','core'}, dimensions={0}, use_global_device_ids=true | all-gather | bytes 135168 | tf_op jit(solution)/shard_map/all_gather | solution.py:873
  317.2 45.2 %all-gather.4.cloned.1.call-done = bf16[4096,2048]{1,0:T(8,128)(2,1)} async-done(((bf16[512,2048]{1,0:T(8,128)(2,1)}), bf16[4096,2048]{1,0:T(8,128)(2,1)}) %all-gather.4.cloned.1.call-update) | async-done | bytes 16777232 | tf_op jit(solution)/shard_map/all_gather | solution.py:871
  362.4 26.3 %dispatch.1 = (bf16[16,160,2048]{2,1,0:T(8,128)(2,1)}, bf16[16,160,2048]{2,1,0:T(8,128)(2,1)}, f32[16,256,1]{2,1,0:T(8,128)S(1)}) custom-call(s32[4]{0:T(128)S(1)} %pad_add_fusion.me, bf16[4,2,4,128,2048]{4,3,2,1,0:T(8,128)(2,1)} %bitcast.319, bf16[4,2,4,128,2048]{4,3,2,1,0:T(8,128)(2,1)} %bitcast.300, s32[16,1,256]{2,1,0:T(1,128)S(1)} %broadcast_in_dim.45.slot, ...), custom_call_target="tpu_custom_call" | custom-call | flops 7516192768 | bytes 54525952 | tf_op jit(solution)/shard_map/dispatch/pallas_call | solution.py:609
  390.1 85.9 %expert_units.2 = (bf16[2560,2048]{1,0:T(8,128)(2,1)}, bf16[2560,2048]{1,0:T(8,128)(2,1)}, bf16[2560,2048]{1,0:T(8,128)(2,1)}) custom-call(bf16[2560,2048]{1,0:T(8,128)(2,1)} %bitcast.360, bf16[2560,2048]{1,0:T(8,128)(2,1)} %bitcast.366, bf16[2048,2816]{1,0:T(8,128)(2,1)} %bitcast.349, bf16[2048,2816]{1,0:T(8,128)(2,1)} %bitcast.353, ...), custom_call_target="tpu_custom_call" | custom-call | flops 64424509440 | bytes 77594624 | tf_op jit(solution)/shard_map/expert_units/pallas_call | solution.py:530
  475.9 28.9 %convolution_convert_fusion.3.rest_0_ = bf16[2048,2048]{1,0:T(8,128)(2,1)} fusion(bf16[2560,2048]{1,0:T(8,128)(2,1)} %bitcast.367, bf16[2560,2048]{1,0:T(8,128)(2,1)} %get-tuple-element.41.units_a), kind=kOutput, calls=%fused_computation.17 | convolution fusion | flops 21479030784 | bytes 29360128 | tf_op jit(solution)/shard_map/dot_general | solution.py:35
  504.9 39.6 %expert_units.3 = (bf16[2560,768]{1,0:T(8,128)(2,1)}, bf16[2560,768]{1,0:T(8,128)(2,1)}, bf16[2560,768]{1,0:T(8,128)(2,1)}) custom-call(bf16[2560,2048]{1,0:T(8,128)(2,1)} %bitcast.361, bf16[2560,2048]{1,0:T(8,128)(2,1)} %bitcast.368, bf16[2048,2816]{1,0:T(8,128)(2,1)} %bitcast.350, bf16[2048,2816]{1,0:T(8,128)(2,1)} %bitcast.354, ...), custom_call_target="tpu_custom_call" | custom-call | flops 24159191040 | bytes 42205184 | tf_op jit(solution)/shard_map/expert_units/pallas_call | solution.py:530
  558.1 38.8 %expert_input_grad.2.rest_0_ = bf16[2560,1024]{1,0:T(8,128)(2,1)} custom-call(bf16[2560,2048]{1,0:T(8,128)(2,1)} %get-tuple-element.43.dgate_a.refs_0_, bf16[2560,768]{1,0:T(8,128)(2,1)} %get-tuple-element.44.dgate_b.refs_0_, bf16[2560,2048]{1,0:T(8,128)(2,1)} %get-tuple-element.45.dup_a.refs_0_, bf16[2560,768]{1,0:T(8,128)(2,1)} %get-tuple-element.46.dup_b.refs_0_, ...), custom_call_target="tpu_custom_call" | custom-call | flops 29527900160 | bytes 45613056 | tf_op jit(solution)/shard_map/expert_input_grad/pallas_call | solution.py:744
  597.0 39.0 %expert_input_grad.3 = bf16[2560,1024]{1,0:T(8,128)(2,1)} custom-call(bf16[2560,2048]{1,0:T(8,128)(2,1)} %get-tuple-element.43.dgate_a.refs_0_, bf16[2560,768]{1,0:T(8,128)(2,1)} %get-tuple-element.44.dgate_b.refs_0_, bf16[2560,2048]{1,0:T(8,128)(2,1)} %get-tuple-element.45.dup_a.refs_0_, bf16[2560,768]{1,0:T(8,128)(2,1)} %get-tuple-element.46.dup_b.refs_0_, ...), custom_call_target="tpu_custom_call" | custom-call | flops 29527900160 | bytes 45613056 | tf_op jit(solution)/shard_map/expert_input_grad/pallas_call | solution.py:744
  690.4 20.0 %collective-permute-done.6 = bf16[2,128,2048]{2,1,0:T(8,128)(2,1)} collective-permute-done((bf16[2,128,2048]{2,1,0:T(8,128)(2,1)}, bf16[2,128,2048]{2,1,0:T(8,128)(2,1)}, u32[]{:S(2)}, u32[]{:S(2)}) %collective-permute-start.6) | collective-permute-done | bytes 1048608 | tf_op jit(solution)/shard_map/ppermute | solution.py:39
  718.4 28.9 %convolution_convert_fusion.2.rest_0_ = bf16[2048,2048]{1,0:T(8,128)(2,1)} fusion(bf16[2560,2048]{1,0:T(8,128)(2,1)} %bitcast.362, bf16[2560,2048]{1,0:T(8,128)(2,1)} %after.10), kind=kOutput, calls=%fused_computation.16 | convolution fusion | flops 21479030784 | bytes 29360128 | tf_op jit(solution)/shard_map/dot_general | solution.py:35
  749.5 40.8 %expert_down.1 = bf16[2560,2048]{1,0:T(8,128)(2,1)} custom-call(bf16[2560,2048]{1,0:T(8,128)(2,1)} %get-tuple-element.41.units_a, bf16[2560,768]{1,0:T(8,128)(2,1)S(1)} %copy-done.18, bf16[2816,2048]{1,0:T(8,128)(2,1)} %bitcast.359, bf16[2048,2048]{1,0:T(8,128)(2,1)} %convolution_convert_fusion.2.rest_0_), custom_call_target="tpu_custom_call" | custom-call | flops 29527900160 | bytes 36438016 | tf_op jit(solution)/shard_map/expert_down/pallas_call | solution.py:708
  790.3 24.2 %combine.1 = (bf16[2,2,2,4,128,2048]{5,4,3,2,1,0:T(8,128)(2,1)}, f32[16,256,1]{2,1,0:T(8,128)S(1)}) custom-call(s32[4]{0:T(128)S(1)} %pad_add_fusion.me, bf16[16,160,2048]{2,1,0:T(8,128)(2,1)} %bitcast.320, s32[16,256,1]{2,1,0:T(8,128)S(1)} %copy-done, f32[16,256,1]{2,1,0:T(8,128)S(1)} %copy-done.10, bf16[4,2,4,128,2048]{4,3,2,1,0:T(8,128)(2,1)} %bitcast.301), custom_call_target="tpu_custom_call" | custom-call | flops 2684354560 | bytes 44040192 | tf_op jit(solution)/shard_map/combine/pallas_call | solution.py:683
  900.8 31.8 %attend_back.1 = (bf16[1024,1024]{1,0:T(8,128)(2,1)S(1)}, bf16[1024,1024]{1,0:T(8,128)(2,1)}, bf16[1024,1024]{1,0:T(8,128)(2,1)}) custom-call(bf16[1024,1024]{1,0:T(8,128)(2,1)} %copy-done.16, bf16[1024,1024]{1,0:T(8,128)(2,1)} %copy-done.17, bf16[1024,1024]{1,0:T(8,128)(2,1)} %get-tuple-element.52.v, bf16[1024,1024]{1,0:T(8,128)(2,1)} %get-tuple-element.37.mixed, ...), custom_call_target="tpu_custom_call" | custom-call | flops 6710886400 | bytes 16777216 | tf_op jit(solution)/shard_map/attend_back/pallas_call | solution.py:486
  943.7 19.3 %fusion.24.refs_1_ = bf16[1024,2048]{1,0:T(8,128)(2,1)} fusion(bf16[1024,3072]{1,0:T(8,128)(2,1)} %after.12.refs_0_, bf16[2048,4096]{1,0:T(8,128)(2,1)} %bitcast.348), kind=kOutput, calls=%fused_computation.64 | convolution fusion | flops 12886999040 | bytes 23068672 | tf_op jit(solution)/shard_map/dot_general | solution.py:31
  967.5 18.9 %convolution_convert_fusion.refs_1_ = bf16[2048,3072]{1,0:T(8,128)(2,1)} fusion(bf16[1024,2048]{1,0:T(8,128)(2,1)S(1)} %bitcast.328, bf16[1024,3072]{1,0:T(8,128)(2,1)} %after.13), kind=kOutput, calls=%fused_computation.4 | convolution fusion | flops 12891193344 | bytes 23068672 | tf_op jit(solution)/shard_map/dot_general | solution.py:35
  1023.1 29.0 %convolution_convert_fusion.1 = bf16[2048,2048]{1,0:T(8,128)(2,1)} fusion(bf16[2560,2048]{1,0:T(8,128)(2,1)} %bitcast.365, bf16[2560,2048]{1,0:T(8,128)(2,1)} %after.16), kind=kOutput, calls=%fused_computation.15 | convolution fusion | flops 21479030784 | bytes 29360128 | tf_op jit(solution)/shard_map/dot_general | solution.py:35
  1124.8 39.9 %collective-permute-done.24 = bf16[4,1,2,128,1024]{4,3,0,2,1:T(8,128)(2,1)} collective-permute-done((bf16[4,1,2,128,1024]{4,3,0,2,1:T(8,128)(2,1)}, bf16[4,1,2,128,1024]{4,3,0,2,1:T(8,128)(2,1)}, u32[]{:S(2)}, u32[]{:S(2)}) %collective-permute-start.24) | collective-permute-done | bytes 2097184 | tf_op jit(solution)/shard_map/ppermute | solution.py:39
  1171.5 25.0 %collective-permute-done.21 = bf16[128,2048]{1,0:T(8,128)(2,1)S(1)} collective-permute-done((bf16[128,2048]{1,0:T(8,128)(2,1)S(1)}, bf16[128,2048]{1,0:T(8,128)(2,1)S(1)}, u32[]{:S(2)}, u32[]{:S(2)}) %collective-permute-start.21) | collective-permute-done | bytes 524320 | tf_op jit(solution)/shard_map/ppermute | solution.py:86
  1212.6 90.5 %collective-permute-done.15 = bf16[128,2048]{1,0:T(8,128)(2,1)} collective-permute-done((bf16[128,2048]{1,0:T(8,128)(2,1)}, bf16[128,2048]{1,0:T(8,128)(2,1)}, u32[]{:S(2)}, u32[]{:S(2)}) %collective-permute-start.15) | collective-permute-done | bytes 524320 | tf_op jit(solution)/shard_map/ppermute | solution.py:86
  1340.1 20.9 %collective-permute-done.32 = bf16[1,128,4096]{2,1,0:T(8,128)(2,1)} collective-permute-done((bf16[1,128,4096]{2,1,0:T(8,128)(2,1)}, bf16[1,128,4096]{2,1,0:T(8,128)(2,1)}, u32[]{:S(2)}, u32[]{:S(2)}) %collective-permute-start.32) | collective-permute-done | bytes 1048608 | tf_op jit(solution)/shard_map/ppermute | solution.py:86
  1361.0 49.7 %collective-permute-done.31 = bf16[1,128,4096]{2,1,0:T(8,128)(2,1)} collective-permute-done((bf16[1,128,4096]{2,1,0:T(8,128)(2,1)}, bf16[1,128,4096]{2,1,0:T(8,128)(2,1)}, u32[]{:S(2)}, u32[]{:S(2)}) %collective-permute-start.31) | collective-permute-done | bytes 1048608 | tf_op jit(solution)/shard_map/ppermute | solution.py:86
  (386 shorter events, 430.2 us)
Async XLA Ops:
  7.2 310.1 %all-gather.6.cloned.1.call-start = ((), (), s32[]{:S(2)}) async-start(), calls=%async_computation.9 | async-start | bytes 18874368 | tf_op jit(solution)/shard_map/all_gather | solution.py:852
  169.7 192.7 %all-gather.4.cloned.1.call-start = ((), (), s32[]{:S(2)}) async-start(), calls=%async_computation.8 | async-start | bytes 18874368 | tf_op jit(solution)/shard_map/all_gather | solution.py:871
  266.8 451.6 %reduce-scatter.7.cloned.1.call-start = ((), (), s32[]{:S(2)}) async-start(), calls=%async_computation.10 | async-start | bytes 10485760 | tf_op jit(solution)/shard_map/reduce_scatter | solution.py:912
  504.8 394.8 %reduce-scatter.9.cloned.1.call-start = ((), (), s32[]{:S(2)}) async-start(), calls=%async_computation.11 | async-start | bytes 3932160 | tf_op jit(solution)/shard_map/reduce_scatter | solution.py:912
  660.3 283.3 %reduce-scatter.11.cloned.1.call-start = ((), (), s32[]{:S(2)}) async-start(), calls=%async_computation.12 | async-start | bytes 10485760 | tf_op jit(solution)/shard_map/reduce_scatter | solution.py:912
  715.9 108.6 %collective-permute-start.7 = (bf16[4,128,2048]{2,1,0:T(8,128)(2,1)}, bf16[4,128,2048]{2,1,0:T(8,128)(2,1)}, u32[]{:S(2)}, u32[]{:S(2)}) collective-permute-start(bf16[4,128,2048]{2,1,0:T(8,128)(2,1)} %pad_maximum_fusion.8), channel_id=1, source_target_pairs={{0,2},{2,0},{1,3},{3,1},{4,6},{6,4},{5,7},{7,5},{8,10},{10,8},{9,1... | collective-permute-start | bytes 6291464 | tf_op jit(solution)/shard_map/ppermute | solution.py:39
  717.9 106.6 %collective-permute-start.5 = (bf16[4,128,2048]{2,1,0:T(8,128)(2,1)}, bf16[4,128,2048]{2,1,0:T(8,128)(2,1)}, u32[]{:S(2)}, u32[]{:S(2)}) collective-permute-start(bf16[4,128,2048]{2,1,0:T(8,128)(2,1)} %pad_maximum_fusion.7), channel_id=1, source_target_pairs={{0,16},{16,0},{1,17},{17,1},{2,18},{18,2},{3,19},{19,3},{4,20},{20... | collective-permute-start | bytes 6291464 | tf_op jit(solution)/shard_map/ppermute | solution.py:39
  824.1 492.8 %reduce-scatter.13.cloned.1.call-start = ((), (), s32[]{:S(2)}) async-start(), calls=%async_computation.13 | async-start | bytes 3932160 | tf_op jit(solution)/shard_map/reduce_scatter | solution.py:912
  880.7 551.0 %reduce-scatter.17.cloned.1.call-start = ((), (), s32[]{:S(2)}) async-start(), calls=%async_computation.15 | async-start | bytes 3932160 | tf_op jit(solution)/shard_map/reduce_scatter | solution.py:912
  941.4 54.6 %collective-permute-start.13 = (bf16[4,128,2048]{2,1,0:T(8,128)(2,1)S(1)}, bf16[4,128,2048]{2,1,0:T(8,128)(2,1)}, u32[]{:S(2)}, u32[]{:S(2)}) collective-permute-start(bf16[4,128,2048]{2,1,0:T(8,128)(2,1)S(1)} %pad_maximum_fusion.10.refs_3_), channel_id=1, source_target_pairs={{0,2},{2,0},{1,3},{3,1},{4,6},{6,4},{5,7},{7,5},{8,10},{10,8},{9,1... | collective-permute-start | bytes 6291464 | tf_op jit(solution)/shard_map/ppermute | solution.py:39
  943.5 52.6 %collective-permute-start.11 = (bf16[4,128,2048]{2,1,0:T(8,128)(2,1)}, bf16[4,128,2048]{2,1,0:T(8,128)(2,1)}, u32[]{:S(2)}, u32[]{:S(2)}) collective-permute-start(bf16[4,128,2048]{2,1,0:T(8,128)(2,1)} %pad_maximum_fusion.9.refs_2_), channel_id=1, source_target_pairs={{0,16},{16,0},{1,17},{17,1},{2,18},{18,2},{3,19},{19,3},{4,20},{20... | collective-permute-start | bytes 6291464 | tf_op jit(solution)/shard_map/ppermute | solution.py:39
  1023.1 408.6 %reduce-scatter.15.cloned.1.call-start = ((), (), s32[]{:S(2)}) async-start(), calls=%async_computation.14 | async-start | bytes 10485760 | tf_op jit(solution)/shard_map/reduce_scatter | solution.py:912
  1065.3 132.9 %collective-permute-start.28 = (bf16[2,4,1,128,2048]{4,3,1,2,0:T(8,128)(2,1)}, bf16[2,4,1,128,2048]{4,3,1,2,0:T(8,128)(2,1)}, u32[]{:S(2)}, u32[]{:S(2)}) collective-permute-start(bf16[2,4,1,128,2048]{4,3,1,2,0:T(8,128)(2,1)} %dynamic-slice_bitcast_fusion), channel_id=1, source_target_pairs={{0,2},{2,0},{1,3},{3,1},{4,6},{6,4},{5,7},{7,5},{8,10},{10,8},{9,1... | collective-permute-start | bytes 12582920 | tf_op jit(solution)/shard_map/ppermute | solution.py:39
  1076.9 87.7 %collective-permute-start.24 = (bf16[4,1,2,128,1024]{4,3,0,2,1:T(8,128)(2,1)}, bf16[4,1,2,128,1024]{4,3,0,2,1:T(8,128)(2,1)}, u32[]{:S(2)}, u32[]{:S(2)}) collective-permute-start(bf16[4,1,2,128,1024]{4,3,0,2,1:T(8,128)(2,1)} %bitcast.296), channel_id=1, source_target_pairs={{0,16},{16,0},{1,17},{17,1},{2,18},{18,2},{3,19},{19,3},{4,20},{20... | collective-permute-start | bytes 6291464 | tf_op jit(solution)/shard_map/ppermute | solution.py:39
  1095.6 226.2 %all-to-all-start.1 = ((f32[32,1,384]{2,1,0:T(1,128)}), f32[32,1,384]{2,1,0:T(1,128)S(1)}, u32[]{:S(2)}, u32[]{:S(2)}) async-start(f32[32,1,384]{2,1,0:T(1,128)} %reshape.491), calls=%async_computation.4 | async-start | bytes 98304 | tf_op jit(solution)/shard_map/all_to_all | solution.py:1013
  1101.2 70.3 %collective-permute-start.22 = (bf16[128,2048]{1,0:T(8,128)(2,1)S(1)}, bf16[128,2048]{1,0:T(8,128)(2,1)S(1)}, u32[]{:S(2)}, u32[]{:S(2)}) collective-permute-start(bf16[128,2048]{1,0:T(8,128)(2,1)S(1)} %get-tuple-element.192), channel_id=1, source_target_pairs={{0,12},{4,0},{8,4},{12,8},{1,13},{5,1},{9,5},{13,9},{2,14},{6,2},{... | collective-permute-start | bytes 1572872 | tf_op jit(solution)/shard_map/ppermute | solution.py:86
  1104.6 92.0 %collective-permute-start.21 = (bf16[128,2048]{1,0:T(8,128)(2,1)S(1)}, bf16[128,2048]{1,0:T(8,128)(2,1)S(1)}, u32[]{:S(2)}, u32[]{:S(2)}) collective-permute-start(bf16[128,2048]{1,0:T(8,128)(2,1)S(1)} %get-tuple-element.193), channel_id=1, source_target_pairs={{0,8},{4,12},{8,0},{12,4},{1,9},{5,13},{9,1},{13,5},{2,10},{6,14},... | collective-permute-start | bytes 1572872 | tf_op jit(solution)/shard_map/ppermute | solution.py:86
  1119.7 76.8 %collective-permute-start.20 = (bf16[128,2048]{1,0:T(8,128)(2,1)S(1)}, bf16[128,2048]{1,0:T(8,128)(2,1)S(1)}, u32[]{:S(2)}, u32[]{:S(2)}) collective-permute-start(bf16[128,2048]{1,0:T(8,128)(2,1)S(1)} %get-tuple-element.194), channel_id=1, source_target_pairs={{0,4},{4,8},{8,12},{12,0},{1,5},{5,9},{9,13},{13,1},{2,6},{6,10},{... | collective-permute-start | bytes 1572872 | tf_op jit(solution)/shard_map/ppermute | solution.py:86
  1171.5 131.7 %collective-permute-start.15 = (bf16[128,2048]{1,0:T(8,128)(2,1)}, bf16[128,2048]{1,0:T(8,128)(2,1)}, u32[]{:S(2)}, u32[]{:S(2)}) collective-permute-start(bf16[128,2048]{1,0:T(8,128)(2,1)} %get-tuple-element.202), channel_id=1, source_target_pairs={{0,8},{4,12},{8,0},{12,4},{1,9},{5,13},{9,1},{13,5},{2,10},{6,14},... | collective-permute-start | bytes 1572872 | tf_op jit(solution)/shard_map/ppermute | solution.py:86
  1196.5 107.0 %collective-permute-start.14 = (bf16[128,2048]{1,0:T(8,128)(2,1)S(1)}, bf16[128,2048]{1,0:T(8,128)(2,1)}, u32[]{:S(2)}, u32[]{:S(2)}) collective-permute-start(bf16[128,2048]{1,0:T(8,128)(2,1)S(1)} %get-tuple-element.203), channel_id=1, source_target_pairs={{0,4},{4,8},{8,12},{12,0},{1,5},{5,9},{9,13},{13,1},{2,6},{6,10},{... | collective-permute-start | bytes 1572872 | tf_op jit(solution)/shard_map/ppermute | solution.py:86
  1196.5 109.5 %collective-permute-start.27 = (bf16[4,1,128,1024]{3,2,1,0:T(8,128)(2,1)}, bf16[4,1,128,1024]{3,2,1,0:T(8,128)(2,1)}, u32[]{:S(2)}, u32[]{:S(2)}) collective-permute-start(bf16[4,1,128,1024]{3,2,1,0:T(8,128)(2,1)} %dynamic-slice_bitcast_fusion.6), channel_id=1, source_target_pairs={{0,2},{2,0},{1,3},{3,1},{4,6},{6,4},{5,7},{7,5},{8,10},{10,8},{9,1... | collective-permute-start | bytes 3145736 | tf_op jit(solution)/shard_map/ppermute | solution.py:39
  1204.3 104.2 %collective-permute-start.29 = (bf16[4,1,128,2048]{3,2,1,0:T(8,128)(2,1)S(1)}, bf16[4,1,128,2048]{3,2,1,0:T(8,128)(2,1)S(1)}, u32[]{:S(2)}, u32[]{:S(2)}) collective-permute-start(bf16[4,1,128,2048]{3,2,1,0:T(8,128)(2,1)S(1)} %dynamic-slice_bitcast_fusion.1), channel_id=1, source_target_pairs={{0,16},{16,0},{1,17},{17,1},{2,18},{18,2},{3,19},{19,3},{4,20},{20... | collective-permute-start | bytes 6291464 | tf_op jit(solution)/shard_map/ppermute | solution.py:39
  1211.5 96.6 %collective-permute-start.25 = (bf16[4,1,128,1024]{3,2,1,0:T(8,128)(2,1)S(1)}, bf16[4,1,128,1024]{3,2,1,0:T(8,128)(2,1)S(1)}, u32[]{:S(2)}, u32[]{:S(2)}) collective-permute-start(bf16[4,1,128,1024]{3,2,1,0:T(8,128)(2,1)S(1)} %copy-done.54), channel_id=1, source_target_pairs={{0,2},{2,0},{1,3},{3,1},{4,6},{6,4},{5,7},{7,5},{8,10},{10,8},{9,1... | collective-permute-start | bytes 3145736 | tf_op jit(solution)/shard_map/ppermute | solution.py:39
  1316.9 93.8 %collective-permute-start.31 = (bf16[1,128,4096]{2,1,0:T(8,128)(2,1)}, bf16[1,128,4096]{2,1,0:T(8,128)(2,1)}, u32[]{:S(2)}, u32[]{:S(2)}) collective-permute-start(bf16[1,128,4096]{2,1,0:T(8,128)(2,1)} %get-tuple-element.167), channel_id=1, source_target_pairs={{0,8},{4,12},{8,0},{12,4},{1,9},{5,13},{9,1},{13,5},{2,10},{6,14},... | collective-permute-start | bytes 3145736 | tf_op jit(solution)/shard_map/ppermute | solution.py:86
  (97 other events, 1512.0 us)
Sparse Core Ops, SparseCore 0:
  169.8 96.0 all-gather.5
  267.8 94.6 all-gather.3
  504.9 143.7 reduce-scatter.6
  660.4 59.5 reduce-scatter.8
  747.5 145.8 reduce-scatter.10
  895.6 60.9 reduce-scatter.12
  1023.2 60.3 reduce-scatter.16
  1086.0 228.7 reduce-scatter.14

commit v7 on v6

--- a/solution.py
+++ b/solution.py
@@ -944,7 +944,10 @@
     dsel = gates * (dgate - jnp.sum(gates * dgate, axis=0, keepdims=True))
     dlogits = jnp.sum(jnp.where(hot, dsel[:, :, None], 0.0), axis=0).astype(bf16)
     router_grad = t_product(hidden_two, dlogits)
-    dhidden_two = plane_scatter(back).reshape(home, width) + product_t(dlogits, router)
+    def once_gate(stage, *arrays):
+        return (after(arrays[0], gate_a),) + arrays[1:] if stage == 0 else arrays
+
+    dhidden_two = plane_scatter(back, once_gate).reshape(home, width) + product_t(dlogits, router)
 
     flat_two = normed_two.reshape(home, width)
     dresid, expert_norm_grad = norm_backward(
@@ -962,11 +965,13 @@
         return arrays
 
     mixture = plane_scatter(after(mixed_rows, dbranch), check)
+    up_b = rows_product(expert_in, after(dupre_b, dbranch))
     dqpre, dkpre, dvpre = attend_back(
-        query, keys, values, mixed, dmixed, cosine, sine, seg_row, seg_col, heads, down_sum_b, *stages[0]
+        query, keys, values, mixed, dmixed, cosine, sine, seg_row, seg_col, heads, down_sum_b, up_b, *stages[0]
     )
     dqkv = jnp.concatenate([dqpre, dkpre, dvpre], axis=1)
-    dqkv = after(dqkv, gate_sum_a)
+    up_a = rows_product(expert_in, after(dupre_a, dqpre))
+    dqkv = after(dqkv, up_a)
     dhidden_part = product_t(dqkv, weight_in).astype(bf16)
     in_grad = t_product(hidden_full, after(dqkv, dhidden_part, *stages[1])).astype(bf16)
     dhidden_one = chip_scatter(
@@ -981,9 +986,7 @@
     )
     dtokens = (dtokens + dresid).astype(bf16).reshape(seq_n, piece, width)
     out_grad = t_product(mixed_full, after(dbranch_here, in_grad)).astype(bf16)
-    up_b = rows_product(expert_in, after(dupre_b, out_grad, dtokens))
     output = (residual + mixture).astype(bf16)
-    up_a = rows_product(expert_in, after(dupre_a, out_grad, output))
 
     grad_down = jnp.concatenate([down_sum_a, down_sum_b], axis=1).astype(f32).T[None]
     grad_gate = jnp.concatenate([gate_sum_a, gate_sum_b], axis=1).astype(f32)[None]

time: 1450 us -> 1400 us (0.966); the launches traced: 1440 us -> 1370 us
  waiting for transfers between devices: 350 us -> 273 us
  starting transfers between devices: 40.2 us -> 55.3 us
    ppermute x9, waiting for transfers between devices: 203 us -> 130 us  [seq_pieces(): lax.ppermute(give, 'seq', [(i, (i + step) % count) for i in range(count)])]
    ppermute x9, starting transfers between devices: 11.2 us -> 31.3 us  [seq_pieces(): lax.ppermute(give, 'seq', [(i, (i + step) % count) for i in range(count)])]
    unnamed x157 -> x151, local copies, waits for them, and re-layouts: 34.1 us -> 35 us
  transfers between devices with their start and end apart: 44 -> 44, of which waited for: 16 -> 16; matrix products, arithmetic and copies ran while one was open for 28% -> 29% of each run, Pallas kernels for 18% -> 19%
where the time goes in v7:
time: 1400 us; the launch traced here: 1370 us
  Pallas kernels  529 us (38%)
  waiting for transfers between devices  273 us (20%)
  matrix products  213 us (15%)
  other arithmetic  132 us (9%)
  local copies, waits for them, and re-layouts  110 us (8%)
  starting transfers between devices  55.3 us (4%)
  blocking collectives  44.9 us (3%)
  between operations  15.8 us (1%)
    pallas_call x1, Pallas kernels, first_transfers(): pl.pallas_call(first_kernel, in_specs=[held] * 7, out_specs=[held] * 4, o...  162 us
    dot_general x9, matrix products, t_product(): lax.dot_general(a, b, (((0,), (0,)), ((), ())), preferred_element_type=f32)  154 us
    ppermute x9, waiting for transfers between devices, seq_pieces(): lax.ppermute(give, 'seq', [(i, (i + step) % count) for i in range(count)])  130 us
    pallas_call x2, Pallas kernels, expert_units(): pl.pallas_call(functools.partial(units_kernel, chunk), grid=(units // til...  125 us
    ppermute x25, waiting for transfers between devices, swap(): return lax.ppermute(a, axis, [(0, 1), (1, 0)])  92.4 us
    pallas_call x2, Pallas kernels, expert_input_grad(): pl.pallas_call(functools.partial(input_kernel, cut), grid=(width // n, ro...  77.8 us
    all_gather x1, waiting for transfers between devices, on_device(): hidden_plane = lax.all_gather(hidden_two, PLANE, axis=0, tiled=True)  47.1 us
    all_gather x1, blocking collectives, on_device(): lax.all_gather(small, EVERY, axis=0, tiled=True)  44.9 us
  transfers between devices with their start and end apart: 44, of which 16 were waited for; matrix products, arithmetic and copies ran while one was open for 29% of the time, Pallas kernels for 19%

profile of v7, /device:TPU:1, one launch (start us, length us, event | category | flops | bytes accessed | tf_op | source)
XLA Modules:
  0.0 1374.4 jit_solution(16753136054186163299)
XLA Ops:
  7.2 162.4 %first_transfers.1 = (bf16[2,4,2,128,4096]{4,3,2,1,0:T(8,128)(2,1)}, bf16[4,128,2048]{2,1,0:T(8,128)(2,1)}, bf16[4,128,2048]{2,1,0:T(8,128)(2,1)}, s32[2,2,1024]{2,1,0:T(2,128)}) custom-call(bf16[64,2048]{1,0:T(8,128)(2,1)} %query.1, bf16[64,2048]{1,0:T(8,128)(2,1)} %key.1, bf16[64,2048]{1,0:T(8,128)(2,1)} %value.1, bf16[64,2048]{1,0:T(8,128)(2,1)} %output.1, ...), custom_call_target="tpu_custom_call" | custom-call | bytes 16777216 | tf_op jit(solution)/shard_map/first_transfers/pallas_call | solution.py:360
  183.8 19.9 %fusion.4.qp.kp.vp = f32[1024,3072]{1,0:T(8,128)} fusion(bf16[1024,2048]{1,0:T(8,128)(2,1)S(1)} %bitcast.327, bf16[2048,4096]{1,0:T(8,128)(2,1)} %bitcast.347), kind=kOutput, calls=%fused_computation.7 | convolution fusion | flops 12884901888 | bytes 29360128 | tf_op jit(solution)/shard_map/dot_general | solution.py:27
  203.7 27.9 %attend.1 = (bf16[1024,1024]{1,0:T(8,128)(2,1)S(1)}, bf16[1024,1024]{1,0:T(8,128)(2,1)S(1)}, bf16[1024,1024]{1,0:T(8,128)(2,1)}, bf16[1024,1024]{1,0:T(8,128)(2,1)}) custom-call(f32[1024,3072]{1,0:T(8,128)} %fusion.4.qp.kp.vp, f32[1024,3072]{1,0:T(8,128)} %fusion.4.qp.kp.vp, f32[1024,3072]{1,0:T(8,128)} %fusion.4.qp.kp.vp, ...), custom_call_target="tpu_custom_call" | custom-call | flops 2684354560 | bytes 20971520 | tf_op jit(solution)/shard_map/attend/pallas_call | solution.py:426
  268.3 44.9 %all-gather = s32[32,4,256]{2,1,0:T(4,128)S(1)} all-gather(s32[1,4,256]{2,1,0:T(4,128)} %bitcast.339), channel_id=1, replica_groups=mesh['dp'=2,'seq'=4,'r'=1,'y'=2,'core'=2] {'dp','seq','r','y','core'}, dimensions={0}, use_global_device_ids=true | all-gather | bytes 135168 | tf_op jit(solution)/shard_map/all_gather | solution.py:873
  315.5 47.1 %all-gather.4.cloned.1.call-done = bf16[4096,2048]{1,0:T(8,128)(2,1)} async-done(((bf16[512,2048]{1,0:T(8,128)(2,1)}), bf16[4096,2048]{1,0:T(8,128)(2,1)}) %all-gather.4.cloned.1.call-update) | async-done | bytes 16777232 | tf_op jit(solution)/shard_map/all_gather | solution.py:871
  362.6 26.1 %dispatch.1 = (bf16[16,160,2048]{2,1,0:T(8,128)(2,1)}, bf16[16,160,2048]{2,1,0:T(8,128)(2,1)}, f32[16,256,1]{2,1,0:T(8,128)S(1)}) custom-call(s32[4]{0:T(128)S(1)} %pad_add_fusion.me, bf16[4,2,4,128,2048]{4,3,2,1,0:T(8,128)(2,1)} %bitcast.319, bf16[4,2,4,128,2048]{4,3,2,1,0:T(8,128)(2,1)} %bitcast.302, s32[16,1,256]{2,1,0:T(1,128)S(1)} %broadcast_in_dim.45.slot, ...), custom_call_target="tpu_custom_call" | custom-call | flops 7516192768 | bytes 54525952 | tf_op jit(solution)/shard_map/dispatch/pallas_call | solution.py:609
  390.2 85.9 %expert_units.2 = (bf16[2560,2048]{1,0:T(8,128)(2,1)}, bf16[2560,2048]{1,0:T(8,128)(2,1)}, bf16[2560,2048]{1,0:T(8,128)(2,1)}) custom-call(bf16[2560,2048]{1,0:T(8,128)(2,1)} %bitcast.362, bf16[2560,2048]{1,0:T(8,128)(2,1)} %bitcast.368, bf16[2048,2816]{1,0:T(8,128)(2,1)} %bitcast.351, bf16[2048,2816]{1,0:T(8,128)(2,1)} %bitcast.355, ...), custom_call_target="tpu_custom_call" | custom-call | flops 64424509440 | bytes 77594624 | tf_op jit(solution)/shard_map/expert_units/pallas_call | solution.py:530
  476.1 28.9 %convolution_convert_fusion.3.rest_0_ = bf16[2048,2048]{1,0:T(8,128)(2,1)} fusion(bf16[2560,2048]{1,0:T(8,128)(2,1)} %bitcast.369, bf16[2560,2048]{1,0:T(8,128)(2,1)} %get-tuple-element.41.units_a), kind=kOutput, calls=%fused_computation.17 | convolution fusion | flops 21479030784 | bytes 29360128 | tf_op jit(solution)/shard_map/dot_general | solution.py:35
  505.6 39.6 %expert_units.3 = (bf16[2560,768]{1,0:T(8,128)(2,1)}, bf16[2560,768]{1,0:T(8,128)(2,1)}, bf16[2560,768]{1,0:T(8,128)(2,1)}) custom-call(bf16[2560,2048]{1,0:T(8,128)(2,1)} %bitcast.363, bf16[2560,2048]{1,0:T(8,128)(2,1)} %bitcast.370, bf16[2048,2816]{1,0:T(8,128)(2,1)} %bitcast.352, bf16[2048,2816]{1,0:T(8,128)(2,1)} %bitcast.356, ...), custom_call_target="tpu_custom_call" | custom-call | flops 24159191040 | bytes 42205184 | tf_op jit(solution)/shard_map/expert_units/pallas_call | solution.py:530
  558.8 38.8 %expert_input_grad.2.rest_0_ = bf16[2560,1024]{1,0:T(8,128)(2,1)} custom-call(bf16[2560,2048]{1,0:T(8,128)(2,1)} %get-tuple-element.43.dgate_a.refs_0_, bf16[2560,768]{1,0:T(8,128)(2,1)} %get-tuple-element.44.dgate_b.refs_0_, bf16[2560,2048]{1,0:T(8,128)(2,1)} %get-tuple-element.45.dup_a.refs_0_, bf16[2560,768]{1,0:T(8,128)(2,1)} %get-tuple-element.46.dup_b.refs_0_, ...), custom_call_target="tpu_custom_call" | custom-call | flops 29527900160 | bytes 45613056 | tf_op jit(solution)/shard_map/expert_input_grad/pallas_call | solution.py:744
  597.6 39.0 %expert_input_grad.3 = bf16[2560,1024]{1,0:T(8,128)(2,1)} custom-call(bf16[2560,2048]{1,0:T(8,128)(2,1)} %get-tuple-element.43.dgate_a.refs_0_, bf16[2560,768]{1,0:T(8,128)(2,1)} %get-tuple-element.44.dgate_b.refs_0_, bf16[2560,2048]{1,0:T(8,128)(2,1)} %get-tuple-element.45.dup_a.refs_0_, bf16[2560,768]{1,0:T(8,128)(2,1)} %get-tuple-element.46.dup_b.refs_0_, ...), custom_call_target="tpu_custom_call" | custom-call | flops 29527900160 | bytes 45613056 | tf_op jit(solution)/shard_map/expert_input_grad/pallas_call | solution.py:744
  685.5 28.9 %convolution_convert_fusion.2.rest_0_.refs_1_ = bf16[2048,2048]{1,0:T(8,128)(2,1)} fusion(bf16[2560,2048]{1,0:T(8,128)(2,1)} %bitcast.365, bf16[2560,2048]{1,0:T(8,128)(2,1)} %after.11), kind=kOutput, calls=%fused_computation.16 | convolution fusion | flops 21479030784 | bytes 29360128 | tf_op jit(solution)/shard_map/dot_general | solution.py:35
  722.8 20.7 %collective-permute-done.6 = bf16[2,128,2048]{2,1,0:T(8,128)(2,1)} collective-permute-done((bf16[2,128,2048]{2,1,0:T(8,128)(2,1)}, bf16[2,128,2048]{2,1,0:T(8,128)(2,1)}, u32[]{:S(2)}, u32[]{:S(2)}) %collective-permute-start.6) | collective-permute-done | bytes 1048608 | tf_op jit(solution)/shard_map/ppermute | solution.py:39
  751.1 40.4 %expert_down.1 = bf16[2560,2048]{1,0:T(8,128)(2,1)} custom-call(bf16[2560,2048]{1,0:T(8,128)(2,1)} %get-tuple-element.41.units_a, bf16[2560,768]{1,0:T(8,128)(2,1)S(1)} %copy-done.18, bf16[2816,2048]{1,0:T(8,128)(2,1)} %bitcast.361, bf16[2048,2048]{1,0:T(8,128)(2,1)} %convolution_convert_fusion.2.rest_0_.refs_1_), custom_call_target="tpu_custom_call" | custom-call | flops 29527900160 | bytes 36438016 | tf_op jit(solution)/shard_map/expert_down/pallas_call | solution.py:708
  791.5 24.4 %combine.1 = (bf16[2,2,2,4,128,2048]{5,4,3,2,1,0:T(8,128)(2,1)}, f32[16,256,1]{2,1,0:T(8,128)S(1)}) custom-call(s32[4]{0:T(128)S(1)} %pad_add_fusion.me, bf16[16,160,2048]{2,1,0:T(8,128)(2,1)} %bitcast.320, s32[16,256,1]{2,1,0:T(8,128)S(1)} %copy.186.slot, f32[16,256,1]{2,1,0:T(8,128)S(1)} %copy-done.11, bf16[4,2,4,128,2048]{4,3,2,1,0:T(8,128)(2,1)} %bitcast.303), custom_call_target="tpu_custom_call" | custom-call | flops 2684354560 | bytes 44040192 | tf_op jit(solution)/shard_map/combine/pallas_call | solution.py:683
  912.7 31.8 %attend_back.1 = (bf16[1024,1024]{1,0:T(8,128)(2,1)S(1)}, bf16[1024,1024]{1,0:T(8,128)(2,1)}, bf16[1024,1024]{1,0:T(8,128)(2,1)}) custom-call(bf16[1024,1024]{1,0:T(8,128)(2,1)} %copy-done.16, bf16[1024,1024]{1,0:T(8,128)(2,1)} %copy-done.17, bf16[1024,1024]{1,0:T(8,128)(2,1)} %get-tuple-element.52.v, bf16[1024,1024]{1,0:T(8,128)(2,1)} %get-tuple-element.37.mixed, ...), custom_call_target="tpu_custom_call" | custom-call | flops 6710886400 | bytes 16777216 | tf_op jit(solution)/shard_map/attend_back/pallas_call | solution.py:486
  954.9 26.9 %convolution_convert_fusion.1.refs_1_ = bf16[2048,2048]{1,0:T(8,128)(2,1)} fusion(bf16[2560,2048]{1,0:T(8,128)(2,1)} %bitcast.367, bf16[2560,2048]{1,0:T(8,128)(2,1)S(1)} %copy-done.34), kind=kOutput, calls=%fused_computation.15 | convolution fusion | flops 21479030784 | bytes 29360128 | tf_op jit(solution)/shard_map/dot_general | solution.py:35
  981.8 19.8 %fusion.24.refs_1_ = bf16[1024,2048]{1,0:T(8,128)(2,1)} fusion(bf16[1024,3072]{1,0:T(8,128)(2,1)} %after.16.refs_0_, bf16[2048,4096]{1,0:T(8,128)(2,1)} %bitcast.350), kind=kOutput, calls=%fused_computation.64 | convolution fusion | flops 12886999040 | bytes 23068672 | tf_op jit(solution)/shard_map/dot_general | solution.py:31
  1012.7 19.6 %convolution_convert_fusion.refs_1_ = bf16[2048,3072]{1,0:T(8,128)(2,1)} fusion(bf16[1024,2048]{1,0:T(8,128)(2,1)} %bitcast.328, bf16[1024,3072]{1,0:T(8,128)(2,1)} %after.17), kind=kOutput, calls=%fused_computation.4 | convolution fusion | flops 12891193344 | bytes 23068672 | tf_op jit(solution)/shard_map/dot_general | solution.py:35
  1109.1 39.8 %collective-permute-done.26 = bf16[4,1,2,128,1024]{4,3,0,2,1:T(8,128)(2,1)} collective-permute-done((bf16[4,1,2,128,1024]{4,3,0,2,1:T(8,128)(2,1)}, bf16[4,1,2,128,1024]{4,3,0,2,1:T(8,128)(2,1)}, u32[]{:S(2)}, u32[]{:S(2)}) %collective-permute-start.26) | collective-permute-done | bytes 2097184 | tf_op jit(solution)/shard_map/ppermute | solution.py:39
  1155.7 22.1 %collective-permute-done.21 = bf16[128,2048]{1,0:T(8,128)(2,1)S(1)} collective-permute-done((bf16[128,2048]{1,0:T(8,128)(2,1)S(1)}, bf16[128,2048]{1,0:T(8,128)(2,1)S(1)}, u32[]{:S(2)}, u32[]{:S(2)}) %collective-permute-start.21) | collective-permute-done | bytes 524320 | tf_op jit(solution)/shard_map/ppermute | solution.py:86
  1195.2 41.3 %collective-permute-done.15 = bf16[128,2048]{1,0:T(8,128)(2,1)} collective-permute-done((bf16[128,2048]{1,0:T(8,128)(2,1)}, bf16[128,2048]{1,0:T(8,128)(2,1)}, u32[]{:S(2)}, u32[]{:S(2)}) %collective-permute-start.15) | collective-permute-done | bytes 524320 | tf_op jit(solution)/shard_map/ppermute | solution.py:86
  1287.5 22.5 %collective-permute-done.32 = bf16[1,128,4096]{2,1,0:T(8,128)(2,1)} collective-permute-done((bf16[1,128,4096]{2,1,0:T(8,128)(2,1)}, bf16[1,128,4096]{2,1,0:T(8,128)(2,1)}, u32[]{:S(2)}, u32[]{:S(2)}) %collective-permute-start.32) | collective-permute-done | bytes 1048608 | tf_op jit(solution)/shard_map/ppermute | solution.py:86
  1310.0 31.5 %collective-permute-done.31 = bf16[1,128,4096]{2,1,0:T(8,128)(2,1)} collective-permute-done((bf16[1,128,4096]{2,1,0:T(8,128)(2,1)}, bf16[1,128,4096]{2,1,0:T(8,128)(2,1)}, u32[]{:S(2)}, u32[]{:S(2)}) %collective-permute-start.31) | collective-permute-done | bytes 1048608 | tf_op jit(solution)/shard_map/ppermute | solution.py:86
  (380 shorter events, 428.6 us)
Async XLA Ops:
  7.2 308.3 %all-gather.6.cloned.1.call-start = ((), (), s32[]{:S(2)}) async-start(), calls=%async_computation.9 | async-start | bytes 18874368 | tf_op jit(solution)/shard_map/all_gather | solution.py:852
  169.7 192.9 %all-gather.4.cloned.1.call-start = ((), (), s32[]{:S(2)}) async-start(), calls=%async_computation.8 | async-start | bytes 18874368 | tf_op jit(solution)/shard_map/all_gather | solution.py:871
  267.0 418.5 %reduce-scatter.7.cloned.1.call-start = ((), (), s32[]{:S(2)}) async-start(), calls=%async_computation.10 | async-start | bytes 10485760 | tf_op jit(solution)/shard_map/reduce_scatter | solution.py:912
  504.9 351.0 %reduce-scatter.9.cloned.1.call-start = ((), (), s32[]{:S(2)}) async-start(), calls=%async_computation.11 | async-start | bytes 3932160 | tf_op jit(solution)/shard_map/reduce_scatter | solution.py:912
  660.8 609.4 %reduce-scatter.13.cloned.1.call-start = ((), (), s32[]{:S(2)}) async-start(), calls=%async_computation.13 | async-start | bytes 3932160 | tf_op jit(solution)/shard_map/reduce_scatter | solution.py:912
  674.9 595.3 %reduce-scatter.11.cloned.1.call-start = ((), (), s32[]{:S(2)}) async-start(), calls=%async_computation.12 | async-start | bytes 10485760 | tf_op jit(solution)/shard_map/reduce_scatter | solution.py:912
  749.0 80.2 %collective-permute-start.7 = (bf16[4,128,2048]{2,1,0:T(8,128)(2,1)}, bf16[4,128,2048]{2,1,0:T(8,128)(2,1)}, u32[]{:S(2)}, u32[]{:S(2)}) collective-permute-start(bf16[4,128,2048]{2,1,0:T(8,128)(2,1)} %pad_maximum_fusion.8), channel_id=1, source_target_pairs={{0,2},{2,0},{1,3},{3,1},{4,6},{6,4},{5,7},{7,5},{8,10},{10,8},{9,1... | collective-permute-start | bytes 6291464 | tf_op jit(solution)/shard_map/ppermute | solution.py:39
  750.5 78.7 %collective-permute-start.5 = (bf16[4,128,2048]{2,1,0:T(8,128)(2,1)}, bf16[4,128,2048]{2,1,0:T(8,128)(2,1)}, u32[]{:S(2)}, u32[]{:S(2)}) collective-permute-start(bf16[4,128,2048]{2,1,0:T(8,128)(2,1)} %pad_maximum_fusion.7), channel_id=1, source_target_pairs={{0,16},{16,0},{1,17},{17,1},{2,18},{18,2},{3,19},{19,3},{4,20},{20... | collective-permute-start | bytes 6291464 | tf_op jit(solution)/shard_map/ppermute | solution.py:39
  825.0 537.2 %reduce-scatter.17.cloned.1.call-start = ((), (), s32[]{:S(2)}) async-start(), calls=%async_computation.15 | async-start | bytes 3932160 | tf_op jit(solution)/shard_map/reduce_scatter | solution.py:912
  895.9 466.3 %reduce-scatter.15.cloned.1.call-start = ((), (), s32[]{:S(2)}) async-start(), calls=%async_computation.14 | async-start | bytes 10485760 | tf_op jit(solution)/shard_map/reduce_scatter | solution.py:912
  945.8 59.0 %collective-permute-start.12 = (bf16[2,128,2048]{2,1,0:T(8,128)(2,1)}, bf16[2,128,2048]{2,1,0:T(8,128)(2,1)}, u32[]{:S(2)}, u32[]{:S(2)}) collective-permute-start(bf16[2,128,2048]{2,1,0:T(8,128)(2,1)} %get-tuple-element.153), channel_id=1, source_target_pairs={{0,16},{16,0},{1,17},{17,1},{2,18},{18,2},{3,19},{19,3},{4,20},{20... | collective-permute-start | bytes 3145736 | tf_op jit(solution)/shard_map/ppermute | solution.py:39
  945.8 59.0 %collective-permute-start.10 = (bf16[2,128,2048]{2,1,0:T(8,128)(2,1)}, bf16[2,128,2048]{2,1,0:T(8,128)(2,1)}, u32[]{:S(2)}, u32[]{:S(2)}) collective-permute-start(bf16[2,128,2048]{2,1,0:T(8,128)(2,1)} %get-tuple-element.154), channel_id=1, source_target_pairs={{0,2},{2,0},{1,3},{3,1},{4,6},{6,4},{5,7},{7,5},{8,10},{10,8},{9,1... | collective-permute-start | bytes 3145736 | tf_op jit(solution)/shard_map/ppermute | solution.py:39
  1004.8 54.3 %collective-permute-start.19 = (bf16[4,128,2048]{2,1,0:T(8,128)(2,1)}, bf16[4,128,2048]{2,1,0:T(8,128)(2,1)}, u32[]{:S(2)}, u32[]{:S(2)}) collective-permute-start(bf16[4,128,2048]{2,1,0:T(8,128)(2,1)} %constant_dynamic-slice_fusion.12), channel_id=1, source_target_pairs={{0,1},{1,0},{2,3},{3,2},{4,5},{5,4},{6,7},{7,6},{8,9},{9,8},{10,11... | collective-permute-start | bytes 6291464 | tf_op jit(solution)/shard_map/ppermute | solution.py:39
  1054.5 94.4 %collective-permute-start.26 = (bf16[4,1,2,128,1024]{4,3,0,2,1:T(8,128)(2,1)}, bf16[4,1,2,128,1024]{4,3,0,2,1:T(8,128)(2,1)}, u32[]{:S(2)}, u32[]{:S(2)}) collective-permute-start(bf16[4,1,2,128,1024]{4,3,0,2,1:T(8,128)(2,1)} %bitcast.297), channel_id=1, source_target_pairs={{0,16},{16,0},{1,17},{17,1},{2,18},{18,2},{3,19},{19,3},{4,20},{20... | collective-permute-start | bytes 6291464 | tf_op jit(solution)/shard_map/ppermute | solution.py:39
  1059.1 120.2 %collective-permute-start.28 = (bf16[2,4,1,128,2048]{4,3,1,2,0:T(8,128)(2,1)}, bf16[2,4,1,128,2048]{4,3,1,2,0:T(8,128)(2,1)}, u32[]{:S(2)}, u32[]{:S(2)}) collective-permute-start(bf16[2,4,1,128,2048]{4,3,1,2,0:T(8,128)(2,1)} %dynamic-slice_bitcast_fusion), channel_id=1, source_target_pairs={{0,2},{2,0},{1,3},{3,1},{4,6},{6,4},{5,7},{7,5},{8,10},{10,8},{9,1... | collective-permute-start | bytes 12582920 | tf_op jit(solution)/shard_map/ppermute | solution.py:39
  1069.5 205.5 %all-to-all-start.1 = ((f32[32,1,384]{2,1,0:T(1,128)}), f32[32,1,384]{2,1,0:T(1,128)S(1)}, u32[]{:S(2)}, u32[]{:S(2)}) async-start(f32[32,1,384]{2,1,0:T(1,128)} %reshape.491), calls=%async_computation.3 | async-start | bytes 98304 | tf_op jit(solution)/shard_map/all_to_all | solution.py:1016
  1082.2 73.5 %collective-permute-start.22 = (bf16[128,2048]{1,0:T(8,128)(2,1)S(1)}, bf16[128,2048]{1,0:T(8,128)(2,1)S(1)}, u32[]{:S(2)}, u32[]{:S(2)}) collective-permute-start(bf16[128,2048]{1,0:T(8,128)(2,1)S(1)} %get-tuple-element.192), channel_id=1, source_target_pairs={{0,12},{4,0},{8,4},{12,8},{1,13},{5,1},{9,5},{13,9},{2,14},{6,2},{... | collective-permute-start | bytes 1572872 | tf_op jit(solution)/shard_map/ppermute | solution.py:86
  1085.5 92.3 %collective-permute-start.21 = (bf16[128,2048]{1,0:T(8,128)(2,1)S(1)}, bf16[128,2048]{1,0:T(8,128)(2,1)S(1)}, u32[]{:S(2)}, u32[]{:S(2)}) collective-permute-start(bf16[128,2048]{1,0:T(8,128)(2,1)S(1)} %get-tuple-element.193), channel_id=1, source_target_pairs={{0,8},{4,12},{8,0},{12,4},{1,9},{5,13},{9,1},{13,5},{2,10},{6,14},... | collective-permute-start | bytes 1572872 | tf_op jit(solution)/shard_map/ppermute | solution.py:86
  1104.0 74.1 %collective-permute-start.20 = (bf16[128,2048]{1,0:T(8,128)(2,1)S(1)}, bf16[128,2048]{1,0:T(8,128)(2,1)S(1)}, u32[]{:S(2)}, u32[]{:S(2)}) collective-permute-start(bf16[128,2048]{1,0:T(8,128)(2,1)S(1)} %get-tuple-element.194), channel_id=1, source_target_pairs={{0,4},{4,8},{8,12},{12,0},{1,5},{5,9},{9,13},{13,1},{2,6},{6,10},{... | collective-permute-start | bytes 1572872 | tf_op jit(solution)/shard_map/ppermute | solution.py:86
  1155.7 80.8 %collective-permute-start.15 = (bf16[128,2048]{1,0:T(8,128)(2,1)}, bf16[128,2048]{1,0:T(8,128)(2,1)}, u32[]{:S(2)}, u32[]{:S(2)}) collective-permute-start(bf16[128,2048]{1,0:T(8,128)(2,1)} %get-tuple-element.202), channel_id=1, source_target_pairs={{0,8},{4,12},{8,0},{12,4},{1,9},{5,13},{9,1},{13,5},{2,10},{6,14},... | collective-permute-start | bytes 1572872 | tf_op jit(solution)/shard_map/ppermute | solution.py:86
  1177.8 59.1 %collective-permute-start.14 = (bf16[128,2048]{1,0:T(8,128)(2,1)S(1)}, bf16[128,2048]{1,0:T(8,128)(2,1)}, u32[]{:S(2)}, u32[]{:S(2)}) collective-permute-start(bf16[128,2048]{1,0:T(8,128)(2,1)S(1)} %get-tuple-element.203), channel_id=1, source_target_pairs={{0,4},{4,8},{8,12},{12,0},{1,5},{5,9},{9,13},{13,1},{2,6},{6,10},{... | collective-permute-start | bytes 1572872 | tf_op jit(solution)/shard_map/ppermute | solution.py:86
  1178.1 61.3 %collective-permute-start.25 = (bf16[4,1,128,1024]{3,2,1,0:T(8,128)(2,1)}, bf16[4,1,128,1024]{3,2,1,0:T(8,128)(2,1)}, u32[]{:S(2)}, u32[]{:S(2)}) collective-permute-start(bf16[4,1,128,1024]{3,2,1,0:T(8,128)(2,1)} %dynamic-slice_bitcast_fusion.7), channel_id=1, source_target_pairs={{0,2},{2,0},{1,3},{3,1},{4,6},{6,4},{5,7},{7,5},{8,10},{10,8},{9,1... | collective-permute-start | bytes 3145736 | tf_op jit(solution)/shard_map/ppermute | solution.py:39
  1185.3 56.6 %collective-permute-start.29 = (bf16[4,1,128,2048]{3,2,1,0:T(8,128)(2,1)S(1)}, bf16[4,1,128,2048]{3,2,1,0:T(8,128)(2,1)S(1)}, u32[]{:S(2)}, u32[]{:S(2)}) collective-permute-start(bf16[4,1,128,2048]{3,2,1,0:T(8,128)(2,1)S(1)} %dynamic-slice_bitcast_fusion.1), channel_id=1, source_target_pairs={{0,16},{16,0},{1,17},{17,1},{2,18},{18,2},{3,19},{19,3},{4,20},{20... | collective-permute-start | bytes 6291464 | tf_op jit(solution)/shard_map/ppermute | solution.py:39
  1266.6 74.9 %collective-permute-start.31 = (bf16[1,128,4096]{2,1,0:T(8,128)(2,1)}, bf16[1,128,4096]{2,1,0:T(8,128)(2,1)}, u32[]{:S(2)}, u32[]{:S(2)}) collective-permute-start(bf16[1,128,4096]{2,1,0:T(8,128)(2,1)} %get-tuple-element.167), channel_id=1, source_target_pairs={{0,8},{4,12},{8,0},{12,4},{1,9},{5,13},{9,1},{13,5},{2,10},{6,14},... | collective-permute-start | bytes 3145736 | tf_op jit(solution)/shard_map/ppermute | solution.py:86
  (94 other events, 1518.2 us)
Sparse Core Ops, SparseCore 0:
  169.8 96.0 all-gather.5
  267.8 94.8 all-gather.3
  505.1 143.8 reduce-scatter.6
  661.0 59.5 reduce-scatter.8
  722.7 60.2 reduce-scatter.12
  785.2 144.4 reduce-scatter.10
  932.0 60.9 reduce-scatter.16
  1001.7 201.5 reduce-scatter.14

commit v8 on v7

--- a/solution.py
+++ b/solution.py
@@ -384,6 +384,132 @@
     return weights.reshape(width, 4 * columns), tokens, grads, segments
 
 
+def last_kernel(grads, tokens, output, grads_out, tokens_out, output_out, send, recv, row_send, row_recv, local):
+    z, core = lax.axis_index("seq"), lax.axis_index("core")
+    seq_n, piece = tokens.shape[:2]
+    seq_count = tokens_out.shape[0]
+    rows = grads.shape[1] // 2
+
+    barrier = pltpu.get_barrier_semaphore()
+    partners = [
+        {"seq": lax.rem(z + dz, seq_n), "core": lax.rem(core + dc, 2)}
+        for dz in range(seq_n)
+        for dc in range(2)
+        if dz or dc
+    ]
+    for partner in partners:
+        pl.semaphore_signal(barrier, inc=1, device_id=partner, device_id_type=MESH)
+    pl.semaphore_wait(barrier, len(partners))
+
+    def grad_copy(dz, dc):
+        z_to, core_to = lax.rem(z + dz, seq_n), lax.rem(core + dc, 2)
+        source = grads.at[z_to, pl.ds(pl.multiple_of(core_to * rows, rows), rows), :]
+        target = grads_out.at[core, z]
+        if not (dz or dc):
+            return pltpu.make_async_copy(source, target, local.at[2])
+        return pltpu.make_async_remote_copy(
+            source,
+            target,
+            send.at[dz, dc],
+            recv.at[dz, dc],
+            device_id={"seq": z_to, "core": core_to},
+            device_id_type=MESH,
+        )
+
+    def grad_arrival(dz, dc):
+        z_from, core_from = lax.rem(z + seq_n - dz, seq_n), lax.rem(core + dc, 2)
+        ref = grads_out.at[core_from, z_from]
+        return pltpu.make_async_remote_copy(
+            ref, ref, send.at[dz, dc], recv.at[dz, dc], device_id=partners[0], device_id_type=MESH
+        )
+
+    group, member = z // seq_count, lax.rem(z, seq_count)
+
+    def row_place(target, s, c):
+        return target.at[s, pl.ds(pl.multiple_of(c * piece, piece), piece), :]
+
+    def row_copy(n, source, target, dz):
+        z_to = lax.rem(z + dz, seq_n)
+        return pltpu.make_async_remote_copy(
+            source.at[z_to],
+            row_place(target, member, core),
+            row_send.at[n, dz],
+            row_recv.at[n, member, core],
+            device_id={"seq": z_to, "core": group},
+            device_id_type=MESH,
+        )
+
+    def each_row(remote, kept):
+        for n, source, target in ((0, tokens, tokens_out), (1, output, output_out)):
+            for dz in range(seq_n):
+                if dz:
+                    remote(row_copy(n, source, target, dz))
+                else:
+
+                    @pl.when(group != core)
+                    def _(copy=row_copy(n, source, target, 0)):
+                        remote(copy)
+
+                    @pl.when(group == core)
+                    def _(n=n, source=source, target=target):
+                        kept(
+                            pltpu.make_async_copy(
+                                source.at[z], row_place(target, member, core), local.at[n]
+                            )
+                        )
+
+    every = [(dz, dc) for dz in range(seq_n) for dc in range(2)]
+    for dz, dc in reversed(every):
+        grad_copy(dz, dc).start()
+    each_row(lambda copy: copy.start(), lambda copy: copy.start())
+
+    grad_copy(0, 0).wait()
+    for dz, dc in every[1:]:
+        grad_copy(dz, dc).wait_send()
+        grad_arrival(dz, dc).wait_recv()
+    each_row(lambda copy: copy.wait_send(), lambda copy: copy.wait())
+    for n, target in ((0, tokens_out), (1, output_out)):
+        for s in range(seq_count):
+            for c in range(2):
+                ref = row_place(target, s, c)
+                copy = pltpu.make_async_remote_copy(
+                    ref,
+                    ref,
+                    row_send.at[n, 0],
+                    row_recv.at[n, s, c],
+                    device_id=partners[0],
+                    device_id_type=MESH,
+                )
+
+                @pl.when((z != seq_count * core + s) | (core != c))
+                def _(copy=copy):
+                    copy.wait_recv()
+
+
+def last_transfers(grads, tokens, output, seq_count):
+    seq_n, piece, width = tokens.shape
+    rows = grads.shape[1] // 2
+    held = pl.BlockSpec(memory_space=pl.ANY)
+    out = jax.ShapeDtypeStruct((seq_count, 2 * piece, width), bf16)
+    dma = pltpu.SemaphoreType.DMA
+    return pl.pallas_call(
+        last_kernel,
+        in_specs=[held] * 3,
+        out_specs=[held] * 3,
+        out_shape=[jax.ShapeDtypeStruct((2, seq_n, rows, grads.shape[2]), bf16), out, out],
+        scratch_shapes=[
+            dma((seq_n, 2)),
+            dma((seq_n, 2)),
+            dma((2, seq_n)),
+            dma((2, seq_count, 2)),
+            dma((3,)),
+        ],
+        compiler_params=pltpu.CompilerParams(collective_id=1, has_side_effects=True),
+        cost_estimate=pl.CostEstimate(flops=0, bytes_accessed=4 * grads.size, transcendentals=0),
+        name="last_transfers",
+    )(grads, tokens, output)
+
+
 def visible_block(seg_row, seg_col, start, rows, cols):
     row_place = start + lax.broadcasted_iota(jnp.int32, (rows, cols), 0)
     col_place = lax.broadcasted_iota(jnp.int32, (rows, cols), 1)
@@ -519,13 +645,14 @@
     lax.fori_loop(0, x.shape[0] // chunk, step, 0)
 
 
-def expert_units(x, dy, gate, up, down, start, stop, *before):
+def expert_units(x, dy, gate, up, down, start, stop, half=None, made=(), before=()):
     rows, width = x.shape
     units = stop - start
-    chunk = tile_of(rows)
+    part, at = (rows, 0) if half is None else (rows // 2, half)
+    chunk = tile_of(part)
     tile = unit_tile(gate.shape[1])
     first = start // tile
-    once = pl.BlockSpec((rows, width), lambda j: (0, 0), pipeline_mode=pl.Buffered(1))
+    once = pl.BlockSpec((part, width), lambda j: (at, 0), pipeline_mode=pl.Buffered(1))
     out = jax.ShapeDtypeStruct((rows, units), bf16)
     return pl.pallas_call(
         functools.partial(units_kernel, chunk),
@@ -537,17 +664,18 @@
             pl.BlockSpec((width, tile), lambda j: (0, first + j)),
             pl.BlockSpec((tile, width), lambda j: (first + j, 0)),
         ]
-        + [pl.BlockSpec(memory_space=pl.ANY)] * len(before),
-        out_specs=[pl.BlockSpec((rows, tile), lambda j: (0, j))] * 3,
+        + [pl.BlockSpec(memory_space=pl.ANY)] * (len(made) + len(before)),
+        out_specs=[pl.BlockSpec((part, tile), lambda j: (at, j))] * 3,
         out_shape=[out] * 3,
+        input_output_aliases={5 + i: i for i in range(len(made))},
         compiler_params=pltpu.CompilerParams(vmem_limit_bytes=56 * 2**20),
         cost_estimate=pl.CostEstimate(
-            flops=6 * rows * width * units,
-            bytes_accessed=4 * rows * width + 6 * width * units + 6 * rows * units,
-            transcendentals=rows * units,
+            flops=6 * part * width * units,
+            bytes_accessed=4 * part * width + 6 * width * units + 6 * part * units,
+            transcendentals=part * units,
         ),
         name="expert_units",
-    )(x, dy, gate, up, down, *before)
+    )(x, dy, gate, up, down, *made, *before)
 
 
 def unit_tile(units):
@@ -559,7 +687,8 @@
     return units // tile * 3 // 4 * tile
 
 
-def dispatch_kernel(me, hidden, dout, slot, routes, router, rows, dy_rows, gate):
+def dispatch_kernel(me, hidden, dout, slot, routes, router, *rest):
+    rows, dy_rows, gate = rest[-3:]
     size = hidden.shape[1] * hidden.shape[3]
     width = hidden.shape[4]
     mine = me[3]
@@ -581,60 +710,72 @@
     dy_rows[0] = product(chosen, dy).astype(bf16)
 
 
-def plane_block(seq_n, piece, width):
-    return pl.BlockSpec((1, 2, 1, piece, width), lambda b, me: (b // seq_n, 0, b % seq_n, 0, 0))
+def block_place(b, span):
+    return lax.rem(b, 4 * span) // span, (b // (4 * span)) * span + lax.rem(b, span)
+
+
+def plane_block(seq_n, piece, width, first=0, seen=None):
+    span = seq_n // 2
+
+    def index(b, me):
+        device, place = block_place(b + first, span)
+        return (device, 0, place if seen is None else lax.rem(place, seen), 0, 0)
+
+    return pl.BlockSpec((1, 2, 1, piece, width), index)
 
 
 def relative_block(seq_n, piece, width):
-    return pl.BlockSpec(
-        (1, 1, 2, 1, piece, width),
-        lambda b, me: (
-            lax.rem(b // (2 * seq_n) + me[0], 2),
-            lax.rem(b // seq_n + me[1], 2),
-            0,
-            b % seq_n,
-            0,
-            0,
-        ),
-    )
-
-
-def dispatch(me, hidden, dout, slot, routes, router, seq_n, piece, cap):
+    def index(b, me):
+        device, place = block_place(b, seq_n // 2)
+        return (lax.rem(device // 2 + me[0], 2), lax.rem(device + me[1], 2), 0, place, 0, 0)
+
+    return pl.BlockSpec((1, 1, 2, 1, piece, width), index)
+
+
+def dispatch(me, hidden, dout, slot, routes, router, seq_n, piece, cap, half, made=()):
     blocks, size = slot.shape[0], slot.shape[2]
     width = hidden.shape[1]
-    seen = (4, 2, seq_n, piece, width)
-    each = pl.BlockSpec((1, cap, width), lambda b, me: (b, 0, 0))
+    span = seq_n // 2
+    count = blocks // 2
+    first = half * count
+
+    def each(*shape):
+        return pl.BlockSpec((1,) + shape, lambda b, me: (first + b, 0, 0))
+
     out = jax.ShapeDtypeStruct((blocks, cap, width), bf16)
     spare = jnp.zeros((width, 128 - router.shape[1]), router.dtype)
     return pl.pallas_call(
         dispatch_kernel,
         grid_spec=pltpu.PrefetchScalarGridSpec(
             num_scalar_prefetch=1,
-            grid=(blocks,),
+            grid=(count,),
             in_specs=[
-                plane_block(seq_n, piece, width),
-                plane_block(seq_n, piece, width),
-                pl.BlockSpec((1, 1, size), lambda b, me: (b, 0, 0)),
-                pl.BlockSpec((1, size, routes.shape[2]), lambda b, me: (b, 0, 0)),
+                plane_block(seq_n, piece, width, first, span),
+                plane_block(seq_n, piece, width, first),
+                each(1, size),
+                each(size, routes.shape[2]),
                 pl.BlockSpec((width, 128), lambda b, me: (0, 0)),
-            ],
-            out_specs=[each, each, pl.BlockSpec((1, size, 1), lambda b, me: (b, 0, 0))],
+            ]
+            + [pl.BlockSpec(memory_space=pl.ANY)] * len(made),
+            out_specs=[each(cap, width), each(cap, width), each(size, 1)],
         ),
         out_shape=[out, out, jax.ShapeDtypeStruct((blocks, size, 1), f32)],
+        input_output_aliases={6 + i: i for i in range(len(made))},
         compiler_params=pltpu.CompilerParams(vmem_limit_bytes=40 * 2**20),
         cost_estimate=pl.CostEstimate(
-            flops=4 * blocks * size * width * (cap + 64),
-            bytes_accessed=4 * blocks * (size + cap) * width,
-            transcendentals=2 * blocks * size,
+            flops=4 * count * size * width * (cap + 64),
+            bytes_accessed=4 * count * (size + cap) * width,
+            transcendentals=2 * count * size,
         ),
         name="dispatch",
     )(
         me,
-        hidden.reshape(seen),
-        dout.reshape(seen),
+        hidden.reshape(4, 2, span, piece, width),
+        dout.reshape(4, 2, seq_n, piece, width),
         slot,
         routes,
         jnp.concatenate([router, spare], axis=1),
+        *made,
     )
 
 
@@ -867,15 +1008,19 @@
     inverse_two = lax.rsqrt(jnp.mean(residual * residual, axis=-1, keepdims=True) + epsilon)
     normed_two = residual * inverse_two
     hidden_two = (normed_two * expert_norm).astype(bf16).reshape(home, width)
-
-    hidden_plane = lax.all_gather(hidden_two, PLANE, axis=0, tiled=True)
+    hidden_two = after(hidden_two, grad_plane)
+
+    hidden_parts = [
+        lax.all_gather(part, PLANE, axis=0, tiled=True) for part in jnp.split(hidden_two, 2)
+    ]
     small = after(jnp.transpose(routes, (2, 0, 1)).reshape(topk * seq_count, seq_dev), hidden_two)
     small = lax.all_gather(small, EVERY, axis=0, tiled=True).reshape(
         dp_n, seq_n, r_n, y_n, core_n, topk, seq_count, seq_dev
     )
     small = pick(pick(small, group, 4), member, 5)
     plane_routes = pick(small, r_i, 2).transpose(0, 2, 1, 3, 4)
-    block_routes = plane_routes.reshape(blocks, topk, seq_dev)
+    block_routes = plane_routes.reshape(4, 2, seq_n // 2, topk, seq_dev)
+    block_routes = block_routes.transpose(1, 0, 2, 3, 4).reshape(blocks, topk, seq_dev)
     home_routes = (
         pick(pick(plane_routes, dp_i, 0), y_i, 0)
         .reshape(seq_n, topk, core_n, piece)
@@ -889,24 +1034,20 @@
     slot = jnp.where(chosen, rank.astype(jnp.int32), -1)
     slot_row, slot_col = slot[:, None, :], slot[:, :, None]
     me = jnp.stack([dp_i, y_i, core_i, mine]).astype(jnp.int32)
-    expert_rows, dy_rows, row_gate = dispatch(
-        me,
-        hidden_plane,
-        grad_plane,
-        slot_row,
-        jnp.transpose(block_routes, (0, 2, 1)),
-        router,
-        seq_n,
-        piece,
-        cap,
-    )
-    expert_in = expert_rows.reshape(blocks * cap, width)
-    dy_rows = dy_rows.reshape(blocks * cap, width)
-
     gate_one, up_one, down_one = gate_weight[0], up_weight[0], down_weight[0]
     inner = gate_one.shape[1]
     cut = unit_cut(inner)
     full = (gate_one, up_one, down_one)
+    route_col = jnp.transpose(block_routes, (0, 2, 1))
+    picked, unit_parts = (), ()
+    for part, hidden_part in enumerate(hidden_parts):
+        picked = dispatch(
+            me, hidden_part, grad_plane, slot_row, route_col, router, seq_n, piece, cap, part, picked
+        )
+        expert_in, dy_rows = (rows.reshape(blocks * cap, width) for rows in picked[:2])
+        unit_parts = expert_units(expert_in, dy_rows, *full, 0, cut, part, unit_parts)
+    row_gate = picked[2]
+    units_a, dgpre_a, dupre_a = unit_parts
 
     def over_ctx(part):
         return lax.psum_scatter(part, CTX, scatter_dimension=0, tiled=True)
@@ -914,9 +1055,8 @@
     def rows_product(rows, part):
         return t_product(rows, part).astype(bf16)
 
-    units_a, dgpre_a, dupre_a = expert_units(expert_in, dy_rows, *full, 0, cut)
     down_a = rows_product(dy_rows, units_a)
-    units_b, dgpre_b, dupre_b = expert_units(expert_in, dy_rows, *full, cut, inner, down_a)
+    units_b, dgpre_b, dupre_b = expert_units(expert_in, dy_rows, *full, cut, inner, before=(down_a,))
     down_b = rows_product(dy_rows, units_b)
     down_sum_a, down_sum_b = over_ctx(down_a), over_ctx(down_b)
     grads = (dgpre_a, dgpre_b, dupre_a, dupre_b, gate_one, up_one)
@@ -932,7 +1072,7 @@
         me, ypair.reshape(blocks, cap, width), slot_col, seq_n, piece, row_gate, grad_plane
     )
 
-    dgate_plane = dgate_plane.reshape(dp_n * y_n, seq_n, core_n, piece).transpose(0, 2, 1, 3)
+    dgate_plane = dgate_plane.reshape(2, 4, seq_n // 2, core_n, piece).transpose(1, 3, 0, 2, 4)
     dgate_home = lax.all_to_all(
         dgate_plane.reshape(8, home), PLANE, split_axis=0, concat_axis=0, tiled=True
     ).reshape(dp_n, experts, home).sum(axis=0)
@@ -970,10 +1110,10 @@
         query, keys, values, mixed, dmixed, cosine, sine, seg_row, seg_col, heads, down_sum_b, up_b, *stages[0]
     )
     dqkv = jnp.concatenate([dqpre, dkpre, dvpre], axis=1)
-    up_a = rows_product(expert_in, after(dupre_a, dqpre))
-    dqkv = after(dqkv, up_a)
-    dhidden_part = product_t(dqkv, weight_in).astype(bf16)
-    in_grad = t_product(hidden_full, after(dqkv, dhidden_part, *stages[1])).astype(bf16)
+    out_grad = t_product(mixed_full, after(dbranch_here, dqpre)).astype(bf16)
+    in_grad = t_product(hidden_full, after(dqkv, out_grad)).astype(bf16)
+    up_a = rows_product(expert_in, after(dupre_a, in_grad))
+    dhidden_part = product_t(after(dqkv, up_a, *stages[1]), weight_in).astype(bf16)
     dhidden_one = chip_scatter(
         dhidden_part.reshape(seq_n, parts * piece, width), 1, parts
     )
@@ -985,7 +1125,6 @@
         attn_norm,
     )
     dtokens = (dtokens + dresid).astype(bf16).reshape(seq_n, piece, width)
-    out_grad = t_product(mixed_full, after(dbranch_here, in_grad)).astype(bf16)
     output = (residual + mixture).astype(bf16)
 
     grad_down = jnp.concatenate([down_sum_a, down_sum_b], axis=1).astype(f32).T[None]
@@ -1002,11 +1141,19 @@
     first = [half(seen(a), 0, dp_i, "dp") for a in (out_grad, in_grad[:, :columns])]
     first.append(half(seen(in_grad[:, columns:]), 3, y_i, "y"))
     second = [half(a, 2, y_i, "y") for a in first[:2]] + [half(first[2], 0, dp_i, "dp")]
-    grad_tokens = from_sequences(dtokens)
-    output = from_sequences(output)
-    part = total(*seq_pieces(jnp.concatenate(second, axis=-1))).astype(bf16)
-    part = part.reshape(parts, rows_here, 4, 1, columns)
-    part = chip_exchange(part, 0, 3, parts).reshape(rows_here, 4, width).astype(f32)
+    second = jnp.concatenate(second, axis=-1)
+    if r_n == 1 and parts == 2 and seq_n == 2 * seq_count:
+        part, grad_tokens, output = last_transfers(
+            second.reshape(seq_n, core_n * rows_here, 4 * columns), dtokens, output, seq_count
+        )
+        part = total(*(part[:, i] for i in range(seq_n))).reshape(core_n, rows_here, 4, columns)
+        part = part.transpose(1, 2, 0, 3).reshape(rows_here, 4, width)
+    else:
+        grad_tokens = from_sequences(dtokens)
+        output = from_sequences(output)
+        part = total(*seq_pieces(second)).astype(bf16)
+        part = part.reshape(parts, rows_here, 4, 1, columns)
+        part = chip_exchange(part, 0, 3, parts).reshape(rows_here, 4, width).astype(f32)
     grad_output, grad_query, grad_key, grad_value = (part[:, i] for i in range(4))
     grad_tokens = grad_tokens.astype(f32)
 

time: 1400 us -> 1450 us (1.036)
  Pallas kernels: 529 us -> 714 us
  waiting for transfers between devices: 273 us -> 167 us
  starting transfers between devices: 55.3 us -> 26.8 us
    pallas_call x0 -> x1, Pallas kernels: none -> 175 us  [last_transfers(): pl.pallas_call(last_kernel, in_specs=[held] * 3, out_specs=[held] * 3, ou...]
    ppermute x9 -> x0, waiting for transfers between devices: 130 us -> none  [seq_pieces(): lax.ppermute(give, 'seq', [(i, (i + step) % count) for i in range(count)])]
    ppermute x25 -> x22, waiting for transfers between devices: 92.4 us -> 150 us  [swap(): return lax.ppermute(a, axis, [(0, 1), (1, 0)])]
    all_gather x1 -> x2, waiting for transfers between devices: 47.1 us -> 11.6 us  [on_device(): lax.all_gather(part, PLANE, axis=0, tiled=True)]
    ppermute x9 -> x0, starting transfers between devices: 31.3 us -> none  [seq_pieces(): lax.ppermute(give, 'seq', [(i, (i + step) % count) for i in range(count)])]
    unnamed x151 -> x169, local copies, waits for them, and re-layouts: 35 us -> 50.4 us
    pallas_call x2 -> x3, Pallas kernels: 125 us -> 135 us  [expert_units(): pl.pallas_call(functools.partial(units_kernel, chunk), grid=(units // til...]
  transfers between devices with their start and end apart: 44 -> 33, of which waited for: 16 -> 14; matrix products, arithmetic and copies ran while one was open for 29% -> 27% of each run, Pallas kernels for 19% -> 34%
where the time goes in v8:
time: 1450 us; the launch traced here: 1430 us
  Pallas kernels  714 us (49%)
  matrix products  213 us (15%)
  waiting for transfers between devices  167 us (12%)
  other arithmetic  127 us (9%)
  local copies, waits for them, and re-layouts  123 us (8%)
  blocking collectives  45 us (3%)
  starting transfers between devices  26.8 us (2%)
  between operations  15.2 us (1%)
    pallas_call x1, Pallas kernels, last_transfers(): pl.pallas_call(last_kernel, in_specs=[held] * 3, out_specs=[held] * 3, ou...  175 us
    pallas_call x1, Pallas kernels, first_transfers(): pl.pallas_call(first_kernel, in_specs=[held] * 7, out_specs=[held] * 4, o...  162 us
    dot_general x9, matrix products, t_product(): lax.dot_general(a, b, (((0,), (0,)), ((), ())), preferred_element_type=f32)  155 us
    ppermute x22, waiting for transfers between devices, swap(): return lax.ppermute(a, axis, [(0, 1), (1, 0)])  150 us
    pallas_call x3, Pallas kernels, expert_units(): pl.pallas_call(functools.partial(units_kernel, chunk), grid=(units // til...  135 us
    pallas_call x2, Pallas kernels, expert_input_grad(): pl.pallas_call(functools.partial(input_kernel, cut), grid=(width // n, ro...  77.7 us
    unnamed x169, local copies, waits for them, and re-layouts  50.4 us
    all_gather x1, blocking collectives, on_device(): lax.all_gather(small, EVERY, axis=0, tiled=True)  45 us
  transfers between devices with their start and end apart: 33, of which 14 were waited for; matrix products, arithmetic and copies ran while one was open for 27% of the time, Pallas kernels for 34%

profile of v8, /device:TPU:1, one launch (start us, length us, event | category | flops | bytes accessed | tf_op | source)
XLA Modules:
  0.0 1430.0 jit_solution(18162608070589754270)
XLA Ops:
  7.2 162.4 %first_transfers.1 = (bf16[2,4,2,128,4096]{4,3,2,1,0:T(8,128)(2,1)}, bf16[4,128,2048]{2,1,0:T(8,128)(2,1)}, bf16[4,128,2048]{2,1,0:T(8,128)(2,1)}, s32[2,2,1024]{2,1,0:T(2,128)}) custom-call(bf16[64,2048]{1,0:T(8,128)(2,1)} %query.1, bf16[64,2048]{1,0:T(8,128)(2,1)} %key.1, bf16[64,2048]{1,0:T(8,128)(2,1)} %value.1, bf16[64,2048]{1,0:T(8,128)(2,1)} %output.1, ...), custom_call_target="tpu_custom_call" | custom-call | bytes 16777216 | tf_op jit(solution)/shard_map/first_transfers/pallas_call | solution.py:360
  183.8 20.1 %fusion.4.qp.kp.vp = f32[1024,3072]{1,0:T(8,128)} fusion(bf16[1024,2048]{1,0:T(8,128)(2,1)S(1)} %bitcast.316, bf16[2048,4096]{1,0:T(8,128)(2,1)} %bitcast.334), kind=kOutput, calls=%fused_computation.7 | convolution fusion | flops 12884901888 | bytes 29360128 | tf_op jit(solution)/shard_map/dot_general | solution.py:27
  203.9 27.9 %attend.1 = (bf16[1024,1024]{1,0:T(8,128)(2,1)S(1)}, bf16[1024,1024]{1,0:T(8,128)(2,1)S(1)}, bf16[1024,1024]{1,0:T(8,128)(2,1)}, bf16[1024,1024]{1,0:T(8,128)(2,1)}) custom-call(f32[1024,3072]{1,0:T(8,128)} %fusion.4.qp.kp.vp, f32[1024,3072]{1,0:T(8,128)} %fusion.4.qp.kp.vp, f32[1024,3072]{1,0:T(8,128)} %fusion.4.qp.kp.vp, ...), custom_call_target="tpu_custom_call" | custom-call | flops 2684354560 | bytes 20971520 | tf_op jit(solution)/shard_map/attend/pallas_call | solution.py:552
  272.4 45.0 %all-gather = s32[32,4,256]{2,1,0:T(4,128)S(1)} all-gather(s32[1,4,256]{2,1,0:T(4,128)} %bitcast.326), channel_id=1, replica_groups=mesh['dp'=2,'seq'=4,'r'=1,'y'=2,'core'=2] {'dp','seq','r','y','core'}, dimensions={0}, use_global_device_ids=true | all-gather | bytes 135168 | tf_op jit(solution)/shard_map/all_gather | solution.py:1017
  348.4 47.7 %expert_units.3 = (bf16[2560,2048]{1,0:T(8,128)(2,1)}, bf16[2560,2048]{1,0:T(8,128)(2,1)}, bf16[2560,2048]{1,0:T(8,128)(2,1)}) custom-call(bf16[2560,2048]{1,0:T(8,128)(2,1)} %bitcast.296, bf16[2560,2048]{1,0:T(8,128)(2,1)} %bitcast.303, bf16[2048,2816]{1,0:T(8,128)(2,1)} %bitcast.338, bf16[2048,2816]{1,0:T(8,128)(2,1)} %bitcast.343, ...), custom_call_target="tpu_custom_call" | custom-call | flops 32212254720 | bytes 51380224 | tf_op jit(solution)/shard_map/expert_units/pallas_call | solution.py:657
  414.9 47.8 %expert_units.4 = (bf16[2560,2048]{1,0:T(8,128)(2,1)}, bf16[2560,2048]{1,0:T(8,128)(2,1)}, bf16[2560,2048]{1,0:T(8,128)(2,1)}) custom-call(bf16[2560,2048]{1,0:T(8,128)(2,1)} %bitcast.297, bf16[2560,2048]{1,0:T(8,128)(2,1)} %bitcast.304, bf16[2048,2816]{1,0:T(8,128)(2,1)} %bitcast.339, ...), custom_call_target="tpu_custom_call", output_to_operand_aliasing={{0}: (5, {}), {1}: (6, {}), {2}: (7, {})} | custom-call | flops 32212254720 | bytes 51380224 | tf_op jit(solution)/shard_map/expert_units/pallas_call | solution.py:657
  462.7 28.8 %convolution_convert_fusion.3.rest_0_ = bf16[2048,2048]{1,0:T(8,128)(2,1)} fusion(bf16[2560,2048]{1,0:T(8,128)(2,1)} %bitcast.305, bf16[2560,2048]{1,0:T(8,128)(2,1)} %get-tuple-element.57.units_a), kind=kOutput, calls=%fused_computation.17 | convolution fusion | flops 21479030784 | bytes 29360128 | tf_op jit(solution)/shard_map/dot_general | solution.py:35
  492.2 39.9 %expert_units.5 = (bf16[2560,768]{1,0:T(8,128)(2,1)}, bf16[2560,768]{1,0:T(8,128)(2,1)}, bf16[2560,768]{1,0:T(8,128)(2,1)}) custom-call(bf16[2560,2048]{1,0:T(8,128)(2,1)} %bitcast.298, bf16[2560,2048]{1,0:T(8,128)(2,1)} %bitcast.306, bf16[2048,2816]{1,0:T(8,128)(2,1)} %bitcast.340, bf16[2048,2816]{1,0:T(8,128)(2,1)} %bitcast.345, ...), custom_call_target="tpu_custom_call" | custom-call | flops 24159191040 | bytes 42205184 | tf_op jit(solution)/shard_map/expert_units/pallas_call | solution.py:657
  545.6 38.8 %expert_input_grad.2.rest_0_ = bf16[2560,1024]{1,0:T(8,128)(2,1)} custom-call(bf16[2560,2048]{1,0:T(8,128)(2,1)} %get-tuple-element.56.dgate_a.refs_0_, bf16[2560,768]{1,0:T(8,128)(2,1)} %get-tuple-element.58.dgate_b.refs_0_, bf16[2560,2048]{1,0:T(8,128)(2,1)} %get-tuple-element.59.dup_a.refs_0_, bf16[2560,768]{1,0:T(8,128)(2,1)} %get-tuple-element.60.dup_b.refs_0_, ...), custom_call_target="tpu_custom_call" | custom-call | flops 29527900160 | bytes 45613056 | tf_op jit(solution)/shard_map/expert_input_grad/pallas_call | solution.py:885
  584.4 39.0 %expert_input_grad.3 = bf16[2560,1024]{1,0:T(8,128)(2,1)} custom-call(bf16[2560,2048]{1,0:T(8,128)(2,1)} %get-tuple-element.56.dgate_a.refs_0_, bf16[2560,768]{1,0:T(8,128)(2,1)} %get-tuple-element.58.dgate_b.refs_0_, bf16[2560,2048]{1,0:T(8,128)(2,1)} %get-tuple-element.59.dup_a.refs_0_, bf16[2560,768]{1,0:T(8,128)(2,1)} %get-tuple-element.60.dup_b.refs_0_, ...), custom_call_target="tpu_custom_call" | custom-call | flops 29527900160 | bytes 45613056 | tf_op jit(solution)/shard_map/expert_input_grad/pallas_call | solution.py:885
  647.8 13.7 convolution_convert_fusion.6
  672.1 28.9 %convolution_convert_fusion.2.refs_1_.rest_0_ = bf16[2048,2048]{1,0:T(8,128)(2,1)} fusion(bf16[2560,2048]{1,0:T(8,128)(2,1)} %bitcast.300, bf16[2560,2048]{1,0:T(8,128)(2,1)} %after.13), kind=kOutput, calls=%fused_computation.16 | convolution fusion | flops 21479030784 | bytes 29360128 | tf_op jit(solution)/shard_map/dot_general | solution.py:35
  709.6 20.3 %collective-permute-done.6 = bf16[2,128,2048]{2,1,0:T(8,128)(2,1)} collective-permute-done((bf16[2,128,2048]{2,1,0:T(8,128)(2,1)}, bf16[2,128,2048]{2,1,0:T(8,128)(2,1)}, u32[]{:S(2)}, u32[]{:S(2)}) %collective-permute-start.6) | collective-permute-done | bytes 1048608 | tf_op jit(solution)/shard_map/ppermute | solution.py:39
  738.1 40.3 %expert_down.1 = bf16[2560,2048]{1,0:T(8,128)(2,1)} custom-call(bf16[2560,2048]{1,0:T(8,128)(2,1)} %get-tuple-element.57.units_a, bf16[2560,768]{1,0:T(8,128)(2,1)S(1)} %copy-done.23, bf16[2816,2048]{1,0:T(8,128)(2,1)} %bitcast.351, bf16[2048,2048]{1,0:T(8,128)(2,1)} %convolution_convert_fusion.2.refs_1_.rest_0_), custom_call_target="tpu_custom_call" | custom-call | flops 29527900160 | bytes 36438016 | tf_op jit(solution)/shard_map/expert_down/pallas_call | solution.py:849
  778.4 24.6 %combine.1 = (bf16[2,2,2,4,128,2048]{5,4,3,2,1,0:T(8,128)(2,1)}, f32[16,256,1]{2,1,0:T(8,128)S(1)}) custom-call(s32[4]{0:T(128)S(1)} %pad_add_fusion.me, bf16[16,160,2048]{2,1,0:T(8,128)(2,1)} %bitcast.295, s32[16,256,1]{2,1,0:T(8,128)S(1)} %copy.137.slot, f32[16,256,1]{2,1,0:T(8,128)S(1)} %copy-done.4, bf16[4,2,4,128,2048]{4,3,2,1,0:T(8,128)(2,1)} %bitcast.283), custom_call_target="tpu_custom_call" | custom-call | flops 2684354560 | bytes 44040192 | tf_op jit(solution)/shard_map/combine/pallas_call | solution.py:824
  883.0 31.8 %attend_back.1 = (bf16[1024,1024]{1,0:T(8,128)(2,1)S(1)}, bf16[1024,1024]{1,0:T(8,128)(2,1)}, bf16[1024,1024]{1,0:T(8,128)(2,1)}) custom-call(bf16[1024,1024]{1,0:T(8,128)(2,1)} %copy-done.21, bf16[1024,1024]{1,0:T(8,128)(2,1)} %copy-done.22, bf16[1024,1024]{1,0:T(8,128)(2,1)} %get-tuple-element.66.v, bf16[1024,1024]{1,0:T(8,128)(2,1)} %get-tuple-element.46.mixed, ...), custom_call_target="tpu_custom_call" | custom-call | flops 6710886400 | bytes 16777216 | tf_op jit(solution)/shard_map/attend_back/pallas_call | solution.py:612
  934.3 19.5 %convolution_convert_fusion.refs_1_ = bf16[2048,3072]{1,0:T(8,128)(2,1)} fusion(bf16[1024,2048]{1,0:T(8,128)(2,1)} %bitcast.317, bf16[1024,3072]{1,0:T(8,128)(2,1)} %after.18), kind=kOutput, calls=%fused_computation.4 | convolution fusion | flops 12891193344 | bytes 23068672 | tf_op jit(solution)/shard_map/dot_general | solution.py:35
  953.8 29.3 %convolution_convert_fusion.1.refs_1_ = bf16[2048,2048]{1,0:T(8,128)(2,1)} fusion(bf16[2560,2048]{1,0:T(8,128)(2,1)} %bitcast.302, bf16[2560,2048]{1,0:T(8,128)(2,1)} %after.19), kind=kOutput, calls=%fused_computation.15 | convolution fusion | flops 21479030784 | bytes 29360128 | tf_op jit(solution)/shard_map/dot_general | solution.py:35
  1019.2 17.6 %fusion.24 = bf16[1024,2048]{1,0:T(8,128)(2,1)S(1)} fusion(bf16[1024,3072]{1,0:T(8,128)(2,1)} %after.20, bf16[2048,4096]{1,0:T(8,128)(2,1)} %bitcast.337), kind=kOutput, calls=%fused_computation.63 | convolution fusion | flops 12886999040 | bytes 23068672 | tf_op jit(solution)/shard_map/dot_general | solution.py:31
  1040.4 16.5 %collective-permute-done.11 = bf16[4,1,2,128,1024]{4,3,0,2,1:T(8,128)(2,1)} collective-permute-done((bf16[4,1,2,128,1024]{4,3,0,2,1:T(8,128)(2,1)}, bf16[4,1,2,128,1024]{4,3,0,2,1:T(8,128)(2,1)}, u32[]{:S(2)}, u32[]{:S(2)}) %collective-permute-start.11) | collective-permute-done | bytes 2097184 | tf_op jit(solution)/shard_map/ppermute | solution.py:39
  1072.2 29.6 %collective-permute-done.13 = bf16[4,1,2,128,1024]{4,3,0,2,1:T(8,128)(2,1)} collective-permute-done((bf16[4,1,2,128,1024]{4,3,0,2,1:T(8,128)(2,1)}, bf16[4,1,2,128,1024]{4,3,0,2,1:T(8,128)(2,1)}, u32[]{:S(2)}, u32[]{:S(2)}) %collective-permute-start.13) | collective-permute-done | bytes 2097184 | tf_op jit(solution)/shard_map/ppermute | solution.py:39
  1105.7 41.0 %collective-permute-done.20 = bf16[4,128,2048]{2,1,0:T(8,128)(2,1)} collective-permute-done((bf16[4,128,2048]{2,1,0:T(8,128)(2,1)}, bf16[4,128,2048]{2,1,0:T(8,128)(2,1)}, u32[]{:S(2)}, u32[]{:S(2)}) %collective-permute-start.20) | collective-permute-done | bytes 2097184 | tf_op jit(solution)/shard_map/ppermute | solution.py:39
  1196.6 21.7 %collective-permute-done.16 = bf16[4,1,128,2048]{3,2,0,1:T(8,128)(2,1)} collective-permute-done((bf16[4,1,128,2048]{3,2,0,1:T(8,128)(2,1)}, bf16[4,1,128,2048]{3,2,0,1:T(8,128)(2,1)}, u32[]{:S(2)}, u32[]{:S(2)}) %collective-permute-start.16) | collective-permute-done | bytes 2097184 | tf_op jit(solution)/shard_map/ppermute | solution.py:39
  1223.5 175.1 %last_transfers.1 = (bf16[2,4,64,4096]{3,2,1,0:T(8,128)(2,1)}, bf16[2,256,2048]{2,1,0:T(8,128)(2,1)}, bf16[2,256,2048]{2,1,0:T(8,128)(2,1)}) custom-call(bf16[4,128,4096]{2,1,0:T(8,128)(2,1)} %maximum_bitcast_fusion.1.grads, bf16[4,128,2048]{2,1,0:T(8,128)(2,1)} %bitcast.311, bf16[4,128,2048]{2,1,0:T(8,128)(2,1)} %get-tuple-element.174.output), custom_call_target="tpu_custom_call" | custom-call | bytes 8388608 | tf_op jit(solution)/shard_map/last_transfers/pallas_call | solution.py:495
  (368 shorter events, 407.5 us)
Async XLA Ops:
  7.2 260.0 %all-gather.5.cloned.1.call-start = ((), (), s32[]{:S(2)}) async-start(), calls=%async_computation.8 | async-start | bytes 18874368 | tf_op jit(solution)/shard_map/all_gather | solution.py:993
  169.7 161.0 %all-gather.9.cloned.1.call-start = ((), (), s32[]{:S(2)}) async-start(), calls=%async_computation.10 | async-start | bytes 9437184 | tf_op jit(solution)/shard_map/all_gather | solution.py:1014
  270.4 125.7 %all-gather.7.cloned.1.call-start = ((), (), s32[]{:S(2)}) async-start(), calls=%async_computation.9 | async-start | bytes 9437184 | tf_op jit(solution)/shard_map/all_gather | solution.py:1014
  271.1 401.0 %reduce-scatter.7.cloned.1.call-start = ((), (), s32[]{:S(2)}) async-start(), calls=%async_computation.11 | async-start | bytes 10485760 | tf_op jit(solution)/shard_map/reduce_scatter | solution.py:1053
  491.5 390.3 %reduce-scatter.9.cloned.1.call-start = ((), (), s32[]{:S(2)}) async-start(), calls=%async_computation.12 | async-start | bytes 3932160 | tf_op jit(solution)/shard_map/reduce_scatter | solution.py:1053
  647.8 524.6 %reduce-scatter.13.cloned.1.call-start = ((), (), s32[]{:S(2)}) async-start(), calls=%async_computation.14 | async-start | bytes 3932160 | tf_op jit(solution)/shard_map/reduce_scatter | solution.py:1053
  661.6 510.8 %reduce-scatter.11.cloned.1.call-start = ((), (), s32[]{:S(2)}) async-start(), calls=%async_computation.13 | async-start | bytes 10485760 | tf_op jit(solution)/shard_map/reduce_scatter | solution.py:1053
  705.0 24.9 %collective-permute-start.6 = (bf16[2,128,2048]{2,1,0:T(8,128)(2,1)}, bf16[2,128,2048]{2,1,0:T(8,128)(2,1)}, u32[]{:S(2)}, u32[]{:S(2)}) collective-permute-start(bf16[2,128,2048]{2,1,0:T(8,128)(2,1)} %get-tuple-element.153), channel_id=1, source_target_pairs={{0,16},{16,0},{1,17},{17,1},{2,18},{18,2},{3,19},{19,3},{4,20},{20... | collective-permute-start | bytes 3145736 | tf_op jit(solution)/shard_map/ppermute | solution.py:39
  735.6 80.6 %collective-permute-start.7 = (bf16[4,128,2048]{2,1,0:T(8,128)(2,1)}, bf16[4,128,2048]{2,1,0:T(8,128)(2,1)}, u32[]{:S(2)}, u32[]{:S(2)}) collective-permute-start(bf16[4,128,2048]{2,1,0:T(8,128)(2,1)} %pad_maximum_fusion.6), channel_id=1, source_target_pairs={{0,2},{2,0},{1,3},{3,1},{4,6},{6,4},{5,7},{7,5},{8,10},{10,8},{9,1... | collective-permute-start | bytes 6291464 | tf_op jit(solution)/shard_map/ppermute | solution.py:39
  737.3 78.8 %collective-permute-start.5 = (bf16[4,128,2048]{2,1,0:T(8,128)(2,1)}, bf16[4,128,2048]{2,1,0:T(8,128)(2,1)}, u32[]{:S(2)}, u32[]{:S(2)}) collective-permute-start(bf16[4,128,2048]{2,1,0:T(8,128)(2,1)} %pad_maximum_fusion.5), channel_id=1, source_target_pairs={{0,16},{16,0},{1,17},{17,1},{2,18},{18,2},{3,19},{19,3},{4,20},{20... | collective-permute-start | bytes 6291464 | tf_op jit(solution)/shard_map/ppermute | solution.py:39
  811.8 605.1 %reduce-scatter.17.cloned.1.call-start = ((), (), s32[]{:S(2)}) async-start(), calls=%async_computation.16 | async-start | bytes 3932160 | tf_op jit(solution)/shard_map/reduce_scatter | solution.py:1053
  840.3 30.6 %collective-permute-start.10 = (bf16[2,2,4,128,2048]{4,3,2,1,0:T(8,128)(2,1)}, bf16[2,2,4,128,2048]{4,3,2,1,0:T(8,128)(2,1)}, u32[]{:S(2)}, u32[]{:S(2)}) collective-permute-start(bf16[2,2,4,128,2048]{4,3,2,1,0:T(8,128)(2,1)} %slice_bitcast_fusion), channel_id=1, source_target_pairs={{0,1},{1,0},{2,3},{3,2},{4,5},{5,4},{6,7},{7,6},{8,9},{9,8},{10,11... | collective-permute-start | bytes 25165832 | tf_op jit(solution)/shard_map/ppermute | solution.py:39
  867.0 550.0 %reduce-scatter.15.cloned.1.call-start = ((), (), s32[]{:S(2)}) async-start(), calls=%async_computation.15 | async-start | bytes 10485760 | tf_op jit(solution)/shard_map/reduce_scatter | solution.py:1053
  987.1 24.8 %collective-permute-start.18 = (bf16[2,128,2048]{2,1,0:T(8,128)(2,1)}, bf16[2,128,2048]{2,1,0:T(8,128)(2,1)}, u32[]{:S(2)}, u32[]{:S(2)}) collective-permute-start(bf16[2,128,2048]{2,1,0:T(8,128)(2,1)} %get-tuple-element.147), channel_id=1, source_target_pairs={{0,16},{16,0},{1,17},{17,1},{2,18},{18,2},{3,19},{19,3},{4,20},{20... | collective-permute-start | bytes 3145736 | tf_op jit(solution)/shard_map/ppermute | solution.py:39
  1000.2 56.7 %collective-permute-start.11 = (bf16[4,1,2,128,1024]{4,3,0,2,1:T(8,128)(2,1)}, bf16[4,1,2,128,1024]{4,3,0,2,1:T(8,128)(2,1)}, u32[]{:S(2)}, u32[]{:S(2)}) collective-permute-start(bf16[4,1,2,128,1024]{4,3,0,2,1:T(8,128)(2,1)} %bitcast.274), channel_id=1, source_target_pairs={{0,16},{16,0},{1,17},{17,1},{2,18},{18,2},{3,19},{19,3},{4,20},{20... | collective-permute-start | bytes 6291464 | tf_op jit(solution)/shard_map/ppermute | solution.py:39
  1005.4 96.4 %collective-permute-start.13 = (bf16[4,1,2,128,1024]{4,3,0,2,1:T(8,128)(2,1)}, bf16[4,1,2,128,1024]{4,3,0,2,1:T(8,128)(2,1)}, u32[]{:S(2)}, u32[]{:S(2)}) collective-permute-start(bf16[4,1,2,128,1024]{4,3,0,2,1:T(8,128)(2,1)} %bitcast.273), channel_id=1, source_target_pairs={{0,16},{16,0},{1,17},{17,1},{2,18},{18,2},{3,19},{19,3},{4,20},{20... | collective-permute-start | bytes 6291464 | tf_op jit(solution)/shard_map/ppermute | solution.py:39
  1009.0 153.2 %collective-permute-start.15 = (bf16[2,4,1,128,2048]{4,3,1,2,0:T(8,128)(2,1)}, bf16[2,4,1,128,2048]{4,3,1,2,0:T(8,128)(2,1)}, u32[]{:S(2)}, u32[]{:S(2)}) collective-permute-start(bf16[2,4,1,128,2048]{4,3,1,2,0:T(8,128)(2,1)} %dynamic-slice_bitcast_fusion), channel_id=1, source_target_pairs={{0,2},{2,0},{1,3},{3,1},{4,6},{6,4},{5,7},{7,5},{8,10},{10,8},{9,1... | collective-permute-start | bytes 12582920 | tf_op jit(solution)/shard_map/ppermute | solution.py:39
  1016.5 130.2 %collective-permute-start.20 = (bf16[4,128,2048]{2,1,0:T(8,128)(2,1)}, bf16[4,128,2048]{2,1,0:T(8,128)(2,1)}, u32[]{:S(2)}, u32[]{:S(2)}) collective-permute-start(bf16[4,128,2048]{2,1,0:T(8,128)(2,1)} %pad_maximum_fusion.7.refs_2_), channel_id=1, source_target_pairs={{0,16},{16,0},{1,17},{17,1},{2,18},{18,2},{3,19},{19,3},{4,20},{20... | collective-permute-start | bytes 6291464 | tf_op jit(solution)/shard_map/ppermute | solution.py:39
  1019.2 127.5 %collective-permute-start.21 = (bf16[4,128,2048]{2,1,0:T(8,128)(2,1)}, bf16[4,128,2048]{2,1,0:T(8,128)(2,1)}, u32[]{:S(2)}, u32[]{:S(2)}) collective-permute-start(bf16[4,128,2048]{2,1,0:T(8,128)(2,1)} %pad_maximum_fusion.8.refs_3_), channel_id=1, source_target_pairs={{0,2},{2,0},{1,3},{3,1},{4,6},{6,4},{5,7},{7,5},{8,10},{10,8},{9,1... | collective-permute-start | bytes 6291464 | tf_op jit(solution)/shard_map/ppermute | solution.py:39
  1056.9 89.9 %collective-permute-start.19 = (bf16[4,128,2048]{2,1,0:T(8,128)(2,1)}, bf16[4,128,2048]{2,1,0:T(8,128)(2,1)}, u32[]{:S(2)}, u32[]{:S(2)}) collective-permute-start(bf16[4,128,2048]{2,1,0:T(8,128)(2,1)} %constant_dynamic-slice_fusion), channel_id=1, source_target_pairs={{0,1},{1,0},{2,3},{3,2},{4,5},{5,4},{6,7},{7,6},{8,9},{9,8},{10,11... | collective-permute-start | bytes 6291464 | tf_op jit(solution)/shard_map/ppermute | solution.py:39
  1101.8 76.1 %collective-permute-start.12 = (bf16[4,1,128,1024]{3,2,0,1:T(8,128)(2,1)S(1)}, bf16[4,1,128,1024]{3,2,0,1:T(8,128)(2,1)}, u32[]{:S(2)}, u32[]{:S(2)}) collective-permute-start(bf16[4,1,128,1024]{3,2,0,1:T(8,128)(2,1)S(1)} %dynamic-slice_bitcast_fusion.4), channel_id=1, source_target_pairs={{0,2},{2,0},{1,3},{3,1},{4,6},{6,4},{5,7},{7,5},{8,10},{10,8},{9,1... | collective-permute-start | bytes 3145736 | tf_op jit(solution)/shard_map/ppermute | solution.py:39
  1146.7 44.8 %collective-permute-start.14 = (bf16[4,1,128,1024]{3,2,0,1:T(8,128)(2,1)}, bf16[4,1,128,1024]{3,2,0,1:T(8,128)(2,1)}, u32[]{:S(2)}, u32[]{:S(2)}) collective-permute-start(bf16[4,1,128,1024]{3,2,0,1:T(8,128)(2,1)} %dynamic-slice_bitcast_fusion.3), channel_id=1, source_target_pairs={{0,2},{2,0},{1,3},{3,1},{4,6},{6,4},{5,7},{7,5},{8,10},{10,8},{9,1... | collective-permute-start | bytes 3145736 | tf_op jit(solution)/shard_map/ppermute | solution.py:39
  1155.4 38.7 %all-to-all-start.1 = ((f32[32,1,384]{2,1,0:T(1,128)}), f32[32,1,384]{2,1,0:T(1,128)S(1)}, u32[]{:S(2)}, u32[]{:S(2)}) async-start(f32[32,1,384]{2,1,0:T(1,128)} %reshape.503), calls=%async_computation.3 | async-start | bytes 98304 | tf_op jit(solution)/shard_map/all_to_all | solution.py:1163
  1171.0 47.3 %collective-permute-start.16 = (bf16[4,1,128,2048]{3,2,0,1:T(8,128)(2,1)}, bf16[4,1,128,2048]{3,2,0,1:T(8,128)(2,1)}, u32[]{:S(2)}, u32[]{:S(2)}) collective-permute-start(bf16[4,1,128,2048]{3,2,0,1:T(8,128)(2,1)} %dynamic-slice_bitcast_fusion.1), channel_id=1, source_target_pairs={{0,16},{16,0},{1,17},{17,1},{2,18},{18,2},{3,19},{19,3},{4,20},{20... | collective-permute-start | bytes 6291464 | tf_op jit(solution)/shard_map/ppermute | solution.py:39
  (90 other events, 1260.8 us)
Sparse Core Ops, SparseCore 0:
  169.8 96.0 all-gather.4
  270.5 60.0 all-gather.8
  333.1 54.2 all-gather.6
  491.6 143.8 reduce-scatter.6
  647.9 59.6 reduce-scatter.8
  709.7 60.2 reduce-scatter.12
  772.4 144.4 reduce-scatter.10
  919.3 60.9 reduce-scatter.16
  983.3 143.7 reduce-scatter.14

commit v9 on v8

--- a/solution.py
+++ b/solution.py
@@ -384,11 +384,30 @@
     return weights.reshape(width, 4 * columns), tokens, grads, segments
 
 
-def last_kernel(grads, tokens, output, grads_out, tokens_out, output_out, send, recv, row_send, row_recv, local):
+def last_kernel(
+    grads,
+    tokens,
+    output,
+    grads_out,
+    tokens_out,
+    output_out,
+    mine,
+    theirs,
+    pair_send,
+    pair_recv,
+    send,
+    recv,
+    row_send,
+    row_recv,
+    local,
+):
     z, core = lax.axis_index("seq"), lax.axis_index("core")
     seq_n, piece = tokens.shape[:2]
     seq_count = tokens_out.shape[0]
     rows = grads.shape[1] // 2
+    odd = lax.rem(z, 2)
+    neighbour = z + 1 - 2 * odd
+    far = lax.rem(z + 2, seq_n)
 
     barrier = pltpu.get_barrier_semaphore()
     partners = [
@@ -401,26 +420,57 @@
         pl.semaphore_signal(barrier, inc=1, device_id=partner, device_id_type=MESH)
     pl.semaphore_wait(barrier, len(partners))
 
-    def grad_copy(dz, dc):
-        z_to, core_to = lax.rem(z + dz, seq_n), lax.rem(core + dc, 2)
-        source = grads.at[z_to, pl.ds(pl.multiple_of(core_to * rows, rows), rows), :]
-        target = grads_out.at[core, z]
-        if not (dz or dc):
-            return pltpu.make_async_copy(source, target, local.at[2])
-        return pltpu.make_async_remote_copy(
-            source,
-            target,
-            send.at[dz, dc],
-            recv.at[dz, dc],
-            device_id={"seq": z_to, "core": core_to},
+    pair = [
+        pltpu.make_async_remote_copy(
+            grads.at[2 * i + 1 - odd],
+            theirs.at[i],
+            pair_send.at[i],
+            pair_recv.at[i],
+            device_id={"seq": neighbour},
             device_id_type=MESH,
         )
-
-    def grad_arrival(dz, dc):
-        z_from, core_from = lax.rem(z + seq_n - dz, seq_n), lax.rem(core + dc, 2)
-        ref = grads_out.at[core_from, z_from]
+        for i in range(2)
+    ]
+    kept = [pltpu.make_async_copy(grads.at[2 * i + odd], mine.at[i], local.at[3 + i]) for i in range(2)]
+
+    def rows_to(core_to):
+        return pl.ds(pl.multiple_of(core_to * rows, rows), rows)
+
+    def far_copy(dc):
+        core_to = lax.rem(core + dc, 2)
         return pltpu.make_async_remote_copy(
-            ref, ref, send.at[dz, dc], recv.at[dz, dc], device_id=partners[0], device_id_type=MESH
+            mine.at[far // 2, rows_to(core_to), :],
+            grads_out.at[core, 1],
+            send.at[1, dc],
+            recv.at[1, dc],
+            device_id={"seq": far, "core": core_to},
+            device_id_type=MESH,
+        )
+
+    def near_copy():
+        return pltpu.make_async_remote_copy(
+            mine.at[z // 2, rows_to(1 - core), :],
+            grads_out.at[core, 0],
+            send.at[0, 1],
+            recv.at[0, 1],
+            device_id={"core": 1 - core},
+            device_id_type=MESH,
+        )
+
+    def own_copy():
+        return pltpu.make_async_copy(
+            mine.at[z // 2, rows_to(core), :], grads_out.at[core, 0], local.at[2]
+        )
+
+    def arrival(place, dc):
+        ref = grads_out.at[lax.rem(core + dc, 2), place]
+        return pltpu.make_async_remote_copy(
+            ref,
+            ref,
+            send.at[place, dc],
+            recv.at[place, dc],
+            device_id={"core": 1 - core},
+            device_id_type=MESH,
         )
 
     group, member = z // seq_count, lax.rem(z, seq_count)
@@ -458,15 +508,32 @@
                             )
                         )
 
-    every = [(dz, dc) for dz in range(seq_n) for dc in range(2)]
-    for dz, dc in reversed(every):
-        grad_copy(dz, dc).start()
+    for copy in pair + kept:
+        copy.start()
     each_row(lambda copy: copy.start(), lambda copy: copy.start())
 
-    grad_copy(0, 0).wait()
-    for dz, dc in every[1:]:
-        grad_copy(dz, dc).wait_send()
-        grad_arrival(dz, dc).wait_recv()
+    for copy in kept:
+        copy.wait()
+    for copy in pair:
+        copy.wait_recv()
+    step = mine.shape[1] // 8
+
+    def add(i, carry):
+        span = pl.ds(pl.multiple_of(i * step, step), step)
+        for part in range(2):
+            mine[part, span, :] = total(mine[part, span, :], theirs[part, span, :]).astype(bf16)
+        return carry
+
+    lax.fori_loop(0, 8, add, 0)
+    for copy in (far_copy(0), far_copy(1), near_copy(), own_copy()):
+        copy.start()
+    for copy in pair:
+        copy.wait_send()
+    own_copy().wait()
+    for copy in (far_copy(0), far_copy(1), near_copy()):
+        copy.wait_send()
+    for place, dc in ((1, 0), (1, 1), (0, 1)):
+        arrival(place, dc).wait_recv()
     each_row(lambda copy: copy.wait_send(), lambda copy: copy.wait())
     for n, target in ((0, tokens_out), (1, output_out)):
         for s in range(seq_count):
@@ -496,15 +563,21 @@
         last_kernel,
         in_specs=[held] * 3,
         out_specs=[held] * 3,
-        out_shape=[jax.ShapeDtypeStruct((2, seq_n, rows, grads.shape[2]), bf16), out, out],
+        out_shape=[jax.ShapeDtypeStruct((2, 2, rows, grads.shape[2]), bf16), out, out],
         scratch_shapes=[
-            dma((seq_n, 2)),
-            dma((seq_n, 2)),
+            pltpu.VMEM((2,) + grads.shape[1:], bf16),
+            pltpu.VMEM((2,) + grads.shape[1:], bf16),
+            dma((2,)),
+            dma((2,)),
+            dma((2, 2)),
+            dma((2, 2)),
             dma((2, seq_n)),
             dma((2, seq_count, 2)),
-            dma((3,)),
+            dma((5,)),
         ],
-        compiler_params=pltpu.CompilerParams(collective_id=1, has_side_effects=True),
+        compiler_params=pltpu.CompilerParams(
+            collective_id=1, has_side_effects=True, vmem_limit_bytes=24 * 2**20
+        ),
         cost_estimate=pl.CostEstimate(flops=0, bytes_accessed=4 * grads.size, transcendentals=0),
         name="last_transfers",
     )(grads, tokens, output)
@@ -1084,8 +1157,10 @@
     dsel = gates * (dgate - jnp.sum(gates * dgate, axis=0, keepdims=True))
     dlogits = jnp.sum(jnp.where(hot, dsel[:, :, None], 0.0), axis=0).astype(bf16)
     router_grad = t_product(hidden_two, dlogits)
+    up_b = rows_product(expert_in, after(dupre_b, gate_a))
+
     def once_gate(stage, *arrays):
-        return (after(arrays[0], gate_a),) + arrays[1:] if stage == 0 else arrays
+        return (after(arrays[0], up_b if stage else gate_a),) + arrays[1:]
 
     dhidden_two = plane_scatter(back, once_gate).reshape(home, width) + product_t(dlogits, router)
 
@@ -1105,15 +1180,15 @@
         return arrays
 
     mixture = plane_scatter(after(mixed_rows, dbranch), check)
-    up_b = rows_product(expert_in, after(dupre_b, dbranch))
     dqpre, dkpre, dvpre = attend_back(
         query, keys, values, mixed, dmixed, cosine, sine, seg_row, seg_col, heads, down_sum_b, up_b, *stages[0]
     )
     dqkv = jnp.concatenate([dqpre, dkpre, dvpre], axis=1)
-    out_grad = t_product(mixed_full, after(dbranch_here, dqpre)).astype(bf16)
+    out_grad = t_product(mixed_full, after(dbranch_here, dqpre, *stages[1])).astype(bf16)
     in_grad = t_product(hidden_full, after(dqkv, out_grad)).astype(bf16)
     up_a = rows_product(expert_in, after(dupre_a, in_grad))
-    dhidden_part = product_t(after(dqkv, up_a, *stages[1]), weight_in).astype(bf16)
+    output = (residual + mixture).astype(bf16)
+    dhidden_part = product_t(after(dqkv, up_a, output), weight_in).astype(bf16)
     dhidden_one = chip_scatter(
         dhidden_part.reshape(seq_n, parts * piece, width), 1, parts
     )
@@ -1125,7 +1200,6 @@
         attn_norm,
     )
     dtokens = (dtokens + dresid).astype(bf16).reshape(seq_n, piece, width)
-    output = (residual + mixture).astype(bf16)
 
     grad_down = jnp.concatenate([down_sum_a, down_sum_b], axis=1).astype(f32).T[None]
     grad_gate = jnp.concatenate([gate_sum_a, gate_sum_b], axis=1).astype(f32)[None]
@@ -1142,11 +1216,11 @@
     first.append(half(seen(in_grad[:, columns:]), 3, y_i, "y"))
     second = [half(a, 2, y_i, "y") for a in first[:2]] + [half(first[2], 0, dp_i, "dp")]
     second = jnp.concatenate(second, axis=-1)
-    if r_n == 1 and parts == 2 and seq_n == 2 * seq_count:
+    if r_n == 1 and parts == 2 and seq_n == 2 * seq_count == 4:
         part, grad_tokens, output = last_transfers(
             second.reshape(seq_n, core_n * rows_here, 4 * columns), dtokens, output, seq_count
         )
-        part = total(*(part[:, i] for i in range(seq_n))).reshape(core_n, rows_here, 4, columns)
+        part = total(part[:, 0], part[:, 1]).reshape(core_n, rows_here, 4, columns)
         part = part.transpose(1, 2, 0, 3).reshape(rows_here, 4, width)
     else:
         grad_tokens = from_sequences(dtokens)

time: 1450 us -> 1420 us (0.979)
  Pallas kernels: 714 us -> 679 us
    pallas_call x1, Pallas kernels: 175 us -> 140 us  [last_transfers(): pl.pallas_call(last_kernel, in_specs=[held] * 3, out_specs=[held] * 3, ou...]
    all_to_all x1, waiting for transfers between devices: 0.01 us -> 23.8 us  [on_device(): lax.all_to_all(gains, EVERY, split_axis=0, concat_axis=0, tiled=True)]
    unnamed x169 -> x175, local copies, waits for them, and re-layouts: 50.4 us -> 56.5 us
  transfers between devices with their start and end apart: 33 -> 33, of which waited for: 14 -> 15; matrix products, arithmetic and copies ran while one was open for 27% -> 27% of each run, Pallas kernels for 34% -> 32%
where the time goes in v9:
time: 1420 us; the launch traced here: 1410 us
  Pallas kernels  679 us (48%)
  matrix products  214 us (15%)
  waiting for transfers between devices  178 us (13%)
  local copies, waits for them, and re-layouts  129 us (9%)
  other arithmetic  121 us (9%)
  blocking collectives  44.7 us (3%)
  starting transfers between devices  31.3 us (2%)
  between operations  15.2 us (1%)
    pallas_call x1, Pallas kernels, first_transfers(): pl.pallas_call(first_kernel, in_specs=[held] * 7, out_specs=[held] * 4, o...  162 us
    dot_general x9, matrix products, t_product(): lax.dot_general(a, b, (((0,), (0,)), ((), ())), preferred_element_type=f32)  156 us
    pallas_call x1, Pallas kernels, last_transfers(): pl.pallas_call(last_kernel, in_specs=[held] * 3, out_specs=[held] * 3, ou...  140 us
    ppermute x22, waiting for transfers between devices, swap(): return lax.ppermute(a, axis, [(0, 1), (1, 0)])  137 us
    pallas_call x3, Pallas kernels, expert_units(): pl.pallas_call(functools.partial(units_kernel, chunk), grid=(units // til...  135 us
    pallas_call x2, Pallas kernels, expert_input_grad(): pl.pallas_call(functools.partial(input_kernel, cut), grid=(width // n, ro...  77.9 us
    unnamed x175, local copies, waits for them, and re-layouts  56.5 us
    all_gather x1, blocking collectives, on_device(): lax.all_gather(small, EVERY, axis=0, tiled=True)  44.7 us
  transfers between devices with their start and end apart: 33, of which 15 were waited for; matrix products, arithmetic and copies ran while one was open for 27% of the time, Pallas kernels for 32%

profile of v9, /device:TPU:1, one launch (start us, length us, event | category | flops | bytes accessed | tf_op | source)
XLA Modules:
  0.0 1411.9 jit_solution(13847864710615332055)
XLA Ops:
  7.2 162.4 %first_transfers.1 = (bf16[2,4,2,128,4096]{4,3,2,1,0:T(8,128)(2,1)}, bf16[4,128,2048]{2,1,0:T(8,128)(2,1)}, bf16[4,128,2048]{2,1,0:T(8,128)(2,1)}, s32[2,2,1024]{2,1,0:T(2,128)}) custom-call(bf16[64,2048]{1,0:T(8,128)(2,1)} %query.1, bf16[64,2048]{1,0:T(8,128)(2,1)} %key.1, bf16[64,2048]{1,0:T(8,128)(2,1)} %value.1, bf16[64,2048]{1,0:T(8,128)(2,1)} %output.1, ...), custom_call_target="tpu_custom_call" | custom-call | bytes 16777216 | tf_op jit(solution)/shard_map/first_transfers/pallas_call | solution.py:360
  183.7 19.9 %fusion.4.qp.kp.vp = f32[1024,3072]{1,0:T(8,128)} fusion(bf16[1024,2048]{1,0:T(8,128)(2,1)S(1)} %bitcast.311, bf16[2048,4096]{1,0:T(8,128)(2,1)} %bitcast.331), kind=kOutput, calls=%fused_computation.7 | convolution fusion | flops 12884901888 | bytes 29360128 | tf_op jit(solution)/shard_map/dot_general | solution.py:27
  203.6 27.9 %attend.1 = (bf16[1024,1024]{1,0:T(8,128)(2,1)S(1)}, bf16[1024,1024]{1,0:T(8,128)(2,1)S(1)}, bf16[1024,1024]{1,0:T(8,128)(2,1)}, bf16[1024,1024]{1,0:T(8,128)(2,1)}) custom-call(f32[1024,3072]{1,0:T(8,128)} %fusion.4.qp.kp.vp, f32[1024,3072]{1,0:T(8,128)} %fusion.4.qp.kp.vp, f32[1024,3072]{1,0:T(8,128)} %fusion.4.qp.kp.vp, ...), custom_call_target="tpu_custom_call" | custom-call | flops 2684354560 | bytes 20971520 | tf_op jit(solution)/shard_map/attend/pallas_call | solution.py:625
  272.1 44.7 %all-gather = s32[32,4,256]{2,1,0:T(4,128)S(1)} all-gather(s32[1,4,256]{2,1,0:T(4,128)} %bitcast.323), channel_id=1, replica_groups=mesh['dp'=2,'seq'=4,'r'=1,'y'=2,'core'=2] {'dp','seq','r','y','core'}, dimensions={0}, use_global_device_ids=true | all-gather | bytes 135168 | tf_op jit(solution)/shard_map/all_gather | solution.py:1090
  347.9 47.7 %expert_units.3 = (bf16[2560,2048]{1,0:T(8,128)(2,1)}, bf16[2560,2048]{1,0:T(8,128)(2,1)}, bf16[2560,2048]{1,0:T(8,128)(2,1)}) custom-call(bf16[2560,2048]{1,0:T(8,128)(2,1)} %bitcast.294, bf16[2560,2048]{1,0:T(8,128)(2,1)} %bitcast.301, bf16[2048,2816]{1,0:T(8,128)(2,1)} %bitcast.335, bf16[2048,2816]{1,0:T(8,128)(2,1)} %bitcast.340, ...), custom_call_target="tpu_custom_call" | custom-call | flops 32212254720 | bytes 51380224 | tf_op jit(solution)/shard_map/expert_units/pallas_call | solution.py:730
  414.5 47.8 %expert_units.4 = (bf16[2560,2048]{1,0:T(8,128)(2,1)}, bf16[2560,2048]{1,0:T(8,128)(2,1)}, bf16[2560,2048]{1,0:T(8,128)(2,1)}) custom-call(bf16[2560,2048]{1,0:T(8,128)(2,1)} %bitcast.295, bf16[2560,2048]{1,0:T(8,128)(2,1)} %bitcast.302, bf16[2048,2816]{1,0:T(8,128)(2,1)} %bitcast.336, ...), custom_call_target="tpu_custom_call", output_to_operand_aliasing={{0}: (5, {}), {1}: (6, {}), {2}: (7, {})} | custom-call | flops 32212254720 | bytes 51380224 | tf_op jit(solution)/shard_map/expert_units/pallas_call | solution.py:730
  462.3 28.9 %convolution_convert_fusion.3.rest_0_ = bf16[2048,2048]{1,0:T(8,128)(2,1)} fusion(bf16[2560,2048]{1,0:T(8,128)(2,1)} %bitcast.303, bf16[2560,2048]{1,0:T(8,128)(2,1)} %get-tuple-element.57.units_a), kind=kOutput, calls=%fused_computation.17 | convolution fusion | flops 21479030784 | bytes 29360128 | tf_op jit(solution)/shard_map/dot_general | solution.py:35
  491.9 40.0 %expert_units.5 = (bf16[2560,768]{1,0:T(8,128)(2,1)}, bf16[2560,768]{1,0:T(8,128)(2,1)}, bf16[2560,768]{1,0:T(8,128)(2,1)}) custom-call(bf16[2560,2048]{1,0:T(8,128)(2,1)} %bitcast.296, bf16[2560,2048]{1,0:T(8,128)(2,1)} %bitcast.304, bf16[2048,2816]{1,0:T(8,128)(2,1)} %bitcast.337, bf16[2048,2816]{1,0:T(8,128)(2,1)} %bitcast.342, ...), custom_call_target="tpu_custom_call" | custom-call | flops 24159191040 | bytes 42205184 | tf_op jit(solution)/shard_map/expert_units/pallas_call | solution.py:730
  531.9 13.6 convolution_convert_fusion.8.rest_0_
  545.6 39.0 %expert_input_grad.2.rest_0_ = bf16[2560,1024]{1,0:T(8,128)(2,1)} custom-call(bf16[2560,2048]{1,0:T(8,128)(2,1)} %get-tuple-element.56.dgate_a.refs_0_, bf16[2560,768]{1,0:T(8,128)(2,1)} %get-tuple-element.58.dgate_b.refs_0_, bf16[2560,2048]{1,0:T(8,128)(2,1)} %get-tuple-element.59.dup_a.refs_0_, bf16[2560,768]{1,0:T(8,128)(2,1)} %get-tuple-element.60.dup_b.refs_0_, ...), custom_call_target="tpu_custom_call" | custom-call | flops 29527900160 | bytes 45613056 | tf_op jit(solution)/shard_map/expert_input_grad/pallas_call | solution.py:958
  584.5 39.0 %expert_input_grad.3 = bf16[2560,1024]{1,0:T(8,128)(2,1)} custom-call(bf16[2560,2048]{1,0:T(8,128)(2,1)} %get-tuple-element.56.dgate_a.refs_0_, bf16[2560,768]{1,0:T(8,128)(2,1)} %get-tuple-element.58.dgate_b.refs_0_, bf16[2560,2048]{1,0:T(8,128)(2,1)} %get-tuple-element.59.dup_a.refs_0_, bf16[2560,768]{1,0:T(8,128)(2,1)} %get-tuple-element.60.dup_b.refs_0_, ...), custom_call_target="tpu_custom_call" | custom-call | flops 29527900160 | bytes 45613056 | tf_op jit(solution)/shard_map/expert_input_grad/pallas_call | solution.py:958
  675.3 29.0 %convolution_convert_fusion.2.refs_1_.rest_0_ = bf16[2048,2048]{1,0:T(8,128)(2,1)} fusion(bf16[2560,2048]{1,0:T(8,128)(2,1)} %bitcast.298, bf16[2560,2048]{1,0:T(8,128)(2,1)} %after.14), kind=kOutput, calls=%fused_computation.16 | convolution fusion | flops 21479030784 | bytes 29360128 | tf_op jit(solution)/shard_map/dot_general | solution.py:35
  743.8 40.7 %expert_down.1 = bf16[2560,2048]{1,0:T(8,128)(2,1)} custom-call(bf16[2560,2048]{1,0:T(8,128)(2,1)} %get-tuple-element.57.units_a, bf16[2560,768]{1,0:T(8,128)(2,1)S(1)} %copy-done.27, bf16[2816,2048]{1,0:T(8,128)(2,1)} %bitcast.348, bf16[2048,2048]{1,0:T(8,128)(2,1)} %convolution_convert_fusion.2.refs_1_.rest_0_), custom_call_target="tpu_custom_call" | custom-call | flops 29527900160 | bytes 36438016 | tf_op jit(solution)/shard_map/expert_down/pallas_call | solution.py:922
  784.5 24.2 %combine.1 = (bf16[2,2,2,4,128,2048]{5,4,3,2,1,0:T(8,128)(2,1)}, f32[16,256,1]{2,1,0:T(8,128)S(1)}) custom-call(s32[4]{0:T(128)S(1)} %pad_add_fusion.me, bf16[16,160,2048]{2,1,0:T(8,128)(2,1)} %bitcast.293, s32[16,256,1]{2,1,0:T(8,128)S(1)} %copy.138.slot, f32[16,256,1]{2,1,0:T(8,128)S(1)} %copy-done.5, bf16[4,2,4,128,2048]{4,3,2,1,0:T(8,128)(2,1)} %bitcast.284), custom_call_target="tpu_custom_call" | custom-call | flops 2684354560 | bytes 44040192 | tf_op jit(solution)/shard_map/combine/pallas_call | solution.py:897
  881.4 31.8 %attend_back.1 = (bf16[1024,1024]{1,0:T(8,128)(2,1)S(1)}, bf16[1024,1024]{1,0:T(8,128)(2,1)}, bf16[1024,1024]{1,0:T(8,128)(2,1)}) custom-call(bf16[1024,1024]{1,0:T(8,128)(2,1)} %copy-done.25, bf16[1024,1024]{1,0:T(8,128)(2,1)} %copy-done.26, bf16[1024,1024]{1,0:T(8,128)(2,1)} %get-tuple-element.66.v, bf16[1024,1024]{1,0:T(8,128)(2,1)} %get-tuple-element.46.mixed, ...), custom_call_target="tpu_custom_call" | custom-call | flops 6710886400 | bytes 16777216 | tf_op jit(solution)/shard_map/attend_back/pallas_call | solution.py:685
  937.4 19.7 %convolution_convert_fusion.refs_1_ = bf16[2048,3072]{1,0:T(8,128)(2,1)} fusion(bf16[1024,2048]{1,0:T(8,128)(2,1)} %bitcast.312, bf16[1024,3072]{1,0:T(8,128)(2,1)} %after.20), kind=kOutput, calls=%fused_computation.4 | convolution fusion | flops 12891193344 | bytes 23068672 | tf_op jit(solution)/shard_map/dot_general | solution.py:35
  957.1 29.3 %convolution_convert_fusion.1.refs_1_ = bf16[2048,2048]{1,0:T(8,128)(2,1)} fusion(bf16[2560,2048]{1,0:T(8,128)(2,1)} %bitcast.300, bf16[2560,2048]{1,0:T(8,128)(2,1)} %after.21), kind=kOutput, calls=%fused_computation.15 | convolution fusion | flops 21479030784 | bytes 29360128 | tf_op jit(solution)/shard_map/dot_general | solution.py:35
  1019.9 18.8 %collective-permute-done.13 = bf16[4,1,2,128,1024]{4,3,0,2,1:T(8,128)(2,1)} collective-permute-done((bf16[4,1,2,128,1024]{4,3,0,2,1:T(8,128)(2,1)}, bf16[4,1,2,128,1024]{4,3,0,2,1:T(8,128)(2,1)}, u32[]{:S(2)}, u32[]{:S(2)}) %collective-permute-start.13) | collective-permute-done | bytes 2097184 | tf_op jit(solution)/shard_map/ppermute | solution.py:39
  1044.3 39.3 %collective-permute-done.19 = bf16[4,128,2048]{2,1,0:T(8,128)(2,1)} collective-permute-done((bf16[4,128,2048]{2,1,0:T(8,128)(2,1)}, bf16[4,128,2048]{2,1,0:T(8,128)(2,1)}, u32[]{:S(2)}, u32[]{:S(2)}) %collective-permute-start.19) | collective-permute-done | bytes 2097184 | tf_op jit(solution)/shard_map/ppermute | solution.py:39
  1088.3 17.8 %fusion.24 = bf16[1024,2048]{1,0:T(8,128)(2,1)S(1)} fusion(bf16[1024,3072]{1,0:T(8,128)(2,1)} %after.22, bf16[2048,4096]{1,0:T(8,128)(2,1)} %bitcast.334), kind=kOutput, calls=%fused_computation.63 | convolution fusion | flops 12886999040 | bytes 23068672 | tf_op jit(solution)/shard_map/dot_general | solution.py:31
  1110.5 18.1 %collective-permute-done.15 = bf16[4,1,2,128,1024]{4,3,0,2,1:T(8,128)(2,1)} collective-permute-done((bf16[4,1,2,128,1024]{4,3,0,2,1:T(8,128)(2,1)}, bf16[4,1,2,128,1024]{4,3,0,2,1:T(8,128)(2,1)}, u32[]{:S(2)}, u32[]{:S(2)}) %collective-permute-start.15) | collective-permute-done | bytes 2097184 | tf_op jit(solution)/shard_map/ppermute | solution.py:39
  1153.6 20.8 %collective-permute-done.16 = bf16[4,1,128,1024]{3,2,0,1:T(8,128)(2,1)} collective-permute-done((bf16[4,1,128,1024]{3,2,0,1:T(8,128)(2,1)}, bf16[4,1,128,1024]{3,2,0,1:T(8,128)(2,1)}, u32[]{:S(2)}, u32[]{:S(2)}) %collective-permute-start.16) | collective-permute-done | bytes 1048608 | tf_op jit(solution)/shard_map/ppermute | solution.py:39
  1209.6 23.8 %all-to-all-done.1 = f32[32,1,384]{2,1,0:T(1,128)S(1)} async-done(((f32[32,1,384]{2,1,0:T(1,128)}), f32[32,1,384]{2,1,0:T(1,128)S(1)}, u32[]{:S(2)}, u32[]{:S(2)}) %all-to-all-start.1) | async-done | bytes 49184 | tf_op jit(solution)/shard_map/all_to_all | solution.py:1237
  1240.7 140.2 %last_transfers.1 = (bf16[2,2,64,4096]{3,2,1,0:T(8,128)(2,1)S(1)}, bf16[2,256,2048]{2,1,0:T(8,128)(2,1)S(1)}, bf16[2,256,2048]{2,1,0:T(8,128)(2,1)S(1)}) custom-call(bf16[4,128,4096]{2,1,0:T(8,128)(2,1)S(1)} %maximum_bitcast_fusion.1.grads, bf16[4,128,2048]{2,1,0:T(8,128)(2,1)S(1)} %bitcast.279, bf16[4,128,2048]{2,1,0:T(8,128)(2,1)S(1)} %copy-done), custom_call_target="tpu_custom_call" | custom-call | bytes 8388608 | tf_op jit(solution)/shard_map/last_transfers/pallas_call | solution.py:562
  (375 shorter events, 432.2 us)
Async XLA Ops:
  7.2 259.8 %all-gather.5.cloned.1.call-start = ((), (), s32[]{:S(2)}) async-start(), calls=%async_computation.8 | async-start | bytes 18874368 | tf_op jit(solution)/shard_map/all_gather | solution.py:1066
  169.7 160.4 %all-gather.9.cloned.1.call-start = ((), (), s32[]{:S(2)}) async-start(), calls=%async_computation.10 | async-start | bytes 9437184 | tf_op jit(solution)/shard_map/all_gather | solution.py:1087
  270.1 125.5 %all-gather.7.cloned.1.call-start = ((), (), s32[]{:S(2)}) async-start(), calls=%async_computation.9 | async-start | bytes 9437184 | tf_op jit(solution)/shard_map/all_gather | solution.py:1087
  270.9 404.4 %reduce-scatter.7.cloned.1.call-start = ((), (), s32[]{:S(2)}) async-start(), calls=%async_computation.11 | async-start | bytes 10485760 | tf_op jit(solution)/shard_map/reduce_scatter | solution.py:1126
  491.2 387.9 %reduce-scatter.9.cloned.1.call-start = ((), (), s32[]{:S(2)}) async-start(), calls=%async_computation.12 | async-start | bytes 3932160 | tf_op jit(solution)/shard_map/reduce_scatter | solution.py:1126
  545.5 590.2 %reduce-scatter.13.cloned.1.call-start = ((), (), s32[]{:S(2)}) async-start(), calls=%async_computation.14 | async-start | bytes 3932160 | tf_op jit(solution)/shard_map/reduce_scatter | solution.py:1126
  661.5 474.3 %reduce-scatter.11.cloned.1.call-start = ((), (), s32[]{:S(2)}) async-start(), calls=%async_computation.13 | async-start | bytes 10485760 | tf_op jit(solution)/shard_map/reduce_scatter | solution.py:1126
  708.4 25.0 %collective-permute-start.6 = (bf16[2,128,2048]{2,1,0:T(8,128)(2,1)}, bf16[2,128,2048]{2,1,0:T(8,128)(2,1)}, u32[]{:S(2)}, u32[]{:S(2)}) collective-permute-start(bf16[2,128,2048]{2,1,0:T(8,128)(2,1)} %get-tuple-element.153), channel_id=1, source_target_pairs={{0,16},{16,0},{1,17},{17,1},{2,18},{18,2},{3,19},{19,3},{4,20},{20... | collective-permute-start | bytes 3145736 | tf_op jit(solution)/shard_map/ppermute | solution.py:39
  738.8 83.6 %collective-permute-start.7 = (bf16[4,128,2048]{2,1,0:T(8,128)(2,1)}, bf16[4,128,2048]{2,1,0:T(8,128)(2,1)}, u32[]{:S(2)}, u32[]{:S(2)}) collective-permute-start(bf16[4,128,2048]{2,1,0:T(8,128)(2,1)} %pad_maximum_fusion.6), channel_id=1, source_target_pairs={{0,2},{2,0},{1,3},{3,1},{4,6},{6,4},{5,7},{7,5},{8,10},{10,8},{9,1... | collective-permute-start | bytes 6291464 | tf_op jit(solution)/shard_map/ppermute | solution.py:39
  740.9 81.5 %collective-permute-start.5 = (bf16[4,128,2048]{2,1,0:T(8,128)(2,1)}, bf16[4,128,2048]{2,1,0:T(8,128)(2,1)}, u32[]{:S(2)}, u32[]{:S(2)}) collective-permute-start(bf16[4,128,2048]{2,1,0:T(8,128)(2,1)} %after.17), channel_id=1, source_target_pairs={{0,16},{16,0},{1,17},{17,1},{2,18},{18,2},{3,19},{19,3},{4,20},{20... | collective-permute-start | bytes 6291464 | tf_op jit(solution)/shard_map/ppermute | solution.py:39
  817.8 581.1 %reduce-scatter.17.cloned.1.call-start = ((), (), s32[]{:S(2)}) async-start(), calls=%async_computation.16 | async-start | bytes 3932160 | tf_op jit(solution)/shard_map/reduce_scatter | solution.py:1126
  859.3 539.6 %reduce-scatter.15.cloned.1.call-start = ((), (), s32[]{:S(2)}) async-start(), calls=%async_computation.15 | async-start | bytes 10485760 | tf_op jit(solution)/shard_map/reduce_scatter | solution.py:1126
  879.0 41.8 %collective-permute-start.12 = (bf16[2,128,2048]{2,1,0:T(8,128)(2,1)}, bf16[2,128,2048]{2,1,0:T(8,128)(2,1)}, u32[]{:S(2)}, u32[]{:S(2)}) collective-permute-start(bf16[2,128,2048]{2,1,0:T(8,128)(2,1)} %get-tuple-element.147), channel_id=1, source_target_pairs={{0,16},{16,0},{1,17},{17,1},{2,18},{18,2},{3,19},{19,3},{4,20},{20... | collective-permute-start | bytes 3145736 | tf_op jit(solution)/shard_map/ppermute | solution.py:39
  879.1 41.8 %collective-permute-start.11 = (bf16[2,128,2048]{2,1,0:T(8,128)(2,1)}, bf16[2,128,2048]{2,1,0:T(8,128)(2,1)}, u32[]{:S(2)}, u32[]{:S(2)}) collective-permute-start(bf16[2,128,2048]{2,1,0:T(8,128)(2,1)} %get-tuple-element.149), channel_id=1, source_target_pairs={{0,2},{2,0},{1,3},{3,1},{4,6},{6,4},{5,7},{7,5},{8,10},{10,8},{9,1... | collective-permute-start | bytes 3145736 | tf_op jit(solution)/shard_map/ppermute | solution.py:39
  992.0 46.7 %collective-permute-start.13 = (bf16[4,1,2,128,1024]{4,3,0,2,1:T(8,128)(2,1)}, bf16[4,1,2,128,1024]{4,3,0,2,1:T(8,128)(2,1)}, u32[]{:S(2)}, u32[]{:S(2)}) collective-permute-start(bf16[4,1,2,128,1024]{4,3,0,2,1:T(8,128)(2,1)} %bitcast.274), channel_id=1, source_target_pairs={{0,16},{16,0},{1,17},{17,1},{2,18},{18,2},{3,19},{19,3},{4,20},{20... | collective-permute-start | bytes 6291464 | tf_op jit(solution)/shard_map/ppermute | solution.py:39
  993.4 90.3 %collective-permute-start.19 = (bf16[4,128,2048]{2,1,0:T(8,128)(2,1)}, bf16[4,128,2048]{2,1,0:T(8,128)(2,1)}, u32[]{:S(2)}, u32[]{:S(2)}) collective-permute-start(bf16[4,128,2048]{2,1,0:T(8,128)(2,1)} %pad_maximum_fusion.7.refs_2_), channel_id=1, source_target_pairs={{0,16},{16,0},{1,17},{17,1},{2,18},{18,2},{3,19},{19,3},{4,20},{20... | collective-permute-start | bytes 6291464 | tf_op jit(solution)/shard_map/ppermute | solution.py:39
  993.5 90.2 %collective-permute-start.20 = (bf16[4,128,2048]{2,1,0:T(8,128)(2,1)}, bf16[4,128,2048]{2,1,0:T(8,128)(2,1)}, u32[]{:S(2)}, u32[]{:S(2)}) collective-permute-start(bf16[4,128,2048]{2,1,0:T(8,128)(2,1)} %pad_maximum_fusion.8.refs_3_), channel_id=1, source_target_pairs={{0,2},{2,0},{1,3},{3,1},{4,6},{6,4},{5,7},{7,5},{8,10},{10,8},{9,1... | collective-permute-start | bytes 6291464 | tf_op jit(solution)/shard_map/ppermute | solution.py:39
  1015.8 112.8 %collective-permute-start.15 = (bf16[4,1,2,128,1024]{4,3,0,2,1:T(8,128)(2,1)}, bf16[4,1,2,128,1024]{4,3,0,2,1:T(8,128)(2,1)}, u32[]{:S(2)}, u32[]{:S(2)}) collective-permute-start(bf16[4,1,2,128,1024]{4,3,0,2,1:T(8,128)(2,1)} %bitcast.273), channel_id=1, source_target_pairs={{0,16},{16,0},{1,17},{17,1},{2,18},{18,2},{3,19},{19,3},{4,20},{20... | collective-permute-start | bytes 6291464 | tf_op jit(solution)/shard_map/ppermute | solution.py:39
  1019.8 157.3 %collective-permute-start.17 = (bf16[2,4,1,128,2048]{4,3,1,2,0:T(8,128)(2,1)}, bf16[2,4,1,128,2048]{4,3,1,2,0:T(8,128)(2,1)}, u32[]{:S(2)}, u32[]{:S(2)}) collective-permute-start(bf16[2,4,1,128,2048]{4,3,1,2,0:T(8,128)(2,1)} %dynamic-slice_bitcast_fusion), channel_id=1, source_target_pairs={{0,2},{2,0},{1,3},{3,1},{4,6},{6,4},{5,7},{7,5},{8,10},{10,8},{9,1... | collective-permute-start | bytes 12582920 | tf_op jit(solution)/shard_map/ppermute | solution.py:39
  1042.9 109.0 %collective-permute-start.14 = (bf16[4,1,128,1024]{3,2,0,1:T(8,128)(2,1)S(1)}, bf16[4,1,128,1024]{3,2,0,1:T(8,128)(2,1)}, u32[]{:S(2)}, u32[]{:S(2)}) collective-permute-start(bf16[4,1,128,1024]{3,2,0,1:T(8,128)(2,1)S(1)} %dynamic-slice_bitcast_fusion.4), channel_id=1, source_target_pairs={{0,2},{2,0},{1,3},{3,1},{4,6},{6,4},{5,7},{7,5},{8,10},{10,8},{9,1... | collective-permute-start | bytes 3145736 | tf_op jit(solution)/shard_map/ppermute | solution.py:39
  1107.7 77.7 %collective-permute-start.21 = (bf16[4,128,2048]{2,1,0:T(8,128)(2,1)}, bf16[4,128,2048]{2,1,0:T(8,128)(2,1)}, u32[]{:S(2)}, u32[]{:S(2)}) collective-permute-start(bf16[4,128,2048]{2,1,0:T(8,128)(2,1)} %constant_dynamic-slice_fusion), channel_id=1, source_target_pairs={{0,1},{1,0},{2,3},{3,2},{4,5},{5,4},{6,7},{7,6},{8,9},{9,8},{10,11... | collective-permute-start | bytes 6291464 | tf_op jit(solution)/shard_map/ppermute | solution.py:39
  1133.8 40.7 %collective-permute-start.16 = (bf16[4,1,128,1024]{3,2,0,1:T(8,128)(2,1)}, bf16[4,1,128,1024]{3,2,0,1:T(8,128)(2,1)}, u32[]{:S(2)}, u32[]{:S(2)}) collective-permute-start(bf16[4,1,128,1024]{3,2,0,1:T(8,128)(2,1)} %dynamic-slice_bitcast_fusion.3), channel_id=1, source_target_pairs={{0,2},{2,0},{1,3},{3,1},{4,6},{6,4},{5,7},{7,5},{8,10},{10,8},{9,1... | collective-permute-start | bytes 3145736 | tf_op jit(solution)/shard_map/ppermute | solution.py:39
  1184.0 52.0 %collective-permute-start.18 = (bf16[4,1,128,2048]{3,2,0,1:T(8,128)(2,1)}, bf16[4,1,128,2048]{3,2,0,1:T(8,128)(2,1)}, u32[]{:S(2)}, u32[]{:S(2)}) collective-permute-start(bf16[4,1,128,2048]{3,2,0,1:T(8,128)(2,1)} %dynamic-slice_bitcast_fusion.1), channel_id=1, source_target_pairs={{0,16},{16,0},{1,17},{17,1},{2,18},{18,2},{3,19},{19,3},{4,20},{20... | collective-permute-start | bytes 6291464 | tf_op jit(solution)/shard_map/ppermute | solution.py:39
  1194.2 39.2 %all-to-all-start.1 = ((f32[32,1,384]{2,1,0:T(1,128)}), f32[32,1,384]{2,1,0:T(1,128)S(1)}, u32[]{:S(2)}, u32[]{:S(2)}) async-start(f32[32,1,384]{2,1,0:T(1,128)} %reshape.497), calls=%async_computation.3 | async-start | bytes 98304 | tf_op jit(solution)/shard_map/all_to_all | solution.py:1237
  (93 other events, 1059.9 us)
Sparse Core Ops, SparseCore 0:
  169.8 96.0 all-gather.4
  270.3 59.8 all-gather.8
  332.6 54.2 all-gather.6
  491.4 143.8 reduce-scatter.6
  637.4 60.9 reduce-scatter.8
  700.6 60.2 reduce-scatter.12
  763.3 144.4 reduce-scatter.10
  910.1 60.9 reduce-scatter.16
  986.6 145.5 reduce-scatter.14

commit v10 on v9

--- a/solution.py
+++ b/solution.py
@@ -1183,12 +1183,14 @@
     dqpre, dkpre, dvpre = attend_back(
         query, keys, values, mixed, dmixed, cosine, sine, seg_row, seg_col, heads, down_sum_b, up_b, *stages[0]
     )
-    dqkv = jnp.concatenate([dqpre, dkpre, dvpre], axis=1)
-    out_grad = t_product(mixed_full, after(dbranch_here, dqpre, *stages[1])).astype(bf16)
-    in_grad = t_product(hidden_full, after(dqkv, out_grad)).astype(bf16)
-    up_a = rows_product(expert_in, after(dupre_a, in_grad))
+    up_a = rows_product(expert_in, after(dupre_a, dqpre, *stages[1]))
     output = (residual + mixture).astype(bf16)
-    dhidden_part = product_t(after(dqkv, up_a, output), weight_in).astype(bf16)
+    out_grad = t_product(mixed_full, after(dbranch_here, up_a, output)).astype(bf16)
+    dkv = jnp.concatenate([dkpre, dvpre], axis=1)
+    kv_grad = t_product(hidden_full, after(dkv, out_grad)).astype(bf16)
+    query_grad = t_product(hidden_full, after(dqpre, out_grad)).astype(bf16)
+    dqkv = after(jnp.concatenate([dqpre, dkpre, dvpre], axis=1), kv_grad, query_grad)
+    dhidden_part = product_t(dqkv, weight_in).astype(bf16)
     dhidden_one = chip_scatter(
         dhidden_part.reshape(seq_n, parts * piece, width), 1, parts
     )
@@ -1212,8 +1214,8 @@
         keep, give = pick(a, index, axis), pick(a, 1 - index, axis)
         return total(keep, swap(give, name)).astype(bf16)
 
-    first = [half(seen(a), 0, dp_i, "dp") for a in (out_grad, in_grad[:, :columns])]
-    first.append(half(seen(in_grad[:, columns:]), 3, y_i, "y"))
+    first = [half(seen(a), 0, dp_i, "dp") for a in (out_grad, query_grad)]
+    first.append(half(seen(kv_grad), 3, y_i, "y"))
     second = [half(a, 2, y_i, "y") for a in first[:2]] + [half(first[2], 0, dp_i, "dp")]
     second = jnp.concatenate(second, axis=-1)
     if r_n == 1 and parts == 2 and seq_n == 2 * seq_count == 4:

time: 1420 us -> 1370 us (0.965)
  waiting for transfers between devices: 178 us -> 132 us
  local copies, waits for them, and re-layouts: 129 us -> 113 us
    ppermute x22, waiting for transfers between devices: 137 us -> 85.3 us  [swap(): return lax.ppermute(a, axis, [(0, 1), (1, 0)])]
    unnamed x175 -> x170, local copies, waits for them, and re-layouts: 56.5 us -> 49.3 us
    dot_general x9 -> x10, matrix products: 156 us -> 160 us  [t_product(): lax.dot_general(a, b, (((0,), (0,)), ((), ())), preferred_element_type=f32)]
  transfers between devices with their start and end apart: 33 -> 33, of which waited for: 15 -> 13; matrix products, arithmetic and copies ran while one was open for 27% -> 28% of each run, Pallas kernels for 32% -> 34%
where the time goes in v10:
time: 1370 us; the launch traced here: 1360 us
  Pallas kernels  680 us (50%)
  matrix products  215 us (16%)
  waiting for transfers between devices  132 us (10%)
  other arithmetic  130 us (9%)
  local copies, waits for them, and re-layouts  113 us (8%)
  blocking collectives  44.9 us (3%)
  starting transfers between devices  32.9 us (2%)
  between operations  15.2 us (1%)
    pallas_call x1, Pallas kernels, first_transfers(): pl.pallas_call(first_kernel, in_specs=[held] * 7, out_specs=[held] * 4, o...  162 us
    dot_general x10, matrix products, t_product(): lax.dot_general(a, b, (((0,), (0,)), ((), ())), preferred_element_type=f32)  160 us
    pallas_call x1, Pallas kernels, last_transfers(): pl.pallas_call(last_kernel, in_specs=[held] * 3, out_specs=[held] * 3, ou...  141 us
    pallas_call x3, Pallas kernels, expert_units(): pl.pallas_call(functools.partial(units_kernel, chunk), grid=(units // til...  135 us
    ppermute x22, waiting for transfers between devices, swap(): return lax.ppermute(a, axis, [(0, 1), (1, 0)])  85.3 us
    pallas_call x2, Pallas kernels, expert_input_grad(): pl.pallas_call(functools.partial(input_kernel, cut), grid=(width // n, ro...  77.9 us
    unnamed x170, local copies, waits for them, and re-layouts  49.3 us
    all_gather x1, blocking collectives, on_device(): lax.all_gather(small, EVERY, axis=0, tiled=True)  44.9 us
  transfers between devices with their start and end apart: 33, of which 13 were waited for; matrix products, arithmetic and copies ran while one was open for 28% of the time, Pallas kernels for 34%

profile of v10, /device:TPU:1, one launch (start us, length us, event | category | flops | bytes accessed | tf_op | source)
XLA Modules:
  0.0 1364.1 jit_solution(10753322584622773468)
XLA Ops:
  7.2 162.4 %first_transfers.1 = (bf16[2,4,2,128,4096]{4,3,2,1,0:T(8,128)(2,1)}, bf16[4,128,2048]{2,1,0:T(8,128)(2,1)}, bf16[4,128,2048]{2,1,0:T(8,128)(2,1)}, s32[2,2,1024]{2,1,0:T(2,128)}) custom-call(bf16[64,2048]{1,0:T(8,128)(2,1)} %query.1, bf16[64,2048]{1,0:T(8,128)(2,1)} %key.1, bf16[64,2048]{1,0:T(8,128)(2,1)} %value.1, bf16[64,2048]{1,0:T(8,128)(2,1)} %output.1, ...), custom_call_target="tpu_custom_call" | custom-call | bytes 16777216 | tf_op jit(solution)/shard_map/first_transfers/pallas_call | solution.py:360
  183.7 19.9 %fusion.4.qp.kp.vp = f32[1024,3072]{1,0:T(8,128)} fusion(bf16[1024,2048]{1,0:T(8,128)(2,1)S(1)} %bitcast.317, bf16[2048,4096]{1,0:T(8,128)(2,1)} %bitcast.338), kind=kOutput, calls=%fused_computation.6 | convolution fusion | flops 12884901888 | bytes 29360128 | tf_op jit(solution)/shard_map/dot_general | solution.py:27
  203.7 27.9 %attend.1 = (bf16[1024,1024]{1,0:T(8,128)(2,1)S(1)}, bf16[1024,1024]{1,0:T(8,128)(2,1)S(1)}, bf16[1024,1024]{1,0:T(8,128)(2,1)}, bf16[1024,1024]{1,0:T(8,128)(2,1)}) custom-call(f32[1024,3072]{1,0:T(8,128)} %fusion.4.qp.kp.vp, f32[1024,3072]{1,0:T(8,128)} %fusion.4.qp.kp.vp, f32[1024,3072]{1,0:T(8,128)} %fusion.4.qp.kp.vp, ...), custom_call_target="tpu_custom_call" | custom-call | flops 2684354560 | bytes 20971520 | tf_op jit(solution)/shard_map/attend/pallas_call | solution.py:625
  272.2 44.9 %all-gather = s32[32,4,256]{2,1,0:T(4,128)S(1)} all-gather(s32[1,4,256]{2,1,0:T(4,128)} %bitcast.330), channel_id=1, replica_groups=mesh['dp'=2,'seq'=4,'r'=1,'y'=2,'core'=2] {'dp','seq','r','y','core'}, dimensions={0}, use_global_device_ids=true | all-gather | bytes 135168 | tf_op jit(solution)/shard_map/all_gather | solution.py:1090
  333.5 13.1 dispatch.2
  347.9 47.7 %expert_units.3 = (bf16[2560,2048]{1,0:T(8,128)(2,1)}, bf16[2560,2048]{1,0:T(8,128)(2,1)}, bf16[2560,2048]{1,0:T(8,128)(2,1)}) custom-call(bf16[2560,2048]{1,0:T(8,128)(2,1)} %bitcast.300, bf16[2560,2048]{1,0:T(8,128)(2,1)} %bitcast.307, bf16[2048,2816]{1,0:T(8,128)(2,1)} %bitcast.342, bf16[2048,2816]{1,0:T(8,128)(2,1)} %bitcast.347, ...), custom_call_target="tpu_custom_call" | custom-call | flops 32212254720 | bytes 51380224 | tf_op jit(solution)/shard_map/expert_units/pallas_call | solution.py:730
  414.5 47.7 %expert_units.4 = (bf16[2560,2048]{1,0:T(8,128)(2,1)}, bf16[2560,2048]{1,0:T(8,128)(2,1)}, bf16[2560,2048]{1,0:T(8,128)(2,1)}) custom-call(bf16[2560,2048]{1,0:T(8,128)(2,1)} %bitcast.301, bf16[2560,2048]{1,0:T(8,128)(2,1)} %bitcast.308, bf16[2048,2816]{1,0:T(8,128)(2,1)} %bitcast.343, ...), custom_call_target="tpu_custom_call", output_to_operand_aliasing={{0}: (5, {}), {1}: (6, {}), {2}: (7, {})} | custom-call | flops 32212254720 | bytes 51380224 | tf_op jit(solution)/shard_map/expert_units/pallas_call | solution.py:730
  462.2 28.8 %convolution_convert_fusion.3.rest_0_ = bf16[2048,2048]{1,0:T(8,128)(2,1)} fusion(bf16[2560,2048]{1,0:T(8,128)(2,1)} %bitcast.309, bf16[2560,2048]{1,0:T(8,128)(2,1)} %get-tuple-element.57.units_a), kind=kOutput, calls=%fused_computation.17 | convolution fusion | flops 21479030784 | bytes 29360128 | tf_op jit(solution)/shard_map/dot_general | solution.py:35
  491.8 39.9 %expert_units.5 = (bf16[2560,768]{1,0:T(8,128)(2,1)}, bf16[2560,768]{1,0:T(8,128)(2,1)}, bf16[2560,768]{1,0:T(8,128)(2,1)}) custom-call(bf16[2560,2048]{1,0:T(8,128)(2,1)} %bitcast.302, bf16[2560,2048]{1,0:T(8,128)(2,1)} %bitcast.310, bf16[2048,2816]{1,0:T(8,128)(2,1)} %bitcast.344, bf16[2048,2816]{1,0:T(8,128)(2,1)} %bitcast.349, ...), custom_call_target="tpu_custom_call" | custom-call | flops 24159191040 | bytes 42205184 | tf_op jit(solution)/shard_map/expert_units/pallas_call | solution.py:730
  531.7 13.6 convolution_convert_fusion.9.rest_0_
  545.3 39.0 %expert_input_grad.2.rest_0_ = bf16[2560,1024]{1,0:T(8,128)(2,1)} custom-call(bf16[2560,2048]{1,0:T(8,128)(2,1)} %get-tuple-element.56.dgate_a.refs_0_, bf16[2560,768]{1,0:T(8,128)(2,1)} %get-tuple-element.58.dgate_b.refs_0_, bf16[2560,2048]{1,0:T(8,128)(2,1)} %get-tuple-element.59.dup_a.refs_0_, bf16[2560,768]{1,0:T(8,128)(2,1)} %get-tuple-element.60.dup_b.refs_0_, ...), custom_call_target="tpu_custom_call" | custom-call | flops 29527900160 | bytes 45613056 | tf_op jit(solution)/shard_map/expert_input_grad/pallas_call | solution.py:958
  584.3 39.0 %expert_input_grad.3 = bf16[2560,1024]{1,0:T(8,128)(2,1)} custom-call(bf16[2560,2048]{1,0:T(8,128)(2,1)} %get-tuple-element.56.dgate_a.refs_0_, bf16[2560,768]{1,0:T(8,128)(2,1)} %get-tuple-element.58.dgate_b.refs_0_, bf16[2560,2048]{1,0:T(8,128)(2,1)} %get-tuple-element.59.dup_a.refs_0_, bf16[2560,768]{1,0:T(8,128)(2,1)} %get-tuple-element.60.dup_b.refs_0_, ...), custom_call_target="tpu_custom_call" | custom-call | flops 29527900160 | bytes 45613056 | tf_op jit(solution)/shard_map/expert_input_grad/pallas_call | solution.py:958
  625.8 13.2 collect.1.refs_1_
  647.7 13.6 convolution_convert_fusion.7
  675.2 28.9 %convolution_convert_fusion.2.refs_1_.rest_0_ = bf16[2048,2048]{1,0:T(8,128)(2,1)} fusion(bf16[2560,2048]{1,0:T(8,128)(2,1)} %bitcast.304, bf16[2560,2048]{1,0:T(8,128)(2,1)} %after.15), kind=kOutput, calls=%fused_computation.16 | convolution fusion | flops 21479030784 | bytes 29360128 | tf_op jit(solution)/shard_map/dot_general | solution.py:35
  743.6 40.7 %expert_down.1 = bf16[2560,2048]{1,0:T(8,128)(2,1)} custom-call(bf16[2560,2048]{1,0:T(8,128)(2,1)} %get-tuple-element.57.units_a, bf16[2560,768]{1,0:T(8,128)(2,1)S(1)} %copy-done.27, bf16[2816,2048]{1,0:T(8,128)(2,1)} %bitcast.355, bf16[2048,2048]{1,0:T(8,128)(2,1)} %convolution_convert_fusion.2.refs_1_.rest_0_), custom_call_target="tpu_custom_call" | custom-call | flops 29527900160 | bytes 36438016 | tf_op jit(solution)/shard_map/expert_down/pallas_call | solution.py:922
  784.2 24.3 %combine.1 = (bf16[2,2,2,4,128,2048]{5,4,3,2,1,0:T(8,128)(2,1)}, f32[16,256,1]{2,1,0:T(8,128)S(1)}) custom-call(s32[4]{0:T(128)S(1)} %pad_add_fusion.me, bf16[16,160,2048]{2,1,0:T(8,128)(2,1)} %bitcast.299, s32[16,256,1]{2,1,0:T(8,128)S(1)} %copy.139.slot, f32[16,256,1]{2,1,0:T(8,128)S(1)} %copy-done.6, bf16[4,2,4,128,2048]{4,3,2,1,0:T(8,128)(2,1)} %bitcast.286), custom_call_target="tpu_custom_call" | custom-call | flops 2684354560 | bytes 44040192 | tf_op jit(solution)/shard_map/combine/pallas_call | solution.py:897
  881.2 31.8 %attend_back.1 = (bf16[1024,1024]{1,0:T(8,128)(2,1)S(1)}, bf16[1024,1024]{1,0:T(8,128)(2,1)}, bf16[1024,1024]{1,0:T(8,128)(2,1)}) custom-call(bf16[1024,1024]{1,0:T(8,128)(2,1)} %copy-done.25, bf16[1024,1024]{1,0:T(8,128)(2,1)} %copy-done.26, bf16[1024,1024]{1,0:T(8,128)(2,1)} %get-tuple-element.66.v, bf16[1024,1024]{1,0:T(8,128)(2,1)} %get-tuple-element.46.mixed, ...), custom_call_target="tpu_custom_call" | custom-call | flops 6710886400 | bytes 16777216 | tf_op jit(solution)/shard_map/attend_back/pallas_call | solution.py:685
  930.4 29.0 %convolution_convert_fusion.1.refs_1_ = bf16[2048,2048]{1,0:T(8,128)(2,1)} fusion(bf16[2560,2048]{1,0:T(8,128)(2,1)} %bitcast.306, bf16[2560,2048]{1,0:T(8,128)(2,1)} %after.20), kind=kOutput, calls=%fused_computation.15 | convolution fusion | flops 21479030784 | bytes 29360128 | tf_op jit(solution)/shard_map/dot_general | solution.py:35
  959.4 13.4 collective-permute-done.13
  1028.1 15.7 %fusion.24 = bf16[1024,2048]{1,0:T(8,128)(2,1)S(1)} fusion(bf16[1024,3072]{1,0:T(8,128)(2,1)S(1)} %bitcast.296, bf16[2048,4096]{1,0:T(8,128)(2,1)} %bitcast.341), kind=kOutput, calls=%fused_computation.65 | convolution fusion | flops 12886999040 | bytes 23068672 | tf_op jit(solution)/shard_map/dot_general | solution.py:31
  1071.3 40.5 %collective-permute-done.17 = bf16[4,1,2,128,1024]{4,3,0,2,1:T(8,128)(2,1)} collective-permute-done((bf16[4,1,2,128,1024]{4,3,0,2,1:T(8,128)(2,1)}, bf16[4,1,2,128,1024]{4,3,0,2,1:T(8,128)(2,1)}, u32[]{:S(2)}, u32[]{:S(2)}) %collective-permute-start.17) | collective-permute-done | bytes 2097184 | tf_op jit(solution)/shard_map/ppermute | solution.py:39
  1151.3 30.1 %all-to-all-done.1 = f32[32,1,384]{2,1,0:T(1,128)S(1)} async-done(((f32[32,1,384]{2,1,0:T(1,128)}), f32[32,1,384]{2,1,0:T(1,128)S(1)}, u32[]{:S(2)}, u32[]{:S(2)}) %all-to-all-start.1) | async-done | bytes 49184 | tf_op jit(solution)/shard_map/all_to_all | solution.py:1239
  1192.1 141.0 %last_transfers.1 = (bf16[2,2,64,4096]{3,2,1,0:T(8,128)(2,1)S(1)}, bf16[2,256,2048]{2,1,0:T(8,128)(2,1)S(1)}, bf16[2,256,2048]{2,1,0:T(8,128)(2,1)S(1)}) custom-call(bf16[4,128,4096]{2,1,0:T(8,128)(2,1)S(1)} %maximum_bitcast_fusion.1.grads, bf16[4,128,2048]{2,1,0:T(8,128)(2,1)S(1)} %bitcast.281, bf16[4,128,2048]{2,1,0:T(8,128)(2,1)S(1)} %copy-done), custom_call_target="tpu_custom_call" | custom-call | bytes 8388608 | tf_op jit(solution)/shard_map/last_transfers/pallas_call | solution.py:562
  (372 shorter events, 402.8 us)
Async XLA Ops:
  7.2 259.8 %all-gather.5.cloned.1.call-start = ((), (), s32[]{:S(2)}) async-start(), calls=%async_computation.8 | async-start | bytes 18874368 | tf_op jit(solution)/shard_map/all_gather | solution.py:1066
  169.7 160.4 %all-gather.9.cloned.1.call-start = ((), (), s32[]{:S(2)}) async-start(), calls=%async_computation.10 | async-start | bytes 9437184 | tf_op jit(solution)/shard_map/all_gather | solution.py:1087
  270.2 125.5 %all-gather.7.cloned.1.call-start = ((), (), s32[]{:S(2)}) async-start(), calls=%async_computation.9 | async-start | bytes 9437184 | tf_op jit(solution)/shard_map/all_gather | solution.py:1087
  270.9 404.3 %reduce-scatter.7.cloned.1.call-start = ((), (), s32[]{:S(2)}) async-start(), calls=%async_computation.11 | async-start | bytes 10485760 | tf_op jit(solution)/shard_map/reduce_scatter | solution.py:1126
  491.1 387.9 %reduce-scatter.9.cloned.1.call-start = ((), (), s32[]{:S(2)}) async-start(), calls=%async_computation.12 | async-start | bytes 3932160 | tf_op jit(solution)/shard_map/reduce_scatter | solution.py:1126
  545.3 518.0 %reduce-scatter.13.cloned.1.call-start = ((), (), s32[]{:S(2)}) async-start(), calls=%async_computation.14 | async-start | bytes 3932160 | tf_op jit(solution)/shard_map/reduce_scatter | solution.py:1126
  661.3 402.0 %reduce-scatter.11.cloned.1.call-start = ((), (), s32[]{:S(2)}) async-start(), calls=%async_computation.13 | async-start | bytes 10485760 | tf_op jit(solution)/shard_map/reduce_scatter | solution.py:1126
  708.2 25.0 %collective-permute-start.6 = (bf16[2,128,2048]{2,1,0:T(8,128)(2,1)}, bf16[2,128,2048]{2,1,0:T(8,128)(2,1)}, u32[]{:S(2)}, u32[]{:S(2)}) collective-permute-start(bf16[2,128,2048]{2,1,0:T(8,128)(2,1)} %get-tuple-element.153), channel_id=1, source_target_pairs={{0,16},{16,0},{1,17},{17,1},{2,18},{18,2},{3,19},{19,3},{4,20},{20... | collective-permute-start | bytes 3145736 | tf_op jit(solution)/shard_map/ppermute | solution.py:39
  738.5 83.6 %collective-permute-start.7 = (bf16[4,128,2048]{2,1,0:T(8,128)(2,1)}, bf16[4,128,2048]{2,1,0:T(8,128)(2,1)}, u32[]{:S(2)}, u32[]{:S(2)}) collective-permute-start(bf16[4,128,2048]{2,1,0:T(8,128)(2,1)} %pad_maximum_fusion.8), channel_id=1, source_target_pairs={{0,2},{2,0},{1,3},{3,1},{4,6},{6,4},{5,7},{7,5},{8,10},{10,8},{9,1... | collective-permute-start | bytes 6291464 | tf_op jit(solution)/shard_map/ppermute | solution.py:39
  740.7 81.5 %collective-permute-start.5 = (bf16[4,128,2048]{2,1,0:T(8,128)(2,1)}, bf16[4,128,2048]{2,1,0:T(8,128)(2,1)}, u32[]{:S(2)}, u32[]{:S(2)}) collective-permute-start(bf16[4,128,2048]{2,1,0:T(8,128)(2,1)} %after.18), channel_id=1, source_target_pairs={{0,16},{16,0},{1,17},{17,1},{2,18},{18,2},{3,19},{19,3},{4,20},{20... | collective-permute-start | bytes 6291464 | tf_op jit(solution)/shard_map/ppermute | solution.py:39
  817.5 533.5 %reduce-scatter.17.cloned.1.call-start = ((), (), s32[]{:S(2)}) async-start(), calls=%async_computation.16 | async-start | bytes 3932160 | tf_op jit(solution)/shard_map/reduce_scatter | solution.py:1126
  859.0 492.0 %reduce-scatter.15.cloned.1.call-start = ((), (), s32[]{:S(2)}) async-start(), calls=%async_computation.15 | async-start | bytes 10485760 | tf_op jit(solution)/shard_map/reduce_scatter | solution.py:1126
  878.8 42.7 %collective-permute-start.12 = (bf16[2,128,2048]{2,1,0:T(8,128)(2,1)}, bf16[2,128,2048]{2,1,0:T(8,128)(2,1)}, u32[]{:S(2)}, u32[]{:S(2)}) collective-permute-start(bf16[2,128,2048]{2,1,0:T(8,128)(2,1)} %get-tuple-element.147), channel_id=1, source_target_pairs={{0,16},{16,0},{1,17},{17,1},{2,18},{18,2},{3,19},{19,3},{4,20},{20... | collective-permute-start | bytes 3145736 | tf_op jit(solution)/shard_map/ppermute | solution.py:39
  878.9 42.6 %collective-permute-start.11 = (bf16[2,128,2048]{2,1,0:T(8,128)(2,1)}, bf16[2,128,2048]{2,1,0:T(8,128)(2,1)}, u32[]{:S(2)}, u32[]{:S(2)}) collective-permute-start(bf16[2,128,2048]{2,1,0:T(8,128)(2,1)} %get-tuple-element.149), channel_id=1, source_target_pairs={{0,2},{2,0},{1,3},{3,1},{4,6},{6,4},{5,7},{7,5},{8,10},{10,8},{9,1... | collective-permute-start | bytes 3145736 | tf_op jit(solution)/shard_map/ppermute | solution.py:39
  926.1 46.7 %collective-permute-start.13 = (bf16[4,128,2048]{2,1,0:T(8,128)(2,1)}, bf16[4,128,2048]{2,1,0:T(8,128)(2,1)}, u32[]{:S(2)}, u32[]{:S(2)}) collective-permute-start(bf16[4,128,2048]{2,1,0:T(8,128)(2,1)} %pad_maximum_fusion.9.refs_2_), channel_id=1, source_target_pairs={{0,16},{16,0},{1,17},{17,1},{2,18},{18,2},{3,19},{19,3},{4,20},{20... | collective-permute-start | bytes 6291464 | tf_op jit(solution)/shard_map/ppermute | solution.py:39
  929.0 46.3 %collective-permute-start.14 = (bf16[4,128,2048]{2,1,0:T(8,128)(2,1)}, bf16[4,128,2048]{2,1,0:T(8,128)(2,1)}, u32[]{:S(2)}, u32[]{:S(2)}) collective-permute-start(bf16[4,128,2048]{2,1,0:T(8,128)(2,1)} %pad_maximum_fusion.10.refs_3_), channel_id=1, source_target_pairs={{0,2},{2,0},{1,3},{3,1},{4,6},{6,4},{5,7},{7,5},{8,10},{10,8},{9,1... | collective-permute-start | bytes 6291464 | tf_op jit(solution)/shard_map/ppermute | solution.py:39
  1022.8 45.6 %collective-permute-start.15 = (bf16[4,1,2,128,1024]{4,3,0,2,1:T(8,128)(2,1)}, bf16[4,1,2,128,1024]{4,3,0,2,1:T(8,128)(2,1)}, u32[]{:S(2)}, u32[]{:S(2)}) collective-permute-start(bf16[4,1,2,128,1024]{4,3,0,2,1:T(8,128)(2,1)} %bitcast.276), channel_id=1, source_target_pairs={{0,16},{16,0},{1,17},{17,1},{2,18},{18,2},{3,19},{19,3},{4,20},{20... | collective-permute-start | bytes 6291464 | tf_op jit(solution)/shard_map/ppermute | solution.py:39
  1023.1 88.8 %collective-permute-start.17 = (bf16[4,1,2,128,1024]{4,3,0,2,1:T(8,128)(2,1)}, bf16[4,1,2,128,1024]{4,3,0,2,1:T(8,128)(2,1)}, u32[]{:S(2)}, u32[]{:S(2)}) collective-permute-start(bf16[4,1,2,128,1024]{4,3,0,2,1:T(8,128)(2,1)} %bitcast.275), channel_id=1, source_target_pairs={{0,16},{16,0},{1,17},{17,1},{2,18},{18,2},{3,19},{19,3},{4,20},{20... | collective-permute-start | bytes 6291464 | tf_op jit(solution)/shard_map/ppermute | solution.py:39
  1026.8 97.3 %collective-permute-start.19 = (bf16[2,4,1,128,2048]{4,3,1,2,0:T(8,128)(2,1)}, bf16[2,4,1,128,2048]{4,3,1,2,0:T(8,128)(2,1)}, u32[]{:S(2)}, u32[]{:S(2)}) collective-permute-start(bf16[2,4,1,128,2048]{4,3,1,2,0:T(8,128)(2,1)} %dynamic-slice_bitcast_fusion), channel_id=1, source_target_pairs={{0,2},{2,0},{1,3},{3,1},{4,6},{6,4},{5,7},{7,5},{8,10},{10,8},{9,1... | collective-permute-start | bytes 12582920 | tf_op jit(solution)/shard_map/ppermute | solution.py:39
  1047.6 70.0 %collective-permute-start.21 = (bf16[4,128,2048]{2,1,0:T(8,128)(2,1)}, bf16[4,128,2048]{2,1,0:T(8,128)(2,1)}, u32[]{:S(2)}, u32[]{:S(2)}) collective-permute-start(bf16[4,128,2048]{2,1,0:T(8,128)(2,1)} %constant_dynamic-slice_fusion), channel_id=1, source_target_pairs={{0,1},{1,0},{2,3},{3,2},{4,5},{5,4},{6,7},{7,6},{8,9},{9,8},{10,11... | collective-permute-start | bytes 6291464 | tf_op jit(solution)/shard_map/ppermute | solution.py:39
  1071.1 112.8 %collective-permute-start.16 = (bf16[4,1,128,1024]{3,2,0,1:T(8,128)(2,1)S(1)}, bf16[4,1,128,1024]{3,2,0,1:T(8,128)(2,1)}, u32[]{:S(2)}, u32[]{:S(2)}) collective-permute-start(bf16[4,1,128,1024]{3,2,0,1:T(8,128)(2,1)S(1)} %dynamic-slice_bitcast_fusion.4), channel_id=1, source_target_pairs={{0,2},{2,0},{1,3},{3,1},{4,6},{6,4},{5,7},{7,5},{8,10},{10,8},{9,1... | collective-permute-start | bytes 3145736 | tf_op jit(solution)/shard_map/ppermute | solution.py:39
  1116.2 69.9 %collective-permute-start.18 = (bf16[4,1,128,1024]{3,2,0,1:T(8,128)(2,1)}, bf16[4,1,128,1024]{3,2,0,1:T(8,128)(2,1)}, u32[]{:S(2)}, u32[]{:S(2)}) collective-permute-start(bf16[4,1,128,1024]{3,2,0,1:T(8,128)(2,1)} %dynamic-slice_bitcast_fusion.3), channel_id=1, source_target_pairs={{0,2},{2,0},{1,3},{3,1},{4,6},{6,4},{5,7},{7,5},{8,10},{10,8},{9,1... | collective-permute-start | bytes 3145736 | tf_op jit(solution)/shard_map/ppermute | solution.py:39
  1133.0 55.0 %collective-permute-start.20 = (bf16[4,1,128,2048]{3,2,0,1:T(8,128)(2,1)}, bf16[4,1,128,2048]{3,2,0,1:T(8,128)(2,1)}, u32[]{:S(2)}, u32[]{:S(2)}) collective-permute-start(bf16[4,1,128,2048]{3,2,0,1:T(8,128)(2,1)} %dynamic-slice_bitcast_fusion.1), channel_id=1, source_target_pairs={{0,16},{16,0},{1,17},{17,1},{2,18},{18,2},{3,19},{19,3},{4,20},{20... | collective-permute-start | bytes 6291464 | tf_op jit(solution)/shard_map/ppermute | solution.py:39
  1134.8 46.7 %all-to-all-start.1 = ((f32[32,1,384]{2,1,0:T(1,128)}), f32[32,1,384]{2,1,0:T(1,128)S(1)}, u32[]{:S(2)}, u32[]{:S(2)}) async-start(f32[32,1,384]{2,1,0:T(1,128)} %reshape.497), calls=%async_computation.3 | async-start | bytes 98304 | tf_op jit(solution)/shard_map/all_to_all | solution.py:1239
  (91 other events, 915.9 us)
Sparse Core Ops, SparseCore 0:
  169.8 96.0 all-gather.4
  270.3 59.7 all-gather.8
  332.6 54.2 all-gather.6
  491.2 143.8 reduce-scatter.6
  637.2 60.9 reduce-scatter.8
  700.4 60.2 reduce-scatter.12
  763.1 144.4 reduce-scatter.10
  909.9 60.9 reduce-scatter.16
  973.3 144.4 reduce-scatter.14

commit v11 on v10

--- a/solution.py
+++ b/solution.py
@@ -87,11 +87,15 @@
     return pieces
 
 
+def seq_order(pieces):
+    count = len(pieces)
+    me = lax.axis_index("seq")
+    pieces = jnp.stack(pieces)
+    return jnp.stack([pick(pieces, lax.rem(me + count - s, count), 0) for s in range(count)])
+
+
 def seq_exchange(a):
-    count = a.shape[0]
-    me = lax.axis_index("seq")
-    pieces = jnp.stack(seq_pieces(a))
-    return jnp.stack([pick(pieces, lax.rem(me + count - s, count), 0) for s in range(count)])
+    return seq_order(seq_pieces(a))
 
 
 def to_sequences(a):
@@ -387,10 +391,9 @@
 def last_kernel(
     grads,
     tokens,
-    output,
+    before,
     grads_out,
     tokens_out,
-    output_out,
     mine,
     theirs,
     pair_send,
@@ -490,7 +493,7 @@
         )
 
     def each_row(remote, kept):
-        for n, source, target in ((0, tokens, tokens_out), (1, output, output_out)):
+        for n, source, target in ((0, tokens, tokens_out),):
             for dz in range(seq_n):
                 if dz:
                     remote(row_copy(n, source, target, dz))
@@ -535,7 +538,7 @@
     for place, dc in ((1, 0), (1, 1), (0, 1)):
         arrival(place, dc).wait_recv()
     each_row(lambda copy: copy.wait_send(), lambda copy: copy.wait())
-    for n, target in ((0, tokens_out), (1, output_out)):
+    for n, target in ((0, tokens_out),):
         for s in range(seq_count):
             for c in range(2):
                 ref = row_place(target, s, c)
@@ -553,7 +556,7 @@
                     copy.wait_recv()
 
 
-def last_transfers(grads, tokens, output, seq_count):
+def last_transfers(grads, tokens, before, seq_count):
     seq_n, piece, width = tokens.shape
     rows = grads.shape[1] // 2
     held = pl.BlockSpec(memory_space=pl.ANY)
@@ -562,8 +565,8 @@
     return pl.pallas_call(
         last_kernel,
         in_specs=[held] * 3,
-        out_specs=[held] * 3,
-        out_shape=[jax.ShapeDtypeStruct((2, 2, rows, grads.shape[2]), bf16), out, out],
+        out_specs=[held] * 2,
+        out_shape=[jax.ShapeDtypeStruct((2, 2, rows, grads.shape[2]), bf16), out],
         scratch_shapes=[
             pltpu.VMEM((2,) + grads.shape[1:], bf16),
             pltpu.VMEM((2,) + grads.shape[1:], bf16),
@@ -571,8 +574,8 @@
             dma((2,)),
             dma((2, 2)),
             dma((2, 2)),
-            dma((2, seq_n)),
-            dma((2, seq_count, 2)),
+            dma((1, seq_n)),
+            dma((1, seq_count, 2)),
             dma((5,)),
         ],
         compiler_params=pltpu.CompilerParams(
@@ -580,7 +583,7 @@
         ),
         cost_estimate=pl.CostEstimate(flops=0, bytes_accessed=4 * grads.size, transcendentals=0),
         name="last_transfers",
-    )(grads, tokens, output)
+    )(grads, tokens, before)
 
 
 def visible_block(seg_row, seg_col, start, rows, cols):
@@ -1216,17 +1219,18 @@
 
     first = [half(seen(a), 0, dp_i, "dp") for a in (out_grad, query_grad)]
     first.append(half(seen(kv_grad), 3, y_i, "y"))
+    output = [after(piece, first[2]) for piece in seq_pieces(output)]
+    output = core_exchange(seq_order(output), 0, 1)
     second = [half(a, 2, y_i, "y") for a in first[:2]] + [half(first[2], 0, dp_i, "dp")]
     second = jnp.concatenate(second, axis=-1)
     if r_n == 1 and parts == 2 and seq_n == 2 * seq_count == 4:
-        part, grad_tokens, output = last_transfers(
+        part, grad_tokens = last_transfers(
             second.reshape(seq_n, core_n * rows_here, 4 * columns), dtokens, output, seq_count
         )
         part = total(part[:, 0], part[:, 1]).reshape(core_n, rows_here, 4, columns)
         part = part.transpose(1, 2, 0, 3).reshape(rows_here, 4, width)
     else:
         grad_tokens = from_sequences(dtokens)
-        output = from_sequences(output)
         part = total(*seq_pieces(second)).astype(bf16)
         part = part.reshape(parts, rows_here, 4, 1, columns)
         part = chip_exchange(part, 0, 3, parts).reshape(rows_here, 4, width).astype(f32)

time: 1370 us -> 1370 us (level)
  Pallas kernels: 680 us -> 658 us
  waiting for transfers between devices: 132 us -> 150 us
    ppermute x22 -> x23, waiting for transfers between devices: 85.3 us -> 124 us  [swap(): return lax.ppermute(a, axis, [(0, 1), (1, 0)])]
    all_to_all x1, waiting for transfers between devices: 30.1 us -> 0.01 us  [on_device(): lax.all_to_all(gains, EVERY, split_axis=0, concat_axis=0, tiled=True)]
    pallas_call x1, Pallas kernels: 141 us -> 119 us  [last_transfers(): pl.pallas_call(last_kernel, in_specs=[held] * 3, out_specs=[held] * 2, ou...]
    unnamed x170 -> x169, local copies, waits for them, and re-layouts: 49.3 us -> 43.7 us
  transfers between devices with their start and end apart: 33 -> 37, of which waited for: 13 -> 16; matrix products, arithmetic and copies ran while one was open for 28% -> 29% of each run, Pallas kernels for 34% -> 32%
where the time goes in v11:
time: 1370 us
  Pallas kernels  658 us (48%)
  matrix products  216 us (16%)
  waiting for transfers between devices  150 us (11%)
  other arithmetic  131 us (10%)
  local copies, waits for them, and re-layouts  116 us (8%)
  blocking collectives  44.7 us (3%)
  starting transfers between devices  34.5 us (3%)
  between operations  15.3 us (1%)
    pallas_call x1, Pallas kernels, first_transfers(): pl.pallas_call(first_kernel, in_specs=[held] * 7, out_specs=[held] * 4, o...  162 us
    dot_general x10, matrix products, t_product(): lax.dot_general(a, b, (((0,), (0,)), ((), ())), preferred_element_type=f32)  160 us
    pallas_call x3, Pallas kernels, expert_units(): pl.pallas_call(functools.partial(units_kernel, chunk), grid=(units // til...  135 us
    ppermute x23, waiting for transfers between devices, swap(): return lax.ppermute(a, axis, [(0, 1), (1, 0)])  124 us
    pallas_call x1, Pallas kernels, last_transfers(): pl.pallas_call(last_kernel, in_specs=[held] * 3, out_specs=[held] * 2, ou...  119 us
    pallas_call x2, Pallas kernels, expert_input_grad(): pl.pallas_call(functools.partial(input_kernel, cut), grid=(width // n, ro...  78 us
    all_gather x1, blocking collectives, on_device(): lax.all_gather(small, EVERY, axis=0, tiled=True)  44.7 us
    unnamed x169, local copies, waits for them, and re-layouts  43.7 us
  transfers between devices with their start and end apart: 37, of which 16 were waited for; matrix products, arithmetic and copies ran while one was open for 29% of the time, Pallas kernels for 32%

profile of v11, /device:TPU:1, one launch (start us, length us, event | category | flops | bytes accessed | tf_op | source)
XLA Modules:
  0.0 1365.0 jit_solution(4552313491659308679)
XLA Ops:
  7.2 162.4 %first_transfers.1 = (bf16[2,4,2,128,4096]{4,3,2,1,0:T(8,128)(2,1)}, bf16[4,128,2048]{2,1,0:T(8,128)(2,1)}, bf16[4,128,2048]{2,1,0:T(8,128)(2,1)}, s32[2,2,1024]{2,1,0:T(2,128)}) custom-call(bf16[64,2048]{1,0:T(8,128)(2,1)} %query.1, bf16[64,2048]{1,0:T(8,128)(2,1)} %key.1, bf16[64,2048]{1,0:T(8,128)(2,1)} %value.1, bf16[64,2048]{1,0:T(8,128)(2,1)} %output.1, ...), custom_call_target="tpu_custom_call" | custom-call | bytes 16777216 | tf_op jit(solution)/shard_map/first_transfers/pallas_call | solution.py:364
  183.7 19.9 %fusion.4.qp.kp.vp = f32[1024,3072]{1,0:T(8,128)} fusion(bf16[1024,2048]{1,0:T(8,128)(2,1)S(1)} %bitcast.336, bf16[2048,4096]{1,0:T(8,128)(2,1)} %bitcast.358), kind=kOutput, calls=%fused_computation.6 | convolution fusion | flops 12884901888 | bytes 29360128 | tf_op jit(solution)/shard_map/dot_general | solution.py:27
  203.7 27.9 %attend.1 = (bf16[1024,1024]{1,0:T(8,128)(2,1)S(1)}, bf16[1024,1024]{1,0:T(8,128)(2,1)S(1)}, bf16[1024,1024]{1,0:T(8,128)(2,1)}, bf16[1024,1024]{1,0:T(8,128)(2,1)}) custom-call(f32[1024,3072]{1,0:T(8,128)} %fusion.4.qp.kp.vp, f32[1024,3072]{1,0:T(8,128)} %fusion.4.qp.kp.vp, f32[1024,3072]{1,0:T(8,128)} %fusion.4.qp.kp.vp, ...), custom_call_target="tpu_custom_call" | custom-call | flops 2684354560 | bytes 20971520 | tf_op jit(solution)/shard_map/attend/pallas_call | solution.py:628
  272.3 44.7 %all-gather = s32[32,4,256]{2,1,0:T(4,128)S(1)} all-gather(s32[1,4,256]{2,1,0:T(4,128)} %bitcast.350), channel_id=1, replica_groups=mesh['dp'=2,'seq'=4,'r'=1,'y'=2,'core'=2] {'dp','seq','r','y','core'}, dimensions={0}, use_global_device_ids=true | all-gather | bytes 135168 | tf_op jit(solution)/shard_map/all_gather | solution.py:1093
  333.7 13.4 dispatch.2
  348.5 47.7 %expert_units.3 = (bf16[2560,2048]{1,0:T(8,128)(2,1)}, bf16[2560,2048]{1,0:T(8,128)(2,1)}, bf16[2560,2048]{1,0:T(8,128)(2,1)}) custom-call(bf16[2560,2048]{1,0:T(8,128)(2,1)} %bitcast.318, bf16[2560,2048]{1,0:T(8,128)(2,1)} %bitcast.325, bf16[2048,2816]{1,0:T(8,128)(2,1)} %bitcast.362, bf16[2048,2816]{1,0:T(8,128)(2,1)} %bitcast.367, ...), custom_call_target="tpu_custom_call" | custom-call | flops 32212254720 | bytes 51380224 | tf_op jit(solution)/shard_map/expert_units/pallas_call | solution.py:733
  415.1 47.8 %expert_units.4 = (bf16[2560,2048]{1,0:T(8,128)(2,1)}, bf16[2560,2048]{1,0:T(8,128)(2,1)}, bf16[2560,2048]{1,0:T(8,128)(2,1)}) custom-call(bf16[2560,2048]{1,0:T(8,128)(2,1)} %bitcast.319, bf16[2560,2048]{1,0:T(8,128)(2,1)} %bitcast.326, bf16[2048,2816]{1,0:T(8,128)(2,1)} %bitcast.363, ...), custom_call_target="tpu_custom_call", output_to_operand_aliasing={{0}: (5, {}), {1}: (6, {}), {2}: (7, {})} | custom-call | flops 32212254720 | bytes 51380224 | tf_op jit(solution)/shard_map/expert_units/pallas_call | solution.py:733
  462.9 28.9 %convolution_convert_fusion.3.rest_0_ = bf16[2048,2048]{1,0:T(8,128)(2,1)} fusion(bf16[2560,2048]{1,0:T(8,128)(2,1)} %bitcast.327, bf16[2560,2048]{1,0:T(8,128)(2,1)} %get-tuple-element.55.units_a), kind=kOutput, calls=%fused_computation.17 | convolution fusion | flops 21479030784 | bytes 29360128 | tf_op jit(solution)/shard_map/dot_general | solution.py:35
  492.5 39.6 %expert_units.5 = (bf16[2560,768]{1,0:T(8,128)(2,1)}, bf16[2560,768]{1,0:T(8,128)(2,1)}, bf16[2560,768]{1,0:T(8,128)(2,1)}) custom-call(bf16[2560,2048]{1,0:T(8,128)(2,1)} %bitcast.320, bf16[2560,2048]{1,0:T(8,128)(2,1)} %bitcast.328, bf16[2048,2816]{1,0:T(8,128)(2,1)} %bitcast.364, bf16[2048,2816]{1,0:T(8,128)(2,1)} %bitcast.369, ...), custom_call_target="tpu_custom_call" | custom-call | flops 24159191040 | bytes 42205184 | tf_op jit(solution)/shard_map/expert_units/pallas_call | solution.py:733
  532.1 13.6 convolution_convert_fusion.9.rest_0_
  545.8 39.0 %expert_input_grad.2.rest_0_ = bf16[2560,1024]{1,0:T(8,128)(2,1)} custom-call(bf16[2560,2048]{1,0:T(8,128)(2,1)} %get-tuple-element.57.dgate_a.refs_0_, bf16[2560,768]{1,0:T(8,128)(2,1)} %get-tuple-element.58.dgate_b.refs_0_, bf16[2560,2048]{1,0:T(8,128)(2,1)} %get-tuple-element.59.dup_a.refs_0_, bf16[2560,768]{1,0:T(8,128)(2,1)} %get-tuple-element.60.dup_b.refs_0_, ...), custom_call_target="tpu_custom_call" | custom-call | flops 29527900160 | bytes 45613056 | tf_op jit(solution)/shard_map/expert_input_grad/pallas_call | solution.py:961
  584.8 39.0 %expert_input_grad.3 = bf16[2560,1024]{1,0:T(8,128)(2,1)} custom-call(bf16[2560,2048]{1,0:T(8,128)(2,1)} %get-tuple-element.57.dgate_a.refs_0_, bf16[2560,768]{1,0:T(8,128)(2,1)} %get-tuple-element.58.dgate_b.refs_0_, bf16[2560,2048]{1,0:T(8,128)(2,1)} %get-tuple-element.59.dup_a.refs_0_, bf16[2560,768]{1,0:T(8,128)(2,1)} %get-tuple-element.60.dup_b.refs_0_, ...), custom_call_target="tpu_custom_call" | custom-call | flops 29527900160 | bytes 45613056 | tf_op jit(solution)/shard_map/expert_input_grad/pallas_call | solution.py:961
  648.2 13.6 convolution_convert_fusion.7
  675.8 29.0 %convolution_convert_fusion.2.rest_0_.refs_1_ = bf16[2048,2048]{1,0:T(8,128)(2,1)} fusion(bf16[2560,2048]{1,0:T(8,128)(2,1)} %bitcast.322, bf16[2560,2048]{1,0:T(8,128)(2,1)} %after.19), kind=kOutput, calls=%fused_computation.16 | convolution fusion | flops 21479030784 | bytes 29360128 | tf_op jit(solution)/shard_map/dot_general | solution.py:35
  744.1 40.6 %expert_down.1 = bf16[2560,2048]{1,0:T(8,128)(2,1)} custom-call(bf16[2560,2048]{1,0:T(8,128)(2,1)} %get-tuple-element.55.units_a, bf16[2560,768]{1,0:T(8,128)(2,1)S(1)} %copy-done.24, bf16[2816,2048]{1,0:T(8,128)(2,1)} %bitcast.375, bf16[2048,2048]{1,0:T(8,128)(2,1)} %convolution_convert_fusion.2.rest_0_.refs_1_), custom_call_target="tpu_custom_call" | custom-call | flops 29527900160 | bytes 36438016 | tf_op jit(solution)/shard_map/expert_down/pallas_call | solution.py:925
  784.8 24.3 %combine.1 = (bf16[2,2,2,4,128,2048]{5,4,3,2,1,0:T(8,128)(2,1)}, f32[16,256,1]{2,1,0:T(8,128)S(1)}) custom-call(s32[4]{0:T(128)S(1)} %pad_add_fusion.me, bf16[16,160,2048]{2,1,0:T(8,128)(2,1)} %bitcast.317, s32[16,256,1]{2,1,0:T(8,128)S(1)} %copy.159.slot, f32[16,256,1]{2,1,0:T(8,128)S(1)} %copy-done.5, bf16[4,2,4,128,2048]{4,3,2,1,0:T(8,128)(2,1)} %bitcast.302), custom_call_target="tpu_custom_call" | custom-call | flops 2684354560 | bytes 44040192 | tf_op jit(solution)/shard_map/combine/pallas_call | solution.py:900
  882.0 31.8 %attend_back.1 = (bf16[1024,1024]{1,0:T(8,128)(2,1)S(1)}, bf16[1024,1024]{1,0:T(8,128)(2,1)}, bf16[1024,1024]{1,0:T(8,128)(2,1)}) custom-call(bf16[1024,1024]{1,0:T(8,128)(2,1)} %copy-done.22, bf16[1024,1024]{1,0:T(8,128)(2,1)} %copy-done.23, bf16[1024,1024]{1,0:T(8,128)(2,1)} %get-tuple-element.66.v, bf16[1024,1024]{1,0:T(8,128)(2,1)} %get-tuple-element.45.mixed, ...), custom_call_target="tpu_custom_call" | custom-call | flops 6710886400 | bytes 16777216 | tf_op jit(solution)/shard_map/attend_back/pallas_call | solution.py:688
  931.2 29.0 %convolution_convert_fusion.1.refs_1_ = bf16[2048,2048]{1,0:T(8,128)(2,1)} fusion(bf16[2560,2048]{1,0:T(8,128)(2,1)} %bitcast.324, bf16[2560,2048]{1,0:T(8,128)(2,1)} %after.24), kind=kOutput, calls=%fused_computation.15 | convolution fusion | flops 21479030784 | bytes 29360128 | tf_op jit(solution)/shard_map/dot_general | solution.py:35
  960.3 13.3 collective-permute-done.13
  991.7 14.2 %convolution_convert_fusion.refs_1_ = bf16[2048,2048]{1,0:T(8,128)(2,1)} fusion(bf16[1024,2048]{1,0:T(8,128)(2,1)} %bitcast.337, bf16[1024,2048]{1,0:T(8,128)(2,1)} %after.26), kind=kOutput, calls=%fused_computation.14 | convolution fusion | flops 8594128896 | bytes 16777216 | tf_op jit(solution)/shard_map/dot_general | solution.py:35
  1020.5 15.7 %fusion.24 = bf16[1024,2048]{1,0:T(8,128)(2,1)S(1)} fusion(bf16[1024,3072]{1,0:T(8,128)(2,1)S(1)} %copy-done.37, bf16[2048,4096]{1,0:T(8,128)(2,1)} %bitcast.361), kind=kOutput, calls=%fused_computation.65 | convolution fusion | flops 12886999040 | bytes 23068672 | tf_op jit(solution)/shard_map/dot_general | solution.py:31
  1101.7 39.3 %collective-permute-done.20 = bf16[4,1,2,128,1024]{4,3,0,2,1:T(8,128)(2,1)} collective-permute-done((bf16[4,1,2,128,1024]{4,3,0,2,1:T(8,128)(2,1)}, bf16[4,1,2,128,1024]{4,3,0,2,1:T(8,128)(2,1)}, u32[]{:S(2)}, u32[]{:S(2)}) %collective-permute-start.20) | collective-permute-done | bytes 2097184 | tf_op jit(solution)/shard_map/ppermute | solution.py:39
  1191.0 25.1 %collective-permute-done.24 = bf16[4,1,128,2048]{3,2,0,1:T(8,128)(2,1)} collective-permute-done((bf16[4,1,128,2048]{3,2,0,1:T(8,128)(2,1)}, bf16[4,1,128,2048]{3,2,0,1:T(8,128)(2,1)}, u32[]{:S(2)}, u32[]{:S(2)}) %collective-permute-start.24) | collective-permute-done | bytes 2097184 | tf_op jit(solution)/shard_map/ppermute | solution.py:39
  1220.1 119.1 %last_transfers.1 = (bf16[2,2,64,4096]{3,2,1,0:T(8,128)(2,1)S(1)}, bf16[2,256,2048]{2,1,0:T(8,128)(2,1)S(1)}) custom-call(bf16[4,128,4096]{2,1,0:T(8,128)(2,1)S(1)} %maximum_bitcast_fusion.1.grads, bf16[4,128,2048]{2,1,0:T(8,128)(2,1)S(1)} %bitcast.297, bf16[2,256,2048]{2,1,0:T(8,128)(2,1)S(1)} %pad_maximum_fusion.13.before), custom_call_target="tpu_custom_call" | custom-call | bytes 8388608 | tf_op jit(solution)/shard_map/last_transfers/pallas_call | solution.py:565
  (389 shorter events, 430.9 us)
Async XLA Ops:
  7.2 260.0 %all-gather.5.cloned.1.call-start = ((), (), s32[]{:S(2)}) async-start(), calls=%async_computation.8 | async-start | bytes 18874368 | tf_op jit(solution)/shard_map/all_gather | solution.py:1069
  169.7 160.6 %all-gather.9.cloned.1.call-start = ((), (), s32[]{:S(2)}) async-start(), calls=%async_computation.10 | async-start | bytes 9437184 | tf_op jit(solution)/shard_map/all_gather | solution.py:1090
  270.4 125.8 %all-gather.7.cloned.1.call-start = ((), (), s32[]{:S(2)}) async-start(), calls=%async_computation.9 | async-start | bytes 9437184 | tf_op jit(solution)/shard_map/all_gather | solution.py:1090
  271.1 404.7 %reduce-scatter.7.cloned.1.call-start = ((), (), s32[]{:S(2)}) async-start(), calls=%async_computation.11 | async-start | bytes 10485760 | tf_op jit(solution)/shard_map/reduce_scatter | solution.py:1129
  491.8 388.0 %reduce-scatter.9.cloned.1.call-start = ((), (), s32[]{:S(2)}) async-start(), calls=%async_computation.12 | async-start | bytes 3932160 | tf_op jit(solution)/shard_map/reduce_scatter | solution.py:1129
  545.7 526.8 %reduce-scatter.13.cloned.1.call-start = ((), (), s32[]{:S(2)}) async-start(), calls=%async_computation.14 | async-start | bytes 3932160 | tf_op jit(solution)/shard_map/reduce_scatter | solution.py:1129
  661.8 410.8 %reduce-scatter.11.cloned.1.call-start = ((), (), s32[]{:S(2)}) async-start(), calls=%async_computation.13 | async-start | bytes 10485760 | tf_op jit(solution)/shard_map/reduce_scatter | solution.py:1129
  739.5 83.3 %collective-permute-start.7 = (bf16[4,128,2048]{2,1,0:T(8,128)(2,1)}, bf16[4,128,2048]{2,1,0:T(8,128)(2,1)}, u32[]{:S(2)}, u32[]{:S(2)}) collective-permute-start(bf16[4,128,2048]{2,1,0:T(8,128)(2,1)} %pad_maximum_fusion.8), channel_id=1, source_target_pairs={{0,2},{2,0},{1,3},{3,1},{4,6},{6,4},{5,7},{7,5},{8,10},{10,8},{9,1... | collective-permute-start | bytes 6291464 | tf_op jit(solution)/shard_map/ppermute | solution.py:39
  741.2 81.6 %collective-permute-start.5 = (bf16[4,128,2048]{2,1,0:T(8,128)(2,1)}, bf16[4,128,2048]{2,1,0:T(8,128)(2,1)}, u32[]{:S(2)}, u32[]{:S(2)}) collective-permute-start(bf16[4,128,2048]{2,1,0:T(8,128)(2,1)} %after.22), channel_id=1, source_target_pairs={{0,16},{16,0},{1,17},{17,1},{2,18},{18,2},{3,19},{19,3},{4,20},{20... | collective-permute-start | bytes 6291464 | tf_op jit(solution)/shard_map/ppermute | solution.py:39
  818.3 535.1 %reduce-scatter.17.cloned.1.call-start = ((), (), s32[]{:S(2)}) async-start(), calls=%async_computation.16 | async-start | bytes 3932160 | tf_op jit(solution)/shard_map/reduce_scatter | solution.py:1129
  859.7 493.6 %reduce-scatter.15.cloned.1.call-start = ((), (), s32[]{:S(2)}) async-start(), calls=%async_computation.15 | async-start | bytes 10485760 | tf_op jit(solution)/shard_map/reduce_scatter | solution.py:1129
  879.7 42.7 %collective-permute-start.12 = (bf16[2,128,2048]{2,1,0:T(8,128)(2,1)}, bf16[2,128,2048]{2,1,0:T(8,128)(2,1)}, u32[]{:S(2)}, u32[]{:S(2)}) collective-permute-start(bf16[2,128,2048]{2,1,0:T(8,128)(2,1)} %get-tuple-element.145), channel_id=1, source_target_pairs={{0,16},{16,0},{1,17},{17,1},{2,18},{18,2},{3,19},{19,3},{4,20},{20... | collective-permute-start | bytes 3145736 | tf_op jit(solution)/shard_map/ppermute | solution.py:39
  879.7 42.6 %collective-permute-start.10 = (bf16[2,128,2048]{2,1,0:T(8,128)(2,1)}, bf16[2,128,2048]{2,1,0:T(8,128)(2,1)}, u32[]{:S(2)}, u32[]{:S(2)}) collective-permute-start(bf16[2,128,2048]{2,1,0:T(8,128)(2,1)} %get-tuple-element.146), channel_id=1, source_target_pairs={{0,2},{2,0},{1,3},{3,1},{4,6},{6,4},{5,7},{7,5},{8,10},{10,8},{9,1... | collective-permute-start | bytes 3145736 | tf_op jit(solution)/shard_map/ppermute | solution.py:39
  926.9 46.6 %collective-permute-start.13 = (bf16[4,128,2048]{2,1,0:T(8,128)(2,1)}, bf16[4,128,2048]{2,1,0:T(8,128)(2,1)}, u32[]{:S(2)}, u32[]{:S(2)}) collective-permute-start(bf16[4,128,2048]{2,1,0:T(8,128)(2,1)} %pad_maximum_fusion.10.refs_3_), channel_id=1, source_target_pairs={{0,2},{2,0},{1,3},{3,1},{4,6},{6,4},{5,7},{7,5},{8,10},{10,8},{9,1... | collective-permute-start | bytes 6291464 | tf_op jit(solution)/shard_map/ppermute | solution.py:39
  929.8 46.3 %collective-permute-start.11 = (bf16[4,128,2048]{2,1,0:T(8,128)(2,1)}, bf16[4,128,2048]{2,1,0:T(8,128)(2,1)}, u32[]{:S(2)}, u32[]{:S(2)}) collective-permute-start(bf16[4,128,2048]{2,1,0:T(8,128)(2,1)} %pad_maximum_fusion.9.refs_2_), channel_id=1, source_target_pairs={{0,16},{16,0},{1,17},{17,1},{2,18},{18,2},{3,19},{19,3},{4,20},{20... | collective-permute-start | bytes 6291464 | tf_op jit(solution)/shard_map/ppermute | solution.py:39
  1020.2 126.5 %collective-permute-start.15 = (bf16[2,4,1,128,2048]{4,3,1,2,0:T(8,128)(2,1)}, bf16[2,4,1,128,2048]{4,3,1,2,0:T(8,128)(2,1)}, u32[]{:S(2)}, u32[]{:S(2)}) collective-permute-start(bf16[2,4,1,128,2048]{4,3,1,2,0:T(8,128)(2,1)} %dynamic-slice_bitcast_fusion), channel_id=1, source_target_pairs={{0,2},{2,0},{1,3},{3,1},{4,6},{6,4},{5,7},{7,5},{8,10},{10,8},{9,1... | collective-permute-start | bytes 12582920 | tf_op jit(solution)/shard_map/ppermute | solution.py:39
  1048.2 47.6 %collective-permute-start.22 = (bf16[4,1,2,128,1024]{4,3,0,2,1:T(8,128)(2,1)}, bf16[4,1,2,128,1024]{4,3,0,2,1:T(8,128)(2,1)}, u32[]{:S(2)}, u32[]{:S(2)}) collective-permute-start(bf16[4,1,2,128,1024]{4,3,0,2,1:T(8,128)(2,1)} %bitcast.291), channel_id=1, source_target_pairs={{0,16},{16,0},{1,17},{17,1},{2,18},{18,2},{3,19},{19,3},{4,20},{20... | collective-permute-start | bytes 6291464 | tf_op jit(solution)/shard_map/ppermute | solution.py:39
  1064.4 76.6 %collective-permute-start.20 = (bf16[4,1,2,128,1024]{4,3,0,2,1:T(8,128)(2,1)}, bf16[4,1,2,128,1024]{4,3,0,2,1:T(8,128)(2,1)}, u32[]{:S(2)}, u32[]{:S(2)}) collective-permute-start(bf16[4,1,2,128,1024]{4,3,0,2,1:T(8,128)(2,1)} %bitcast.292), channel_id=1, source_target_pairs={{0,16},{16,0},{1,17},{17,1},{2,18},{18,2},{3,19},{19,3},{4,20},{20... | collective-permute-start | bytes 6291464 | tf_op jit(solution)/shard_map/ppermute | solution.py:39
  1068.9 84.0 %collective-permute-start.18 = (bf16[128,2048]{1,0:T(8,128)(2,1)S(1)}, bf16[128,2048]{1,0:T(8,128)(2,1)S(1)}, u32[]{:S(2)}, u32[]{:S(2)}) collective-permute-start(bf16[128,2048]{1,0:T(8,128)(2,1)S(1)} %get-tuple-element.179), channel_id=1, source_target_pairs={{0,12},{4,0},{8,4},{12,8},{1,13},{5,1},{9,5},{13,9},{2,14},{6,2},{... | collective-permute-start | bytes 1572872 | tf_op jit(solution)/shard_map/ppermute | solution.py:86
  1077.5 85.5 %collective-permute-start.17 = (bf16[128,2048]{1,0:T(8,128)(2,1)}, bf16[128,2048]{1,0:T(8,128)(2,1)}, u32[]{:S(2)}, u32[]{:S(2)}) collective-permute-start(bf16[128,2048]{1,0:T(8,128)(2,1)} %get-tuple-element.180), channel_id=1, source_target_pairs={{0,8},{4,12},{8,0},{12,4},{1,9},{5,13},{9,1},{13,5},{2,10},{6,14},... | collective-permute-start | bytes 1572872 | tf_op jit(solution)/shard_map/ppermute | solution.py:86
  1084.8 91.9 %all-to-all-start.1 = ((f32[32,1,384]{2,1,0:T(1,128)}), f32[32,1,384]{2,1,0:T(1,128)S(1)}, u32[]{:S(2)}, u32[]{:S(2)}) async-start(f32[32,1,384]{2,1,0:T(1,128)} %reshape.497), calls=%async_computation.3 | async-start | bytes 98304 | tf_op jit(solution)/shard_map/all_to_all | solution.py:1243
  1095.7 67.3 %collective-permute-start.16 = (bf16[128,2048]{1,0:T(8,128)(2,1)}, bf16[128,2048]{1,0:T(8,128)(2,1)}, u32[]{:S(2)}, u32[]{:S(2)}) collective-permute-start(bf16[128,2048]{1,0:T(8,128)(2,1)} %get-tuple-element.181), channel_id=1, source_target_pairs={{0,4},{4,8},{8,12},{12,0},{1,5},{5,9},{9,13},{13,1},{2,6},{6,10},{... | collective-permute-start | bytes 1572872 | tf_op jit(solution)/shard_map/ppermute | solution.py:86
  1146.7 41.9 %collective-permute-start.21 = (bf16[4,1,128,1024]{3,2,0,1:T(8,128)(2,1)}, bf16[4,1,128,1024]{3,2,0,1:T(8,128)(2,1)}, u32[]{:S(2)}, u32[]{:S(2)}) collective-permute-start(bf16[4,1,128,1024]{3,2,0,1:T(8,128)(2,1)} %dynamic-slice_bitcast_fusion.4), channel_id=1, source_target_pairs={{0,2},{2,0},{1,3},{3,1},{4,6},{6,4},{5,7},{7,5},{8,10},{10,8},{9,1... | collective-permute-start | bytes 3145736 | tf_op jit(solution)/shard_map/ppermute | solution.py:39
  1169.9 46.2 %collective-permute-start.24 = (bf16[4,1,128,2048]{3,2,0,1:T(8,128)(2,1)}, bf16[4,1,128,2048]{3,2,0,1:T(8,128)(2,1)}, u32[]{:S(2)}, u32[]{:S(2)}) collective-permute-start(bf16[4,1,128,2048]{3,2,0,1:T(8,128)(2,1)} %dynamic-slice_bitcast_fusion.1), channel_id=1, source_target_pairs={{0,16},{16,0},{1,17},{17,1},{2,18},{18,2},{3,19},{19,3},{4,20},{20... | collective-permute-start | bytes 6291464 | tf_op jit(solution)/shard_map/ppermute | solution.py:39
  (95 other events, 1062.1 us)
Sparse Core Ops, SparseCore 0:
  169.8 96.1 all-gather.4
  270.5 59.8 all-gather.8
  332.8 54.2 all-gather.6
  491.9 143.7 reduce-scatter.6
  637.8 60.9 reduce-scatter.8
  701.0 60.2 reduce-scatter.12
  763.7 144.4 reduce-scatter.10
  910.5 60.9 reduce-scatter.16
  973.9 178.6 reduce-scatter.14

commit v12 on v11

--- a/solution.py
+++ b/solution.py
@@ -1186,14 +1186,14 @@
     dqpre, dkpre, dvpre = attend_back(
         query, keys, values, mixed, dmixed, cosine, sine, seg_row, seg_col, heads, down_sum_b, up_b, *stages[0]
     )
-    up_a = rows_product(expert_in, after(dupre_a, dqpre, *stages[1]))
+    dqkv = jnp.concatenate([dqpre, dkpre, dvpre], axis=1)
+    dhidden_part = product_t(dqkv, weight_in).astype(bf16)
+    up_a = rows_product(expert_in, after(dupre_a, dhidden_part, *stages[1]))
     output = (residual + mixture).astype(bf16)
     out_grad = t_product(mixed_full, after(dbranch_here, up_a, output)).astype(bf16)
     dkv = jnp.concatenate([dkpre, dvpre], axis=1)
     kv_grad = t_product(hidden_full, after(dkv, out_grad)).astype(bf16)
     query_grad = t_product(hidden_full, after(dqpre, out_grad)).astype(bf16)
-    dqkv = after(jnp.concatenate([dqpre, dkpre, dvpre], axis=1), kv_grad, query_grad)
-    dhidden_part = product_t(dqkv, weight_in).astype(bf16)
     dhidden_one = chip_scatter(
         dhidden_part.reshape(seq_n, parts * piece, width), 1, parts
     )

time: 1370 us -> 1350 us (0.985)
  waiting for transfers between devices: 150 us -> 132 us
    ppermute x23, waiting for transfers between devices: 124 us -> 106 us  [swap(): return lax.ppermute(a, axis, [(0, 1), (1, 0)])]
    unnamed x169 -> x173, local copies, waits for them, and re-layouts: 43.7 us -> 52.5 us
  transfers between devices with their start and end apart: 37 -> 37, of which waited for: 16 -> 14; matrix products, arithmetic and copies ran while one was open for 29% -> 28% of each run, Pallas kernels for 32% -> 33%
where the time goes in v12:
time: 1350 us; the launch traced here: 1340 us
  Pallas kernels  659 us (49%)
  matrix products  214 us (16%)
  waiting for transfers between devices  132 us (10%)
  other arithmetic  124 us (9%)
  local copies, waits for them, and re-layouts  122 us (9%)
  blocking collectives  44.8 us (3%)
  starting transfers between devices  29.9 us (2%)
  between operations  15.4 us (1%)
    pallas_call x1, Pallas kernels, first_transfers(): pl.pallas_call(first_kernel, in_specs=[held] * 7, out_specs=[held] * 4, o...  162 us
    dot_general x10, matrix products, t_product(): lax.dot_general(a, b, (((0,), (0,)), ((), ())), preferred_element_type=f32)  153 us
    pallas_call x3, Pallas kernels, expert_units(): pl.pallas_call(functools.partial(units_kernel, chunk), grid=(units // til...  135 us
    pallas_call x1, Pallas kernels, last_transfers(): pl.pallas_call(last_kernel, in_specs=[held] * 3, out_specs=[held] * 2, ou...  120 us
    ppermute x23, waiting for transfers between devices, swap(): return lax.ppermute(a, axis, [(0, 1), (1, 0)])  106 us
    pallas_call x2, Pallas kernels, expert_input_grad(): pl.pallas_call(functools.partial(input_kernel, cut), grid=(width // n, ro...  78 us
    unnamed x173, local copies, waits for them, and re-layouts  52.5 us
    all_gather x1, blocking collectives, on_device(): lax.all_gather(small, EVERY, axis=0, tiled=True)  44.8 us
  transfers between devices with their start and end apart: 37, of which 14 were waited for; matrix products, arithmetic and copies ran while one was open for 28% of the time, Pallas kernels for 33%

profile of v12, /device:TPU:1, one launch (start us, length us, event | category | flops | bytes accessed | tf_op | source)
XLA Modules:
  0.0 1342.3 jit_solution(2808237133663472236)
XLA Ops:
  7.2 162.4 %first_transfers.1 = (bf16[2,4,2,128,4096]{4,3,2,1,0:T(8,128)(2,1)}, bf16[4,128,2048]{2,1,0:T(8,128)(2,1)}, bf16[4,128,2048]{2,1,0:T(8,128)(2,1)}, s32[2,2,1024]{2,1,0:T(2,128)}) custom-call(bf16[64,2048]{1,0:T(8,128)(2,1)} %query.1, bf16[64,2048]{1,0:T(8,128)(2,1)} %key.1, bf16[64,2048]{1,0:T(8,128)(2,1)} %value.1, bf16[64,2048]{1,0:T(8,128)(2,1)} %output.1, ...), custom_call_target="tpu_custom_call" | custom-call | bytes 16777216 | tf_op jit(solution)/shard_map/first_transfers/pallas_call | solution.py:364
  183.8 19.9 %fusion.4.qp.kp.vp = f32[1024,3072]{1,0:T(8,128)} fusion(bf16[1024,2048]{1,0:T(8,128)(2,1)S(1)} %bitcast.336, bf16[2048,4096]{1,0:T(8,128)(2,1)} %bitcast.358), kind=kOutput, calls=%fused_computation.6 | convolution fusion | flops 12884901888 | bytes 29360128 | tf_op jit(solution)/shard_map/dot_general | solution.py:27
  203.7 27.9 %attend.1 = (bf16[1024,1024]{1,0:T(8,128)(2,1)S(1)}, bf16[1024,1024]{1,0:T(8,128)(2,1)S(1)}, bf16[1024,1024]{1,0:T(8,128)(2,1)}, bf16[1024,1024]{1,0:T(8,128)(2,1)}) custom-call(f32[1024,3072]{1,0:T(8,128)} %fusion.4.qp.kp.vp, f32[1024,3072]{1,0:T(8,128)} %fusion.4.qp.kp.vp, f32[1024,3072]{1,0:T(8,128)} %fusion.4.qp.kp.vp, ...), custom_call_target="tpu_custom_call" | custom-call | flops 2684354560 | bytes 20971520 | tf_op jit(solution)/shard_map/attend/pallas_call | solution.py:628
  272.3 44.8 %all-gather = s32[32,4,256]{2,1,0:T(4,128)S(1)} all-gather(s32[1,4,256]{2,1,0:T(4,128)} %bitcast.350), channel_id=1, replica_groups=mesh['dp'=2,'seq'=4,'r'=1,'y'=2,'core'=2] {'dp','seq','r','y','core'}, dimensions={0}, use_global_device_ids=true | all-gather | bytes 135168 | tf_op jit(solution)/shard_map/all_gather | solution.py:1093
  333.6 13.4 %dispatch.2 = (bf16[16,160,2048]{2,1,0:T(8,128)(2,1)}, bf16[16,160,2048]{2,1,0:T(8,128)(2,1)}, f32[16,256,1]{2,1,0:T(8,128)S(1)}) custom-call(s32[4]{0:T(128)S(1)} %pad_add_fusion.me, bf16[4,2,2,128,2048]{4,3,2,1,0:T(8,128)(2,1)S(1)} %bitcast.295, bf16[4,2,4,128,2048]{4,3,2,1,0:T(8,128)(2,1)} %bitcast.299, s32[16,1,256]{2,1,0:T(1,128)S(1)} %broadcast_in_dim.45.slot, ...), custom_call_target="tpu_custom_call" | custom-call | flops 3758096384 | bytes 27262976 | tf_op jit(solution)/shard_map/dispatch/pallas_call | solution.py:823
  348.4 47.7 %expert_units.3 = (bf16[2560,2048]{1,0:T(8,128)(2,1)}, bf16[2560,2048]{1,0:T(8,128)(2,1)}, bf16[2560,2048]{1,0:T(8,128)(2,1)}) custom-call(bf16[2560,2048]{1,0:T(8,128)(2,1)} %bitcast.314, bf16[2560,2048]{1,0:T(8,128)(2,1)} %bitcast.321, bf16[2048,2816]{1,0:T(8,128)(2,1)} %bitcast.362, bf16[2048,2816]{1,0:T(8,128)(2,1)} %bitcast.367, ...), custom_call_target="tpu_custom_call" | custom-call | flops 32212254720 | bytes 51380224 | tf_op jit(solution)/shard_map/expert_units/pallas_call | solution.py:733
  415.0 47.8 %expert_units.4 = (bf16[2560,2048]{1,0:T(8,128)(2,1)}, bf16[2560,2048]{1,0:T(8,128)(2,1)}, bf16[2560,2048]{1,0:T(8,128)(2,1)}) custom-call(bf16[2560,2048]{1,0:T(8,128)(2,1)} %bitcast.315, bf16[2560,2048]{1,0:T(8,128)(2,1)} %bitcast.322, bf16[2048,2816]{1,0:T(8,128)(2,1)} %bitcast.363, ...), custom_call_target="tpu_custom_call", output_to_operand_aliasing={{0}: (5, {}), {1}: (6, {}), {2}: (7, {})} | custom-call | flops 32212254720 | bytes 51380224 | tf_op jit(solution)/shard_map/expert_units/pallas_call | solution.py:733
  462.8 28.9 %convolution_convert_fusion.3.rest_0_ = bf16[2048,2048]{1,0:T(8,128)(2,1)} fusion(bf16[2560,2048]{1,0:T(8,128)(2,1)} %bitcast.323, bf16[2560,2048]{1,0:T(8,128)(2,1)} %get-tuple-element.55.units_a), kind=kOutput, calls=%fused_computation.17 | convolution fusion | flops 21479030784 | bytes 29360128 | tf_op jit(solution)/shard_map/dot_general | solution.py:35
  492.4 39.6 %expert_units.5 = (bf16[2560,768]{1,0:T(8,128)(2,1)}, bf16[2560,768]{1,0:T(8,128)(2,1)}, bf16[2560,768]{1,0:T(8,128)(2,1)}) custom-call(bf16[2560,2048]{1,0:T(8,128)(2,1)} %bitcast.316, bf16[2560,2048]{1,0:T(8,128)(2,1)} %bitcast.324, bf16[2048,2816]{1,0:T(8,128)(2,1)} %bitcast.364, bf16[2048,2816]{1,0:T(8,128)(2,1)} %bitcast.369, ...), custom_call_target="tpu_custom_call" | custom-call | flops 24159191040 | bytes 42205184 | tf_op jit(solution)/shard_map/expert_units/pallas_call | solution.py:733
  532.0 13.6 %convolution_convert_fusion.9.rest_0_ = bf16[2048,768]{1,0:T(8,128)(2,1)} fusion(bf16[2560,2048]{1,0:T(8,128)(2,1)} %bitcast.325, bf16[2560,768]{1,0:T(8,128)(2,1)} %get-tuple-element.56.units_b), kind=kOutput, calls=%fused_computation.78 | convolution fusion | flops 8054636544 | bytes 17563648 | tf_op jit(solution)/shard_map/dot_general | solution.py:35
  545.7 39.0 %expert_input_grad.2.rest_0_ = bf16[2560,1024]{1,0:T(8,128)(2,1)} custom-call(bf16[2560,2048]{1,0:T(8,128)(2,1)} %get-tuple-element.57.dgate_a.refs_0_, bf16[2560,768]{1,0:T(8,128)(2,1)} %get-tuple-element.58.dgate_b.refs_0_, bf16[2560,2048]{1,0:T(8,128)(2,1)} %get-tuple-element.59.dup_a.refs_0_, bf16[2560,768]{1,0:T(8,128)(2,1)} %get-tuple-element.60.dup_b.refs_0_, ...), custom_call_target="tpu_custom_call" | custom-call | flops 29527900160 | bytes 45613056 | tf_op jit(solution)/shard_map/expert_input_grad/pallas_call | solution.py:961
  584.7 39.0 %expert_input_grad.3 = bf16[2560,1024]{1,0:T(8,128)(2,1)} custom-call(bf16[2560,2048]{1,0:T(8,128)(2,1)} %get-tuple-element.57.dgate_a.refs_0_, bf16[2560,768]{1,0:T(8,128)(2,1)} %get-tuple-element.58.dgate_b.refs_0_, bf16[2560,2048]{1,0:T(8,128)(2,1)} %get-tuple-element.59.dup_a.refs_0_, bf16[2560,768]{1,0:T(8,128)(2,1)} %get-tuple-element.60.dup_b.refs_0_, ...), custom_call_target="tpu_custom_call" | custom-call | flops 29527900160 | bytes 45613056 | tf_op jit(solution)/shard_map/expert_input_grad/pallas_call | solution.py:961
  626.2 13.1 collect.1.refs_1_
  648.1 13.6 %convolution_convert_fusion.7 = bf16[2048,768]{1,0:T(8,128)(2,1)} fusion(bf16[2560,2048]{1,0:T(8,128)(2,1)} %bitcast.317, bf16[2560,768]{1,0:T(8,128)(2,1)} %after.31), kind=kOutput, calls=%fused_computation.76 | convolution fusion | flops 8054636544 | bytes 17563648 | tf_op jit(solution)/shard_map/dot_general | solution.py:35
  675.7 29.0 %convolution_convert_fusion.2.rest_0_.refs_1_ = bf16[2048,2048]{1,0:T(8,128)(2,1)} fusion(bf16[2560,2048]{1,0:T(8,128)(2,1)} %bitcast.318, bf16[2560,2048]{1,0:T(8,128)(2,1)} %after.18), kind=kOutput, calls=%fused_computation.16 | convolution fusion | flops 21479030784 | bytes 29360128 | tf_op jit(solution)/shard_map/dot_general | solution.py:35
  710.4 12.8 convolution_convert_fusion.8.refs_1_.rest_1_
  743.9 40.5 %expert_down.1 = bf16[2560,2048]{1,0:T(8,128)(2,1)} custom-call(bf16[2560,2048]{1,0:T(8,128)(2,1)} %get-tuple-element.55.units_a, bf16[2560,768]{1,0:T(8,128)(2,1)S(1)} %copy-done.25, bf16[2816,2048]{1,0:T(8,128)(2,1)} %bitcast.375, bf16[2048,2048]{1,0:T(8,128)(2,1)} %convolution_convert_fusion.2.rest_0_.refs_1_), custom_call_target="tpu_custom_call" | custom-call | flops 29527900160 | bytes 36438016 | tf_op jit(solution)/shard_map/expert_down/pallas_call | solution.py:925
  784.5 24.3 %combine.1 = (bf16[2,2,2,4,128,2048]{5,4,3,2,1,0:T(8,128)(2,1)}, f32[16,256,1]{2,1,0:T(8,128)S(1)}) custom-call(s32[4]{0:T(128)S(1)} %pad_add_fusion.me, bf16[16,160,2048]{2,1,0:T(8,128)(2,1)} %bitcast.313, s32[16,256,1]{2,1,0:T(8,128)S(1)} %copy.158.slot, f32[16,256,1]{2,1,0:T(8,128)S(1)} %copy-done.4, bf16[4,2,4,128,2048]{4,3,2,1,0:T(8,128)(2,1)} %bitcast.301), custom_call_target="tpu_custom_call" | custom-call | flops 2684354560 | bytes 44040192 | tf_op jit(solution)/shard_map/combine/pallas_call | solution.py:900
  881.2 31.8 %attend_back.1 = (bf16[1024,1024]{1,0:T(8,128)(2,1)S(1)}, bf16[1024,1024]{1,0:T(8,128)(2,1)}, bf16[1024,1024]{1,0:T(8,128)(2,1)}) custom-call(bf16[1024,1024]{1,0:T(8,128)(2,1)} %copy-done.23, bf16[1024,1024]{1,0:T(8,128)(2,1)} %copy-done.24, bf16[1024,1024]{1,0:T(8,128)(2,1)} %get-tuple-element.66.v, bf16[1024,1024]{1,0:T(8,128)(2,1)} %get-tuple-element.45.mixed, ...), custom_call_target="tpu_custom_call" | custom-call | flops 6710886400 | bytes 16777216 | tf_op jit(solution)/shard_map/attend_back/pallas_call | solution.py:688
  914.4 20.7 %fusion.29.refs_1_ = bf16[1024,2048]{1,0:T(8,128)(2,1)} fusion(bf16[2048,4096]{1,0:T(8,128)(2,1)} %bitcast.361, bf16[1024,1024]{1,0:T(8,128)(2,1)} %get-tuple-element.68, bf16[1024,1024]{1,0:T(8,128)(2,1)} %get-tuple-element.67, bf16[1024,1024]{1,0:T(8,128)(2,1)} %copy-done.17), kind=kOutput, calls=%fused_computation.72 | convolution fusion | flops 12905873408 | bytes 23068672 | tf_op jit(solution)/shard_map/dot_general | solution.py:31
  946.3 29.3 %convolution_convert_fusion.1.refs_1_ = bf16[2048,2048]{1,0:T(8,128)(2,1)} fusion(bf16[2560,2048]{1,0:T(8,128)(2,1)} %bitcast.320, bf16[2560,2048]{1,0:T(8,128)(2,1)} %after.23), kind=kOutput, calls=%fused_computation.15 | convolution fusion | flops 21479030784 | bytes 29360128 | tf_op jit(solution)/shard_map/dot_general | solution.py:35
  1065.7 20.6 %collective-permute-done.22 = bf16[4,1,2,128,1024]{4,3,0,2,1:T(8,128)(2,1)} collective-permute-done((bf16[4,1,2,128,1024]{4,3,0,2,1:T(8,128)(2,1)}, bf16[4,1,2,128,1024]{4,3,0,2,1:T(8,128)(2,1)}, u32[]{:S(2)}, u32[]{:S(2)}) %collective-permute-start.22) | collective-permute-done | bytes 2097184 | tf_op jit(solution)/shard_map/ppermute | solution.py:39
  1091.5 39.8 %collective-permute-done.20 = bf16[4,1,2,128,1024]{4,3,0,2,1:T(8,128)(2,1)} collective-permute-done((bf16[4,1,2,128,1024]{4,3,0,2,1:T(8,128)(2,1)}, bf16[4,1,2,128,1024]{4,3,0,2,1:T(8,128)(2,1)}, u32[]{:S(2)}, u32[]{:S(2)}) %collective-permute-start.20) | collective-permute-done | bytes 2097184 | tf_op jit(solution)/shard_map/ppermute | solution.py:39
  1196.2 120.2 %last_transfers.1 = (bf16[2,2,64,4096]{3,2,1,0:T(8,128)(2,1)S(1)}, bf16[2,256,2048]{2,1,0:T(8,128)(2,1)S(1)}) custom-call(bf16[4,128,4096]{2,1,0:T(8,128)(2,1)S(1)} %maximum_bitcast_fusion.1.grads, bf16[4,128,2048]{2,1,0:T(8,128)(2,1)S(1)} %bitcast.296, bf16[2,256,2048]{2,1,0:T(8,128)(2,1)S(1)} %pad_maximum_fusion.12.before), custom_call_target="tpu_custom_call" | custom-call | bytes 8388608 | tf_op jit(solution)/shard_map/last_transfers/pallas_call | solution.py:565
  (390 shorter events, 407.3 us)
Async XLA Ops:
  7.2 260.0 %all-gather.5.cloned.1.call-start = ((), (), s32[]{:S(2)}) async-start(), calls=%async_computation.8 | async-start | bytes 18874368 | tf_op jit(solution)/shard_map/all_gather | solution.py:1069
  169.7 160.6 %all-gather.9.cloned.1.call-start = ((), (), s32[]{:S(2)}) async-start(), calls=%async_computation.10 | async-start | bytes 9437184 | tf_op jit(solution)/shard_map/all_gather | solution.py:1090
  270.3 125.8 %all-gather.7.cloned.1.call-start = ((), (), s32[]{:S(2)}) async-start(), calls=%async_computation.9 | async-start | bytes 9437184 | tf_op jit(solution)/shard_map/all_gather | solution.py:1090
  271.0 404.7 %reduce-scatter.7.cloned.1.call-start = ((), (), s32[]{:S(2)}) async-start(), calls=%async_computation.11 | async-start | bytes 10485760 | tf_op jit(solution)/shard_map/reduce_scatter | solution.py:1129
  491.7 388.3 %reduce-scatter.9.cloned.1.call-start = ((), (), s32[]{:S(2)}) async-start(), calls=%async_computation.12 | async-start | bytes 3932160 | tf_op jit(solution)/shard_map/reduce_scatter | solution.py:1129
  545.7 618.6 %reduce-scatter.13.cloned.1.call-start = ((), (), s32[]{:S(2)}) async-start(), calls=%async_computation.14 | async-start | bytes 3932160 | tf_op jit(solution)/shard_map/reduce_scatter | solution.py:1129
  661.7 502.6 %reduce-scatter.11.cloned.1.call-start = ((), (), s32[]{:S(2)}) async-start(), calls=%async_computation.13 | async-start | bytes 10485760 | tf_op jit(solution)/shard_map/reduce_scatter | solution.py:1129
  739.1 83.5 %collective-permute-start.7 = (bf16[4,128,2048]{2,1,0:T(8,128)(2,1)}, bf16[4,128,2048]{2,1,0:T(8,128)(2,1)}, u32[]{:S(2)}, u32[]{:S(2)}) collective-permute-start(bf16[4,128,2048]{2,1,0:T(8,128)(2,1)} %pad_maximum_fusion.7), channel_id=1, source_target_pairs={{0,2},{2,0},{1,3},{3,1},{4,6},{6,4},{5,7},{7,5},{8,10},{10,8},{9,1... | collective-permute-start | bytes 6291464 | tf_op jit(solution)/shard_map/ppermute | solution.py:39
  741.1 81.6 %collective-permute-start.5 = (bf16[4,128,2048]{2,1,0:T(8,128)(2,1)}, bf16[4,128,2048]{2,1,0:T(8,128)(2,1)}, u32[]{:S(2)}, u32[]{:S(2)}) collective-permute-start(bf16[4,128,2048]{2,1,0:T(8,128)(2,1)} %after.21), channel_id=1, source_target_pairs={{0,16},{16,0},{1,17},{17,1},{2,18},{18,2},{3,19},{19,3},{4,20},{20... | collective-permute-start | bytes 6291464 | tf_op jit(solution)/shard_map/ppermute | solution.py:39
  818.0 512.6 %reduce-scatter.17.cloned.1.call-start = ((), (), s32[]{:S(2)}) async-start(), calls=%async_computation.16 | async-start | bytes 3932160 | tf_op jit(solution)/shard_map/reduce_scatter | solution.py:1129
  859.5 471.2 %reduce-scatter.15.cloned.1.call-start = ((), (), s32[]{:S(2)}) async-start(), calls=%async_computation.15 | async-start | bytes 10485760 | tf_op jit(solution)/shard_map/reduce_scatter | solution.py:1129
  879.9 59.0 %collective-permute-start.12 = (bf16[2,128,2048]{2,1,0:T(8,128)(2,1)}, bf16[2,128,2048]{2,1,0:T(8,128)(2,1)S(1)}, u32[]{:S(2)}, u32[]{:S(2)}) collective-permute-start(bf16[2,128,2048]{2,1,0:T(8,128)(2,1)} %get-tuple-element.145), channel_id=1, source_target_pairs={{0,16},{16,0},{1,17},{17,1},{2,18},{18,2},{3,19},{19,3},{4,20},{20... | collective-permute-start | bytes 3145736 | tf_op jit(solution)/shard_map/ppermute | solution.py:39
  880.1 58.9 %collective-permute-start.10 = (bf16[2,128,2048]{2,1,0:T(8,128)(2,1)}, bf16[2,128,2048]{2,1,0:T(8,128)(2,1)}, u32[]{:S(2)}, u32[]{:S(2)}) collective-permute-start(bf16[2,128,2048]{2,1,0:T(8,128)(2,1)} %get-tuple-element.146), channel_id=1, source_target_pairs={{0,2},{2,0},{1,3},{3,1},{4,6},{6,4},{5,7},{7,5},{8,10},{10,8},{9,1... | collective-permute-start | bytes 3145736 | tf_op jit(solution)/shard_map/ppermute | solution.py:39
  938.1 54.7 %collective-permute-start.25 = (bf16[4,128,2048]{2,1,0:T(8,128)(2,1)}, bf16[4,128,2048]{2,1,0:T(8,128)(2,1)}, u32[]{:S(2)}, u32[]{:S(2)}) collective-permute-start(bf16[4,128,2048]{2,1,0:T(8,128)(2,1)} %constant_dynamic-slice_fusion), channel_id=1, source_target_pairs={{0,1},{1,0},{2,3},{3,2},{4,5},{5,4},{6,7},{7,6},{8,9},{9,8},{10,11... | collective-permute-start | bytes 6291464 | tf_op jit(solution)/shard_map/ppermute | solution.py:39
  941.9 51.0 %collective-permute-start.13 = (bf16[4,128,2048]{2,1,0:T(8,128)(2,1)S(1)}, bf16[4,128,2048]{2,1,0:T(8,128)(2,1)}, u32[]{:S(2)}, u32[]{:S(2)}) collective-permute-start(bf16[4,128,2048]{2,1,0:T(8,128)(2,1)S(1)} %pad_maximum_fusion.9.refs_3_), channel_id=1, source_target_pairs={{0,2},{2,0},{1,3},{3,1},{4,6},{6,4},{5,7},{7,5},{8,10},{10,8},{9,1... | collective-permute-start | bytes 6291464 | tf_op jit(solution)/shard_map/ppermute | solution.py:39
  944.9 48.0 %collective-permute-start.11 = (bf16[4,128,2048]{2,1,0:T(8,128)(2,1)}, bf16[4,128,2048]{2,1,0:T(8,128)(2,1)}, u32[]{:S(2)}, u32[]{:S(2)}) collective-permute-start(bf16[4,128,2048]{2,1,0:T(8,128)(2,1)} %pad_maximum_fusion.8.refs_2_), channel_id=1, source_target_pairs={{0,16},{16,0},{1,17},{17,1},{2,18},{18,2},{3,19},{19,3},{4,20},{20... | collective-permute-start | bytes 6291464 | tf_op jit(solution)/shard_map/ppermute | solution.py:39
  1029.7 106.7 %collective-permute-start.15 = (bf16[2,4,1,128,2048]{4,3,1,2,0:T(8,128)(2,1)}, bf16[2,4,1,128,2048]{4,3,1,2,0:T(8,128)(2,1)}, u32[]{:S(2)}, u32[]{:S(2)}) collective-permute-start(bf16[2,4,1,128,2048]{4,3,1,2,0:T(8,128)(2,1)} %dynamic-slice_bitcast_fusion), channel_id=1, source_target_pairs={{0,2},{2,0},{1,3},{3,1},{4,6},{6,4},{5,7},{7,5},{8,10},{10,8},{9,1... | collective-permute-start | bytes 12582920 | tf_op jit(solution)/shard_map/ppermute | solution.py:39
  1039.1 47.2 %collective-permute-start.22 = (bf16[4,1,2,128,1024]{4,3,0,2,1:T(8,128)(2,1)}, bf16[4,1,2,128,1024]{4,3,0,2,1:T(8,128)(2,1)}, u32[]{:S(2)}, u32[]{:S(2)}) collective-permute-start(bf16[4,1,2,128,1024]{4,3,0,2,1:T(8,128)(2,1)} %bitcast.290), channel_id=1, source_target_pairs={{0,16},{16,0},{1,17},{17,1},{2,18},{18,2},{3,19},{19,3},{4,20},{20... | collective-permute-start | bytes 6291464 | tf_op jit(solution)/shard_map/ppermute | solution.py:39
  1046.2 85.0 %collective-permute-start.20 = (bf16[4,1,2,128,1024]{4,3,0,2,1:T(8,128)(2,1)}, bf16[4,1,2,128,1024]{4,3,0,2,1:T(8,128)(2,1)}, u32[]{:S(2)}, u32[]{:S(2)}) collective-permute-start(bf16[4,1,2,128,1024]{4,3,0,2,1:T(8,128)(2,1)} %bitcast.291), channel_id=1, source_target_pairs={{0,16},{16,0},{1,17},{17,1},{2,18},{18,2},{3,19},{19,3},{4,20},{20... | collective-permute-start | bytes 6291464 | tf_op jit(solution)/shard_map/ppermute | solution.py:39
  1047.8 121.3 %all-to-all-start.1 = ((f32[32,1,384]{2,1,0:T(1,128)}), f32[32,1,384]{2,1,0:T(1,128)S(1)}, u32[]{:S(2)}, u32[]{:S(2)}) async-start(f32[32,1,384]{2,1,0:T(1,128)} %reshape.497), calls=%async_computation.3 | async-start | bytes 98304 | tf_op jit(solution)/shard_map/all_to_all | solution.py:1243
  1054.9 92.1 %collective-permute-start.18 = (bf16[128,2048]{1,0:T(8,128)(2,1)}, bf16[128,2048]{1,0:T(8,128)(2,1)S(1)}, u32[]{:S(2)}, u32[]{:S(2)}) collective-permute-start(bf16[128,2048]{1,0:T(8,128)(2,1)} %get-tuple-element.180), channel_id=1, source_target_pairs={{0,12},{4,0},{8,4},{12,8},{1,13},{5,1},{9,5},{13,9},{2,14},{6,2},{... | collective-permute-start | bytes 1572872 | tf_op jit(solution)/shard_map/ppermute | solution.py:86
  1058.1 99.3 %collective-permute-start.17 = (bf16[128,2048]{1,0:T(8,128)(2,1)}, bf16[128,2048]{1,0:T(8,128)(2,1)S(1)}, u32[]{:S(2)}, u32[]{:S(2)}) collective-permute-start(bf16[128,2048]{1,0:T(8,128)(2,1)} %get-tuple-element.181), channel_id=1, source_target_pairs={{0,8},{4,12},{8,0},{12,4},{1,9},{5,13},{9,1},{13,5},{2,10},{6,14},... | collective-permute-start | bytes 1572872 | tf_op jit(solution)/shard_map/ppermute | solution.py:86
  1086.3 71.8 %collective-permute-start.16 = (bf16[128,2048]{1,0:T(8,128)(2,1)}, bf16[128,2048]{1,0:T(8,128)(2,1)}, u32[]{:S(2)}, u32[]{:S(2)}) collective-permute-start(bf16[128,2048]{1,0:T(8,128)(2,1)} %get-tuple-element.182), channel_id=1, source_target_pairs={{0,4},{4,8},{8,12},{12,0},{1,5},{5,9},{9,13},{13,1},{2,6},{6,10},{... | collective-permute-start | bytes 1572872 | tf_op jit(solution)/shard_map/ppermute | solution.py:86
  1146.9 45.3 %collective-permute-start.24 = (bf16[4,1,128,2048]{3,2,0,1:T(8,128)(2,1)}, bf16[4,1,128,2048]{3,2,0,1:T(8,128)(2,1)}, u32[]{:S(2)}, u32[]{:S(2)}) collective-permute-start(bf16[4,1,128,2048]{3,2,0,1:T(8,128)(2,1)} %dynamic-slice_bitcast_fusion.1), channel_id=1, source_target_pairs={{0,16},{16,0},{1,17},{17,1},{2,18},{18,2},{3,19},{19,3},{4,20},{20... | collective-permute-start | bytes 6291464 | tf_op jit(solution)/shard_map/ppermute | solution.py:39
  (97 other events, 1169.6 us)
Sparse Core Ops, SparseCore 0:
  169.8 96.0 all-gather.4
  270.4 59.7 all-gather.8
  332.7 54.2 all-gather.6
  491.9 143.7 reduce-scatter.6
  637.8 60.9 reduce-scatter.8
  701.0 60.2 reduce-scatter.12
  763.6 144.4 reduce-scatter.10
  910.4 60.9 reduce-scatter.16
  975.8 184.0 reduce-scatter.14
